TPU v7x, 32 devices: a whole 2x2x4 slice. The times are simulated.
32 devices in a mesh: seq: 8 (over z, y), head: 4 (over x, core).
Axes of the slice: x: 2, y: 2, z: 4, core: 2. Of those that a mesh axis runs over, the one named last changes fastest.
Arguments:
- tokens: bfloat16 [6, 2048, 2048], P(None, 'seq'), may hold values from -6 to 6
- doc_reset: int32 [6, 2048], P(None, 'seq'), may hold values from 0 to 1, as said below
- gain_attn: bfloat16 [2048], P('seq'), may hold values from 0.5 to 1.5
- gain_ffn: bfloat16 [2048], P('seq'), may hold values from 0.5 to 1.5
- query_weight: bfloat16 [2048, 256], P('seq', 'head'), may hold values from -0.125 to 0.125
- key_weight: bfloat16 [2048, 256], P('seq', 'head'), may hold values from -0.125 to 0.125
- value_weight: bfloat16 [2048, 2048], P('seq', 'head'), may hold values from -0.125 to 0.125
- out_weight: bfloat16 [2048, 2048], P('head', 'seq'), may hold values from -3 to 3
- gate_weight: bfloat16 [2048, 5632], P('seq', 'head'), may hold values from -0.125 to 0.125
- up_weight: bfloat16 [2048, 5632], P('seq', 'head'), may hold values from -0.125 to 0.125
- down_weight: bfloat16 [5632, 2048], P('head', 'seq'), may hold values from -0.078125 to 0.078125
- grad_out: bfloat16 [6, 2048, 2048], P(None, 'seq'), may hold values from -6 to 6
Outputs:
- block_out: bfloat16 [6, 2048, 2048], P(None, 'seq')
- grad_tokens: float32 [6, 2048, 2048], P(None, 'seq')
- grad_gain_attn: float32 [2048], P('seq')
- grad_gain_ffn: float32 [2048], P('seq')
- grad_query_weight: float32 [2048, 256], P('seq', 'head')
- grad_key_weight: float32 [2048, 256], P('seq', 'head')
- grad_value_weight: float32 [2048, 2048], P('seq', 'head')
- grad_out_weight: float32 [2048, 2048], P('head', 'seq')
- grad_gate_weight: float32 [2048, 5632], P('seq', 'head')
- grad_up_weight: float32 [2048, 5632], P('seq', 'head')
- grad_down_weight: float32 [5632, 2048], P('head', 'seq')
Inputs may be any that keep to these rules, and one draw needn't show every extreme that they name: `doc_reset`: 1 marks a token that begins a new document; the first token of a row always begins one and is marked 0. Each micro-batch of 3 rows holds a row without any mark, and every other row has 1 to 4 marks.
All inputs are finite; a program needn't handle non-finite values.
Results may differ from a plain program's by a relative error of at most 0.017.
Values may be sent and summed in bfloat16 or wider, within the bound.
No kernel may reach another device: no remote copies, remote signals or barrier semaphores. Data moves between devices by JAX's collectives and lax.ppermute only.
A program may use at most 448 MiB of HBM per device.

v0:
```python
import math

import jax
import jax.numpy as jnp
from jax import lax
from jax.sharding import PartitionSpec as P

FEAT = 16
VHEAD = 128
MB = 2
ROWS_MB = 3


epsilon = 1e-06
highest = lax.Precision.HIGHEST
quad_scale = 0.25 / math.sqrt(2.0)


def carried_in(value, axis, join, neutral):
    count, mine = (lax.axis_size(axis), lax.axis_index(axis))
    pieces = jax.tree.map(lambda part: lax.all_gather(part, axis), value)
    subtotal = jax.tree.map(
        lambda part, zero: jnp.full_like(part, 0) + jnp.asarray(zero, part.dtype), value, neutral
    )

    def hop(position, subtotal):
        longer = join(subtotal, jax.tree.map(lambda part: part[position], pieces))
        return jax.tree.map(lambda new, old: jnp.where(position < mine, new, old), longer, subtotal)

    return lax.fori_loop(0, count - 1, hop, subtotal)


def carried_in_2(value, axis, combine, identity):
    length, position = (lax.axis_size(axis), lax.axis_index(axis))
    everything = jax.tree.map(
        lambda part, kind: lax.all_gather(part.astype(kind), axis),
        value,
        jax.tree.map(lambda a: jnp.bfloat16 if a.dtype == jnp.float32 else a.dtype, value),
    )
    start = jax.tree.map(
        lambda part, zero: jnp.broadcast_to(jnp.asarray(zero, part.dtype), part.shape),
        value,
        identity,
    )

    def hop(k, before):
        at = length - 1 - k
        reached = at > position
        new = combine(
            before, jax.tree.map(lambda part, own: part[at].astype(own.dtype), everything, value)
        )
        return jax.tree.map(lambda a, b: jnp.where(reached, a, b), new, before)

    return lax.fori_loop(0, length, hop, start)


def exact_product(pattern, left_operand, right_operand):
    return jnp.einsum(pattern, left_operand, right_operand, precision=highest)


def contract_first(left_operand, right_operand):
    return lax.dot_general(
        left_operand, right_operand, (((0,), (0,)), ((), ())), preferred_element_type=jnp.float32
    )


def contract_last(left_operand, right_operand):
    return lax.dot_general(
        left_operand, right_operand, (((1,), (1,)), ((), ())), preferred_element_type=jnp.float32
    )


def taylor_map(vectors):
    unit_col = jnp.ones(vectors.shape[:-1] + (1,), jnp.float32)
    outer_terms = (vectors[..., :, None] * vectors[..., None, :]).reshape(
        vectors.shape[:-1] + (vectors.shape[-1] * vectors.shape[-1],)
    )
    return jnp.concatenate([unit_col, 0.5 * vectors, outer_terms * quad_scale], axis=-1)


def heads_first(flat_rows, row_count, length, heads, width):
    return flat_rows.reshape(row_count, length, heads, width).transpose(0, 2, 1, 3)


def heads_last(split_rows):
    row_count, heads, length, width = split_rows.shape
    return split_rows.transpose(0, 2, 1, 3).reshape(row_count * length, heads * width)


def join_state(earlier, later_part):
    keep_old = 1.0 - later_part[2]
    return (
        later_part[0] + keep_old[:, None, None, None] * earlier[0],
        later_part[1] + keep_old[:, None, None] * earlier[1],
        jnp.maximum(earlier[2], later_part[2]),
    )


def gather_weights(
    gain_attn,
    gain_ffn,
    query_weight,
    key_weight,
    value_weight,
    out_weight,
    gate_weight,
    up_weight,
    down_weight,
):
    return (
        lax.all_gather(gain_attn, "seq", axis=0, tiled=True),
        lax.all_gather(gain_ffn, "seq", axis=0, tiled=True),
        lax.all_gather(query_weight, "seq", axis=0, tiled=True),
        lax.all_gather(key_weight, "seq", axis=0, tiled=True),
        lax.all_gather(value_weight, "seq", axis=0, tiled=True),
        lax.all_gather(out_weight, "seq", axis=1, tiled=True),
        lax.all_gather(gate_weight, "seq", axis=0, tiled=True),
        lax.all_gather(up_weight, "seq", axis=0, tiled=True),
        lax.all_gather(down_weight, "seq", axis=1, tiled=True),
    )


def scatter_grads(gradients):
    return (
        lax.psum_scatter(
            gradients[0].astype(jnp.bfloat16), "seq", scatter_dimension=0, tiled=True
        ).astype(jnp.float32),
        lax.psum_scatter(
            gradients[1].astype(jnp.bfloat16), "seq", scatter_dimension=0, tiled=True
        ).astype(jnp.float32),
        lax.psum_scatter(
            gradients[2].astype(jnp.bfloat16), "seq", scatter_dimension=0, tiled=True
        ).astype(jnp.float32),
        lax.psum_scatter(
            gradients[3].astype(jnp.bfloat16), "seq", scatter_dimension=0, tiled=True
        ).astype(jnp.float32),
        lax.psum_scatter(
            gradients[4].astype(jnp.bfloat16), "seq", scatter_dimension=0, tiled=True
        ).astype(jnp.float32),
        lax.psum_scatter(
            gradients[5].astype(jnp.bfloat16), "seq", scatter_dimension=1, tiled=True
        ).astype(jnp.float32),
        lax.psum_scatter(
            gradients[6].astype(jnp.bfloat16), "seq", scatter_dimension=0, tiled=True
        ).astype(jnp.float32),
        lax.psum_scatter(
            gradients[7].astype(jnp.bfloat16), "seq", scatter_dimension=0, tiled=True
        ).astype(jnp.float32),
        lax.psum_scatter(
            gradients[8].astype(jnp.bfloat16), "seq", scatter_dimension=1, tiled=True
        ).astype(jnp.float32),
    )


def micro_step(gathered, row_tokens, row_reset, row_grad):
    (
        gain_one,
        gain_two,
        query_weight,
        key_weight,
        value_weight,
        out_weight,
        gate_weight,
        up_weight,
        down_weight,
    ) = gathered
    row_count, length, width = row_tokens.shape
    token_count = row_count * length
    qk_width = query_weight.shape[1]
    local_heads = qk_width // FEAT
    gain_first = gain_one.astype(jnp.float32)
    gain_second = gain_two.astype(jnp.float32)
    inputs = row_tokens.reshape(token_count, width).astype(jnp.float32)
    rstd_one = lax.rsqrt(jnp.mean(inputs * inputs, axis=-1, keepdims=True) + epsilon)
    unit_one = inputs * rstd_one
    normed_one = (unit_one * gain_first).astype(jnp.bfloat16)
    query_flat = jnp.dot(normed_one, query_weight, preferred_element_type=jnp.float32).astype(
        jnp.bfloat16
    )
    key_flat = jnp.dot(normed_one, key_weight, preferred_element_type=jnp.float32).astype(
        jnp.bfloat16
    )
    value_flat = jnp.dot(normed_one, value_weight, preferred_element_type=jnp.float32).astype(
        jnp.bfloat16
    )
    queries = heads_first(query_flat, row_count, length, local_heads, FEAT).astype(jnp.float32)
    key_vecs = heads_first(key_flat, row_count, length, local_heads, FEAT).astype(jnp.float32)
    values = heads_first(value_flat, row_count, length, local_heads, VHEAD).astype(jnp.float32)
    local_doc = jnp.cumsum(row_reset, axis=1)
    first_doc = (local_doc == 0).astype(jnp.float32)
    last_doc = (local_doc == local_doc[:, -1:]).astype(jnp.float32)
    reset_flag = (local_doc[:, -1] > 0).astype(jnp.float32)
    position = jnp.arange(length)
    causal = position[:, None] >= position[None, :]
    allowed = ((local_doc[:, :, None] == local_doc[:, None, :]) & causal[None])[:, None]
    head_mask = first_doc[:, None, :, None]
    tail_mask = last_doc[:, None, :, None]
    feat_query, pull_query = jax.vjp(taylor_map, queries)
    feat_key, pull_key = jax.vjp(taylor_map, key_vecs)
    tail_key = feat_key * tail_mask
    state_local = exact_product("rhsf,rhsv->rhfv", tail_key, values)
    norm_local = jnp.sum(tail_key, axis=2)
    identity = (jnp.zeros_like(state_local), jnp.zeros_like(norm_local), jnp.zeros_like(reset_flag))
    state_in, norm_in, unused_flag = carried_in(
        (state_local, norm_local, reset_flag), "seq", join_state, identity
    )
    scores = exact_product("rhtf,rhsf->rhts", queries, key_vecs) * 0.25
    weights = jnp.where(allowed, 1.0 + scores + 0.5 * scores * scores, 0.0)
    numerator = exact_product("rhts,rhsv->rhtv", weights, values) + head_mask * exact_product(
        "rhtf,rhfv->rhtv", feat_query, state_in
    )
    denominator = jnp.sum(weights, axis=-1) + first_doc[:, None, :] * exact_product(
        "rhtf,rhf->rht", feat_query, norm_in
    )
    attended = numerator / denominator[..., None]
    attended_low = heads_last(attended).astype(jnp.bfloat16)
    branch = lax.psum(jnp.dot(attended_low, out_weight, preferred_element_type=jnp.float32), "head")
    hidden_one = inputs + branch
    rstd_two = lax.rsqrt(jnp.mean(hidden_one * hidden_one, axis=-1, keepdims=True) + epsilon)
    unit_two = hidden_one * rstd_two
    normed_two = (unit_two * gain_second).astype(jnp.bfloat16)
    gate_act = jnp.dot(normed_two, gate_weight, preferred_element_type=jnp.float32)
    up_act = jnp.dot(normed_two, up_weight, preferred_element_type=jnp.float32)
    sigmoid_gate = jax.nn.sigmoid(gate_act)
    silu_gate = gate_act * sigmoid_gate
    mixed_act = (silu_gate * up_act).astype(jnp.bfloat16)
    ffn_out = lax.psum(
        jnp.dot(mixed_act, down_weight, preferred_element_type=jnp.float32).astype(jnp.bfloat16),
        "head",
    ).astype(jnp.float32)
    result = (hidden_one + ffn_out).astype(jnp.bfloat16).reshape(row_count, length, width)
    grad_low = row_grad.reshape(token_count, width)
    grad_mixed = contract_last(grad_low, down_weight)
    grad_down = contract_first(mixed_act, grad_low)
    grad_gate = (
        grad_mixed * up_act * sigmoid_gate * (1.0 + gate_act * (1.0 - sigmoid_gate))
    ).astype(jnp.bfloat16)
    grad_up = (grad_mixed * silu_gate).astype(jnp.bfloat16)
    grad_normed_two = lax.psum(
        contract_last(grad_gate, gate_weight) + contract_last(grad_up, up_weight), "head"
    )
    grad_w_gate = contract_first(normed_two, grad_gate)
    grad_w_up = contract_first(normed_two, grad_up)
    scaled_two = grad_normed_two * gain_second
    grad_hidden = grad_low.astype(jnp.float32) + rstd_two * (
        scaled_two - unit_two * jnp.mean(scaled_two * unit_two, axis=-1, keepdims=True)
    )
    grad_gain_two = jnp.sum(grad_normed_two * unit_two, axis=0)
    grad_branch = grad_hidden.astype(jnp.bfloat16)
    grad_out_w = contract_first(attended_low, grad_branch)
    grad_attended = heads_first(
        contract_last(grad_branch, out_weight), row_count, length, local_heads, VHEAD
    )
    grad_numerator = grad_attended / denominator[..., None]
    grad_denominator = -jnp.sum(grad_attended * attended, axis=-1) / denominator
    head_query = feat_query * head_mask
    carry_local = exact_product("rhtf,rhtv->rhfv", head_query, grad_numerator)
    carry_norm = jnp.sum(head_query * grad_denominator[..., None], axis=2)
    carry_in, carry_norm_in, unused_other = carried_in_2(
        (carry_local, carry_norm, reset_flag), "seq", join_state, identity
    )
    grad_weights = jnp.where(
        allowed,
        exact_product("rhtv,rhsv->rhts", grad_numerator, values) + grad_denominator[..., None],
        0.0,
    )
    grad_scores = grad_weights * (1.0 + scores)
    grad_feat_query = head_mask * (
        exact_product("rhtv,rhfv->rhtf", grad_numerator, state_in)
        + norm_in[:, :, None, :] * grad_denominator[..., None]
    )
    grad_feat_key = tail_mask * (
        exact_product("rhsv,rhfv->rhsf", values, carry_in) + carry_norm_in[:, :, None, :]
    )
    grad_queries = (
        exact_product("rhts,rhsf->rhtf", grad_scores, key_vecs) * 0.25
        + pull_query(grad_feat_query)[0]
    )
    grad_keys = (
        exact_product("rhts,rhtf->rhsf", grad_scores, queries) * 0.25 + pull_key(grad_feat_key)[0]
    )
    grad_values = exact_product(
        "rhts,rhtv->rhsv", weights, grad_numerator
    ) + tail_mask * exact_product("rhsf,rhfv->rhsv", feat_key, carry_in)
    grad_query_flat = heads_last(grad_queries).astype(jnp.bfloat16)
    grad_key_flat = heads_last(grad_keys).astype(jnp.bfloat16)
    grad_value_flat = heads_last(grad_values).astype(jnp.bfloat16)
    grad_w_query = contract_first(normed_one, grad_query_flat)
    grad_w_key = contract_first(normed_one, grad_key_flat)
    grad_w_value = contract_first(normed_one, grad_value_flat)
    back_local = (
        contract_last(grad_query_flat, query_weight)
        + contract_last(grad_key_flat, key_weight)
        + contract_last(grad_value_flat, value_weight)
    )
    grad_normed_one = lax.psum(back_local.astype(jnp.bfloat16), "head").astype(jnp.float32)
    scaled_one = grad_normed_one * gain_first
    grad_inputs = grad_hidden + rstd_one * (
        scaled_one - unit_one * jnp.mean(scaled_one * unit_one, axis=-1, keepdims=True)
    )
    grad_gain_one = jnp.sum(grad_normed_one * unit_one, axis=0)
    gradients = (
        grad_gain_one,
        grad_gain_two,
        grad_w_query,
        grad_w_key,
        grad_w_value,
        grad_out_w,
        grad_w_gate,
        grad_w_up,
        grad_down,
    )
    return (result, grad_inputs.reshape(row_count, length, width), gradients)


def per_device(
    tokens,
    doc_reset,
    gain_attn,
    gain_ffn,
    query_weight,
    key_weight,
    value_weight,
    out_weight,
    gate_weight,
    up_weight,
    down_weight,
    grad_out,
):
    outputs = []
    input_grads = []
    summed = None
    for micro_index in range(MB):
        gathered = gather_weights(
            gain_attn,
            gain_ffn,
            query_weight,
            key_weight,
            value_weight,
            out_weight,
            gate_weight,
            up_weight,
            down_weight,
        )
        row_start = micro_index * ROWS_MB
        row_end = row_start + ROWS_MB
        result, grad_inputs, gradients = micro_step(
            gathered,
            tokens[row_start:row_end],
            doc_reset[row_start:row_end],
            grad_out[row_start:row_end],
        )
        outputs.append(result)
        input_grads.append(grad_inputs)
        shares = scatter_grads(gradients)
        summed = shares if micro_index == 0 else jax.tree.map(jnp.add, summed, shares)
    return (
        jnp.concatenate(outputs, axis=0),
        jnp.concatenate(input_grads, axis=0),
        summed[0],
        summed[1],
        summed[2],
        summed[3],
        summed[4],
        summed[5],
        summed[6],
        summed[7],
        summed[8],
    )


def solution(mesh):
    placed = (
        P(None, "seq", None),
        P(None, "seq"),
        P("seq"),
        P("seq"),
        P("seq", "head"),
        P("seq", "head"),
        P("seq", "head"),
        P("head", "seq"),
        P("seq", "head"),
        P("seq", "head"),
        P("head", "seq"),
        P(None, "seq", None),
    )
    return jax.shard_map(
        per_device,
        mesh=mesh,
        in_specs=placed,
        out_specs=(
            P(None, "seq", None),
            P(None, "seq", None),
            P("seq"),
            P("seq"),
            P("seq", "head"),
            P("seq", "head"),
            P("seq", "head"),
            P("head", "seq"),
            P("seq", "head"),
            P("seq", "head"),
            P("head", "seq"),
        ),
        check_vma=False,
    )
```

profile of v0, /device:TPU:0, one launch (start us, length us, event | category | flops | bytes accessed | tf_op | source)
XLA Modules:
  0.0 3101.0 jit_solution(4540792884937953516)
XLA Ops:
  161.3 33.4 %all-gather.2 = f32[24,4,273]{2,1,0:T(4,128)} all-gather(f32[3,4,273]{2,1,0:T(4,128)S(1)} %copy-done.107), channel_id=4, replica_groups=mesh['seq'=8,'head'=4] {'seq'}, dimensions={0}, use_global_device_ids=true | all-gather | bytes 117936 | tf_op jit(solution)/shard_map/all_gather | solution.py:21
  219.9 34.1 %all-gather.5 = f32[24,4,273]{2,1,0:T(4,128)} all-gather(f32[3,4,273]{2,1,0:T(4,128)S(1)} %copy-done.106), channel_id=7, replica_groups=mesh['seq'=8,'head'=4] {'seq'}, dimensions={0}, use_global_device_ids=true | all-gather | bytes 117936 | tf_op jit(solution)/shard_map/all_gather | solution.py:21
  290.0 41.3 %while.68 = (s32[]{:T(128)}, f32[3,4,273,128]{3,2,1,0:T(8,128)}, f32[3,4,273]{2,1,0:T(4,128)S(1)}, s32[]{:T(128)}, f32[8,3,4,273,128]{4,2,3,1,0:T(4,128)}, /*ind...) while((s32[]{:T(128)}, f32[3,4,273,128]{3,2,1,0:T(8,128)}, ...), condition=%wide.region_5.6_spmd.clone, body=%wide.region_4.5_spmd.clone.sunk | while | flops 1690423 | bytes 8426047 | solution.py:30
  331.4 145.9 %all-gather.36.cloned.1.call-done = f32[24,4,273,128]{3,1,2,0:T(4,128)} async-done(((f32[3,4,273,128]{3,1,2,0:T(4,128)}), f32[24,4,273,128]{3,1,2,0:T(4,128)}) %all-gather.36.cloned.1.call-update) | async-done | bytes 13418512 | tf_op jit(solution)/shard_map/all_gather | solution.py:21
  564.6 194.1 %all-reduce.20.cloned.1.call-done = (f32[768,2048]{1,0:T(8,128)}, f32[768,2048]{1,0:T(8,128)}) async-done(((f32[768,2048]{1,0:T(8,128)}, f32[768,2048]{1,0:T(8,128)}), (f32[768,2048]{1,0:T(8,128)}, f32[768,2048]{1,0:T(8,128)})) %all-reduce.20.cloned.1.call-update) | async-done | bytes 12582928 | tf_op jit(solution)/shard_map/psum | solution.py:217
  774.4 79.2 %all-gather.28.cloned.1.call-done = bf16[2048,1408]{1,0:T(8,128)(2,1)} async-done(((bf16[256,1408]{1,0:T(8,128)(2,1)}), bf16[2048,1408]{1,0:T(8,128)(2,1)}) %all-gather.28.cloned.1.call-update) | async-done | bytes 5767184 | tf_op jit(solution)/shard_map/all_gather | solution.py:117
  863.3 83.4 %all-gather.30.cloned.1.call-done = bf16[2048,1408]{1,0:T(8,128)(2,1)} async-done(((bf16[256,1408]{1,0:T(8,128)(2,1)}), bf16[2048,1408]{1,0:T(8,128)(2,1)}) %all-gather.30.cloned.1.call-update) | async-done | bytes 5767184 | tf_op jit(solution)/shard_map/all_gather | solution.py:118
  969.8 70.7 %all-gather.32.cloned.1.call-done = bf16[1408,2048]{1,0:T(8,128)(2,1)} async-done(((bf16[1408,256]{1,0:T(8,128)(2,1)}), bf16[1408,2048]{1,0:T(8,128)(2,1)}) %all-gather.32.cloned.1.call-update) | async-done | bytes 5767184 | tf_op jit(solution)/shard_map/all_gather | solution.py:119
  1102.2 219.3 %all-reduce.18.cloned.1.call-done = (f32[768,2048]{1,0:T(8,128)}, f32[768,2048]{1,0:T(8,128)}) async-done(((f32[768,2048]{1,0:T(8,128)}, f32[768,2048]{1,0:T(8,128)}), (f32[768,2048]{1,0:T(8,128)}, f32[768,2048]{1,0:T(8,128)})) %all-reduce.18.cloned.1.call-update) | async-done | bytes 12582928 | tf_op jit(solution)/shard_map/psum | solution.py:239
  1582.3 38.4 %while.70 = (s32[]{:T(128)}, f32[3,4,273,128]{3,2,1,0:T(8,128)S(1)}, f32[3,4,273]{2,1,0:T(4,128)S(1)}, s32[]{:T(128)}, bf16[8,3,4,273,128]{4,2,3,1,0:T(4,128)(2,...) while((s32[]{:T(128)}, ...), condition=%wide.region_27.28_spmd.clone, body=%wide.region_26.27_spmd.clone.sunk | while | flops 2113034 | bytes 5903583 | solution.py:54
  1628.1 53.2 %while.71 = (s32[]{:T(128)}, f32[3,4,273,128]{3,2,1,0:T(8,128)S(1)}, f32[3,4,273]{2,1,0:T(4,128)}, s32[]{:T(128)}, bf16[8,3,4,273,128]{4,2,3,1,0:T(4,128)(2,1)},...) while((s32[]{:T(128)}, ...), condition=%wide.region_39.40_spmd.clone, body=%wide.region_38.39_spmd.clone.sunk | while | flops 2113034 | bytes 5903659 | solution.py:54
  1765.0 70.5 %reduce-scatter.29.cloned.1.call-done = bf16[512,256]{1,0:T(8,128)(2,1)} async-done(((bf16[512,2048]{1,0:T(8,128)(2,1)}), bf16[512,256]{1,0:T(8,128)(2,1)}) %reduce-scatter.29.cloned.1.call-update) | async-done | bytes 262160 | tf_op jit(solution)/shard_map/reduce_scatter | solution.py:140
  1837.4 110.6 %reduce-scatter.35.cloned.1.call-done = bf16[256,1408]{1,0:T(8,128)(2,1)} async-done(((bf16[2048,1408]{1,0:T(8,128)(2,1)}), bf16[256,1408]{1,0:T(8,128)(2,1)}) %reduce-scatter.35.cloned.1.call-update) | async-done | bytes 720912 | tf_op jit(solution)/shard_map/reduce_scatter | solution.py:146
  1948.0 113.3 %reduce-scatter.37.cloned.1.call-done = bf16[256,1408]{1,0:T(8,128)(2,1)} async-done(((bf16[2048,1408]{1,0:T(8,128)(2,1)}), bf16[256,1408]{1,0:T(8,128)(2,1)}) %reduce-scatter.37.cloned.1.call-update) | async-done | bytes 720912 | tf_op jit(solution)/shard_map/reduce_scatter | solution.py:146
  2063.9 110.7 %reduce-scatter.31.cloned.1.call-done = bf16[256,1408]{1,0:T(8,128)(2,1)} async-done(((bf16[2048,1408]{1,0:T(8,128)(2,1)}), bf16[256,1408]{1,0:T(8,128)(2,1)}) %reduce-scatter.31.cloned.1.call-update) | async-done | bytes 720912 | tf_op jit(solution)/shard_map/reduce_scatter | solution.py:143
  2174.6 113.5 %reduce-scatter.33.cloned.1.call-done = bf16[256,1408]{1,0:T(8,128)(2,1)} async-done(((bf16[2048,1408]{1,0:T(8,128)(2,1)}), bf16[256,1408]{1,0:T(8,128)(2,1)}) %reduce-scatter.33.cloned.1.call-update) | async-done | bytes 720912 | tf_op jit(solution)/shard_map/reduce_scatter | solution.py:143
  2290.8 110.9 %reduce-scatter.39.cloned.1.call-done = bf16[1408,256]{1,0:T(8,128)(2,1)} async-done(((bf16[1408,2048]{1,0:T(8,128)(2,1)}), bf16[1408,256]{1,0:T(8,128)(2,1)}) %reduce-scatter.39.cloned.1.call-update) | async-done | bytes 720912 | tf_op jit(solution)/shard_map/reduce_scatter | solution.py:149
  2401.7 113.9 %reduce-scatter.41.cloned.1.call-done = bf16[1408,256]{1,0:T(8,128)(2,1)} async-done(((bf16[1408,2048]{1,0:T(8,128)(2,1)}), bf16[1408,256]{1,0:T(8,128)(2,1)}) %reduce-scatter.41.cloned.1.call-update) | async-done | bytes 720912 | tf_op jit(solution)/shard_map/reduce_scatter | solution.py:149
  2518.2 62.2 %reduce-scatter.19.cloned.1.call-done = bf16[256,64]{0,1:T(8,128)(2,1)} async-done(((bf16[2048,64]{0,1:T(8,128)(2,1)}), bf16[256,64]{0,1:T(8,128)(2,1)}) %reduce-scatter.19.cloned.1.call-update) | async-done | bytes 32784 | tf_op jit(solution)/shard_map/reduce_scatter | solution.py:134
  2580.4 64.0 %reduce-scatter.21.cloned.1.call-done = bf16[256,64]{0,1:T(8,128)(2,1)} async-done(((bf16[2048,64]{0,1:T(8,128)(2,1)}), bf16[256,64]{0,1:T(8,128)(2,1)}) %reduce-scatter.21.cloned.1.call-update) | async-done | bytes 32784 | tf_op jit(solution)/shard_map/reduce_scatter | solution.py:134
  2645.9 68.9 %reduce-scatter.23.cloned.1.call-done = bf16[256,512]{1,0:T(8,128)(2,1)} async-done(((bf16[2048,512]{1,0:T(8,128)(2,1)}), bf16[256,512]{1,0:T(8,128)(2,1)}) %reduce-scatter.23.cloned.1.call-update) | async-done | bytes 262160 | tf_op jit(solution)/shard_map/reduce_scatter | solution.py:137
  2714.7 70.3 %reduce-scatter.25.cloned.1.call-done = bf16[256,512]{1,0:T(8,128)(2,1)} async-done(((bf16[2048,512]{1,0:T(8,128)(2,1)}), bf16[256,512]{1,0:T(8,128)(2,1)}) %reduce-scatter.25.cloned.1.call-update) | async-done | bytes 262160 | tf_op jit(solution)/shard_map/reduce_scatter | solution.py:137
  2786.9 221.5 %all-reduce.22.cloned.1.call-done = (bf16[768,2048]{1,0:T(8,128)(2,1)}, bf16[768,2048]{1,0:T(8,128)(2,1)}, bf16[768,2048]{1,0:T(8,128)(2,1)}, bf16[768,2048]{1,0:T(8,128)(2,1)}) async-done(((bf16[768,2048]{1,0:T(8,128)(2,1)}, bf16[768,2048]{1,0:T(8,128)(2,1)}, bf16[768,2048]{1,0:T(8,128)(2,1)}, bf16[768,2048]{1,0:T(8,128)(2,1)}), (bf16[768,2048]{1,0:T(8,128)(2,1)}, bf16[768,2048]{1,0:T(8,128)(2,1)}, ...) | async-done | bytes 12582928 | tf_op jit(solution)/shard_map/psum | solution.py:227
  3024.4 37.1 %all-reduce.11 = (bf16[2048]{0:T(1024)(128)(2,1)S(1)}, bf16[2048]{0:T(1024)(128)(2,1)S(1)}, bf16[2048]{0:T(1024)(128)(2,1)S(1)}, bf16[2048]{0:T(1024)(128)(2,1)S(1)}) all-reduce(bf16[2048]{0:T(1024)(128)(2,1)S(1)} %get-tuple-element.753, ...), channel_id=15, replica_groups=mesh['seq'=8,'head'=4] {'seq'}, use_global_device_ids=true, to_apply=%region_47.48.clone | all-reduce | flops 8192 | bytes 32768
  (749 shorter events, 976.2 us)
Async XLA Ops:
  7.9 282.1 %all-gather.34.cloned.1.call-start = ((), (), s32[]{:S(2)}) async-start(), calls=%async_computation.33 | async-start | bytes 15095808 | tf_op jit(solution)/shard_map/all_gather | solution.py:21
  99.1 378.2 %all-gather.36.cloned.1.call-start = ((), (), s32[]{:S(2)}) async-start(), calls=%async_computation.34 | async-start | bytes 15095808 | tf_op jit(solution)/shard_map/all_gather | solution.py:21
  117.0 411.5 %all-gather.26.cloned.1.call-start = ((), (), s32[]{:S(2)}) async-start(), calls=%async_computation.15 | async-start | bytes 2359296 | tf_op jit(solution)/shard_map/all_gather | solution.py:116
  117.6 641.1 %all-reduce.20.cloned.1.call-start = ((), (), s32[]{:S(2)}) async-start(), calls=%async_computation.38 | async-start | bytes 25165824 | tf_op jit(solution)/shard_map/psum | solution.py:217
  539.4 314.3 %all-gather.28.cloned.1.call-start = ((), (), s32[]{:S(2)}) async-start(), calls=%async_computation.16 | async-start | bytes 6488064 | tf_op jit(solution)/shard_map/all_gather | solution.py:117
  539.9 406.7 %all-gather.30.cloned.1.call-start = ((), (), s32[]{:S(2)}) async-start(), calls=%async_computation.17 | async-start | bytes 6488064 | tf_op jit(solution)/shard_map/all_gather | solution.py:118
  540.7 499.8 %all-gather.32.cloned.1.call-start = ((), (), s32[]{:S(2)}) async-start(), calls=%async_computation.18 | async-start | bytes 6488064 | tf_op jit(solution)/shard_map/all_gather | solution.py:119
  541.4 780.1 %all-reduce.18.cloned.1.call-start = ((), (), s32[]{:S(2)}) async-start(), calls=%async_computation.37 | async-start | bytes 25165824 | tf_op jit(solution)/shard_map/psum | solution.py:239
  1102.1 480.2 %all-gather.38.cloned.1.call-start = ((), (), s32[]{:S(2)}) async-start(), calls=%async_computation.35 | async-start | bytes 7547904 | tf_op jit(solution)/shard_map/all_gather | solution.py:36
  1379.8 383.4 %reduce-scatter.15.cloned.1.call-start = ((), (), s32[]{:S(2)}) async-start(), calls=%async_computation.19 | async-start | bytes 294912 | tf_op jit(solution)/shard_map/reduce_scatter | solution.py:131
  1412.9 350.3 %reduce-scatter.17.cloned.1.call-start = ((), (), s32[]{:S(2)}) async-start(), calls=%async_computation.20 | async-start | bytes 294912 | tf_op jit(solution)/shard_map/reduce_scatter | solution.py:131
  1418.5 346.6 %reduce-scatter.27.cloned.1.call-start = ((), (), s32[]{:S(2)}) async-start(), calls=%async_computation.25 | async-start | bytes 2359296 | tf_op jit(solution)/shard_map/reduce_scatter | solution.py:140
  1424.8 410.7 %reduce-scatter.29.cloned.1.call-start = ((), (), s32[]{:S(2)}) async-start(), calls=%async_computation.26 | async-start | bytes 2359296 | tf_op jit(solution)/shard_map/reduce_scatter | solution.py:140
  1431.0 517.0 %reduce-scatter.35.cloned.1.call-start = ((), (), s32[]{:S(2)}) async-start(), calls=%async_computation.29 | async-start | bytes 6488064 | tf_op jit(solution)/shard_map/reduce_scatter | solution.py:146
  1440.2 621.1 %reduce-scatter.37.cloned.1.call-start = ((), (), s32[]{:S(2)}) async-start(), calls=%async_computation.30 | async-start | bytes 6488064 | tf_op jit(solution)/shard_map/reduce_scatter | solution.py:146
  1450.6 724.0 %reduce-scatter.31.cloned.1.call-start = ((), (), s32[]{:S(2)}) async-start(), calls=%async_computation.27 | async-start | bytes 6488064 | tf_op jit(solution)/shard_map/reduce_scatter | solution.py:143
  1459.6 828.4 %reduce-scatter.33.cloned.1.call-start = ((), (), s32[]{:S(2)}) async-start(), calls=%async_computation.28 | async-start | bytes 6488064 | tf_op jit(solution)/shard_map/reduce_scatter | solution.py:143
  1468.2 933.5 %reduce-scatter.39.cloned.1.call-start = ((), (), s32[]{:S(2)}) async-start(), calls=%async_computation.31 | async-start | bytes 6488064 | tf_op jit(solution)/shard_map/reduce_scatter | solution.py:149
  1478.9 1036.7 %reduce-scatter.41.cloned.1.call-start = ((), (), s32[]{:S(2)}) async-start(), calls=%async_computation.32 | async-start | bytes 6488064 | tf_op jit(solution)/shard_map/reduce_scatter | solution.py:149
  1513.5 1066.9 %reduce-scatter.19.cloned.1.call-start = ((), (), s32[]{:S(2)}) async-start(), calls=%async_computation.21 | async-start | bytes 294912 | tf_op jit(solution)/shard_map/reduce_scatter | solution.py:134
  1690.8 953.6 %reduce-scatter.21.cloned.1.call-start = ((), (), s32[]{:S(2)}) async-start(), calls=%async_computation.22 | async-start | bytes 294912 | tf_op jit(solution)/shard_map/reduce_scatter | solution.py:134
  1702.9 1011.8 %reduce-scatter.23.cloned.1.call-start = ((), (), s32[]{:S(2)}) async-start(), calls=%async_computation.23 | async-start | bytes 2359296 | tf_op jit(solution)/shard_map/reduce_scatter | solution.py:137
  1714.5 1070.5 %reduce-scatter.25.cloned.1.call-start = ((), (), s32[]{:S(2)}) async-start(), calls=%async_computation.24 | async-start | bytes 2359296 | tf_op jit(solution)/shard_map/reduce_scatter | solution.py:137
  1732.2 1276.3 %all-reduce.22.cloned.1.call-start = ((), (), s32[]{:S(2)}) async-start(), calls=%async_computation.39 | async-start | bytes 25165824 | tf_op jit(solution)/shard_map/psum | solution.py:227
  (175 other events, 7214.4 us)
Sparse Core Ops, SparseCore 0:
  99.3 190.7 all-gather.33
  292.2 185.0 all-gather.35
  539.5 219.2 all-reduce.19
  760.8 92.8 all-gather.27
  855.8 90.8 all-gather.29
  948.7 91.7 all-gather.31
  1102.2 219.2 all-reduce.17
  1355.5 104.3 all-gather.37
  1462.7 104.4 all-gather.39
  1570.4 59.9 reduce-scatter.14
  1633.7 60.6 reduce-scatter.16
  1697.8 67.1 reduce-scatter.26
  1768.4 67.0 reduce-scatter.28
  1839.0 108.9 reduce-scatter.34
  1951.5 109.7 reduce-scatter.36
  2064.8 109.7 reduce-scatter.30
  2178.2 109.7 reduce-scatter.32
  2291.6 110.0 reduce-scatter.38
  2405.4 110.1 reduce-scatter.40
  2518.9 61.4 reduce-scatter.18
  2583.7 60.6 reduce-scatter.20
  2647.8 66.8 reduce-scatter.22
  2718.3 66.7 reduce-scatter.24
  2787.6 220.8 all-reduce.21
  (2 shorter events, 103.8 us)
where the time goes:
time: 3110 us; the launch traced here: 3100 us
  waiting for transfers between devices  2050 us (66%)
  matrix products  345 us (11%)
  blocking collectives  312 us (10%)
  other arithmetic  239 us (8%)
  local copies, waits for them, and re-layouts  132 us (4%)
    reduce_scatter x2, waiting for transfers between devices, scatter_grads(): lax.psum_scatter(gradients[8].astype(jnp.bfloat16), 'seq', scatter_dimens...  225 us
    reduce_scatter x2, waiting for transfers between devices, scatter_grads(): lax.psum_scatter(gradients[6].astype(jnp.bfloat16), 'seq', scatter_dimens...  224 us
    reduce_scatter x2, waiting for transfers between devices, scatter_grads(): lax.psum_scatter(gradients[7].astype(jnp.bfloat16), 'seq', scatter_dimens...  224 us
    psum x1, waiting for transfers between devices, micro_step(): lax.psum(jnp.dot(mixed_act, down_weight, preferred_element_type=jnp.float...  222 us
    psum x1, waiting for transfers between devices, micro_step(): lax.psum(contract_last(grad_gate, gate_weight) + contract_last(grad_up, u...  219 us
    psum x1, waiting for transfers between devices, micro_step(): lax.psum(jnp.dot(attended_low, out_weight, preferred_element_type=jnp.flo...  194 us
    all_gather x2, waiting for transfers between devices, carried_in(): pieces = jax.tree.map(lambda part: lax.all_gather(part, axis), value)  171 us
    reduce_scatter x2, waiting for transfers between devices, scatter_grads(): lax.psum_scatter(gradients[4].astype(jnp.bfloat16), 'seq', scatter_dimens...  139 us
  transfers between devices with their start and end apart: 26, of which 21 were waited for; matrix products, arithmetic and copies ran while one was open for 17% of the time, Pallas kernels for 0%

commit v1 on v0

v1 whole, which is shorter than its diff:
```python
import functools

import jax
import jax.numpy as jnp
import numpy as np
from jax import lax
from jax.experimental import pallas as pl
from jax.experimental.pallas import tpu as pltpu
from jax.sharding import PartitionSpec as P

FEAT = 16
VHEAD = 128
EPSILON = 1e-06
PAIRS = [(a, b) for a in range(FEAT + 1) for b in range(a, FEAT + 1)]
WIDE = 256
TALL = 160
NORM_ROW = len(PAIRS)
FLAG_ROW = NORM_ROW + 2
BLOCKS = 8
bf16, f32 = jnp.bfloat16, jnp.float32


def feature_tables(heads):
    lanes = 2 * heads * FEAT
    tables = {name: np.zeros((lanes, heads * WIDE), np.float32) for name in ("qa", "qb", "ka", "kb")}
    rows = np.zeros((8, heads * WIDE), np.float32)
    to_key = np.zeros((lanes, heads * lanes), np.float32)
    to_query = np.zeros((lanes, heads * lanes), np.float32)
    for head in range(heads):
        for place, (a, b) in enumerate(PAIRS):
            column = head * WIDE + place
            for name, entry, row in (("a", a, 0), ("b", b, 1)):
                if entry == 0:
                    rows[row, column] = 1.0
                else:
                    lane = head * FEAT + entry - 1
                    tables["q" + name][lane, column] = 1.0
                    tables["k" + name][heads * FEAT + lane, column] = 1.0
            rows[2, column] = 1.0 if b == 0 else 0.25 if a == 0 else 1 / 32 if a == b else 1 / 16
        for feat in range(FEAT):
            lane = head * FEAT + feat
            to_key[lane, head * lanes + heads * FEAT + lane] = 0.25
            to_query[heads * FEAT + lane, head * lanes + lane] = 0.25
    tables = {name: jnp.asarray(item, bf16) for name, item in tables.items()}
    return tables, jnp.asarray(rows), jnp.asarray(to_key, bf16), jnp.asarray(to_query, bf16)


def nn(left, right):
    return lax.dot_general(left, right, (((1,), (0,)), ((), ())), preferred_element_type=f32)


def nt(left, right):
    return lax.dot_general(left, right, (((1,), (1,)), ((), ())), preferred_element_type=f32)


def tn(left, right):
    return lax.dot_general(left, right, (((0,), (0,)), ((), ())), preferred_element_type=f32)


def params(mib=32):
    return pltpu.CompilerParams(vmem_limit_bytes=mib << 20)


def cost(flops, nbytes):
    return pl.CostEstimate(flops=int(flops), bytes_accessed=int(nbytes), transcendentals=0)


def whole_spec(array):
    zeros = (0,) * array.ndim
    return pl.BlockSpec(array.shape, lambda *_: zeros)


def row_spec(array):
    zeros = (0,) * (array.ndim - 1)
    return pl.BlockSpec((1,) + array.shape[1:], lambda row, *_: (row,) + zeros)


def pack_state(state, norm_row, flag):
    place = lax.broadcasted_iota(jnp.int32, (TALL, VHEAD), 0)
    block = state[:TALL]
    block = jnp.where(place == NORM_ROW, norm_row[:, :VHEAD], block)
    block = jnp.where(place == NORM_ROW + 1, norm_row[:, VHEAD:], block)
    return jnp.where(place == FLAG_ROW, flag, block).astype(bf16)


def unpack_state(block):
    tail = block[TALL - 16 :].astype(f32)
    base = TALL - 16
    low = tail[NORM_ROW - base : NORM_ROW - base + 1]
    high = tail[NORM_ROW + 1 - base : NORM_ROW + 2 - base]
    full = jnp.concatenate([block, jnp.zeros((WIDE - TALL, VHEAD), block.dtype)], axis=0)
    return full, jnp.concatenate([low, high], axis=1)


def state_kernel(heads, qkv_ref, edge_ref, ka_ref, kb_ref, rows_ref, out_ref):
    keys = qkv_ref[0, :, : 2 * heads * FEAT]
    edges = edge_ref[0]
    last, flag = edges[:, 2:3], edges[0:1, 3:4]
    for head in range(heads):
        cols = slice(head * WIDE, (head + 1) * WIDE)
        phi = (nn(keys, ka_ref[:, cols]) + rows_ref[0:1, cols]) * (nn(keys, kb_ref[:, cols]) + rows_ref[1:2, cols])
        phi = phi * last
        start = 2 * heads * FEAT + head * VHEAD
        state = tn(phi.astype(bf16), qkv_ref[0, :, start : start + VHEAD])
        out_ref[0, head] = pack_state(state, jnp.sum(phi, axis=0, keepdims=True), flag)


def local_mask(edges, docs):
    length = edges.shape[0]
    later = lax.broadcasted_iota(jnp.int32, (length, length), 0) >= lax.broadcasted_iota(jnp.int32, (length, length), 1)
    return later & (edges[:, 0:1] == docs)


def inside_kernel(heads, qkv_ref, edge_ref, doc_ref, key_ref, num_ref, den_ref):
    lanes = 2 * heads * FEAT
    both = qkv_ref[0, :, :lanes]
    mask = local_mask(edge_ref[0], doc_ref[0, 0:1])
    moved = nn(both, key_ref[...]).astype(bf16)
    dens = []
    for head in range(heads):
        scores = nt(moved[:, head * lanes : (head + 1) * lanes], both)
        weights = jnp.where(mask, 1.0 + scores + 0.5 * scores * scores, 0.0)
        dens.append(jnp.sum(weights, axis=1, keepdims=True))
        start = lanes + head * VHEAD
        num_ref[0, :, head * VHEAD : (head + 1) * VHEAD] = nn(
            weights.astype(bf16), qkv_ref[0, :, start : start + VHEAD]
        )
    den_ref[0] = jnp.concatenate(dens, axis=1)


def block_at(place_ref, states_ref, row, heads, head):
    per = states_ref.shape[1]
    index = row * heads + head
    return states_ref[place_ref[index // per], index % per]


def query_features(both, qa, qb, rows, first):
    left = nn(both, qa) + rows[0:1]
    right = nn(both, qb) + rows[1:2]
    return left, right, left * right * rows[2:3] * first


def attend_kernel(heads, place_ref, qkv_ref, edge_ref, num_ref, den_ref, states_ref, qa_ref, qb_ref, rows_ref, att_ref, rden_ref):
    both = qkv_ref[0, :, : 2 * heads * FEAT]
    first = edge_ref[0][:, 1:2]
    rdens = []
    for head in range(heads):
        cols = slice(head * WIDE, (head + 1) * WIDE)
        _, _, phi = query_features(both, qa_ref[:, cols], qb_ref[:, cols], rows_ref[:, cols], first)
        factor, norm = unpack_state(block_at(place_ref, states_ref, pl.program_id(0), heads, head))
        den = den_ref[0][:, head : head + 1] + jnp.sum(phi * norm, axis=1, keepdims=True)
        rden = 1.0 / den
        out = slice(head * VHEAD, (head + 1) * VHEAD)
        att_ref[0, :, out] = ((num_ref[0, :, out] + nn(phi.astype(bf16), factor)) * rden).astype(bf16)
        rdens.append(rden)
    rden_ref[0] = jnp.concatenate(rdens, axis=1)


def carry_kernel(heads, qkv_ref, edge_ref, ga_ref, att_ref, rden_ref, qa_ref, qb_ref, rows_ref, carry_ref, gnum_ref, gden_ref):
    both = qkv_ref[0, :, : 2 * heads * FEAT]
    edges = edge_ref[0]
    first, flag = edges[:, 1:2], edges[0:1, 3:4]
    gdens = []
    for head in range(heads):
        cols = slice(head * WIDE, (head + 1) * WIDE)
        out = slice(head * VHEAD, (head + 1) * VHEAD)
        _, _, phi = query_features(both, qa_ref[:, cols], qb_ref[:, cols], rows_ref[:, cols], first)
        grad = ga_ref[0, :, out].astype(f32)
        rden = rden_ref[0][:, head : head + 1]
        gnum = (grad * rden).astype(bf16)
        gden = -jnp.sum(grad * att_ref[0, :, out].astype(f32), axis=1, keepdims=True) * rden
        gnum_ref[0, :, out] = gnum
        carry_ref[0, head] = pack_state(
            tn(phi.astype(bf16), gnum), jnp.sum(phi * gden, axis=0, keepdims=True), flag
        )
        gdens.append(gden)
    gden_ref[0] = jnp.concatenate(gdens, axis=1)


def inside_back_kernel(
    heads, place_ref, qkv_ref, edge_ref, doc_ref, gnum_ref, gden_ref, states_ref, key_ref, query_ref, qa_ref, qb_ref,
    rows_ref, gboth_ref, gval_ref,
):
    lanes = 2 * heads * FEAT
    both = qkv_ref[0, :, :lanes]
    edges = edge_ref[0]
    first = edges[:, 1:2]
    mask = local_mask(edges, doc_ref[0, 0:1])
    moved = nn(both, key_ref[...]).astype(bf16)
    back = nn(both, query_ref[...]).astype(bf16)
    total = jnp.zeros((both.shape[0], lanes), f32)
    for head in range(heads):
        cols = slice(head * WIDE, (head + 1) * WIDE)
        out = slice(head * VHEAD, (head + 1) * VHEAD)
        own = slice(head * lanes, (head + 1) * lanes)
        start = lanes + head * VHEAD
        values = qkv_ref[0, :, start : start + VHEAD]
        gnum = gnum_ref[0, :, out]
        gden = gden_ref[0][:, head : head + 1]
        scores = nt(moved[:, own], both)
        weights = jnp.where(mask, 1.0 + scores + 0.5 * scores * scores, 0.0).astype(bf16)
        gval_ref[0, :, out] = tn(weights, gnum)
        gscores = jnp.where(mask, (nt(gnum, values) + gden) * (1.0 + scores), 0.0).astype(bf16)
        total = total + nn(gscores, back[:, own]) + tn(gscores, moved[:, own])
        left, right, _ = query_features(both, qa_ref[:, cols], qb_ref[:, cols], rows_ref[:, cols], first)
        factor, norm = unpack_state(block_at(place_ref, states_ref, pl.program_id(0), heads, head))
        place = lax.broadcasted_iota(jnp.int32, (1, WIDE), 1)
        gphi = jnp.where(place < NORM_ROW, (nt(gnum, factor) + norm * gden) * rows_ref[2:3, cols], 0.0) * first
        total = total + nt((gphi * right).astype(bf16), qa_ref[:, cols]) + nt((gphi * left).astype(bf16), qb_ref[:, cols])
    gboth_ref[0] = total


def finish_back_kernel(
    heads, place_ref, qkv_ref, edge_ref, carry_ref, gboth_ref, gval_ref, ka_ref, kb_ref, rows_ref, out_ref
):
    lanes = 2 * heads * FEAT
    both = qkv_ref[0, :, :lanes]
    last = edge_ref[0][:, 2:3]
    total = gboth_ref[0]
    for head in range(heads):
        cols = slice(head * WIDE, (head + 1) * WIDE)
        start = lanes + head * VHEAD
        values = qkv_ref[0, :, start : start + VHEAD]
        left = nn(both, ka_ref[:, cols]) + rows_ref[0:1, cols]
        right = nn(both, kb_ref[:, cols]) + rows_ref[1:2, cols]
        factor, norm = unpack_state(block_at(place_ref, carry_ref, pl.program_id(0), heads, head))
        phi = (left * right * last).astype(bf16)
        gval = gval_ref[0, :, head * VHEAD : (head + 1) * VHEAD] + nn(phi, factor)
        out_ref[0, :, start : start + VHEAD] = gval.astype(bf16)
        place = lax.broadcasted_iota(jnp.int32, (1, WIDE), 1)
        gphi = jnp.where(place < NORM_ROW, nt(values, factor) + norm, 0.0) * last
        total = total + nt((gphi * right).astype(bf16), ka_ref[:, cols]) + nt((gphi * left).astype(bf16), kb_ref[:, cols])
    out_ref[0, :, :lanes] = total.astype(bf16)


def by_row(kernel, rows, inputs, outputs, place=None, flops=0):
    arrays = [array for array, _ in inputs]
    specs = [row_spec(array) if per_row else whole_spec(array) for array, per_row in inputs]
    shapes = [jax.ShapeDtypeStruct((rows,) + shape, kind) for shape, kind in outputs]
    nbytes = sum(item.size * item.dtype.itemsize for item in arrays + shapes)
    return pl.pallas_call(
        kernel,
        out_shape=shapes,
        grid_spec=pltpu.PrefetchScalarGridSpec(
            num_scalar_prefetch=0 if place is None else 1,
            grid=(rows,),
            in_specs=specs,
            out_specs=[row_spec(shape) for shape in shapes],
        ),
        compiler_params=params(40),
        cost_estimate=cost(flops, nbytes),
    )(*([] if place is None else [place]), *arrays)


def scan_kernel(backward, count, me_ref, *refs):
    pieces, outs, (held, ahead) = refs[:count], refs[count : 2 * count], refs[2 * count :]
    for rel in range(count):
        held[rel] = pieces[rel][...]
    me = me_ref[0]
    for block in range(held.shape[1]):
        run = jnp.zeros(held.shape[2:], f32)
        for step in range(count):
            rel = me ^ (count - 1 - step if backward else step)
            ahead[rel, block] = run.astype(bf16)
            own = held[rel, block].astype(f32)
            run = own + (1.0 - own[FLAG_ROW : FLAG_ROW + 1]) * run
    for rel in range(count):
        outs[rel][...] = ahead[rel]


def exclusive_scan(states, backward, me, count):
    blocks = states.shape[0] * states.shape[1]
    flat = states.reshape(blocks, TALL, VHEAD)
    if count == 8 and blocks % 8 == 0:
        per = blocks // 8
        split = flat.reshape(8, per * TALL, VHEAD)
        pieces = []
        for rel in range(8):
            part = lax.dynamic_index_in_dim(split, me ^ rel, 0, keepdims=False)
            if rel:
                part = lax.ppermute(part, "seq", [(i, i ^ rel) for i in range(8)])
            pieces.append(part.reshape(per, TALL, VHEAD))
        shape = jax.ShapeDtypeStruct((per, TALL, VHEAD), bf16)
        outs = pl.pallas_call(
            functools.partial(scan_kernel, backward, 8),
            out_shape=[shape] * 8,
            in_specs=[pl.BlockSpec(memory_space=pltpu.SMEM)] + [pl.BlockSpec(memory_space=pltpu.VMEM)] * 8,
            out_specs=[pl.BlockSpec(memory_space=pltpu.VMEM)] * 8,
            scratch_shapes=[pltpu.VMEM((8, per, TALL, VHEAD), bf16)] * 2,
            compiler_params=params(),
        )(me.reshape(1), *pieces)
        back = [outs[0]]
        for rel in range(1, 8):
            back.append(lax.ppermute(outs[rel], "seq", [(i, i ^ rel) for i in range(8)]))
        return jnp.stack(back), me ^ jnp.arange(8, dtype=jnp.int32)
    every = lax.all_gather(flat, "seq").astype(f32)
    keep = 1.0 - every[:, :, FLAG_ROW : FLAG_ROW + 1]
    run = jnp.zeros(flat.shape, f32)
    for step in range(count):
        at = count - 1 - step if backward else step
        reached = at > me if backward else at < me
        run = jnp.where(reached, every[at] + keep[at] * run, run)
    return run.astype(bf16)[None], jnp.zeros((1,), jnp.int32)


SWAP = [(i, i ^ 1) for i in range(8)]


def up_pairs(least):
    return [(i, i + 2) for i in range(6) if i // 2 >= least]


def down_pairs(most):
    return [(i + 2, i) for i in range(6) if i // 2 + 1 <= most]


def send(value, axis, pairs):
    return lax.ppermute(value, axis, pairs)


def join_rows(pieces):
    return jnp.concatenate(pieces, axis=0)


def gather_rows(shard, count, me):
    if count != 8:
        return lax.all_gather(shard, "seq", axis=0, tiled=True)
    z = me // 2
    up, down = [shard], [shard]
    for step in range(3):
        up.append(send(up[-1], "seq", up_pairs(step)))
        down.append(send(down[-1], "seq", down_pairs(3 - step)))
    other = send(shard, "seq", SWAP)
    pieces = [shard, other]
    for k in range(1, 4):
        below, above = up[4 - k], down[k]
        low = [pair for pair in SWAP if pair[0] // 2 >= 4 - k]
        high = [pair for pair in SWAP if pair[0] // 2 < 4 - k]
        from_above = z + k <= 3
        pieces.append(jnp.where(from_above, above, below))
        pieces.append(jnp.where(from_above, send(above, "seq", high), send(below, "seq", low)))
    return join_rows(pieces)


def scatter_rows(whole, count):
    if count != 8:
        return lax.psum_scatter(whole, "seq", scatter_dimension=0, tiled=True).astype(f32)
    rows = whole.shape[0] // 8
    parts = [whole[place * rows : (place + 1) * rows].astype(f32) for place in range(8)]
    low = lambda value: value.astype(bf16)
    pair = [None] * 4
    for k in (3, 1, 2, 0):
        pair[k] = parts[2 * k] + send(whole[(2 * k + 1) * rows : (2 * k + 2) * rows], "seq", SWAP).astype(f32)
    up = send(low(pair[3]), "seq", [(i, i + 2) for i in (0, 1)])
    down = send(low(pair[1]), "seq", [(i + 2, i) for i in (4, 5)])
    up = send(low(pair[2] + up.astype(f32)), "seq", [(i, i + 2) for i in range(4)])
    down = send(low(pair[2] + down.astype(f32)), "seq", [(i + 2, i) for i in range(2, 6)])
    up = send(low(pair[1] + up.astype(f32)), "seq", [(i, i + 2) for i in range(6)])
    down = send(low(pair[3] + down.astype(f32)), "seq", [(i + 2, i) for i in range(6)])
    return pair[0] + up.astype(f32) + down.astype(f32)


CORE = [(i, i ^ 1) for i in range(4)]
ACROSS = [(i, i ^ 2) for i in range(4)]
ORDER = (0, 2, 1, 3)


def scatter_head(partial):
    rows = partial.shape[0] // 4
    quarter = [partial[i * rows : (i + 1) * rows] for i in range(4)]
    far = send(quarter[3], "head", CORE)
    across = send((quarter[1].astype(f32) + far.astype(f32)).astype(bf16), "head", ACROSS)
    near = send(quarter[2], "head", CORE)
    return quarter[0].astype(f32) + near.astype(f32) + across.astype(f32)


def gather_head(own):
    across = send(own, "head", ACROSS)
    core = send(own, "head", CORE)
    both = send(across, "head", CORE)
    return join_rows([own, across, core, both])


def to_own_order(array, me):
    split = array.reshape((4, array.shape[0] // 4) + array.shape[1:])
    return join_rows([lax.dynamic_index_in_dim(split, me ^ mask, 0, keepdims=False) for mask in ORDER])


def to_token_order(array, me):
    split = array.reshape((4, array.shape[0] // 4) + array.shape[1:])
    pieces = []
    for quarter in range(4):
        mask = quarter ^ me
        pieces.append(lax.dynamic_index_in_dim(split, (mask & 1) * 2 + (mask >> 1), 0, keepdims=False))
    return join_rows(pieces)


def move_kernel(split, rows_ref, cols_ref, in_ref, out_ref):
    width = in_ref.shape[1] // BLOCKS
    for block in range(BLOCKS):
        start = pl.multiple_of(cols_ref[block] * width, 128)
        out_ref[:, block * width : (block + 1) * width] = in_ref[:, pl.ds(start, width)].astype(out_ref.dtype)


def move_blocks(array, row_blocks, col_blocks, out_type, quarter):
    width = array.shape[1]
    split = 2 if quarter % 32 == 0 else 1
    tile = quarter // split
    count = row_blocks.shape[0]
    shape = jax.ShapeDtypeStruct((count * quarter, width), out_type)
    return pl.pallas_call(
        functools.partial(move_kernel, split),
        out_shape=shape,
        grid_spec=pltpu.PrefetchScalarGridSpec(
            num_scalar_prefetch=2,
            grid=(count, split),
            in_specs=[pl.BlockSpec((tile, width), lambda i, j, rows, cols: (rows[i] * split + j, 0))],
            out_specs=pl.BlockSpec((tile, width), lambda i, j, rows, cols: (i * split + j, 0)),
        ),
        compiler_params=params(),
        cost_estimate=cost(0, shape.size * (array.dtype.itemsize + shape.dtype.itemsize)),
    )(row_blocks, col_blocks, array)


def unit_kernel(cols_ref, in_ref, out_ref):
    values = in_ref[...].astype(f32)
    rstd = lax.rsqrt(jnp.mean(values * values, axis=1, keepdims=True) + EPSILON)
    width = in_ref.shape[1] // BLOCKS
    for block in range(BLOCKS):
        start = pl.multiple_of(cols_ref[block] * width, 128)
        out_ref[:, block * width : (block + 1) * width] = (in_ref[:, pl.ds(start, width)].astype(f32) * rstd).astype(bf16)


def unit_rows(array, col_blocks, tile):
    rows, width = array.shape
    return pl.pallas_call(
        unit_kernel,
        out_shape=jax.ShapeDtypeStruct((rows, width), bf16),
        grid_spec=pltpu.PrefetchScalarGridSpec(
            num_scalar_prefetch=1,
            grid=(rows // tile,),
            in_specs=[pl.BlockSpec((tile, width), lambda i, cols: (i, 0))],
            out_specs=pl.BlockSpec((tile, width), lambda i, cols: (i, 0)),
        ),
        compiler_params=params(),
        cost_estimate=cost(0, 4 * rows * width),
    )(col_blocks, array)


def ffn_kernel(step, unit_ref, dy_ref, gate_ref, up_ref, down_ref, mixed_ref, ggate_ref, gup_ref):
    width = gate_ref.shape[1]
    unit, dy = unit_ref[...], dy_ref[...]
    for start in range(0, width, step):
        cols = slice(start, min(start + step, width))
        gate = nn(unit, gate_ref[:, cols])
        up = nn(unit, up_ref[:, cols])
        gmixed = nn(dy, down_ref[:, cols])
        sig = jax.nn.sigmoid(gate)
        silu = gate * sig
        mixed_ref[:, cols] = (silu * up).astype(bf16)
        ggate_ref[:, cols] = (gmixed * up * (sig * (1.0 + gate * (1.0 - sig)))).astype(bf16)
        gup_ref[:, cols] = (gmixed * silu).astype(bf16)


def feed_forward(unit, dy, gate_w, up_w, down_w):
    tokens, width = unit.shape
    hidden = gate_w.shape[1]
    tile = 256 if tokens % 256 == 0 else 128
    once = pl.BlockSpec((width, hidden), lambda i: (0, 0), pipeline_mode=pl.Buffered(1))
    lines = pl.BlockSpec((tile, width), lambda i: (i, 0))
    out = pl.BlockSpec((tile, hidden), lambda i: (i, 0))
    return pl.pallas_call(
        functools.partial(ffn_kernel, 256),
        out_shape=[jax.ShapeDtypeStruct((tokens, hidden), bf16)] * 3,
        grid=(tokens // tile,),
        in_specs=[lines, lines, once, once, once],
        out_specs=[out, out, out],
        compiler_params=params(56),
        cost_estimate=cost(6 * tokens * width * hidden, 2 * (2 * tokens * width + 3 * (tokens + width) * hidden)),
    )(unit, dy, gate_w, up_w, down_w)


def per_device(
    n_seq,
    n_head,
    tokens,
    doc_reset,
    gain_attn,
    gain_ffn,
    query_weight,
    key_weight,
    value_weight,
    out_weight,
    gate_weight,
    up_weight,
    down_weight,
    grad_out,
):
    rows, length, width = tokens.shape
    heads = query_weight.shape[1] // FEAT
    count = rows * length
    quarter = count // 4
    me = lax.axis_index("seq").astype(jnp.int32)
    head_me = lax.axis_index("head").astype(jnp.int32)
    ids = jnp.arange(BLOCKS, dtype=jnp.int32)
    if n_seq == 8:
        z, y = me // 2, me % 2
        to_rel = ((z + ids // 2) % 4) * 2 + (y ^ (ids % 2))
        to_abs = ((ids // 2 - z) % 4) * 2 + (y ^ (ids % 2))
    else:
        to_rel = to_abs = ids
    own_order = head_me ^ jnp.array(ORDER, jnp.int32)
    masks = head_me ^ jnp.arange(4, dtype=jnp.int32)
    token_order = (masks & 1) * 2 + (masks >> 1)

    gain_one = gain_attn.astype(f32)[:, None]
    gain_two = gain_ffn.astype(f32)[:, None]
    scaled = lambda weight, gain: (weight.astype(f32) * gain).astype(bf16)
    qkv_own = jnp.concatenate([query_weight, key_weight, value_weight], axis=1)
    gather = functools.partial(gather_rows, count=n_seq, me=me)
    qkv_w = gather(scaled(qkv_own, gain_one))
    out_w = gather(out_weight.T)
    gate_w = gather(scaled(gate_weight, gain_two))
    up_w = gather(scaled(up_weight, gain_two))
    down_w = gather(down_weight.T)

    flat = tokens.reshape(count, width)
    unit_one = unit_rows(flat, to_rel, quarter // 2)
    x_own = move_blocks(flat, own_order[:1], to_rel, f32, quarter)
    dy = move_blocks(grad_out.reshape(count, width), own_order, to_rel, bf16, quarter)
    rstd_one = lax.rsqrt(jnp.mean(x_own * x_own, axis=1, keepdims=True) + EPSILON)

    docs = jnp.cumsum(doc_reset, axis=1)
    final = docs[:, -1:]
    flag = jnp.broadcast_to(final > 0, docs.shape)
    edges = jnp.stack([docs, docs == 0, docs == final, flag] + [jnp.zeros_like(docs)] * 4, axis=2).astype(f32)
    doc_rows = jnp.broadcast_to(docs[:, None, :], (rows, 8, length)).astype(f32)
    tables, feat_rows, to_key, to_query = feature_tables(heads)

    lanes = 2 * heads * FEAT
    values = heads * VHEAD
    unit_flops = 2 * rows * heads * length * WIDE * VHEAD
    qkv = nn(unit_one, qkv_w).astype(bf16).reshape(rows, length, lanes + values)
    (states,) = by_row(
        functools.partial(state_kernel, heads),
        rows,
        [(qkv, True), (edges, True), (tables["ka"], False), (tables["kb"], False), (feat_rows, False)],
        [((heads, TALL, VHEAD), bf16)],
        flops=3 * unit_flops,
    )
    numerator, denominator = by_row(
        functools.partial(inside_kernel, heads),
        rows,
        [(qkv, True), (edges, True), (doc_rows, True), (to_key, False)],
        [((length, values), f32), ((length, heads), f32)],
        flops=3 * unit_flops,
    )
    state_in, place = exclusive_scan(states, False, me, n_seq)
    query_tables = [(tables["qa"], False), (tables["qb"], False), (feat_rows, False)]
    key_tables = [(tables["ka"], False), (tables["kb"], False), (feat_rows, False)]
    attended, rden = by_row(
        functools.partial(attend_kernel, heads),
        rows,
        [(qkv, True), (edges, True), (numerator, True), (denominator, True), (state_in, False)] + query_tables,
        [((length, values), bf16), ((length, heads), f32)],
        place=place,
        flops=3 * unit_flops,
    )
    attended_own = to_own_order(attended.reshape(count, values), head_me)
    branch = nt(attended_own, out_w).astype(bf16)
    hidden = x_own + scatter_head(branch)
    rstd_two = lax.rsqrt(jnp.mean(hidden * hidden, axis=1, keepdims=True) + EPSILON)
    unit_two_own = hidden * rstd_two
    unit_two = gather_head(unit_two_own.astype(bf16))

    mixed, ggate, gup = feed_forward(unit_two, dy, gate_w, up_w, down_w)
    scaled_two = scatter_head((nt(ggate, gate_w) + nt(gup, up_w)).astype(bf16))
    grad_gate = scatter_rows(tn(unit_two, ggate).astype(bf16), n_seq)
    grad_up = scatter_rows(tn(unit_two, gup).astype(bf16), n_seq)
    grad_down = scatter_rows(tn(dy, mixed).astype(bf16), n_seq)

    dy_own = dy[:quarter].astype(f32)
    grad_hidden = dy_own + rstd_two * (
        scaled_two - unit_two_own * jnp.mean(scaled_two * unit_two_own, axis=1, keepdims=True)
    )
    grad_branch = gather_head(grad_hidden.astype(bf16))

    block_own = hidden + scatter_head(nt(mixed, down_w).astype(bf16))
    block_all = gather_head(block_own.astype(bf16))

    grad_att = to_token_order(nn(grad_branch, out_w).astype(bf16), head_me).reshape(rows, length, values)
    carry, gnum, gden = by_row(
        functools.partial(carry_kernel, heads),
        rows,
        [(qkv, True), (edges, True), (grad_att, True), (attended, True), (rden, True)] + query_tables,
        [((heads, TALL, VHEAD), bf16), ((length, values), bf16), ((length, heads), f32)],
        flops=3 * unit_flops,
    )
    gboth, gval = by_row(
        functools.partial(inside_back_kernel, heads),
        rows,
        [(qkv, True), (edges, True), (doc_rows, True), (gnum, True), (gden, True), (state_in, False)]
        + [(to_key, False), (to_query, False)]
        + query_tables,
        [((length, lanes), f32), ((length, values), f32)],
        place=place,
        flops=11 * unit_flops,
    )
    grad_out_w = scatter_rows(tn(grad_branch, attended_own).astype(bf16), n_seq)
    carry_in, place_back = exclusive_scan(carry, True, me, n_seq)
    (gqkv,) = by_row(
        functools.partial(finish_back_kernel, heads),
        rows,
        [(qkv, True), (edges, True), (carry_in, False), (gboth, True), (gval, True)] + key_tables,
        [((length, lanes + values), bf16)],
        place=place_back,
        flops=6 * unit_flops,
    )
    gqkv = gqkv.reshape(count, lanes + values)
    scaled_one = scatter_head(nt(to_own_order(gqkv, head_me), qkv_w).astype(bf16))
    grad_qkv = scatter_rows(tn(unit_one, gqkv).astype(bf16), n_seq)
    unit_one_own = x_own * rstd_one
    grad_x = grad_hidden + rstd_one * (
        scaled_one - unit_one_own * jnp.mean(scaled_one * unit_one_own, axis=1, keepdims=True)
    )
    grad_x_all = gather_head(grad_x.astype(bf16))

    back = lambda value, kind: move_blocks(value, token_order, to_abs, kind, quarter).reshape(rows, length, width)
    gain_sums = jnp.stack(
        [
            jnp.sum(qkv_own.astype(f32) * grad_qkv, axis=1),
            jnp.sum(gate_weight.astype(f32) * grad_gate + up_weight.astype(f32) * grad_up, axis=1),
        ]
    )
    gain_sums = gain_sums + send(gain_sums, "head", CORE)
    gain_sums = gain_sums + send(gain_sums, "head", ACROSS)
    grad_qkv = grad_qkv * gain_one
    narrow = heads * FEAT
    return (
        back(block_all, bf16),
        back(grad_x_all, f32),
        gain_sums[0],
        gain_sums[1],
        grad_qkv[:, :narrow],
        grad_qkv[:, narrow:lanes],
        grad_qkv[:, lanes:],
        grad_out_w.T,
        grad_gate * gain_two,
        grad_up * gain_two,
        grad_down.T,
    )


def solution(mesh):
    placed = (
        P(None, "seq", None),
        P(None, "seq"),
        P("seq"),
        P("seq"),
        P("seq", "head"),
        P("seq", "head"),
        P("seq", "head"),
        P("head", "seq"),
        P("seq", "head"),
        P("seq", "head"),
        P("head", "seq"),
        P(None, "seq", None),
    )
    return jax.shard_map(
        functools.partial(per_device, mesh.shape["seq"], mesh.shape["head"]),
        mesh=mesh,
        in_specs=placed,
        out_specs=(P(None, "seq", None), P(None, "seq", None)) + placed[2:11],
        check_vma=False,
    )
```

time: 3110 us -> 1220 us (0.39)
  waiting for transfers between devices: 2050 us -> 419 us
  starting transfers between devices: 1.71 us -> 394 us
  blocking collectives: 312 us -> 0 us
  matrix products: 345 us -> 122 us
  other arithmetic: 239 us -> 103 us
  Pallas kernels: 0 us -> 109 us
  local copies, waits for them, and re-layouts: 132 us -> 64.4 us
    reduce_scatter x14 -> x0, waiting for transfers between devices: 1010 us -> none  [the longest x2 225 us: scatter_grads(): lax.psum_scatter(gradients[8].astype(jnp.bfloat16), 'seq', scatter_dimens...]
    psum x3 -> x0, waiting for transfers between devices: 635 us -> none  [the longest x1 222 us: micro_step(): lax.psum(jnp.dot(mixed_act, down_weight, preferred_element_type=jnp.float...]
    ppermute x0 -> x169, waiting for transfers between devices: none -> 419 us  [the longest x141 337 us: send(): return lax.ppermute(value, axis, pairs)]
    all_gather x9 -> x0, waiting for transfers between devices: 405 us -> none  [the longest x2 171 us: carried_in(): pieces = jax.tree.map(lambda part: lax.all_gather(part, axis), value)]
    ppermute x0 -> x169, starting transfers between devices: none -> 394 us  [the longest x141 295 us: send(): return lax.ppermute(value, axis, pairs)]
    all_gather x8 -> x0, blocking collectives: 235 us -> none  [the longest x2 67.5 us: carried_in(): pieces = jax.tree.map(lambda part: lax.all_gather(part, axis), value)]
    dot_general x68 -> x12, matrix products: 345 us -> 122 us  [the longest x5 57.9 us: nt(): lax.dot_general(left, right, (((1,), (1,)), ((), ())), preferred_element_...]
    pallas_call x0 -> x14, Pallas kernels: none -> 109 us  [the longest x6 52.9 us: by_row(): pl.pallas_call(kernel, out_shape=shapes, grid_spec=pltpu.PrefetchScalarGr...]
  transfers between devices with their start and end apart: 26 -> 169, of which waited for: 21 -> 49; matrix products, arithmetic and copies ran while one was open for 17% -> 16% of each run, Pallas kernels for 0% -> 5%
where the time goes in v1:
time: 1220 us
  waiting for transfers between devices  419 us (34%)
  starting transfers between devices  394 us (32%)
  matrix products  122 us (10%)
  Pallas kernels  109 us (9%)
  other arithmetic  103 us (8%)
  local copies, waits for them, and re-layouts  64.4 us (5%)
    ppermute x141, waiting for transfers between devices, send(): return lax.ppermute(value, axis, pairs)  337 us
    ppermute x141, starting transfers between devices, send(): return lax.ppermute(value, axis, pairs)  295 us
    ppermute x14, waiting for transfers between devices, exclusive_scan(): lax.ppermute(outs[rel], 'seq', [(i, i ^ rel) for i in range(8)])  82.7 us
    dot_general x5, matrix products, nt(): lax.dot_general(left, right, (((1,), (1,)), ((), ())), preferred_element_...  57.9 us
    ppermute x14, starting transfers between devices, exclusive_scan(): lax.ppermute(outs[rel], 'seq', [(i, i ^ rel) for i in range(8)])  56.7 us
    pallas_call x6, Pallas kernels, by_row(): pl.pallas_call(kernel, out_shape=shapes, grid_spec=pltpu.PrefetchScalarGr...  52.9 us
    dot_general x5, matrix products, tn(): lax.dot_general(left, right, (((0,), (0,)), ((), ())), preferred_element_...  50.6 us
    ppermute x14, starting transfers between devices, exclusive_scan(): part = lax.ppermute(part, 'seq', [(i, i ^ rel) for i in range(8)])  41.6 us
  transfers between devices with their start and end apart: 169, of which 49 were waited for; matrix products, arithmetic and copies ran while one was open for 16% of the time, Pallas kernels for 5%

profile of v1, /device:TPU:0, one launch (start us, length us, event | category | flops | bytes accessed | tf_op | source)
XLA Modules:
  0.0 1216.0 jit_solution(14194072848819232206)
XLA Ops:
  197.8 32.3 %collective-permute-start.23 = (bf16[3,160,128]{2,1,0:T(8,128)(2,1)S(1)}, bf16[3,160,128]{2,1,0:T(8,128)(2,1)S(1)}, u32[]{:S(2)}, u32[]{:S(2)}) collective-permute-start(bf16[3,160,128]{2,1,0:T(8,128)(2,1)S(1)} %get-tuple-element.45), channel_id=1, source_target_pairs={{0,16},{4,20},{8,24},{12,28},{16,0},{20,4},{24,8},{28,12},{1,17},{... | collective-permute-start | bytes 368648 | tf_op jit(solution)/shard_map/ppermute | solution.py:294
  287.3 14.2 %collective-permute-done.73 = bf16[256,1408]{1,0:T(8,128)(2,1)S(1)} collective-permute-done((bf16[256,1408]{1,0:T(8,128)(2,1)S(1)}, bf16[256,1408]{1,0:T(8,128)(2,1)S(1)}, u32[]{:S(2)}, u32[]{:S(2)}) %collective-permute-start.73) | collective-permute-done | bytes 720928 | tf_op jit(solution)/shard_map/ppermute | solution.py:318
  301.5 19.2 %collective-permute-start.64 = (bf16[256,1408]{1,0:T(8,128)(2,1)S(1)}, bf16[256,1408]{1,0:T(8,128)(2,1)S(1)}, u32[]{:S(2)}, u32[]{:S(2)}) collective-permute-start(bf16[256,1408]{1,0:T(8,128)(2,1)S(1)} %collective-permute-done.60), channel_id=1, source_target_pairs={{0,4},{4,0},{8,12},{12,8},{16,20},{20,16},{1,5},{5,1},{9,13},{13,9... | collective-permute-start | bytes 2162696 | tf_op jit(solution)/shard_map/ppermute | solution.py:318
  343.5 26.3 %collective-permute-done.54 = bf16[256,1408]{1,0:T(8,128)(2,1)S(1)} collective-permute-done((bf16[256,1408]{1,0:T(8,128)(2,1)S(1)}, bf16[256,1408]{1,0:T(8,128)(2,1)S(1)}, u32[]{:S(2)}, u32[]{:S(2)}) %collective-permute-start.54) | collective-permute-done | bytes 720928 | tf_op jit(solution)/shard_map/ppermute | solution.py:318
  396.7 17.7 %collective-permute-done.42 = bf16[384,2048]{1,0:T(8,128)(2,1)S(1)} collective-permute-done((bf16[384,2048]{1,0:T(8,128)(2,1)S(1)}, bf16[384,2048]{1,0:T(8,128)(2,1)S(1)}, u32[]{:S(2)}, u32[]{:S(2)}) %collective-permute-start.42) | collective-permute-done | bytes 1572896 | tf_op jit(solution)/shard_map/ppermute | solution.py:318
  439.6 13.5 %collective-permute-start.83 = (bf16[256,1408]{1,0:T(8,128)(2,1)S(1)}, bf16[256,1408]{1,0:T(8,128)(2,1)S(1)}, u32[]{:S(2)}, u32[]{:S(2)}) collective-permute-start(bf16[256,1408]{1,0:T(8,128)(2,1)S(1)} %collective-permute-done.82), channel_id=1, source_target_pairs={{0,4},{4,0},{1,5},{5,1},{2,6},{6,2},{3,7},{7,3}} | collective-permute-start | bytes 2162696 | tf_op jit(solution)/shard_map/ppermute | solution.py:318
  465.4 13.8 %collective-permute-done.83 = bf16[256,1408]{1,0:T(8,128)(2,1)S(1)} collective-permute-done((bf16[256,1408]{1,0:T(8,128)(2,1)S(1)}, bf16[256,1408]{1,0:T(8,128)(2,1)S(1)}, u32[]{:S(2)}, u32[]{:S(2)}) %collective-permute-start.83) | collective-permute-done | bytes 720928 | tf_op jit(solution)/shard_map/ppermute | solution.py:318
  486.6 38.9 %shard_map.282 = (bf16[1536,1408]{1,0:T(8,128)(2,1)}, bf16[1536,1408]{1,0:T(8,128)(2,1)}, bf16[1536,1408]{1,0:T(8,128)(2,1)}) custom-call(bf16[1536,2048]{1,0:T(8,128)(2,1)} %pad_maximum_fusion.unit_ref, bf16[1536,2048]{1,0:T(8,128)(2,1)} %copy-done.8, bf16[2048,1408]{1,0:T(8,128)(2,1)} %select_dynamic-update-slice_fusion.12.gate_ref, ...), custom_call_target="tpu_custom_call" | custom-call | flops 26575110144 | bytes 42860544 | tf_op jit(solution)/shard_map/pallas_call | solution.py:472
  525.5 15.2 %convolution_convert_fusion.4 = bf16[1536,2048]{1,0:T(8,128)(2,1)} fusion(bf16[1536,1408]{1,0:T(8,128)(2,1)} %get-tuple-element.50, bf16[2048,1408]{1,0:T(8,128)(2,1)} %select_dynamic-update-slice_fusion.down_ref), kind=kOutput, calls=%fused_computation.5 | convolution fusion | flops 8861515776 | bytes 16384000 | tf_op jit(solution)/shard_map/dot_general | solution.py:53
  540.7 12.2 %convolution_convert_fusion = bf16[2048,1408]{1,0:T(8,128)(2,1)} fusion(bf16[1536,2048]{1,0:T(8,128)(2,1)S(1)} %bitcast.162, bf16[1536,1408]{1,0:T(8,128)(2,1)S(1)} %copy-done.106), kind=kOutput, calls=%fused_computation.1 | convolution fusion | flops 8861253632 | bytes 16384000 | tf_op jit(solution)/shard_map/dot_general | solution.py:57
  552.9 12.5 %fusion.52 = f32[1536,2048]{1,0:T(8,128)} fusion(bf16[1536,1408]{1,0:T(8,128)(2,1)S(1)} %bitcast.217, bf16[2048,1408]{1,0:T(8,128)(2,1)S(1)} %bitcast.205), kind=kOutput, calls=%fused_computation.239 | convolution fusion | flops 8858370048 | bytes 22675456 | tf_op jit(solution)/shard_map/dot_general | solution.py:53
  565.5 17.0 %add_convert_fusion = bf16[1536,2048]{1,0:T(8,128)(2,1)} fusion(f32[1536,2048]{1,0:T(8,128)} %fusion.52, bf16[1536,1408]{1,0:T(8,128)(2,1)} %get-tuple-element.51, bf16[2048,1408]{1,0:T(8,128)(2,1)} %select_dynamic-update-slice_fusion.12.gate_ref), kind=kOutput, calls=%fused_computation | convolution fusion | flops 8864661504 | bytes 28966912 | tf_op jit(solution)/shard_map/dot_general | solution.py:53
  589.4 12.5 %convolution_convert_fusion.1 = bf16[2048,1408]{1,0:T(8,128)(2,1)S(1)} fusion(bf16[1536,1408]{1,0:T(8,128)(2,1)} %get-tuple-element.52, bf16[384,2048]{1,0:T(8,128)(2,1)S(1)} %copy-done.58, bf16[384,2048]{1,0:T(8,128)(2,1)S(1)} %copy-done.56, bf16[384,2048]{1,0:T(8,128)(2,1)S(1)} %copy-done.54, bf16[384,2048]{1,0:T(8,128)(2,1)S(1)} %multiply_convert_fusion), kind=kOutput, calls=%fused_computation.2 | convolution fusion | flops 8886419456 | bytes 16384000 | tf_op jit(solution)/shard_map/dot_general | solution.py:57
  605.4 16.2 %convolution_convert_fusion.2 = bf16[2048,1408]{1,0:T(8,128)(2,1)} fusion(bf16[1536,1408]{1,0:T(8,128)(2,1)} %get-tuple-element.51, bf16[384,2048]{1,0:T(8,128)(2,1)} %copy-done.57, bf16[384,2048]{1,0:T(8,128)(2,1)} %copy-done.55, bf16[384,2048]{1,0:T(8,128)(2,1)} %copy-done.53, bf16[384,2048]{1,0:T(8,128)(2,1)S(1)} %multiply_convert_fusion), kind=kOutput, calls=%fused_computation.3 | convolution fusion | flops 8886419456 | bytes 16384000 | tf_op jit(solution)/shard_map/dot_general | solution.py:57
  648.7 40.6 %collective-permute-done.162 = bf16[256,1408]{1,0:T(8,128)(2,1)S(1)} collective-permute-done((bf16[256,1408]{1,0:T(8,128)(2,1)S(1)}, bf16[256,1408]{1,0:T(8,128)(2,1)S(1)}, u32[]{:S(2)}, u32[]{:S(2)}) %collective-permute-start.162) | collective-permute-done | bytes 720928 | tf_op jit(solution)/shard_map/ppermute | solution.py:318
  695.4 12.2 %collective-permute-done.131 = bf16[256,1408]{1,0:T(8,128)(2,1)S(1)} collective-permute-done((bf16[256,1408]{1,0:T(8,128)(2,1)S(1)}, bf16[256,1408]{1,0:T(8,128)(2,1)S(1)}, u32[]{:S(2)}, u32[]{:S(2)}) %collective-permute-start.131) | collective-permute-done | bytes 720928 | tf_op jit(solution)/shard_map/ppermute | solution.py:318
  766.7 24.3 %collective-permute-done.87 = bf16[384,2048]{1,0:T(8,128)(2,1)} collective-permute-done((bf16[384,2048]{1,0:T(8,128)(2,1)S(1)}, bf16[384,2048]{1,0:T(8,128)(2,1)}, u32[]{:S(2)}, u32[]{:S(2)}) %collective-permute-start.87) | collective-permute-done | bytes 1572896 | tf_op jit(solution)/shard_map/ppermute | solution.py:318
  819.0 21.1 %collective-permute-done.94 = bf16[384,2048]{1,0:T(8,128)(2,1)S(1)} collective-permute-done((bf16[384,2048]{1,0:T(8,128)(2,1)}, bf16[384,2048]{1,0:T(8,128)(2,1)S(1)}, u32[]{:S(2)}, u32[]{:S(2)}) %collective-permute-start.94) | collective-permute-done | bytes 1572896 | tf_op jit(solution)/shard_map/ppermute | solution.py:318
  867.8 20.9 %collective-permute-start.100 = (bf16[480,128]{1,0:T(8,128)(2,1)S(1)}, bf16[480,128]{1,0:T(8,128)(2,1)S(1)}, u32[]{:S(2)}, u32[]{:S(2)}) collective-permute-start(bf16[480,128]{1,0:T(8,128)(2,1)S(1)} %get-tuple-element.192), channel_id=1, source_target_pairs={{0,16},{4,20},{8,24},{12,28},{16,0},{20,4},{24,8},{28,12},{1,17},{... | collective-permute-start | bytes 368648 | tf_op jit(solution)/shard_map/ppermute | solution.py:281
  894.9 16.8 %shard_map.286 = (f32[6,256,128]{2,1,0:T(8,128)S(1)}, f32[6,256,512]{2,1,0:T(8,128)S(1)}) custom-call(s32[8]{0:T(128)S(1)} %copy-done.30, bf16[6,256,640]{2,1,0:T(8,128)(2,1)S(1)} %bitcast.159, f32[6,256,8]{2,1,0:T(8,128)S(1)} %copy-done.7, f32[6,8,256]{2,1,0:T(8,128)S(1)} %copy-done.28, bf16[6,256,512]{2,1,0:T(8,128)(2,1)S(1)} %get-tuple-element.63.gnum_ref, ...), custom_call_target="tpu_custom_call" | custom-call | flops 4429185024 | bytes 9396224 | tf_op jit(solution)/shard_map/pallas_call | solution.py:241
  927.0 16.5 %collective-permute-done.104 = bf16[3,160,128]{2,1,0:T(8,128)(2,1)S(1)} collective-permute-done((bf16[3,160,128]{2,1,0:T(8,128)(2,1)S(1)}, bf16[3,160,128]{2,1,0:T(8,128)(2,1)S(1)}, u32[]{:S(2)}, u32[]{:S(2)}) %collective-permute-start.104) | collective-permute-done | bytes 122912 | tf_op jit(solution)/shard_map/ppermute | solution.py:294
  1086.1 11.7 collective-permute-done.113
  1114.4 16.7 %collective-permute-done.88 = bf16[384,2048]{1,0:T(8,128)(2,1)} collective-permute-done((bf16[384,2048]{1,0:T(8,128)(2,1)S(1)}, bf16[384,2048]{1,0:T(8,128)(2,1)}, u32[]{:S(2)}, u32[]{:S(2)}) %collective-permute-start.88) | collective-permute-done | bytes 1572896 | tf_op jit(solution)/shard_map/ppermute | solution.py:318
  1135.7 12.2 collective-permute-done.136
  (743 shorter events, 757.6 us)
Async XLA Ops:
  0.7 51.1 %collective-permute-start.27 = (bf16[256,512]{0,1:T(8,128)(2,1)}, bf16[256,512]{0,1:T(8,128)(2,1)}, u32[]{:S(2)}, u32[]{:S(2)}) collective-permute-start(bf16[256,512]{0,1:T(8,128)(2,1)} %bitcast.201), channel_id=1, source_target_pairs={{0,4},{4,0},{8,12},{12,8},{16,20},{20,16},{24,28},{28,24},{1,5},{5... | collective-permute-start | bytes 786440 | tf_op jit(solution)/shard_map/ppermute | solution.py:318
  14.2 50.9 %collective-permute-start.46 = (bf16[256,1408]{1,0:T(8,128)(2,1)}, bf16[256,1408]{1,0:T(8,128)(2,1)}, u32[]{:S(2)}, u32[]{:S(2)}) collective-permute-start(bf16[256,1408]{1,0:T(8,128)(2,1)} %get-tuple-element.214), channel_id=1, source_target_pairs={{0,4},{4,0},{8,12},{12,8},{16,20},{20,16},{24,28},{28,24},{1,5},{5... | collective-permute-start | bytes 2162696 | tf_op jit(solution)/shard_map/ppermute | solution.py:318
  14.4 63.9 %collective-permute-start.59 = (bf16[256,1408]{1,0:T(8,128)(2,1)}, bf16[256,1408]{1,0:T(8,128)(2,1)}, u32[]{:S(2)}, u32[]{:S(2)}) collective-permute-start(bf16[256,1408]{1,0:T(8,128)(2,1)} %get-tuple-element.125), channel_id=1, source_target_pairs={{0,4},{4,0},{8,12},{12,8},{16,20},{20,16},{24,28},{28,24},{1,5},{5... | collective-permute-start | bytes 2162696 | tf_op jit(solution)/shard_map/ppermute | solution.py:318
  103.1 54.1 %collective-permute-start.48 = (bf16[256,1408]{1,0:T(8,128)(2,1)}, bf16[256,1408]{1,0:T(8,128)(2,1)S(1)}, u32[]{:S(2)}, u32[]{:S(2)}) collective-permute-start(bf16[256,1408]{1,0:T(8,128)(2,1)} %get-tuple-element.214), channel_id=1, source_target_pairs={{0,8},{4,12},{8,16},{12,20},{16,24},{20,28},{1,9},{5,13},{9,17},{1... | collective-permute-start | bytes 2162696 | tf_op jit(solution)/shard_map/ppermute | solution.py:318
  108.0 51.5 %collective-permute-start.61 = (bf16[256,1408]{1,0:T(8,128)(2,1)}, bf16[256,1408]{1,0:T(8,128)(2,1)S(1)}, u32[]{:S(2)}, u32[]{:S(2)}) collective-permute-start(bf16[256,1408]{1,0:T(8,128)(2,1)} %get-tuple-element.125), channel_id=1, source_target_pairs={{0,8},{4,12},{8,16},{12,20},{16,24},{20,28},{1,9},{5,13},{9,17},{1... | collective-permute-start | bytes 2162696 | tf_op jit(solution)/shard_map/ppermute | solution.py:318
  172.0 105.4 %collective-permute-start.47 = (bf16[256,1408]{1,0:T(8,128)(2,1)}, bf16[256,1408]{1,0:T(8,128)(2,1)S(1)}, u32[]{:S(2)}, u32[]{:S(2)}) collective-permute-start(bf16[256,1408]{1,0:T(8,128)(2,1)} %get-tuple-element.214), channel_id=1, source_target_pairs={{8,0},{12,4},{16,8},{20,12},{24,16},{28,20},{9,1},{13,5},{17,9},{2... | collective-permute-start | bytes 2162696 | tf_op jit(solution)/shard_map/ppermute | solution.py:318
  173.3 81.3 %collective-permute-start.74 = (bf16[256,1408]{1,0:T(8,128)(2,1)S(1)}, bf16[256,1408]{1,0:T(8,128)(2,1)S(1)}, u32[]{:S(2)}, u32[]{:S(2)}) collective-permute-start(bf16[256,1408]{1,0:T(8,128)(2,1)S(1)} %bitcast.198), channel_id=1, source_target_pairs={{0,8},{4,12},{8,16},{12,20},{16,24},{20,28},{1,9},{5,13},{9,17},{1... | collective-permute-start | bytes 2162696 | tf_op jit(solution)/shard_map/ppermute | solution.py:318
  177.9 79.8 %collective-permute-start.49 = (bf16[256,1408]{1,0:T(8,128)(2,1)S(1)}, bf16[256,1408]{1,0:T(8,128)(2,1)S(1)}, u32[]{:S(2)}, u32[]{:S(2)}) collective-permute-start(bf16[256,1408]{1,0:T(8,128)(2,1)S(1)} %collective-permute-done.48), channel_id=1, source_target_pairs={{8,16},{12,20},{16,24},{20,28},{9,17},{13,21},{17,25},{21,29},{10,... | collective-permute-start | bytes 2162696 | tf_op jit(solution)/shard_map/ppermute | solution.py:318
  178.6 79.8 %collective-permute-start.62 = (bf16[256,1408]{1,0:T(8,128)(2,1)S(1)}, bf16[256,1408]{1,0:T(8,128)(2,1)S(1)}, u32[]{:S(2)}, u32[]{:S(2)}) collective-permute-start(bf16[256,1408]{1,0:T(8,128)(2,1)S(1)} %collective-permute-done.61), channel_id=1, source_target_pairs={{8,16},{12,20},{16,24},{20,28},{9,17},{13,21},{17,25},{21,29},{10,... | collective-permute-start | bytes 2162696 | tf_op jit(solution)/shard_map/ppermute | solution.py:318
  323.1 54.5 %collective-permute-start.77 = (bf16[256,1408]{1,0:T(8,128)(2,1)S(1)}, bf16[256,1408]{1,0:T(8,128)(2,1)S(1)}, u32[]{:S(2)}, u32[]{:S(2)}) collective-permute-start(bf16[256,1408]{1,0:T(8,128)(2,1)S(1)} %collective-permute-done.73), channel_id=1, source_target_pairs={{0,4},{4,0},{8,12},{12,8},{16,20},{20,16},{1,5},{5,1},{9,13},{13,9... | collective-permute-start | bytes 2162696 | tf_op jit(solution)/shard_map/ppermute | solution.py:318
  586.6 124.4 %collective-permute-start.92 = (bf16[384,2048]{1,0:T(8,128)(2,1)}, bf16[384,2048]{1,0:T(8,128)(2,1)}, u32[]{:S(2)}, u32[]{:S(2)}) collective-permute-start(bf16[384,2048]{1,0:T(8,128)(2,1)} %get-tuple-element.144), channel_id=1, source_target_pairs={{0,1},{1,0},{2,3},{3,2},{4,5},{5,4},{6,7},{7,6},{8,9},{9,8},{10,11... | collective-permute-start | bytes 4718600 | tf_op jit(solution)/shard_map/ppermute | solution.py:318
  629.7 63.6 %collective-permute-start.139 = (bf16[256,1408]{1,0:T(8,128)(2,1)S(1)}, bf16[256,1408]{1,0:T(8,128)(2,1)S(1)}, u32[]{:S(2)}, u32[]{:S(2)}) collective-permute-start(bf16[256,1408]{1,0:T(8,128)(2,1)S(1)} %copy-done.71), channel_id=1, source_target_pairs={{0,4},{4,0},{8,12},{12,8},{16,20},{20,16},{24,28},{28,24},{1,5},{5... | collective-permute-start | bytes 2162696 | tf_op jit(solution)/shard_map/ppermute | solution.py:318
  630.3 63.8 %collective-permute-start.129 = (bf16[256,1408]{1,0:T(8,128)(2,1)S(1)}, bf16[256,1408]{1,0:T(8,128)(2,1)S(1)}, u32[]{:S(2)}, u32[]{:S(2)}) collective-permute-start(bf16[256,1408]{1,0:T(8,128)(2,1)S(1)} %get-tuple-element.159), channel_id=1, source_target_pairs={{0,4},{4,0},{8,12},{12,8},{16,20},{20,16},{24,28},{28,24},{1,5},{5... | collective-permute-start | bytes 2162696 | tf_op jit(solution)/shard_map/ppermute | solution.py:318
  632.6 56.7 %collective-permute-start.162 = (bf16[256,1408]{1,0:T(8,128)(2,1)S(1)}, bf16[256,1408]{1,0:T(8,128)(2,1)S(1)}, u32[]{:S(2)}, u32[]{:S(2)}) collective-permute-start(bf16[256,1408]{1,0:T(8,128)(2,1)S(1)} %get-tuple-element.150), channel_id=1, source_target_pairs={{0,4},{4,0},{8,12},{12,8},{16,20},{20,16},{24,28},{28,24},{1,5},{5... | collective-permute-start | bytes 2162696 | tf_op jit(solution)/shard_map/ppermute | solution.py:318
  693.2 53.5 %collective-permute-start.91 = (bf16[384,2048]{1,0:T(8,128)(2,1)S(1)}, bf16[384,2048]{1,0:T(8,128)(2,1)S(1)}, u32[]{:S(2)}, u32[]{:S(2)}) collective-permute-start(bf16[384,2048]{1,0:T(8,128)(2,1)S(1)} %copy-done.59), channel_id=1, source_target_pairs={{0,1},{1,0},{2,3},{3,2},{4,5},{5,4},{6,7},{7,6},{8,9},{9,8},{10,11... | collective-permute-start | bytes 4718600 | tf_op jit(solution)/shard_map/ppermute | solution.py:318
  732.0 59.1 %collective-permute-start.87 = (bf16[384,2048]{1,0:T(8,128)(2,1)S(1)}, bf16[384,2048]{1,0:T(8,128)(2,1)}, u32[]{:S(2)}, u32[]{:S(2)}) collective-permute-start(bf16[384,2048]{1,0:T(8,128)(2,1)S(1)} %add_convert_fusion.5), channel_id=1, source_target_pairs={{0,2},{1,3},{2,0},{3,1},{4,6},{5,7},{6,4},{7,5},{8,10},{9,11},{10,... | collective-permute-start | bytes 4718600 | tf_op jit(solution)/shard_map/ppermute | solution.py:318
  744.4 58.7 %collective-permute-start.128 = (bf16[256,1408]{1,0:T(8,128)(2,1)}, bf16[256,1408]{1,0:T(8,128)(2,1)}, u32[]{:S(2)}, u32[]{:S(2)}) collective-permute-start(bf16[256,1408]{1,0:T(8,128)(2,1)} %get-tuple-element.160), channel_id=1, source_target_pairs={{0,4},{4,0},{8,12},{12,8},{16,20},{20,16},{24,28},{28,24},{1,5},{5... | collective-permute-start | bytes 2162696 | tf_op jit(solution)/shard_map/ppermute | solution.py:318
  746.7 61.0 %collective-permute-start.160 = (bf16[256,1408]{1,0:T(8,128)(2,1)}, bf16[256,1408]{1,0:T(8,128)(2,1)}, u32[]{:S(2)}, u32[]{:S(2)}) collective-permute-start(bf16[256,1408]{1,0:T(8,128)(2,1)} %get-tuple-element.152), channel_id=1, source_target_pairs={{0,4},{4,0},{8,12},{12,8},{16,20},{20,16},{24,28},{28,24},{1,5},{5... | collective-permute-start | bytes 2162696 | tf_op jit(solution)/shard_map/ppermute | solution.py:318
  916.7 128.2 %collective-permute-start.159 = (bf16[256,1408]{1,0:T(8,128)(2,1)S(1)}, bf16[256,1408]{1,0:T(8,128)(2,1)S(1)}, u32[]{:S(2)}, u32[]{:S(2)}) collective-permute-start(bf16[256,1408]{1,0:T(8,128)(2,1)S(1)} %copy-done.68), channel_id=1, source_target_pairs={{0,4},{4,0},{8,12},{12,8},{16,20},{20,16},{24,28},{28,24},{1,5},{5... | collective-permute-start | bytes 2162696 | tf_op jit(solution)/shard_map/ppermute | solution.py:318
  918.1 96.7 %collective-permute-start.135 = (bf16[256,1408]{1,0:T(8,128)(2,1)S(1)}, bf16[256,1408]{1,0:T(8,128)(2,1)S(1)}, u32[]{:S(2)}, u32[]{:S(2)}) collective-permute-start(bf16[256,1408]{1,0:T(8,128)(2,1)S(1)} %copy-done.69), channel_id=1, source_target_pairs={{16,8},{20,12},{24,16},{28,20},{17,9},{21,13},{25,17},{29,21},{18,... | collective-permute-start | bytes 2162696 | tf_op jit(solution)/shard_map/ppermute | solution.py:318
  918.8 107.7 %collective-permute-start.167 = (bf16[256,1408]{1,0:T(8,128)(2,1)S(1)}, bf16[256,1408]{1,0:T(8,128)(2,1)S(1)}, u32[]{:S(2)}, u32[]{:S(2)}) collective-permute-start(bf16[256,1408]{1,0:T(8,128)(2,1)S(1)} %add_convert_fusion.8), channel_id=1, source_target_pairs={{16,8},{20,12},{24,16},{28,20},{17,9},{21,13},{25,17},{29,21},{18,... | collective-permute-start | bytes 2162696 | tf_op jit(solution)/shard_map/ppermute | solution.py:318
  924.5 92.7 %collective-permute-start.152 = (bf16[256,512]{1,0:T(8,128)(2,1)}, bf16[256,512]{1,0:T(8,128)(2,1)S(1)}, u32[]{:S(2)}, u32[]{:S(2)}) collective-permute-start(bf16[256,512]{1,0:T(8,128)(2,1)} %get-tuple-element.174), channel_id=1, source_target_pairs={{0,4},{4,0},{8,12},{12,8},{16,20},{20,16},{24,28},{28,24},{1,5},{5... | collective-permute-start | bytes 786440 | tf_op jit(solution)/shard_map/ppermute | solution.py:318
  1067.8 63.3 %collective-permute-start.88 = (bf16[384,2048]{1,0:T(8,128)(2,1)S(1)}, bf16[384,2048]{1,0:T(8,128)(2,1)}, u32[]{:S(2)}, u32[]{:S(2)}) collective-permute-start(bf16[384,2048]{1,0:T(8,128)(2,1)S(1)} %get-tuple-element.164), channel_id=1, source_target_pairs={{0,2},{1,3},{2,0},{3,1},{4,6},{5,7},{6,4},{7,5},{8,10},{9,11},{10,... | collective-permute-start | bytes 4718600 | tf_op jit(solution)/shard_map/ppermute | solution.py:318
  1102.4 58.7 %collective-permute-start.89 = (bf16[384,2048]{1,0:T(8,128)(2,1)S(1)}, bf16[384,2048]{1,0:T(8,128)(2,1)}, u32[]{:S(2)}, u32[]{:S(2)}) collective-permute-start(bf16[384,2048]{1,0:T(8,128)(2,1)S(1)} %get-tuple-element.164), channel_id=1, source_target_pairs={{0,1},{1,0},{2,3},{3,2},{4,5},{5,4},{6,7},{7,6},{8,9},{9,8},{10,11... | collective-permute-start | bytes 4718600 | tf_op jit(solution)/shard_map/ppermute | solution.py:318
  (266 other events, 6823.1 us)

commit v2 on v1

--- a/solution.py
+++ b/solution.py
@@ -62,7 +62,7 @@
 
 
 def cost(flops, nbytes):
-    return pl.CostEstimate(flops=int(flops), bytes_accessed=int(nbytes), transcendentals=0)
+    return pl.CostEstimate(flops=int(flops) // 32, bytes_accessed=int(nbytes) // 32, transcendentals=0)
 
 
 def whole_spec(array):
@@ -268,131 +268,112 @@
         outs[rel][...] = ahead[rel]
 
 
-def exclusive_scan(states, backward, me, count):
+def scan_begin(states, backward, me, count, earlier=()):
     blocks = states.shape[0] * states.shape[1]
     flat = states.reshape(blocks, TALL, VHEAD)
-    if count == 8 and blocks % 8 == 0:
-        per = blocks // 8
-        split = flat.reshape(8, per * TALL, VHEAD)
-        pieces = []
-        for rel in range(8):
-            part = lax.dynamic_index_in_dim(split, me ^ rel, 0, keepdims=False)
-            if rel:
-                part = lax.ppermute(part, "seq", [(i, i ^ rel) for i in range(8)])
-            pieces.append(part.reshape(per, TALL, VHEAD))
-        shape = jax.ShapeDtypeStruct((per, TALL, VHEAD), bf16)
-        outs = pl.pallas_call(
-            functools.partial(scan_kernel, backward, 8),
-            out_shape=[shape] * 8,
-            in_specs=[pl.BlockSpec(memory_space=pltpu.SMEM)] + [pl.BlockSpec(memory_space=pltpu.VMEM)] * 8,
-            out_specs=[pl.BlockSpec(memory_space=pltpu.VMEM)] * 8,
-            scratch_shapes=[pltpu.VMEM((8, per, TALL, VHEAD), bf16)] * 2,
-            compiler_params=params(),
-        )(me.reshape(1), *pieces)
-        back = [outs[0]]
-        for rel in range(1, 8):
-            back.append(lax.ppermute(outs[rel], "seq", [(i, i ^ rel) for i in range(8)]))
+    if count != 8 or blocks % 8:
+        return lax.all_gather(flat, "seq").astype(f32)
+    per = blocks // 8
+    split = flat.reshape(8, per * TALL, VHEAD)
+    pieces = []
+    for rel in range(8):
+        part = lax.dynamic_index_in_dim(split, me ^ rel, 0, keepdims=False)
+        if rel:
+            part = send(part, "seq", rel, 8)
+        pieces.append(part.reshape(per, TALL, VHEAD))
+    pieces[0] = after(pieces[0], *earlier)
+    return pl.pallas_call(
+        functools.partial(scan_kernel, backward, 8),
+        out_shape=[jax.ShapeDtypeStruct((per, TALL, VHEAD), bf16)] * 8,
+        in_specs=[pl.BlockSpec(memory_space=pltpu.SMEM)] + [pl.BlockSpec(memory_space=pltpu.VMEM)] * 8,
+        out_specs=[pl.BlockSpec(memory_space=pltpu.VMEM)] * 8,
+        scratch_shapes=[pltpu.VMEM((8, per, TALL, VHEAD), bf16)] * 2,
+        compiler_params=params(),
+    )(me.reshape(1), *pieces)
+
+
+def scan_end(found, backward, me, count):
+    if isinstance(found, (list, tuple)):
+        back = [found[0]] + [send(found[rel], "seq", rel, 8) for rel in range(1, 8)]
         return jnp.stack(back), me ^ jnp.arange(8, dtype=jnp.int32)
-    every = lax.all_gather(flat, "seq").astype(f32)
-    keep = 1.0 - every[:, :, FLAG_ROW : FLAG_ROW + 1]
-    run = jnp.zeros(flat.shape, f32)
+    keep = 1.0 - found[:, :, FLAG_ROW : FLAG_ROW + 1]
+    run = jnp.zeros(found.shape[1:], f32)
     for step in range(count):
         at = count - 1 - step if backward else step
         reached = at > me if backward else at < me
-        run = jnp.where(reached, every[at] + keep[at] * run, run)
+        run = jnp.where(reached, found[at] + keep[at] * run, run)
     return run.astype(bf16)[None], jnp.zeros((1,), jnp.int32)
 
 
-SWAP = [(i, i ^ 1) for i in range(8)]
-
-
-def up_pairs(least):
-    return [(i, i + 2) for i in range(6) if i // 2 >= least]
-
-
-def down_pairs(most):
-    return [(i + 2, i) for i in range(6) if i // 2 + 1 <= most]
-
-
-def send(value, axis, pairs):
-    return lax.ppermute(value, axis, pairs)
+def send(value, axis, mask, count):
+    return lax.ppermute(value, axis, [(i, i ^ mask) for i in range(count)])
+
+
+def gather_rows(shard, count):
+    if count != 8:
+        return [lax.all_gather(shard, "seq", axis=0, tiled=True)]
+    pieces = [shard, send(shard, "seq", 1, 8)]
+    for mask in (2, 4, 6):
+        piece = send(shard, "seq", mask, 8)
+        pieces += [piece, send(piece, "seq", 1, 8)]
+    return pieces
+
+
+def after(value, *earlier):
+    return lax.optimization_barrier((value, earlier))[0]
+
+
+def scatter_begin(whole):
+    rows = whole.shape[0] // 8
+    part = lambda i: whole[i * rows : (i + 1) * rows]
+    pairs = [part(mask).astype(f32) + send(part(mask + 1), "seq", 1, 8).astype(f32) for mask in (2, 4, 6, 0)]
+    return [pair.astype(bf16) for pair in pairs[:3]] + [pairs[3]]
+
+
+def scatter_end(pairs):
+    total = pairs[3]
+    for pair, mask in zip(pairs, (2, 4, 6)):
+        total = total + send(pair, "seq", mask, 8).astype(f32)
+    return total
+
+
+def scatter_rows(whole):
+    return lax.psum_scatter(whole, "seq", scatter_dimension=0, tiled=True).astype(f32)
 
 
 def join_rows(pieces):
-    return jnp.concatenate(pieces, axis=0)
-
-
-def gather_rows(shard, count, me):
-    if count != 8:
-        return lax.all_gather(shard, "seq", axis=0, tiled=True)
-    z = me // 2
-    up, down = [shard], [shard]
-    for step in range(3):
-        up.append(send(up[-1], "seq", up_pairs(step)))
-        down.append(send(down[-1], "seq", down_pairs(3 - step)))
-    other = send(shard, "seq", SWAP)
-    pieces = [shard, other]
-    for k in range(1, 4):
-        below, above = up[4 - k], down[k]
-        low = [pair for pair in SWAP if pair[0] // 2 >= 4 - k]
-        high = [pair for pair in SWAP if pair[0] // 2 < 4 - k]
-        from_above = z + k <= 3
-        pieces.append(jnp.where(from_above, above, below))
-        pieces.append(jnp.where(from_above, send(above, "seq", high), send(below, "seq", low)))
-    return join_rows(pieces)
-
-
-def scatter_rows(whole, count):
-    if count != 8:
-        return lax.psum_scatter(whole, "seq", scatter_dimension=0, tiled=True).astype(f32)
-    rows = whole.shape[0] // 8
-    parts = [whole[place * rows : (place + 1) * rows].astype(f32) for place in range(8)]
-    low = lambda value: value.astype(bf16)
-    pair = [None] * 4
-    for k in (3, 1, 2, 0):
-        pair[k] = parts[2 * k] + send(whole[(2 * k + 1) * rows : (2 * k + 2) * rows], "seq", SWAP).astype(f32)
-    up = send(low(pair[3]), "seq", [(i, i + 2) for i in (0, 1)])
-    down = send(low(pair[1]), "seq", [(i + 2, i) for i in (4, 5)])
-    up = send(low(pair[2] + up.astype(f32)), "seq", [(i, i + 2) for i in range(4)])
-    down = send(low(pair[2] + down.astype(f32)), "seq", [(i + 2, i) for i in range(2, 6)])
-    up = send(low(pair[1] + up.astype(f32)), "seq", [(i, i + 2) for i in range(6)])
-    down = send(low(pair[3] + down.astype(f32)), "seq", [(i + 2, i) for i in range(6)])
-    return pair[0] + up.astype(f32) + down.astype(f32)
-
-
-CORE = [(i, i ^ 1) for i in range(4)]
-ACROSS = [(i, i ^ 2) for i in range(4)]
-ORDER = (0, 2, 1, 3)
-
-
-def scatter_head(partial):
-    rows = partial.shape[0] // 4
-    quarter = [partial[i * rows : (i + 1) * rows] for i in range(4)]
-    far = send(quarter[3], "head", CORE)
-    across = send((quarter[1].astype(f32) + far.astype(f32)).astype(bf16), "head", ACROSS)
-    near = send(quarter[2], "head", CORE)
-    return quarter[0].astype(f32) + near.astype(f32) + across.astype(f32)
-
-
-def gather_head(own):
-    across = send(own, "head", ACROSS)
-    core = send(own, "head", CORE)
-    both = send(across, "head", CORE)
-    return join_rows([own, across, core, both])
-
-
-def to_own_order(array, me):
+    return pieces[0] if len(pieces) == 1 else jnp.concatenate(pieces, axis=0)
+
+
+CORE, ACROSS = 1, 2
+
+
+def scatter_head(near_half, far_half, beside=None):
+    rows = near_half.shape[0] // 2
+    core = send(far_half[rows:], "head", CORE, 4)
+    summed = (far_half[:rows].astype(f32) + core.astype(f32)).astype(bf16)
+    across = send(summed, "head", ACROSS, 4)
+    near = near_half[:rows].astype(f32) + send(near_half[rows:], "head", CORE, 4).astype(f32)
+    if beside is None:
+        return near + across.astype(f32)
+    found = beside(summed)
+    return near + after(across, found).astype(f32), found
+
+
+def gather_head(own, between=lambda near: ()):
+    near = join_rows([own, send(own, "head", CORE, 4)])
+    across = after(send(own, "head", ACROSS, 4), *between(near))
+    return near, join_rows([across, send(across, "head", CORE, 4)])
+
+
+def swap_quarters(array, me):
     split = array.reshape((4, array.shape[0] // 4) + array.shape[1:])
-    return join_rows([lax.dynamic_index_in_dim(split, me ^ mask, 0, keepdims=False) for mask in ORDER])
-
-
-def to_token_order(array, me):
-    split = array.reshape((4, array.shape[0] // 4) + array.shape[1:])
-    pieces = []
-    for quarter in range(4):
-        mask = quarter ^ me
-        pieces.append(lax.dynamic_index_in_dim(split, (mask & 1) * 2 + (mask >> 1), 0, keepdims=False))
-    return join_rows(pieces)
+    return join_rows([lax.dynamic_index_in_dim(split, me ^ mask, 0, keepdims=False) for mask in range(4)])
+
+
+def swap_blocks(array, order):
+    split = array.reshape((BLOCKS, array.shape[0] // BLOCKS) + array.shape[1:])
+    return join_rows([lax.dynamic_index_in_dim(split, order[i], 0, keepdims=False) for i in range(BLOCKS)])
 
 
 def move_kernel(split, rows_ref, cols_ref, in_ref, out_ref):
@@ -447,11 +428,32 @@
     )(col_blocks, array)
 
 
-def ffn_kernel(step, unit_ref, dy_ref, gate_ref, up_ref, down_ref, mixed_ref, ggate_ref, gup_ref):
-    width = gate_ref.shape[1]
+def ffn_kernel(n_gate, step, order_ref, unit_ref, dy_ref, *refs):
+    pieces, down_hbm = refs[:n_gate], refs[n_gate]
+    mixed_ref, ggate_ref, gup_ref, gunit_ref, out_ref, gate_ref, up_ref, down_ref, sems = refs[n_gate + 1 :]
+    width, hidden = gate_ref.shape
+    copies = []
+    rows = width // n_gate
+    for place, held in ((0, gate_ref), (hidden, up_ref)):
+        for i, piece in enumerate(pieces):
+            copies.append((piece.at[:, pl.ds(place, hidden)], held.at[pl.ds(i * rows, rows)]))
+    rows = width // BLOCKS
+    for i in range(BLOCKS):
+        start = pl.multiple_of(order_ref[i] * rows, rows)
+        source = down_hbm.at[pl.ds(start, rows), pl.ds(down_hbm.shape[1] - hidden, hidden)]
+        copies.append((source, down_ref.at[pl.ds(i * rows, rows)]))
+    copies = [pltpu.make_async_copy(*ends, sems.at[i]) for i, ends in enumerate(copies)]
+
+    @pl.when(pl.program_id(0) == 0)
+    def _():
+        for copy in copies:
+            copy.start()
+        for copy in copies:
+            copy.wait()
+
     unit, dy = unit_ref[...], dy_ref[...]
-    for start in range(0, width, step):
-        cols = slice(start, min(start + step, width))
+    for start in range(0, hidden, step):
+        cols = slice(start, min(start + step, hidden))
         gate = nn(unit, gate_ref[:, cols])
         up = nn(unit, up_ref[:, cols])
         gmixed = nn(dy, down_ref[:, cols])
@@ -460,24 +462,67 @@
         mixed_ref[:, cols] = (silu * up).astype(bf16)
         ggate_ref[:, cols] = (gmixed * up * (sig * (1.0 + gate * (1.0 - sig)))).astype(bf16)
         gup_ref[:, cols] = (gmixed * silu).astype(bf16)
-
-
-def feed_forward(unit, dy, gate_w, up_w, down_w):
+    ggate, gup, mixed = ggate_ref[...], gup_ref[...], mixed_ref[...]
+    for start in range(0, width, 512):
+        cols = slice(start, start + 512)
+        gunit_ref[:, cols] = (nt(ggate, gate_ref[cols]) + nt(gup, up_ref[cols])).astype(bf16)
+        out_ref[:, cols] = nt(mixed, down_ref[cols]).astype(bf16)
+
+
+def feed_forward(unit, dy, half, pieces, turned, order, tile):
     tokens, width = unit.shape
-    hidden = gate_w.shape[1]
-    tile = 256 if tokens % 256 == 0 else 128
-    once = pl.BlockSpec((width, hidden), lambda i: (0, 0), pipeline_mode=pl.Buffered(1))
-    lines = pl.BlockSpec((tile, width), lambda i: (i, 0))
-    out = pl.BlockSpec((tile, hidden), lambda i: (i, 0))
+    hidden = pieces[0].shape[1] // 2
+    steps = tokens // tile
+    anywhere = pl.BlockSpec(memory_space=pl.ANY)
+    line = lambda cols, first=0: pl.BlockSpec((tile, cols), lambda i, order: (i + first, 0))
+    out_cols = [hidden] * 3 + [width] * 2
     return pl.pallas_call(
-        functools.partial(ffn_kernel, 256),
-        out_shape=[jax.ShapeDtypeStruct((tokens, hidden), bf16)] * 3,
-        grid=(tokens // tile,),
-        in_specs=[lines, lines, once, once, once],
-        out_specs=[out, out, out],
-        compiler_params=params(56),
-        cost_estimate=cost(6 * tokens * width * hidden, 2 * (2 * tokens * width + 3 * (tokens + width) * hidden)),
-    )(unit, dy, gate_w, up_w, down_w)
+        functools.partial(ffn_kernel, len(pieces), 256),
+        out_shape=[jax.ShapeDtypeStruct((tokens, cols), bf16) for cols in out_cols],
+        grid_spec=pltpu.PrefetchScalarGridSpec(
+            num_scalar_prefetch=1,
+            grid=(steps,),
+            in_specs=[line(width), line(width, half * steps)] + [anywhere] * (len(pieces) + 1),
+            out_specs=[line(cols) for cols in out_cols],
+            scratch_shapes=[pltpu.VMEM((width, hidden), bf16)] * 3
+            + [pltpu.SemaphoreType.DMA((2 * len(pieces) + BLOCKS,))],
+        ),
+        compiler_params=params(58),
+        cost_estimate=cost(12 * tokens * width * hidden, 2 * (4 * tokens * width + 3 * (tokens + width) * hidden)),
+    )(order, unit, dy, *pieces, turned)
+
+
+def weight_kernel(n_parts, order_ref, *refs):
+    lefts, rights, out = refs[:n_parts], refs[n_parts:-1], refs[-1]
+    turned = [left[...].T for left in lefts]
+    start = 0
+    for place in range(0, len(rights), n_parts):
+        total = nn(turned[0], rights[place][...])
+        for part in range(1, n_parts):
+            total = total + nn(turned[part], rights[place + part][...])
+        out[:, start : start + total.shape[1]] = total.astype(bf16)
+        start += total.shape[1]
+
+
+def weight_grads(lefts, rights, order):
+    width = lefts[0].shape[1]
+    rows = width // BLOCKS
+    flat = [part for right in rights for part in right]
+    cols = sum(right[0].shape[1] for right in rights)
+    tokens = sum(left.shape[0] for left in lefts)
+    return pl.pallas_call(
+        functools.partial(weight_kernel, len(lefts)),
+        out_shape=jax.ShapeDtypeStruct((width, cols), bf16),
+        grid_spec=pltpu.PrefetchScalarGridSpec(
+            num_scalar_prefetch=1,
+            grid=(BLOCKS,),
+            in_specs=[pl.BlockSpec((left.shape[0], rows), lambda i, order: (0, i)) for left in lefts]
+            + [pl.BlockSpec(part.shape, lambda i, order: (0, 0), pipeline_mode=pl.Buffered(1)) for part in flat],
+            out_specs=pl.BlockSpec((rows, cols), lambda i, order: (order[i], 0)),
+        ),
+        compiler_params=params(48),
+        cost_estimate=cost(2 * tokens * width * cols, 2 * (tokens + width) * (width + cols)),
+    )(order, *lefts, *flat)
 
 
 def per_device(
@@ -500,34 +545,41 @@
     heads = query_weight.shape[1] // FEAT
     count = rows * length
     quarter = count // 4
+    half = 2 * quarter
     me = lax.axis_index("seq").astype(jnp.int32)
     head_me = lax.axis_index("head").astype(jnp.int32)
-    ids = jnp.arange(BLOCKS, dtype=jnp.int32)
+    order = jnp.arange(BLOCKS, dtype=jnp.int32)
     if n_seq == 8:
-        z, y = me // 2, me % 2
-        to_rel = ((z + ids // 2) % 4) * 2 + (y ^ (ids % 2))
-        to_abs = ((ids // 2 - z) % 4) * 2 + (y ^ (ids % 2))
-    else:
-        to_rel = to_abs = ids
-    own_order = head_me ^ jnp.array(ORDER, jnp.int32)
-    masks = head_me ^ jnp.arange(4, dtype=jnp.int32)
-    token_order = (masks & 1) * 2 + (masks >> 1)
+        order = me ^ order
+    quarters = head_me ^ jnp.arange(4, dtype=jnp.int32)
 
     gain_one = gain_attn.astype(f32)[:, None]
     gain_two = gain_ffn.astype(f32)[:, None]
     scaled = lambda weight, gain: (weight.astype(f32) * gain).astype(bf16)
     qkv_own = jnp.concatenate([query_weight, key_weight, value_weight], axis=1)
-    gather = functools.partial(gather_rows, count=n_seq, me=me)
-    qkv_w = gather(scaled(qkv_own, gain_one))
-    out_w = gather(out_weight.T)
-    gate_w = gather(scaled(gate_weight, gain_two))
-    up_w = gather(scaled(up_weight, gain_two))
-    down_w = gather(down_weight.T)
+    qkv_w = gather_rows(scaled(qkv_own, gain_one), n_seq)
+    pair_own = jnp.concatenate([scaled(gate_weight, gain_two), scaled(up_weight, gain_two)], axis=1)
+    if n_seq == 8:
+        pair_own = after(pair_own, qkv_w[2], qkv_w[4], qkv_w[6])
+        pair_one = send(pair_own, "seq", 2, 8)
+        pair_two = send(after(pair_own, pair_one), "seq", 4, 8)
+        pair_three = send(after(pair_own, pair_two), "seq", 6, 8)
+        pair_w = []
+        for piece in (pair_own, pair_one, pair_two, pair_three):
+            pair_w += [piece, send(piece, "seq", 1, 8)]
+        stages = [(pair_one,), (pair_two, pair_w[1]), (pair_w[3], pair_three)]
+    else:
+        pair_w = gather_rows(pair_own, n_seq)
+        stages = [(), (), ()]
+    qkv_w = join_rows(qkv_w)
+    turned = jnp.concatenate([out_weight.T, down_weight.T], axis=1)
+    turned = lax.all_gather(turned, "seq", axis=0, tiled=True)
+    out_w = swap_blocks(turned[:, : out_weight.shape[0]], order)
 
     flat = tokens.reshape(count, width)
-    unit_one = unit_rows(flat, to_rel, quarter // 2)
-    x_own = move_blocks(flat, own_order[:1], to_rel, f32, quarter)
-    dy = move_blocks(grad_out.reshape(count, width), own_order, to_rel, bf16, quarter)
+    unit_one = unit_rows(flat, order, quarter // 2)
+    x_own = move_blocks(flat, quarters[:1], order, f32, quarter)
+    dy = move_blocks(grad_out.reshape(count, width), quarters, order, bf16, quarter)
     rstd_one = lax.rsqrt(jnp.mean(x_own * x_own, axis=1, keepdims=True) + EPSILON)
 
     docs = jnp.cumsum(doc_reset, axis=1)
@@ -555,7 +607,7 @@
         [((length, values), f32), ((length, heads), f32)],
         flops=3 * unit_flops,
     )
-    state_in, place = exclusive_scan(states, False, me, n_seq)
+    state_in, place = scan_end(scan_begin(states, False, me, n_seq, stages[0]), False, me, n_seq)
     query_tables = [(tables["qa"], False), (tables["qb"], False), (feat_rows, False)]
     key_tables = [(tables["ka"], False), (tables["kb"], False), (feat_rows, False)]
     attended, rden = by_row(
@@ -566,18 +618,31 @@
         place=place,
         flops=3 * unit_flops,
     )
-    attended_own = to_own_order(attended.reshape(count, values), head_me)
-    branch = nt(attended_own, out_w).astype(bf16)
-    hidden = x_own + scatter_head(branch)
+    attended_own = after(swap_quarters(attended.reshape(count, values), head_me), *stages[1])
+    far = nt(attended_own[half:], out_w).astype(bf16)
+    near = nt(attended_own[:half], out_w).astype(bf16)
+    hidden = x_own + scatter_head(near, far)
     rstd_two = lax.rsqrt(jnp.mean(hidden * hidden, axis=1, keepdims=True) + EPSILON)
     unit_two_own = hidden * rstd_two
-    unit_two = gather_head(unit_two_own.astype(bf16))
-
-    mixed, ggate, gup = feed_forward(unit_two, dy, gate_w, up_w, down_w)
-    scaled_two = scatter_head((nt(ggate, gate_w) + nt(gup, up_w)).astype(bf16))
-    grad_gate = scatter_rows(tn(unit_two, ggate).astype(bf16), n_seq)
-    grad_up = scatter_rows(tn(unit_two, gup).astype(bf16), n_seq)
-    grad_down = scatter_rows(tn(dy, mixed).astype(bf16), n_seq)
+    first_half = []
+
+    def near_rows(unit):
+        first_half.extend(feed_forward(unit, dy, 0, pair_w, turned, order, quarter))
+        return first_half
+
+    unit_two = gather_head(after(unit_two_own.astype(bf16), *stages[2]), near_rows)
+    second_half = feed_forward(unit_two[1], dy, 1, pair_w, turned, order, quarter)
+    mixed, ggate, gup, gunit, branch = zip(first_half, second_half)
+    parts = [dy[:half], dy[half:]]
+
+    def ffn_weights(sent):
+        left = [after(unit_two[0], sent), unit_two[1]]
+        first = weight_grads(left, [ggate, gup], order)
+        left = [after(parts[0], first), parts[1]]
+        return first, weight_grads(left, [mixed], order)
+
+    scaled_two, found = scatter_head(*gunit, beside=ffn_weights)
+    grad_pair, grad_down = [scatter_rows(item) for item in found]
 
     dy_own = dy[:quarter].astype(f32)
     grad_hidden = dy_own + rstd_two * (
@@ -585,10 +650,9 @@
     )
     grad_branch = gather_head(grad_hidden.astype(bf16))
 
-    block_own = hidden + scatter_head(nt(mixed, down_w).astype(bf16))
-    block_all = gather_head(block_own.astype(bf16))
-
-    grad_att = to_token_order(nn(grad_branch, out_w).astype(bf16), head_me).reshape(rows, length, values)
+
+    grad_att = join_rows([nn(item, out_w).astype(bf16) for item in grad_branch])
+    grad_att = swap_quarters(grad_att, head_me).reshape(rows, length, values)
     carry, gnum, gden = by_row(
         functools.partial(carry_kernel, heads),
         rows,
@@ -606,8 +670,15 @@
         place=place,
         flops=11 * unit_flops,
     )
-    grad_out_w = scatter_rows(tn(grad_branch, attended_own).astype(bf16), n_seq)
-    carry_in, place_back = exclusive_scan(carry, True, me, n_seq)
+    parts = [attended_own[:half], attended_own[half:]]
+    grad_out_w = weight_grads(grad_branch, [parts], order ^ me if n_seq == 8 else order)
+    out_pairs = scatter_begin(grad_out_w) if n_seq == 8 else [grad_out_w]
+    found = scan_begin(carry, True, me, n_seq)
+    block_own, _ = scatter_head(branch[0], after(branch[1], *grad_branch), beside=lambda _: found)
+    block_own = (hidden + block_own).astype(bf16)
+    carry_in, place_back = scan_end(found, True, me, n_seq)
+    carry_in = after(carry_in, block_own)
+    block_all = join_rows(gather_head(block_own))
     (gqkv,) = by_row(
         functools.partial(finish_back_kernel, heads),
         rows,
@@ -617,23 +688,34 @@
         flops=6 * unit_flops,
     )
     gqkv = gqkv.reshape(count, lanes + values)
-    scaled_one = scatter_head(nt(to_own_order(gqkv, head_me), qkv_w).astype(bf16))
-    grad_qkv = scatter_rows(tn(unit_one, gqkv).astype(bf16), n_seq)
+    gqkv_own = after(swap_quarters(gqkv, head_me), block_all, *out_pairs)
+    grad_out_w = scatter_end(out_pairs) if n_seq == 8 else scatter_rows(out_pairs[0])
+    far = nt(gqkv_own[half:], qkv_w).astype(bf16)
+    near = nt(gqkv_own[:half], qkv_w).astype(bf16)
+    scaled_one = scatter_head(near, far)
+    if n_seq == 8:
+        qkv_pairs = scatter_begin(weight_grads([unit_one], [[gqkv]], order ^ me))
+        grad_qkv = scatter_end(qkv_pairs)
+    else:
+        qkv_pairs = []
+        grad_qkv = scatter_rows(weight_grads([unit_one], [[gqkv]], order))
     unit_one_own = x_own * rstd_one
     grad_x = grad_hidden + rstd_one * (
         scaled_one - unit_one_own * jnp.mean(scaled_one * unit_one_own, axis=1, keepdims=True)
     )
-    grad_x_all = gather_head(grad_x.astype(bf16))
-
-    back = lambda value, kind: move_blocks(value, token_order, to_abs, kind, quarter).reshape(rows, length, width)
+    grad_x_all = join_rows(gather_head(after(grad_x.astype(bf16), grad_out_w, grad_pair, *qkv_pairs)))
+
+    back = lambda value, kind: move_blocks(value, quarters, order, kind, quarter).reshape(rows, length, width)
+    hidden_units = gate_weight.shape[1]
+    grad_gate, grad_up = grad_pair[:, :hidden_units], grad_pair[:, hidden_units:]
     gain_sums = jnp.stack(
         [
             jnp.sum(qkv_own.astype(f32) * grad_qkv, axis=1),
             jnp.sum(gate_weight.astype(f32) * grad_gate + up_weight.astype(f32) * grad_up, axis=1),
         ]
     )
-    gain_sums = gain_sums + send(gain_sums, "head", CORE)
-    gain_sums = gain_sums + send(gain_sums, "head", ACROSS)
+    gain_sums = gain_sums + send(gain_sums, "head", CORE, 4)
+    gain_sums = gain_sums + send(gain_sums, "head", ACROSS, 4)
     grad_qkv = grad_qkv * gain_one
     narrow = heads * FEAT
     return (

time: 1220 us -> 969 us (0.79); the launches traced: 1220 us -> 951 us
  starting transfers between devices: 394 us -> 142 us
  Pallas kernels: 109 us -> 211 us
  matrix products: 122 us -> 21 us
  other arithmetic: 103 us -> 57.2 us
  between operations: 4 us -> 30.6 us
    ppermute x169 -> x82, starting transfers between devices: 394 us -> 142 us  [send(): return lax.ppermute(value, axis, [(i, i ^ mask) for i in range(count)])]
    pallas_call x3 -> x8, Pallas kernels: 39.6 us -> 142 us  [the longest x2 81.5 us: feed_forward(): pl.pallas_call(functools.partial(ffn_kernel, len(pieces), 256), out_shape...]
    dot_general x5 -> x0, matrix products: 50.6 us -> none  [tn(): lax.dot_general(left, right, (((0,), (0,)), ((), ())), preferred_element_...]
    dot_general x5 -> x4, matrix products: 57.9 us -> 9.39 us  [nt(): lax.dot_general(left, right, (((1,), (1,)), ((), ())), preferred_element_...]
    unnamed x35 -> x4, other arithmetic: 29.3 us -> 1.09 us
    convert_element_type x31 -> x11, other arithmetic: 33.4 us -> 17 us  [the longest x4 4.78 us: scatter_head(): summed = (far_half[:rows].astype(f32) + core.astype(f32)).astype(bf16)]
    unnamed x269 -> x220, local copies, waits for them, and re-layouts: 40.4 us -> 39.8 us
    ppermute x169 -> x82, waiting for transfers between devices: 419 us -> 420 us  [send(): return lax.ppermute(value, axis, [(i, i ^ mask) for i in range(count)])]
  transfers between devices with their start and end apart: 169 -> 85, of which waited for: 49 -> 38; matrix products, arithmetic and copies ran while one was open for 16% -> 12% of each run, Pallas kernels for 5% -> 15%
where the time goes in v2:
time: 969 us; the launch traced here: 951 us
  waiting for transfers between devices  420 us (43%)
  Pallas kernels  211 us (22%)
  starting transfers between devices  142 us (15%)
  local copies, waits for them, and re-layouts  70.3 us (7%)
  other arithmetic  57.2 us (6%)
  between operations  30.6 us (3%)
  matrix products  21 us (2%)
    ppermute x82, waiting for transfers between devices, send(): return lax.ppermute(value, axis, [(i, i ^ mask) for i in range(count)])  420 us
    ppermute x82, starting transfers between devices, send(): return lax.ppermute(value, axis, [(i, i ^ mask) for i in range(count)])  142 us
    pallas_call x2, Pallas kernels, feed_forward(): pl.pallas_call(functools.partial(ffn_kernel, len(pieces), 256), out_shape...  81.5 us
    pallas_call x4, Pallas kernels, weight_grads(): pl.pallas_call(functools.partial(weight_kernel, len(lefts)), out_shape=ja...  58.3 us
    pallas_call x6, Pallas kernels, by_row(): pl.pallas_call(kernel, out_shape=shapes, grid_spec=pltpu.PrefetchScalarGr...  52.8 us
    unnamed x220, local copies, waits for them, and re-layouts  39.8 us
  transfers between devices with their start and end apart: 85, of which 38 were waited for; matrix products, arithmetic and copies ran while one was open for 12% of the time, Pallas kernels for 15%

profile of v2, /device:TPU:0, one launch (start us, length us, event | category | flops | bytes accessed | tf_op | source)
XLA Modules:
  0.0 951.4 jit_solution(14864937179719617960)
XLA Ops:
  55.7 16.0 %collective-permute-start.7 = (bf16[256,2816]{1,0:T(8,128)(2,1)}, bf16[256,2816]{1,0:T(8,128)(2,1)}, u32[]{:S(2)}, u32[]{:S(2)}) collective-permute-start(bf16[256,2816]{1,0:T(8,128)(2,1)} %pad_maximum_fusion.8.refs_0_), channel_id=1, source_target_pairs={{0,8},{4,12},{8,0},{12,4},{16,24},{20,28},{24,16},{28,20},{1,9},{5... | collective-permute-start | bytes 4325384 | tf_op jit(solution)/shard_map/ppermute | solution.py:309
  106.1 63.7 %collective-permute-done.9 = bf16[480,128]{1,0:T(8,128)(2,1)S(1)} collective-permute-done((bf16[480,128]{1,0:T(8,128)(2,1)S(1)}, bf16[480,128]{1,0:T(8,128)(2,1)S(1)}, u32[]{:S(2)}, u32[]{:S(2)}) %collective-permute-start.9) | collective-permute-done | bytes 122912 | tf_op jit(solution)/shard_map/ppermute | solution.py:309
  207.3 15.9 %collective-permute-done.15 = bf16[3,160,128]{2,1,0:T(8,128)(2,1)S(1)} collective-permute-done((bf16[3,160,128]{2,1,0:T(8,128)(2,1)S(1)}, bf16[3,160,128]{2,1,0:T(8,128)(2,1)S(1)}, u32[]{:S(2)}, u32[]{:S(2)}) %collective-permute-start.15) | collective-permute-done | bytes 122912 | tf_op jit(solution)/shard_map/ppermute | solution.py:309
  228.5 21.8 %collective-permute-done.18 = bf16[3,160,128]{2,1,0:T(8,128)(2,1)S(1)} collective-permute-done((bf16[3,160,128]{2,1,0:T(8,128)(2,1)S(1)}, bf16[3,160,128]{2,1,0:T(8,128)(2,1)S(1)}, u32[]{:S(2)}, u32[]{:S(2)}) %collective-permute-start.18) | collective-permute-done | bytes 122912 | tf_op jit(solution)/shard_map/ppermute | solution.py:309
  268.4 16.8 %collective-permute-done.22.refs_4_ = bf16[256,2816]{1,0:T(8,128)(2,1)} collective-permute-done((bf16[256,2816]{1,0:T(8,128)(2,1)}, bf16[256,2816]{1,0:T(8,128)(2,1)}, u32[]{:S(2)}, u32[]{:S(2)}) %collective-permute-start.22) | collective-permute-done | bytes 1441824 | tf_op jit(solution)/shard_map/ppermute | solution.py:309
  299.9 31.0 %collective-permute-done.26 = bf16[384,2048]{1,0:T(8,128)(2,1)S(1)} collective-permute-done((bf16[384,2048]{1,0:T(8,128)(2,1)S(1)}, bf16[384,2048]{1,0:T(8,128)(2,1)S(1)}, u32[]{:S(2)}, u32[]{:S(2)}) %collective-permute-start.26) | collective-permute-done | bytes 1572896 | tf_op jit(solution)/shard_map/ppermute | solution.py:309
  342.7 25.9 %collective-permute-done.30.refs_5_ = bf16[256,2816]{1,0:T(8,128)(2,1)} collective-permute-done((bf16[256,2816]{1,0:T(8,128)(2,1)}, bf16[256,2816]{1,0:T(8,128)(2,1)}, u32[]{:S(2)}, u32[]{:S(2)}) %collective-permute-start.30) | collective-permute-done | bytes 1441824 | tf_op jit(solution)/shard_map/ppermute | solution.py:309
  368.6 30.1 %collective-permute-done.31.refs_7_ = bf16[256,2816]{1,0:T(8,128)(2,1)} collective-permute-done((bf16[256,2816]{1,0:T(8,128)(2,1)S(1)}, bf16[256,2816]{1,0:T(8,128)(2,1)}, u32[]{:S(2)}, u32[]{:S(2)}) %collective-permute-start.31) | collective-permute-done | bytes 1441824 | tf_op jit(solution)/shard_map/ppermute | solution.py:309
  398.8 40.9 %shard_map.273 = (bf16[768,1408]{1,0:T(8,128)(2,1)}, bf16[768,1408]{1,0:T(8,128)(2,1)}, bf16[768,1408]{1,0:T(8,128)(2,1)}, bf16[768,2048]{1,0:T(8,128)(2,1)}, bf16[768,2048]{1,0:T(8,128)(2,1)}) custom-call(s32[8]{0:T(128)} %copy-done.36, bf16[768,2048]{1,0:T(8,128)(2,1)} %constant_dynamic-update-slice_fusion.8.unit_ref.refs_0_, bf16[1536,2048]{1,0:T(8,128)(2,1)} %copy-done, ...), custom_call_target="tpu_custom_call" | custom-call | flops 830472192 | bytes 1136640 | tf_op jit(solution)/shard_map/pallas_call | solution.py:479
  444.6 40.7 %shard_map.274 = (bf16[768,1408]{1,0:T(8,128)(2,1)}, bf16[768,1408]{1,0:T(8,128)(2,1)}, bf16[768,1408]{1,0:T(8,128)(2,1)}, bf16[768,2048]{1,0:T(8,128)(2,1)}, bf16[768,2048]{1,0:T(8,128)(2,1)}) custom-call(s32[8]{0:T(128)} %copy-done.36, bf16[768,2048]{1,0:T(8,128)(2,1)} %constant_dynamic-update-slice_fusion.10.unit_ref.refs_1_, bf16[1536,2048]{1,0:T(8,128)(2,1)} %copy-done, ...), custom_call_target="tpu_custom_call" | custom-call | flops 830472192 | bytes 1136640 | tf_op jit(solution)/shard_map/pallas_call | solution.py:479
  492.3 25.5 %shard_map.275 = bf16[2048,2816]{1,0:T(8,128)(2,1)} custom-call(s32[8]{0:T(128)S(1)} %copy-done.37, bf16[768,2048]{1,0:T(8,128)(2,1)} %constant_dynamic-update-slice_fusion.8.unit_ref.refs_0_, bf16[768,2048]{1,0:T(8,128)(2,1)} %constant_dynamic-update-slice_fusion.10.unit_ref.refs_1_, bf16[768,1408]{1,0:T(8,128)(2,1)S(1)} %copy-done.17, ...), custom_call_target="tpu_custom_call" | custom-call | flops 553648128 | bytes 1089536 | tf_op jit(solution)/shard_map/pallas_call | solution.py:513
  528.2 14.2 %shard_map.276 = bf16[2048,1408]{1,0:T(8,128)(2,1)} custom-call(s32[8]{0:T(128)S(1)} %copy-done.37, bf16[768,2048]{1,0:T(8,128)(2,1)} %get-tuple-element.89.refs_0_, bf16[768,2048]{1,0:T(8,128)(2,1)} %get-tuple-element.172.refs_1_, bf16[768,1408]{1,0:T(8,128)(2,1)S(1)} %copy-done.15, bf16[768,1408]{1,0:T(8,128)(2,1)S(1)} %copy-done.16), custom_call_target="tpu_custom_call" | custom-call | flops 276824064 | bytes 774144 | tf_op jit(solution)/shard_map/pallas_call | solution.py:513
  542.5 12.3 %collective-permute-done.37 = bf16[384,2048]{1,0:T(8,128)(2,1)} collective-permute-done((bf16[384,2048]{1,0:T(8,128)(2,1)}, bf16[384,2048]{1,0:T(8,128)(2,1)}, u32[]{:S(2)}, u32[]{:S(2)}) %collective-permute-start.37) | collective-permute-done | bytes 1572896 | tf_op jit(solution)/shard_map/ppermute | solution.py:309
  565.6 34.9 %collective-permute-done.39 = bf16[384,2048]{1,0:T(8,128)(2,1)S(1)} collective-permute-done((bf16[384,2048]{1,0:T(8,128)(2,1)S(1)}, bf16[384,2048]{1,0:T(8,128)(2,1)S(1)}, u32[]{:S(2)}, u32[]{:S(2)}) %collective-permute-start.39) | collective-permute-done | bytes 1572896 | tf_op jit(solution)/shard_map/ppermute | solution.py:309
  625.8 30.5 %collective-permute-start.44 = (bf16[480,128]{1,0:T(8,128)(2,1)S(1)}, bf16[480,128]{1,0:T(8,128)(2,1)S(1)}, u32[]{:S(2)}, u32[]{:S(2)}) collective-permute-start(bf16[480,128]{1,0:T(8,128)(2,1)S(1)} %get-tuple-element.213), channel_id=1, source_target_pairs={{0,8},{4,12},{8,0},{12,4},{16,24},{20,28},{24,16},{28,20},{1,9},{5... | collective-permute-start | bytes 368648 | tf_op jit(solution)/shard_map/ppermute | solution.py:309
  698.3 16.7 %shard_map.280 = (f32[6,256,128]{2,1,0:T(8,128)S(1)}, f32[6,256,512]{2,1,0:T(8,128)S(1)}) custom-call(s32[8]{0:T(128)S(1)} %copy-done.37, bf16[6,256,640]{2,1,0:T(8,128)(2,1)S(1)} %bitcast.170, f32[6,256,8]{2,1,0:T(8,128)S(1)} %convert_element_type.264.edge_ref, f32[6,8,256]{2,1,0:T(8,128)S(1)} %copy-done.35, bf16[6,256,512]{2,1,0:T(8,128)(2,1)S(1)} %copy-done.20, ...), custom_call_target="tpu_custom_call" | custom-call | flops 138412032 | bytes 293632 | tf_op jit(solution)/shard_map/pallas_call | solution.py:241
  722.0 11.7 %collective-permute-done.54 = bf16[3,160,128]{2,1,0:T(8,128)(2,1)S(1)} collective-permute-done((bf16[3,160,128]{2,1,0:T(8,128)(2,1)S(1)}, bf16[3,160,128]{2,1,0:T(8,128)(2,1)S(1)}, u32[]{:S(2)}, u32[]{:S(2)}) %collective-permute-start.54) | collective-permute-done | bytes 122912 | tf_op jit(solution)/shard_map/ppermute | solution.py:309
  742.7 11.4 %collective-permute-done.57 = bf16[3,160,128]{2,1,0:T(8,128)(2,1)S(1)} collective-permute-done((bf16[3,160,128]{2,1,0:T(8,128)(2,1)S(1)}, bf16[3,160,128]{2,1,0:T(8,128)(2,1)S(1)}, u32[]{:S(2)}, u32[]{:S(2)}) %collective-permute-start.57) | collective-permute-done | bytes 122912 | tf_op jit(solution)/shard_map/ppermute | solution.py:309
  803.5 9.6 %shard_map.283 = bf16[2048,640]{1,0:T(8,128)(2,1)S(1)} custom-call(s32[8]{0:T(128)S(1)} %broadcast_xor_fusion.order_ref, bf16[1536,2048]{1,0:T(8,128)(2,1)} %copy-done.5, bf16[1536,640]{1,0:T(8,128)(2,1)S(1)} %bitcast.177), custom_call_target="tpu_custom_call" | custom-call | flops 125829120 | bytes 602112 | tf_op jit(solution)/shard_map/pallas_call | solution.py:513
  816.5 11.0 %collective-permute-done.67 = bf16[256,512]{1,0:T(8,128)(2,1)S(1)} collective-permute-done((bf16[256,512]{1,0:T(8,128)(2,1)}, bf16[256,512]{1,0:T(8,128)(2,1)S(1)}, u32[]{:S(2)}, u32[]{:S(2)}) %collective-permute-start.67) | collective-permute-done | bytes 262176 | tf_op jit(solution)/shard_map/ppermute | solution.py:309
  841.5 10.7 %collective-permute-done.71 = bf16[256,640]{1,0:T(8,128)(2,1)S(1)} collective-permute-done((bf16[256,640]{1,0:T(8,128)(2,1)S(1)}, bf16[256,640]{1,0:T(8,128)(2,1)S(1)}, u32[]{:S(2)}, u32[]{:S(2)}) %collective-permute-start.71) | collective-permute-done | bytes 327712 | tf_op jit(solution)/shard_map/ppermute | solution.py:309
  852.2 9.2 collective-permute-done.72
  880.6 14.3 %collective-permute-done.77 = bf16[256,640]{1,0:T(8,128)(2,1)} collective-permute-done((bf16[256,640]{1,0:T(8,128)(2,1)}, bf16[256,640]{1,0:T(8,128)(2,1)}, u32[]{:S(2)}, u32[]{:S(2)}) %collective-permute-start.77) | collective-permute-done | bytes 327712 | tf_op jit(solution)/shard_map/ppermute | solution.py:309
  894.9 18.7 %collective-permute-done.78 = bf16[256,640]{1,0:T(8,128)(2,1)} collective-permute-done((bf16[256,640]{1,0:T(8,128)(2,1)}, bf16[256,640]{1,0:T(8,128)(2,1)}, u32[]{:S(2)}, u32[]{:S(2)}) %collective-permute-start.78) | collective-permute-done | bytes 327712 | tf_op jit(solution)/shard_map/ppermute | solution.py:309
  (486 shorter events, 387.3 us)
Async XLA Ops:
  7.2 278.0 %all-gather.2.cloned.1.call-start = ((), (), s32[]{:S(2)}) async-start(), calls=%async_computation.2 | async-start | bytes 8847360 | tf_op jit(solution)/shard_map/all_gather | solution.py:576
  10.9 856.1 %reduce-scatter.3.cloned.1.call-start = ((), (), s32[]{:S(2)}) async-start(), calls=%async_computation.3 | async-start | bytes 12976128 | tf_op jit(solution)/shard_map/reduce_scatter | solution.py:341
  12.3 61.4 %collective-permute-start = (bf16[256,640]{1,0:T(8,128)(2,1)}, bf16[256,640]{1,0:T(8,128)(2,1)}, u32[]{:S(2)}, u32[]{:S(2)}) collective-permute-start(bf16[256,640]{1,0:T(8,128)(2,1)} %get-tuple-element.171), channel_id=1, source_target_pairs={{0,4},{4,0},{8,12},{12,8},{16,20},{20,16},{24,28},{28,24},{1,5},{5... | collective-permute-start | bytes 983048 | tf_op jit(solution)/shard_map/ppermute | solution.py:309
  39.5 37.6 %collective-permute-start.2 = (bf16[256,640]{1,0:T(8,128)(2,1)}, bf16[256,640]{1,0:T(8,128)(2,1)S(1)}, u32[]{:S(2)}, u32[]{:S(2)}) collective-permute-start(bf16[256,640]{1,0:T(8,128)(2,1)} %collective-permute-done.1), channel_id=1, source_target_pairs={{0,4},{4,0},{8,12},{12,8},{16,20},{20,16},{24,28},{28,24},{1,5},{5... | collective-permute-start | bytes 983048 | tf_op jit(solution)/shard_map/ppermute | solution.py:309
  55.7 124.5 %collective-permute-start.7 = (bf16[256,2816]{1,0:T(8,128)(2,1)}, bf16[256,2816]{1,0:T(8,128)(2,1)}, u32[]{:S(2)}, u32[]{:S(2)}) collective-permute-start(bf16[256,2816]{1,0:T(8,128)(2,1)} %pad_maximum_fusion.8.refs_0_), channel_id=1, source_target_pairs={{0,8},{4,12},{8,0},{12,4},{16,24},{20,28},{24,16},{28,20},{1,9},{5... | collective-permute-start | bytes 4325384 | tf_op jit(solution)/shard_map/ppermute | solution.py:309
  100.2 69.5 %collective-permute-start.9 = (bf16[480,128]{1,0:T(8,128)(2,1)S(1)}, bf16[480,128]{1,0:T(8,128)(2,1)S(1)}, u32[]{:S(2)}, u32[]{:S(2)}) collective-permute-start(bf16[480,128]{1,0:T(8,128)(2,1)S(1)} %get-tuple-element.221), channel_id=1, source_target_pairs={{0,8},{4,12},{8,0},{12,4},{16,24},{20,28},{24,16},{28,20},{1,9},{5... | collective-permute-start | bytes 368648 | tf_op jit(solution)/shard_map/ppermute | solution.py:309
  100.2 73.5 %collective-permute-start.10 = (bf16[480,128]{1,0:T(8,128)(2,1)S(1)}, bf16[480,128]{1,0:T(8,128)(2,1)S(1)}, u32[]{:S(2)}, u32[]{:S(2)}) collective-permute-start(bf16[480,128]{1,0:T(8,128)(2,1)S(1)} %get-tuple-element.220), channel_id=1, source_target_pairs={{0,12},{4,8},{8,4},{12,0},{16,28},{20,24},{24,20},{28,16},{1,13},{... | collective-permute-start | bytes 368648 | tf_op jit(solution)/shard_map/ppermute | solution.py:309
  101.7 98.3 %collective-permute-start.11 = (bf16[480,128]{1,0:T(8,128)(2,1)}, bf16[480,128]{1,0:T(8,128)(2,1)}, u32[]{:S(2)}, u32[]{:S(2)}) collective-permute-start(bf16[480,128]{1,0:T(8,128)(2,1)} %get-tuple-element.219), channel_id=1, source_target_pairs={{0,16},{4,20},{8,24},{12,28},{16,0},{20,4},{24,8},{28,12},{1,17},{... | collective-permute-start | bytes 368648 | tf_op jit(solution)/shard_map/ppermute | solution.py:309
  104.2 97.9 %collective-permute-start.12 = (bf16[480,128]{1,0:T(8,128)(2,1)}, bf16[480,128]{1,0:T(8,128)(2,1)}, u32[]{:S(2)}, u32[]{:S(2)}) collective-permute-start(bf16[480,128]{1,0:T(8,128)(2,1)} %get-tuple-element.218), channel_id=1, source_target_pairs={{0,20},{4,16},{8,28},{12,24},{16,4},{20,0},{24,12},{28,8},{1,21},{... | collective-permute-start | bytes 368648 | tf_op jit(solution)/shard_map/ppermute | solution.py:309
  200.0 67.4 %collective-permute-start.23 = (bf16[256,2816]{1,0:T(8,128)(2,1)}, bf16[256,2816]{1,0:T(8,128)(2,1)S(1)}, u32[]{:S(2)}, u32[]{:S(2)}) collective-permute-start(bf16[256,2816]{1,0:T(8,128)(2,1)} %pad_maximum_fusion.8.refs_0_), channel_id=1, source_target_pairs={{0,4},{4,0},{8,12},{12,8},{16,20},{20,16},{24,28},{28,24},{1,5},{5... | collective-permute-start | bytes 4325384 | tf_op jit(solution)/shard_map/ppermute | solution.py:309
  207.2 43.2 %collective-permute-start.18 = (bf16[3,160,128]{2,1,0:T(8,128)(2,1)S(1)}, bf16[3,160,128]{2,1,0:T(8,128)(2,1)S(1)}, u32[]{:S(2)}, u32[]{:S(2)}) collective-permute-start(bf16[3,160,128]{2,1,0:T(8,128)(2,1)S(1)} %get-tuple-element.69), channel_id=1, source_target_pairs={{0,16},{4,20},{8,24},{12,28},{16,0},{20,4},{24,8},{28,12},{1,17},{... | collective-permute-start | bytes 368648 | tf_op jit(solution)/shard_map/ppermute | solution.py:309
  225.3 59.9 %collective-permute-start.22 = (bf16[256,2816]{1,0:T(8,128)(2,1)}, bf16[256,2816]{1,0:T(8,128)(2,1)}, u32[]{:S(2)}, u32[]{:S(2)}) collective-permute-start(bf16[256,2816]{1,0:T(8,128)(2,1)} %pad_maximum_fusion.8.refs_0_), channel_id=1, source_target_pairs={{0,16},{4,20},{8,24},{12,28},{16,0},{20,4},{24,8},{28,12},{1,17},{... | collective-permute-start | bytes 4325384 | tf_op jit(solution)/shard_map/ppermute | solution.py:309
  332.5 107.1 %collective-permute-start.33 = (bf16[384,2048]{1,0:T(8,128)(2,1)S(1)}, bf16[384,2048]{1,0:T(8,128)(2,1)}, u32[]{:S(2)}, u32[]{:S(2)}) collective-permute-start(bf16[384,2048]{1,0:T(8,128)(2,1)S(1)} %multiply_convert_fusion), channel_id=1, source_target_pairs={{0,2},{1,3},{2,0},{3,1},{4,6},{5,7},{6,4},{7,5},{8,10},{9,11},{10,... | collective-permute-start | bytes 4718600 | tf_op jit(solution)/shard_map/ppermute | solution.py:309
  334.1 64.6 %collective-permute-start.31 = (bf16[256,2816]{1,0:T(8,128)(2,1)S(1)}, bf16[256,2816]{1,0:T(8,128)(2,1)}, u32[]{:S(2)}, u32[]{:S(2)}) collective-permute-start(bf16[256,2816]{1,0:T(8,128)(2,1)S(1)} %collective-permute-done.28.refs_6_), channel_id=1, source_target_pairs={{0,4},{4,0},{8,12},{12,8},{16,20},{20,16},{24,28},{28,24},{1,5},{5... | collective-permute-start | bytes 4325384 | tf_op jit(solution)/shard_map/ppermute | solution.py:309
  517.9 412.7 %reduce-scatter.5.cloned.1.call-start = ((), (), s32[]{:S(2)}) async-start(), calls=%async_computation.4 | async-start | bytes 6488064 | tf_op jit(solution)/shard_map/reduce_scatter | solution.py:341
  608.1 74.2 %collective-permute-start.32 = (bf16[384,2048]{1,0:T(8,128)(2,1)S(1)}, bf16[384,2048]{1,0:T(8,128)(2,1)S(1)}, u32[]{:S(2)}, u32[]{:S(2)}) collective-permute-start(bf16[384,2048]{1,0:T(8,128)(2,1)S(1)} %slice.199), channel_id=1, source_target_pairs={{0,1},{1,0},{2,3},{3,2},{4,5},{5,4},{6,7},{7,6},{8,9},{9,8},{10,11... | collective-permute-start | bytes 4718600 | tf_op jit(solution)/shard_map/ppermute | solution.py:309
  611.0 71.3 %collective-permute-start.42 = (bf16[384,2048]{1,0:T(8,128)(2,1)S(1)}, bf16[384,2048]{1,0:T(8,128)(2,1)S(1)}, u32[]{:S(2)}, u32[]{:S(2)}) collective-permute-start(bf16[384,2048]{1,0:T(8,128)(2,1)S(1)} %add_convert_fusion.3), channel_id=1, source_target_pairs={{0,2},{1,3},{2,0},{3,1},{4,6},{5,7},{6,4},{7,5},{8,10},{9,11},{10,... | collective-permute-start | bytes 4718600 | tf_op jit(solution)/shard_map/ppermute | solution.py:309
  684.6 57.4 %collective-permute-start.51 = (bf16[384,2048]{1,0:T(8,128)(2,1)}, bf16[384,2048]{1,0:T(8,128)(2,1)}, u32[]{:S(2)}, u32[]{:S(2)}) collective-permute-start(bf16[384,2048]{1,0:T(8,128)(2,1)} %add_convert_fusion.2), channel_id=1, source_target_pairs={{0,2},{1,3},{2,0},{3,1},{4,6},{5,7},{6,4},{7,5},{8,10},{9,11},{10,... | collective-permute-start | bytes 4718600 | tf_op jit(solution)/shard_map/ppermute | solution.py:309
  697.5 65.0 %collective-permute-start.60 = (bf16[256,512]{1,0:T(8,128)(2,1)S(1)}, bf16[256,512]{1,0:T(8,128)(2,1)S(1)}, u32[]{:S(2)}, u32[]{:S(2)}) collective-permute-start(bf16[256,512]{1,0:T(8,128)(2,1)S(1)} %get-tuple-element.190), channel_id=1, source_target_pairs={{0,4},{4,0},{8,12},{12,8},{16,20},{20,16},{24,28},{28,24},{1,5},{5... | collective-permute-start | bytes 786440 | tf_op jit(solution)/shard_map/ppermute | solution.py:309
  792.1 70.3 %collective-permute-start.64 = (bf16[384,2048]{1,0:T(8,128)(2,1)}, bf16[384,2048]{1,0:T(8,128)(2,1)S(1)}, u32[]{:S(2)}, u32[]{:S(2)}) collective-permute-start(bf16[384,2048]{1,0:T(8,128)(2,1)} %slice.257), channel_id=1, source_target_pairs={{0,1},{1,0},{2,3},{3,2},{4,5},{5,4},{6,7},{7,6},{8,9},{9,8},{10,11... | collective-permute-start | bytes 4718600 | tf_op jit(solution)/shard_map/ppermute | solution.py:309
  794.4 68.1 %collective-permute-start.66 = (bf16[384,2048]{1,0:T(8,128)(2,1)}, bf16[384,2048]{1,0:T(8,128)(2,1)S(1)}, u32[]{:S(2)}, u32[]{:S(2)}) collective-permute-start(bf16[384,2048]{1,0:T(8,128)(2,1)} %add_convert_fusion.1), channel_id=1, source_target_pairs={{0,2},{1,3},{2,0},{3,1},{4,6},{5,7},{6,4},{7,5},{8,10},{9,11},{10,... | collective-permute-start | bytes 4718600 | tf_op jit(solution)/shard_map/ppermute | solution.py:309
  870.2 45.2 %collective-permute-start.75 = (bf16[384,2048]{1,0:T(8,128)(2,1)}, bf16[384,2048]{1,0:T(8,128)(2,1)}, u32[]{:S(2)}, u32[]{:S(2)}) collective-permute-start(bf16[384,2048]{1,0:T(8,128)(2,1)} %add_convert_fusion), channel_id=1, source_target_pairs={{0,2},{1,3},{2,0},{3,1},{4,6},{5,7},{6,4},{7,5},{8,10},{9,11},{10,... | collective-permute-start | bytes 4718600 | tf_op jit(solution)/shard_map/ppermute | solution.py:309
  873.0 40.6 %collective-permute-start.78 = (bf16[256,640]{1,0:T(8,128)(2,1)}, bf16[256,640]{1,0:T(8,128)(2,1)}, u32[]{:S(2)}, u32[]{:S(2)}) collective-permute-start(bf16[256,640]{1,0:T(8,128)(2,1)} %get-tuple-element.185), channel_id=1, source_target_pairs={{0,16},{4,20},{8,24},{12,28},{16,0},{20,4},{24,8},{28,12},{1,17},{... | collective-permute-start | bytes 983048 | tf_op jit(solution)/shard_map/ppermute | solution.py:309
  874.1 39.5 %collective-permute-start.79 = (bf16[256,640]{1,0:T(8,128)(2,1)}, bf16[256,640]{1,0:T(8,128)(2,1)}, u32[]{:S(2)}, u32[]{:S(2)}) collective-permute-start(bf16[256,640]{1,0:T(8,128)(2,1)} %get-tuple-element.184), channel_id=1, source_target_pairs={{0,24},{4,28},{8,16},{12,20},{16,8},{20,12},{24,0},{28,4},{1,25},{... | collective-permute-start | bytes 983048 | tf_op jit(solution)/shard_map/ppermute | solution.py:309
  (152 other events, 2896.7 us)
Sparse Core Ops, SparseCore 0:
  11.0 172.6 all-gather.1
  518.0 245.0 reduce-scatter.2
  766.7 156.7 reduce-scatter.4

commit v3 on v2

--- a/solution.py
+++ b/solution.py
@@ -323,22 +323,30 @@
     return lax.optimization_barrier((value, earlier))[0]
 
 
-def scatter_begin(whole):
+def split_order(order, n_seq):
+    return jnp.array([0, 4, 1, 5, 2, 6, 3, 7], jnp.int32) if n_seq == 8 else order
+
+
+def scatter_begin(whole, n_seq):
+    if n_seq != 8:
+        return (lax.psum_scatter(whole, "seq", scatter_dimension=0, tiled=True).astype(f32),)
     rows = whole.shape[0] // 8
-    part = lambda i: whole[i * rows : (i + 1) * rows]
-    pairs = [part(mask).astype(f32) + send(part(mask + 1), "seq", 1, 8).astype(f32) for mask in (2, 4, 6, 0)]
-    return [pair.astype(bf16) for pair in pairs[:3]] + [pairs[3]]
-
-
-def scatter_end(pairs):
-    total = pairs[3]
-    for pair, mask in zip(pairs, (2, 4, 6)):
-        total = total + send(pair, "seq", mask, 8).astype(f32)
+    other = send(whole[4 * rows :], "seq", 1, 8)
+    pairs = [
+        whole[i * rows : (i + 1) * rows].astype(f32) + other[i * rows : (i + 1) * rows].astype(f32) for i in range(4)
+    ]
+    return (pairs[0],) + tuple(pair.astype(bf16) for pair in pairs[1:])
+
+
+def scatter_sends(pairs):
+    return [send(pair, "seq", 2 * place + 2, 8) for place, pair in enumerate(pairs[1:])]
+
+
+def scatter_end(pairs, terms):
+    total = pairs[0]
+    for term in terms:
+        total = total + term.astype(f32)
     return total
-
-
-def scatter_rows(whole):
-    return lax.psum_scatter(whole, "seq", scatter_dimension=0, tiled=True).astype(f32)
 
 
 def join_rows(pieces):
@@ -348,50 +356,40 @@
 CORE, ACROSS = 1, 2
 
 
-def scatter_head(near_half, far_half, beside=None):
-    rows = near_half.shape[0] // 2
-    core = send(far_half[rows:], "head", CORE, 4)
-    summed = (far_half[:rows].astype(f32) + core.astype(f32)).astype(bf16)
+def scatter_head(quarters, beside=None):
+    core = send(quarters[3], "head", CORE, 4)
+    summed = (quarters[2].astype(f32) + core.astype(f32)).astype(bf16)
     across = send(summed, "head", ACROSS, 4)
-    near = near_half[:rows].astype(f32) + send(near_half[rows:], "head", CORE, 4).astype(f32)
-    if beside is None:
-        return near + across.astype(f32)
-    found = beside(summed)
-    return near + after(across, found).astype(f32), found
+    near = send(quarters[1], "head", CORE, 4)
+    found = () if beside is None else beside(summed)
+    return (quarters[0], near, after(across, found)), found
 
 
 def gather_head(own, between=lambda near: ()):
-    near = join_rows([own, send(own, "head", CORE, 4)])
+    near = [own, send(own, "head", CORE, 4)]
     across = after(send(own, "head", ACROSS, 4), *between(near))
-    return near, join_rows([across, send(across, "head", CORE, 4)])
-
-
-def swap_quarters(array, me):
-    split = array.reshape((4, array.shape[0] // 4) + array.shape[1:])
-    return join_rows([lax.dynamic_index_in_dim(split, me ^ mask, 0, keepdims=False) for mask in range(4)])
-
-
-def swap_blocks(array, order):
-    split = array.reshape((BLOCKS, array.shape[0] // BLOCKS) + array.shape[1:])
-    return join_rows([lax.dynamic_index_in_dim(split, order[i], 0, keepdims=False) for i in range(BLOCKS)])
-
-
-def move_kernel(split, rows_ref, cols_ref, in_ref, out_ref):
+    return near + [across, send(across, "head", CORE, 4)]
+
+
+def move_columns(cols_ref, in_ref, out_ref):
     width = in_ref.shape[1] // BLOCKS
     for block in range(BLOCKS):
         start = pl.multiple_of(cols_ref[block] * width, 128)
         out_ref[:, block * width : (block + 1) * width] = in_ref[:, pl.ds(start, width)].astype(out_ref.dtype)
 
 
-def move_blocks(array, row_blocks, col_blocks, out_type, quarter):
+def move_kernel(rows_ref, cols_ref, in_ref, out_ref):
+    move_columns(cols_ref, in_ref, out_ref)
+
+
+def move_blocks(array, row_blocks, col_blocks, quarter):
     width = array.shape[1]
     split = 2 if quarter % 32 == 0 else 1
     tile = quarter // split
     count = row_blocks.shape[0]
-    shape = jax.ShapeDtypeStruct((count * quarter, width), out_type)
-    return pl.pallas_call(
-        functools.partial(move_kernel, split),
-        out_shape=shape,
+    return pl.pallas_call(
+        move_kernel,
+        out_shape=jax.ShapeDtypeStruct((count * quarter, width), array.dtype),
         grid_spec=pltpu.PrefetchScalarGridSpec(
             num_scalar_prefetch=2,
             grid=(count, split),
@@ -399,8 +397,37 @@
             out_specs=pl.BlockSpec((tile, width), lambda i, j, rows, cols: (i * split + j, 0)),
         ),
         compiler_params=params(),
-        cost_estimate=cost(0, shape.size * (array.dtype.itemsize + shape.dtype.itemsize)),
+        cost_estimate=cost(0, 2 * count * quarter * width * array.dtype.itemsize),
     )(row_blocks, col_blocks, array)
+
+
+def place_kernel(rows_ref, cols_ref, *refs):
+    pieces, out_ref = refs[:2], refs[-1]
+    for place, piece in enumerate(pieces):
+        pl.when(pl.program_id(0) == place)(functools.partial(move_columns, cols_ref, piece, out_ref))
+
+
+def place_quarters(pieces, row_blocks, col_blocks, out_type):
+    quarter, width = pieces[0].shape
+    shape = jax.ShapeDtypeStruct((4 * quarter, width), out_type)
+    whole = None
+    for start in (0, 2):
+        held = [] if whole is None else [whole]
+        whole = pl.pallas_call(
+            place_kernel,
+            out_shape=shape,
+            grid_spec=pltpu.PrefetchScalarGridSpec(
+                num_scalar_prefetch=2,
+                grid=(2,),
+                in_specs=[pl.BlockSpec((quarter, width), lambda i, rows, cols: (0, 0))] * 2
+                + [pl.BlockSpec(memory_space=pl.ANY)] * len(held),
+                out_specs=pl.BlockSpec((quarter, width), lambda i, rows, cols, start=start: (rows[start + i], 0)),
+            ),
+            input_output_aliases={4: 0} if held else {},
+            compiler_params=params(40),
+            cost_estimate=cost(0, shape.size * 4),
+        )(row_blocks, col_blocks, *pieces[start : start + 2], *held)
+    return whole
 
 
 def unit_kernel(cols_ref, in_ref, out_ref):
@@ -428,35 +455,163 @@
     )(col_blocks, array)
 
 
-def ffn_kernel(n_gate, step, order_ref, unit_ref, dy_ref, *refs):
-    pieces, down_hbm = refs[:n_gate], refs[n_gate]
-    mixed_ref, ggate_ref, gup_ref, gunit_ref, out_ref, gate_ref, up_ref, down_ref, sems = refs[n_gate + 1 :]
+def fit(rows):
+    return next(tile for tile in (128, 96, 64, 48, 32, 16) if rows % tile == 0)
+
+
+def add_norm_kernel(base_ref, a_ref, b_ref, c_ref, sum_ref, unit_ref):
+    total = base_ref[...].astype(f32) + (a_ref[...].astype(f32) + b_ref[...].astype(f32) + c_ref[...].astype(f32))
+    rstd = lax.rsqrt(jnp.mean(total * total, axis=1, keepdims=True) + EPSILON)
+    sum_ref[...] = total
+    unit_ref[...] = (total * rstd).astype(bf16)
+
+
+def norm_back_kernel(base_ref, rest_ref, a_ref, b_ref, c_ref, *outs):
+    base = base_ref[...].astype(f32)
+    rstd = lax.rsqrt(jnp.mean(base * base, axis=1, keepdims=True) + EPSILON)
+    unit = base * rstd
+    grad = a_ref[...].astype(f32) + b_ref[...].astype(f32) + c_ref[...].astype(f32)
+    total = rest_ref[...].astype(f32) + rstd * (grad - unit * jnp.mean(grad * unit, axis=1, keepdims=True))
+    for out in outs:
+        out[...] = total.astype(out.dtype)
+
+
+def on_quarter(kernel, arrays, rows, out_types):
+    width = arrays[0].shape[1]
+    tile = fit(rows)
+    spec = pl.BlockSpec((tile, width), lambda i: (i, 0))
+    return pl.pallas_call(
+        kernel,
+        out_shape=[jax.ShapeDtypeStruct((rows, width), kind) for kind in out_types],
+        grid=(rows // tile,),
+        in_specs=[spec] * len(arrays),
+        out_specs=[spec] * len(out_types),
+        compiler_params=params(),
+        cost_estimate=cost(0, rows * width * 16),
+    )(*arrays)
+
+
+def first_kernel(n, unit_ref, *refs):
+    pieces, (out_ref, joined_ref, held_ref, sems) = refs[:n], refs[n:]
+    rows = held_ref.shape[0] // n
+
+    @pl.when(pl.program_id(0) == 0)
+    def _():
+        copies = [pltpu.make_async_copy(pieces[i], held_ref.at[pl.ds(i * rows, rows)], sems.at[i]) for i in range(n)]
+        for copy in copies:
+            copy.start()
+        for copy in copies:
+            copy.wait()
+        joined_ref[...] = held_ref[...]
+
+    out_ref[...] = nn(unit_ref[...], held_ref[...]).astype(bf16)
+
+
+def first_product(unit, pieces, tile):
+    tokens, width = unit.shape
+    cols = pieces[0].shape[1]
+    return pl.pallas_call(
+        functools.partial(first_kernel, len(pieces)),
+        out_shape=[jax.ShapeDtypeStruct((tokens, cols), bf16), jax.ShapeDtypeStruct((width, cols), bf16)],
+        grid=(tokens // tile,),
+        in_specs=[pl.BlockSpec((tile, width), lambda i: (i, 0))] + [pl.BlockSpec(memory_space=pl.ANY)] * len(pieces),
+        out_specs=[pl.BlockSpec((tile, cols), lambda i: (i, 0)), pl.BlockSpec((width, cols), lambda i: (0, 0))],
+        scratch_shapes=[pltpu.VMEM((width, cols), bf16), pltpu.SemaphoreType.DMA((len(pieces),))],
+        compiler_params=params(),
+        cost_estimate=cost(2 * tokens * width * cols, 2 * (tokens + width) * (width + cols)),
+    )(unit, *pieces)
+
+
+def quarter_kernel(order_ref, in_ref, weight_ref, *outs):
+    values = in_ref[...]
+    width = weight_ref.shape[0]
+    for start in range(0, width, 512):
+        part = nt(values, weight_ref[start : start + 512]).astype(bf16)
+        for place, out in enumerate(outs):
+
+            @pl.when(pl.program_id(0) == place)
+            def _(out=out, part=part, start=start):
+                out[:, start : start + 512] = part
+
+
+def quarter_products(array, weight, quarters, top):
+    width, cols = weight.shape
+    rows = array.shape[0] // 4
+    return pl.pallas_call(
+        quarter_kernel,
+        out_shape=[jax.ShapeDtypeStruct((rows, width), bf16)] * 2,
+        grid_spec=pltpu.PrefetchScalarGridSpec(
+            num_scalar_prefetch=1,
+            grid=(2,),
+            in_specs=[
+                pl.BlockSpec((rows, cols), lambda i, order: (order[top - i], 0)),
+                pl.BlockSpec((width, cols), lambda i, order: (0, 0), pipeline_mode=pl.Buffered(1)),
+            ],
+            out_specs=[pl.BlockSpec((rows, width), lambda i, order: (0, 0))] * 2,
+        ),
+        compiler_params=params(),
+        cost_estimate=cost(4 * rows * width * cols, 4 * rows * width),
+    )(quarters, array, weight)
+
+
+def back_kernel(order_ref, *refs):
+    pieces, weight_ref, out_ref = refs[:4], refs[4], refs[5]
+    for place, piece in enumerate(pieces):
+
+        @pl.when(pl.program_id(0) == place)
+        def _(piece=piece):
+            out_ref[...] = nn(piece[...], weight_ref[...]).astype(bf16)
+
+
+def back_product(pieces, weight, quarters):
+    rows, width = pieces[0].shape
+    cols = weight.shape[1]
+    return pl.pallas_call(
+        back_kernel,
+        out_shape=jax.ShapeDtypeStruct((4 * rows, cols), bf16),
+        grid_spec=pltpu.PrefetchScalarGridSpec(
+            num_scalar_prefetch=1,
+            grid=(4,),
+            in_specs=[pl.BlockSpec((rows, width), lambda i, order: (0, 0), pipeline_mode=pl.Buffered(1))] * 4
+            + [pl.BlockSpec((width, cols), lambda i, order: (0, 0), pipeline_mode=pl.Buffered(1))],
+            out_specs=pl.BlockSpec((rows, cols), lambda i, order: (order[i], 0)),
+        ),
+        compiler_params=params(),
+        cost_estimate=cost(8 * rows * width * cols, 8 * rows * width),
+    )(quarters, *pieces, weight)
+
+
+def ffn_kernel(step, order_ref, near_ref, core_ref, gmixed_ref, gate_hbm, up_hbm, down_hbm, *refs):
+    mixed_ref, ggate_ref, gup_ref, gunit_refs, out_refs = refs[0], refs[1], refs[2], refs[3:5], refs[5:7]
+    gate_ref, up_ref, down_ref, unit_ref, sems = refs[7:]
     width, hidden = gate_ref.shape
+    rows = width // BLOCKS
     copies = []
-    rows = width // n_gate
-    for place, held in ((0, gate_ref), (hidden, up_ref)):
-        for i, piece in enumerate(pieces):
-            copies.append((piece.at[:, pl.ds(place, hidden)], held.at[pl.ds(i * rows, rows)]))
-    rows = width // BLOCKS
     for i in range(BLOCKS):
         start = pl.multiple_of(order_ref[i] * rows, rows)
-        source = down_hbm.at[pl.ds(start, rows), pl.ds(down_hbm.shape[1] - hidden, hidden)]
-        copies.append((source, down_ref.at[pl.ds(i * rows, rows)]))
+        for source, held in ((gate_hbm, gate_ref), (up_hbm, up_ref)):
+            copies.append((source.at[pl.ds(start, rows)], held.at[pl.ds(i * rows, rows)]))
+    copies.append((down_hbm, down_ref))
     copies = [pltpu.make_async_copy(*ends, sems.at[i]) for i, ends in enumerate(copies)]
 
     @pl.when(pl.program_id(0) == 0)
     def _():
         for copy in copies:
             copy.start()
+        unit_ref[...] = near_ref[...]
         for copy in copies:
             copy.wait()
 
-    unit, dy = unit_ref[...], dy_ref[...]
+    @pl.when(pl.program_id(0) == 1)
+    def _():
+        unit_ref[...] = core_ref[...]
+
+    unit = unit_ref[...]
     for start in range(0, hidden, step):
         cols = slice(start, min(start + step, hidden))
         gate = nn(unit, gate_ref[:, cols])
         up = nn(unit, up_ref[:, cols])
-        gmixed = nn(dy, down_ref[:, cols])
+        gmixed = gmixed_ref[:, cols].astype(f32)
         sig = jax.nn.sigmoid(gate)
         silu = gate * sig
         mixed_ref[:, cols] = (silu * up).astype(bf16)
@@ -465,64 +620,109 @@
     ggate, gup, mixed = ggate_ref[...], gup_ref[...], mixed_ref[...]
     for start in range(0, width, 512):
         cols = slice(start, start + 512)
-        gunit_ref[:, cols] = (nt(ggate, gate_ref[cols]) + nt(gup, up_ref[cols])).astype(bf16)
-        out_ref[:, cols] = nt(mixed, down_ref[cols]).astype(bf16)
-
-
-def feed_forward(unit, dy, half, pieces, turned, order, tile):
-    tokens, width = unit.shape
-    hidden = pieces[0].shape[1] // 2
-    steps = tokens // tile
+        gunit = (nt(ggate, gate_ref[cols]) + nt(gup, up_ref[cols])).astype(bf16)
+        out = nt(mixed, down_ref[cols]).astype(bf16)
+        for place in range(2):
+
+            @pl.when(pl.program_id(0) == place)
+            def _(place=place, cols=cols, gunit=gunit, out=out):
+                gunit_refs[place][:, cols] = gunit
+                out_refs[place][:, cols] = out
+
+
+def feed_forward(units, gmixed, half, pair, down, order):
+    rows, width = units[0].shape
+    hidden = down.shape[1]
     anywhere = pl.BlockSpec(memory_space=pl.ANY)
-    line = lambda cols, first=0: pl.BlockSpec((tile, cols), lambda i, order: (i + first, 0))
-    out_cols = [hidden] * 3 + [width] * 2
-    return pl.pallas_call(
-        functools.partial(ffn_kernel, len(pieces), 256),
-        out_shape=[jax.ShapeDtypeStruct((tokens, cols), bf16) for cols in out_cols],
+    fixed = pl.BlockSpec((rows, width), lambda i, order: (0, 0))
+    line = lambda first=0: pl.BlockSpec((rows, hidden), lambda i, order: (i + first, 0))
+    shapes = [jax.ShapeDtypeStruct((2 * rows, hidden), bf16)] * 3 + [jax.ShapeDtypeStruct((rows, width), bf16)] * 4
+    once = pl.BlockSpec((rows, width), lambda i, order: (0, 0), pipeline_mode=pl.Buffered(1))
+    return pl.pallas_call(
+        functools.partial(ffn_kernel, 256),
+        out_shape=shapes,
         grid_spec=pltpu.PrefetchScalarGridSpec(
             num_scalar_prefetch=1,
-            grid=(steps,),
-            in_specs=[line(width), line(width, half * steps)] + [anywhere] * (len(pieces) + 1),
-            out_specs=[line(cols) for cols in out_cols],
+            grid=(2,),
+            in_specs=[once, once, line(2 * half), anywhere, anywhere, anywhere],
+            out_specs=[line()] * 3 + [fixed] * 4,
             scratch_shapes=[pltpu.VMEM((width, hidden), bf16)] * 3
-            + [pltpu.SemaphoreType.DMA((2 * len(pieces) + BLOCKS,))],
+            + [pltpu.VMEM((rows, width), bf16), pltpu.SemaphoreType.DMA((2 * BLOCKS + 1,))],
         ),
-        compiler_params=params(58),
-        cost_estimate=cost(12 * tokens * width * hidden, 2 * (4 * tokens * width + 3 * (tokens + width) * hidden)),
-    )(order, unit, dy, *pieces, turned)
-
-
-def weight_kernel(n_parts, order_ref, *refs):
-    lefts, rights, out = refs[:n_parts], refs[n_parts:-1], refs[-1]
-    turned = [left[...].T for left in lefts]
-    start = 0
-    for place in range(0, len(rights), n_parts):
-        total = nn(turned[0], rights[place][...])
-        for part in range(1, n_parts):
-            total = total + nn(turned[part], rights[place + part][...])
-        out[:, start : start + total.shape[1]] = total.astype(bf16)
-        start += total.shape[1]
-
-
-def weight_grads(lefts, rights, order):
-    width = lefts[0].shape[1]
+        compiler_params=params(60),
+        cost_estimate=cost(20 * rows * width * hidden, 2 * (8 * rows * width + 3 * width * hidden)),
+    )(order, *units, gmixed, *pair, down)
+
+
+def weight_kernel(layout, order_ref, quarters_ref, *refs):
+    refs, out = list(refs[:-1]), refs[-1]
+    total = None
+    for n_left, n_right in layout:
+        lefts, rights = [refs.pop(0)[...] for _ in range(n_left)], [refs.pop(0)[...] for _ in range(n_right)]
+        left, right = [jnp.concatenate(item, axis=0) if len(item) > 1 else item[0] for item in (lefts, rights)]
+        part = nn(left.T, right)
+        total = part if total is None else total + part
+    out[...] = total.astype(bf16)
+
+
+def weight_grads(parts, order, quarters):
+    width = parts[0][0][0][0].shape[1]
     rows = width // BLOCKS
-    flat = [part for right in rights for part in right]
-    cols = sum(right[0].shape[1] for right in rights)
-    tokens = sum(left.shape[0] for left in lefts)
-    return pl.pallas_call(
-        functools.partial(weight_kernel, len(lefts)),
+    cols = parts[0][1][0][0].shape[1]
+    arrays, specs, tokens = [], [], 0
+    for pieces in parts:
+        for side, side_pieces in enumerate(pieces):
+            for array, *place in side_pieces:
+                n = array.shape[0] // (1 if not place else 4 if place[0] == "q" else 2)
+
+                def index(i, order, quarters, side=side, place=tuple(place)):
+                    row = 0 if not place else quarters[place[1]] if place[0] == "q" else place[0]
+                    return (row, 0 if side else i)
+
+                mode = {"pipeline_mode": pl.Buffered(1)} if side else {}
+                specs.append(pl.BlockSpec((n, cols if side else rows), index, **mode))
+                arrays.append(array)
+                tokens += n if side else 0
+    return pl.pallas_call(
+        functools.partial(weight_kernel, tuple((len(lefts), len(rights)) for lefts, rights in parts)),
         out_shape=jax.ShapeDtypeStruct((width, cols), bf16),
+        grid_spec=pltpu.PrefetchScalarGridSpec(
+            num_scalar_prefetch=2,
+            grid=(BLOCKS,),
+            in_specs=specs,
+            out_specs=pl.BlockSpec((rows, cols), lambda i, order, quarters: (order[i], 0)),
+        ),
+        compiler_params=params(48),
+        cost_estimate=cost(2 * tokens * width * cols, 2 * (tokens + width) * (width + cols)),
+    )(order, quarters, *arrays)
+
+
+def pair_kernel(order_ref, *refs):
+    units, (ggate0, gup0, ggate1, gup1), out = refs[:4], refs[4:8], refs[8]
+    cols = ggate0.shape[1]
+    near = jnp.concatenate([units[0][...], units[1][...]], axis=0).T
+    far = jnp.concatenate([units[2][...], units[3][...]], axis=0).T
+    out[:, :cols] = (nn(near, ggate0[...]) + nn(far, ggate1[...])).astype(bf16)
+    out[:, cols:] = (nn(near, gup0[...]) + nn(far, gup1[...])).astype(bf16)
+
+
+def pair_grads(units, grads, order):
+    quarter, width = units[0].shape
+    rows = width // BLOCKS
+    cols = grads[0].shape[1]
+    held = pl.BlockSpec((2 * quarter, cols), lambda i, order: (0, 0), pipeline_mode=pl.Buffered(1))
+    return pl.pallas_call(
+        pair_kernel,
+        out_shape=jax.ShapeDtypeStruct((width, 2 * cols), bf16),
         grid_spec=pltpu.PrefetchScalarGridSpec(
             num_scalar_prefetch=1,
             grid=(BLOCKS,),
-            in_specs=[pl.BlockSpec((left.shape[0], rows), lambda i, order: (0, i)) for left in lefts]
-            + [pl.BlockSpec(part.shape, lambda i, order: (0, 0), pipeline_mode=pl.Buffered(1)) for part in flat],
-            out_specs=pl.BlockSpec((rows, cols), lambda i, order: (order[i], 0)),
+            in_specs=[pl.BlockSpec((quarter, rows), lambda i, order: (0, i))] * 4 + [held] * 4,
+            out_specs=pl.BlockSpec((rows, 2 * cols), lambda i, order: (order[i], 0)),
         ),
         compiler_params=params(48),
-        cost_estimate=cost(2 * tokens * width * cols, 2 * (tokens + width) * (width + cols)),
-    )(order, *lefts, *flat)
+        cost_estimate=cost(16 * quarter * width * cols, 2 * (4 * quarter + width) * (width + 2 * cols)),
+    )(order, *units, *grads)
 
 
 def per_device(
@@ -557,30 +757,18 @@
     gain_two = gain_ffn.astype(f32)[:, None]
     scaled = lambda weight, gain: (weight.astype(f32) * gain).astype(bf16)
     qkv_own = jnp.concatenate([query_weight, key_weight, value_weight], axis=1)
-    qkv_w = gather_rows(scaled(qkv_own, gain_one), n_seq)
-    pair_own = jnp.concatenate([scaled(gate_weight, gain_two), scaled(up_weight, gain_two)], axis=1)
-    if n_seq == 8:
-        pair_own = after(pair_own, qkv_w[2], qkv_w[4], qkv_w[6])
-        pair_one = send(pair_own, "seq", 2, 8)
-        pair_two = send(after(pair_own, pair_one), "seq", 4, 8)
-        pair_three = send(after(pair_own, pair_two), "seq", 6, 8)
-        pair_w = []
-        for piece in (pair_own, pair_one, pair_two, pair_three):
-            pair_w += [piece, send(piece, "seq", 1, 8)]
-        stages = [(pair_one,), (pair_two, pair_w[1]), (pair_w[3], pair_three)]
-    else:
-        pair_w = gather_rows(pair_own, n_seq)
-        stages = [(), (), ()]
-    qkv_w = join_rows(qkv_w)
-    turned = jnp.concatenate([out_weight.T, down_weight.T], axis=1)
-    turned = lax.all_gather(turned, "seq", axis=0, tiled=True)
-    out_w = swap_blocks(turned[:, : out_weight.shape[0]], order)
+    gate_w = lax.all_gather(scaled(gate_weight, gain_two), "seq", axis=0, tiled=True)
+    up_w = lax.all_gather(after(scaled(up_weight, gain_two), gate_w), "seq", axis=0, tiled=True)
+    pair_w = (gate_w, up_w)
+    qkv_pieces = gather_rows(scaled(qkv_own, gain_one), n_seq)
+    tie = lambda value, found: after(value, *found) if n_seq == 8 else value
+    out_pieces = gather_rows(tie(out_weight.T, qkv_pieces), n_seq)
+    down_pieces = gather_rows(tie(down_weight.T, out_pieces[2::2]), n_seq)
 
     flat = tokens.reshape(count, width)
     unit_one = unit_rows(flat, order, quarter // 2)
-    x_own = move_blocks(flat, quarters[:1], order, f32, quarter)
-    dy = move_blocks(grad_out.reshape(count, width), quarters, order, bf16, quarter)
-    rstd_one = lax.rsqrt(jnp.mean(x_own * x_own, axis=1, keepdims=True) + EPSILON)
+    x_own = move_blocks(flat, quarters[:1], order, quarter)
+    dy = move_blocks(grad_out.reshape(count, width), quarters, order, quarter)
 
     docs = jnp.cumsum(doc_reset, axis=1)
     final = docs[:, -1:]
@@ -592,7 +780,8 @@
     lanes = 2 * heads * FEAT
     values = heads * VHEAD
     unit_flops = 2 * rows * heads * length * WIDE * VHEAD
-    qkv = nn(unit_one, qkv_w).astype(bf16).reshape(rows, length, lanes + values)
+    qkv, qkv_w = first_product(unit_one, qkv_pieces, quarter)
+    qkv = qkv.reshape(rows, length, lanes + values)
     (states,) = by_row(
         functools.partial(state_kernel, heads),
         rows,
@@ -607,7 +796,7 @@
         [((length, values), f32), ((length, heads), f32)],
         flops=3 * unit_flops,
     )
-    state_in, place = scan_end(scan_begin(states, False, me, n_seq, stages[0]), False, me, n_seq)
+    state_in, place = scan_end(scan_begin(states, False, me, n_seq, (gate_w,)), False, me, n_seq)
     query_tables = [(tables["qa"], False), (tables["qb"], False), (feat_rows, False)]
     key_tables = [(tables["ka"], False), (tables["kb"], False), (feat_rows, False)]
     attended, rden = by_row(
@@ -618,41 +807,41 @@
         place=place,
         flops=3 * unit_flops,
     )
-    attended_own = after(swap_quarters(attended.reshape(count, values), head_me), *stages[1])
-    far = nt(attended_own[half:], out_w).astype(bf16)
-    near = nt(attended_own[:half], out_w).astype(bf16)
-    hidden = x_own + scatter_head(near, far)
-    rstd_two = lax.rsqrt(jnp.mean(hidden * hidden, axis=1, keepdims=True) + EPSILON)
-    unit_two_own = hidden * rstd_two
+    attended_flat = attended.reshape(count, values)
+    out_w = join_rows(out_pieces)
+    far = quarter_products(attended_flat, out_w, quarters, 3)
+    near = quarter_products(attended_flat, out_w, quarters, 1)
+    branch = [near[1], near[0], far[1], far[0]]
+
+    def grad_mixed(sent):
+        down = join_rows(down_pieces)
+        return down, nn(after(dy, sent), down).astype(bf16)
+
+    branch, (down_w, gmixed) = scatter_head(branch, beside=grad_mixed)
+    hidden, unit_two = on_quarter(add_norm_kernel, [x_own, *branch], quarter, [f32, bf16])
     first_half = []
 
-    def near_rows(unit):
-        first_half.extend(feed_forward(unit, dy, 0, pair_w, turned, order, quarter))
+    def near_rows(units):
+        first_half.extend(feed_forward(units, gmixed, 0, pair_w, down_w, order))
         return first_half
 
-    unit_two = gather_head(after(unit_two_own.astype(bf16), *stages[2]), near_rows)
-    second_half = feed_forward(unit_two[1], dy, 1, pair_w, turned, order, quarter)
-    mixed, ggate, gup, gunit, branch = zip(first_half, second_half)
-    parts = [dy[:half], dy[half:]]
+    units = gather_head(unit_two, near_rows)
+    second_half = feed_forward(units[2:], gmixed, 1, pair_w, down_w, order)
+    halves = first_half, second_half
+    gunit, ffn_out = [[item[i] for item in halves for i in place] for place in ((3, 4), (5, 6))]
 
     def ffn_weights(sent):
-        left = [after(unit_two[0], sent), unit_two[1]]
-        first = weight_grads(left, [ggate, gup], order)
-        left = [after(parts[0], first), parts[1]]
-        return first, weight_grads(left, [mixed], order)
-
-    scaled_two, found = scatter_head(*gunit, beside=ffn_weights)
-    grad_pair, grad_down = [scatter_rows(item) for item in found]
-
-    dy_own = dy[:quarter].astype(f32)
-    grad_hidden = dy_own + rstd_two * (
-        scaled_two - unit_two_own * jnp.mean(scaled_two * unit_two_own, axis=1, keepdims=True)
-    )
-    grad_branch = gather_head(grad_hidden.astype(bf16))
-
-
-    grad_att = join_rows([nn(item, out_w).astype(bf16) for item in grad_branch])
-    grad_att = swap_quarters(grad_att, head_me).reshape(rows, length, values)
+        first = pair_grads([after(units[0], sent), *units[1:]], [item[i] for item in halves for i in (1, 2)], order)
+        left = after(dy, first)
+        parts = [([(left, i)], [(item[0],)]) for i, item in enumerate(halves)]
+        return first, weight_grads(parts, split_order(order, n_seq), quarters)
+
+    terms, (grad_pair, grad_down) = scatter_head(gunit, beside=ffn_weights)
+    grad_pair = lax.psum_scatter(grad_pair, "seq", scatter_dimension=0, tiled=True).astype(f32)
+    grad_hidden, grad_branch = on_quarter(norm_back_kernel, [hidden, dy, *terms], quarter, [f32, bf16])
+    grad_branch = gather_head(grad_branch)
+
+    grad_att = back_product(grad_branch, out_w, quarters).reshape(rows, length, values)
     carry, gnum, gden = by_row(
         functools.partial(carry_kernel, heads),
         rows,
@@ -670,15 +859,19 @@
         place=place,
         flops=11 * unit_flops,
     )
-    parts = [attended_own[:half], attended_own[half:]]
-    grad_out_w = weight_grads(grad_branch, [parts], order ^ me if n_seq == 8 else order)
-    out_pairs = scatter_begin(grad_out_w) if n_seq == 8 else [grad_out_w]
+    sides = [[(grad_branch[i],), (grad_branch[i + 1],)] for i in (0, 2)]
+    parts = [(side, [(attended_flat, "q", i), (attended_flat, "q", i + 1)]) for side, i in zip(sides, (0, 2))]
+    grad_out_w = weight_grads(parts, split_order(order, n_seq), quarters)
     found = scan_begin(carry, True, me, n_seq)
-    block_own, _ = scatter_head(branch[0], after(branch[1], *grad_branch), beside=lambda _: found)
-    block_own = (hidden + block_own).astype(bf16)
+    ffn_out[3] = after(ffn_out[3], grad_att)
+    terms, _ = scatter_head(ffn_out, beside=lambda _: found)
+    block_own = (hidden + (terms[0].astype(f32) + terms[1].astype(f32) + terms[2].astype(f32))).astype(bf16)
+    down_pairs = scatter_begin(after(grad_down, *grad_branch), n_seq)
     carry_in, place_back = scan_end(found, True, me, n_seq)
-    carry_in = after(carry_in, block_own)
-    block_all = join_rows(gather_head(block_own))
+    carry_in = after(carry_in, block_own, *down_pairs)
+    out_pairs = scatter_begin(grad_out_w, n_seq)
+    block_all = gather_head(block_own)
+    down_terms = scatter_sends(down_pairs)
     (gqkv,) = by_row(
         functools.partial(finish_back_kernel, heads),
         rows,
@@ -687,25 +880,27 @@
         place=place_back,
         flops=6 * unit_flops,
     )
-    gqkv = gqkv.reshape(count, lanes + values)
-    gqkv_own = after(swap_quarters(gqkv, head_me), block_all, *out_pairs)
-    grad_out_w = scatter_end(out_pairs) if n_seq == 8 else scatter_rows(out_pairs[0])
-    far = nt(gqkv_own[half:], qkv_w).astype(bf16)
-    near = nt(gqkv_own[:half], qkv_w).astype(bf16)
-    scaled_one = scatter_head(near, far)
-    if n_seq == 8:
-        qkv_pairs = scatter_begin(weight_grads([unit_one], [[gqkv]], order ^ me))
-        grad_qkv = scatter_end(qkv_pairs)
-    else:
-        qkv_pairs = []
-        grad_qkv = scatter_rows(weight_grads([unit_one], [[gqkv]], order))
-    unit_one_own = x_own * rstd_one
-    grad_x = grad_hidden + rstd_one * (
-        scaled_one - unit_one_own * jnp.mean(scaled_one * unit_one_own, axis=1, keepdims=True)
-    )
-    grad_x_all = join_rows(gather_head(after(grad_x.astype(bf16), grad_out_w, grad_pair, *qkv_pairs)))
-
-    back = lambda value, kind: move_blocks(value, quarters, order, kind, quarter).reshape(rows, length, width)
+    gqkv = after(gqkv.reshape(count, lanes + values), *block_all, *out_pairs)
+    far = quarter_products(gqkv, qkv_w, quarters, 3)
+    near = quarter_products(gqkv, qkv_w, quarters, 1)
+    out_terms = scatter_sends(out_pairs)
+    terms, grad_qkv = scatter_head(
+        [near[1], near[0], far[1], far[0]],
+        beside=lambda sent: weight_grads(
+            [([(after(unit_one, sent),)], [(gqkv,)])], split_order(order, n_seq), quarters
+        ),
+    )
+    terms = after(terms, *down_terms[:2], *out_terms)
+    (grad_x,) = on_quarter(norm_back_kernel, [x_own, grad_hidden, *terms], quarter, [bf16])
+    grad_x_all = gather_head(grad_x)
+    grad_x_all[0] = after(grad_x_all[0], *down_terms[2:])
+    grad_down = scatter_end(down_pairs, down_terms)
+    grad_out_w = scatter_end(out_pairs, out_terms)
+    grad_qkv = scatter_begin(grad_qkv, n_seq)
+    grad_qkv = (grad_qkv[0],) + tuple(after(pair, grad_x) for pair in grad_qkv[1:])
+    grad_qkv = scatter_end(grad_qkv, scatter_sends(grad_qkv))
+
+    back = lambda value, kind: place_quarters(value, quarters, order, kind).reshape(rows, length, width)
     hidden_units = gate_weight.shape[1]
     grad_gate, grad_up = grad_pair[:, :hidden_units], grad_pair[:, hidden_units:]
     gain_sums = jnp.stack(

time: 969 us -> 1080 us (1.11)
  waiting for transfers between devices: 420 us -> 539 us
  Pallas kernels: 211 us -> 256 us
  other arithmetic: 57.2 us -> 33.8 us
  between operations: 30.6 us -> 15.4 us
    all_gather x1 -> x2, waiting for transfers between devices: 0.01 us -> 104 us  [the longest x1 104 us: per_device(): lax.all_gather(scaled(gate_weight, gain_two), 'seq', axis=0, tiled=True)]
    pallas_call x10 -> x21, Pallas kernels: 153 us -> 199 us  [the longest x2 79.9 us: feed_forward(): pl.pallas_call(functools.partial(ffn_kernel, 256), out_shape=shapes, grid...]
    concatenate x10 -> x0, other arithmetic: 17.4 us -> none  [the longest x8 15.2 us: join_rows(): return pieces[0] if len(pieces) == 1 else jnp.concatenate(pieces, axis=0)]
    unnamed x220 -> x261, local copies, waits for them, and re-layouts: 39.8 us -> 57.2 us
    ppermute x82 -> x87, waiting for transfers between devices: 420 us -> 435 us  [send(): return lax.ppermute(value, axis, [(i, i ^ mask) for i in range(count)])]
    slice x16 -> x5, local copies, waits for them, and re-layouts: 18.5 us -> 5.49 us  [the longest x3 5.32 us: scatter_begin(): other = send(whole[4 * rows:], 'seq', 1, 8)]
    ppermute x82 -> x87, starting transfers between devices: 142 us -> 136 us  [send(): return lax.ppermute(value, axis, [(i, i ^ mask) for i in range(count)])]
  transfers between devices with their start and end apart: 85 -> 90, of which waited for: 38 -> 38; matrix products, arithmetic and copies ran while one was open for 12% -> 7% of each run, Pallas kernels for 15% -> 18%
where the time goes in v3:
time: 1080 us; the launch traced here: 1060 us
  waiting for transfers between devices  539 us (50%)
  Pallas kernels  256 us (24%)
  starting transfers between devices  136 us (13%)
  local copies, waits for them, and re-layouts  72.5 us (7%)
  other arithmetic  33.8 us (3%)
  between operations  15.4 us (1%)
  matrix products  11.7 us (1%)
    ppermute x87, waiting for transfers between devices, send(): return lax.ppermute(value, axis, [(i, i ^ mask) for i in range(count)])  435 us
    ppermute x87, starting transfers between devices, send(): return lax.ppermute(value, axis, [(i, i ^ mask) for i in range(count)])  136 us
    all_gather x1, waiting for transfers between devices, per_device(): lax.all_gather(scaled(gate_weight, gain_two), 'seq', axis=0, tiled=True)  104 us
    pallas_call x2, Pallas kernels, feed_forward(): pl.pallas_call(functools.partial(ffn_kernel, 256), out_shape=shapes, grid...  79.9 us
    unnamed x261, local copies, waits for them, and re-layouts  57.2 us
    pallas_call x6, Pallas kernels, by_row(): pl.pallas_call(kernel, out_shape=shapes, grid_spec=pltpu.PrefetchScalarGr...  53 us
    pallas_call x3, Pallas kernels, weight_grads(): pl.pallas_call(functools.partial(weight_kernel, tuple(((len(lefts), len(r...  33.4 us
    pallas_call x1, Pallas kernels, pair_grads(): pl.pallas_call(pair_kernel, out_shape=jax.ShapeDtypeStruct((width, 2 * co...  27.1 us
  transfers between devices with their start and end apart: 90, of which 38 were waited for; matrix products, arithmetic and copies ran while one was open for 7% of the time, Pallas kernels for 18%

profile of v3, /device:TPU:0, one launch (start us, length us, event | category | flops | bytes accessed | tf_op | source)
XLA Modules:
  0.0 1064.9 jit_solution(18118982831605640834)
XLA Ops:
  21.1 104.2 %all-gather.3.cloned.1.call-done.gate_hbm = bf16[2048,1408]{1,0:T(8,128)(2,1)} async-done(((bf16[256,1408]{1,0:T(8,128)(2,1)}), bf16[2048,1408]{1,0:T(8,128)(2,1)}) %all-gather.3.cloned.1.call-update) | async-done | bytes 5767184 | tf_op jit(solution)/shard_map/all_gather | solution.py:760
  189.0 8.1 shard_map.297
  205.6 24.0 %collective-permute-done.24 = bf16[256,512]{1,0:T(8,128)(2,1)S(1)} collective-permute-done((bf16[256,512]{1,0:T(8,128)(2,1)}, bf16[256,512]{1,0:T(8,128)(2,1)S(1)}, u32[]{:S(2)}, u32[]{:S(2)}) %collective-permute-start.24) | collective-permute-done | bytes 262176 | tf_op jit(solution)/shard_map/ppermute | solution.py:309
  238.0 37.5 %collective-permute-done.11 = bf16[480,128]{1,0:T(8,128)(2,1)S(1)} collective-permute-done((bf16[480,128]{1,0:T(8,128)(2,1)S(1)}, bf16[480,128]{1,0:T(8,128)(2,1)S(1)}, u32[]{:S(2)}, u32[]{:S(2)}) %collective-permute-start.11) | collective-permute-done | bytes 122912 | tf_op jit(solution)/shard_map/ppermute | solution.py:309
  291.7 8.7 collective-permute-done.9
  304.2 15.2 %collective-permute-done.8 = bf16[480,128]{1,0:T(8,128)(2,1)S(1)} collective-permute-done((bf16[480,128]{1,0:T(8,128)(2,1)S(1)}, bf16[480,128]{1,0:T(8,128)(2,1)S(1)}, u32[]{:S(2)}, u32[]{:S(2)}) %collective-permute-start.8) | collective-permute-done | bytes 122912 | tf_op jit(solution)/shard_map/ppermute | solution.py:309
  325.2 44.4 %collective-permute-done.14 = bf16[3,160,128]{2,1,0:T(8,128)(2,1)S(1)} collective-permute-done((bf16[3,160,128]{2,1,0:T(8,128)(2,1)S(1)}, bf16[3,160,128]{2,1,0:T(8,128)(2,1)S(1)}, u32[]{:S(2)}, u32[]{:S(2)}) %collective-permute-start.14) | collective-permute-done | bytes 122912 | tf_op jit(solution)/shard_map/ppermute | solution.py:309
  434.6 11.7 %convolution_convert_fusion.gmixed_ref = bf16[1536,1408]{1,0:T(8,128)(2,1)} fusion(bf16[1536,2048]{1,0:T(8,128)(2,1)S(1)} %bitcast.111, bf16[2048,1408]{1,0:T(8,128)(2,1)S(1)} %copy-done.78), kind=kOutput, calls=%fused_computation | convolution fusion | flops 8860532736 | bytes 16384000 | tf_op jit(solution)/shard_map/dot_general | solution.py:49
  446.3 23.0 %collective-permute-done.30.c_ref = bf16[384,2048]{1,0:T(8,128)(2,1)S(1)} collective-permute-done((bf16[384,2048]{1,0:T(8,128)(2,1)S(1)}, bf16[384,2048]{1,0:T(8,128)(2,1)S(1)}, u32[]{:S(2)}, u32[]{:S(2)}) %collective-permute-start.30) | collective-permute-done | bytes 1572896 | tf_op jit(solution)/shard_map/ppermute | solution.py:309
  477.3 39.8 %shard_map.304 = (bf16[768,1408]{1,0:T(8,128)(2,1)}, bf16[768,1408]{1,0:T(8,128)(2,1)}, bf16[768,1408]{1,0:T(8,128)(2,1)}, bf16[384,2048]{1,0:T(8,128)(2,1)}, bf...) custom-call(s32[8]{0:T(128)} %copy-done.71, ...), custom_call_target="tpu_custom_call" | custom-call | flops 692060160 | bytes 933888 | tf_op jit(solution)/shard_map/pallas_call | solution.py:641
  521.0 40.1 %shard_map.305 = (bf16[768,1408]{1,0:T(8,128)(2,1)}, bf16[768,1408]{1,0:T(8,128)(2,1)}, bf16[768,1408]{1,0:T(8,128)(2,1)}, bf16[384,2048]{1,0:T(8,128)(2,1)}, bf...) custom-call(s32[8]{0:T(128)} %copy-done.71, ...), custom_call_target="tpu_custom_call" | custom-call | flops 692060160 | bytes 933888 | tf_op jit(solution)/shard_map/pallas_call | solution.py:641
  567.9 27.1 %shard_map.306 = bf16[2048,2816]{1,0:T(8,128)(2,1)} custom-call(s32[8]{0:T(128)S(1)} %copy-done.72, bf16[384,2048]{1,0:T(8,128)(2,1)} %get-tuple-element.124.near_ref.refs_0_, bf16[384,2048]{1,0:T(8,128)(2,1)} %collective-permute-done.38.core_ref.refs_1_, bf16[384,2048]{1,0:T(8,128)(2,1)} %collective-permute-done.40.near_ref.refs_2_, ...), custom_call_target="tpu_custom_call" | custom-call | flops 553648128 | bytes 1089536 | tf_op jit(solution)/shard_map/pallas_call | solution.py:714
  600.2 14.6 %shard_map.307 = bf16[2048,1408]{1,0:T(8,128)(2,1)} custom-call(s32[8]{0:T(128)S(1)} %copy-done.73, s32[4]{0:T(128)S(1)} %iota_xor_fusion.1.order_ref.rows_ref.quarters_ref, bf16[1536,2048]{1,0:T(8,128)(2,1)} %copy-done, bf16[768,1408]{1,0:T(8,128)(2,1)S(1)} %copy-done.33, bf16[1536,2048]{1,0:T(8,128)(2,1)} %copy-done, bf16[768,1408]{1,0:T(8,128)(2,1)S(1)} %copy-done.34), custom_call_target="tpu_custom_call" | custom-call | flops 276824064 | bytes 774144 | tf_op jit(solution)/shard_map/pallas_call | solution.py:686
  614.8 16.9 %collective-permute-done.44.c_ref = bf16[384,2048]{1,0:T(8,128)(2,1)S(1)} collective-permute-done((bf16[384,2048]{1,0:T(8,128)(2,1)}, bf16[384,2048]{1,0:T(8,128)(2,1)S(1)}, u32[]{:S(2)}, u32[]{:S(2)}) %collective-permute-start.44) | collective-permute-done | bytes 1572896 | tf_op jit(solution)/shard_map/ppermute | solution.py:309
  643.2 34.1 %collective-permute-done.46.refs_2_.refs_4_ = bf16[384,2048]{1,0:T(8,128)(2,1)S(1)} collective-permute-done((bf16[384,2048]{1,0:T(8,128)(2,1)S(1)}, bf16[384,2048]{1,0:T(8,128)(2,1)S(1)}, u32[]{:S(2)}, u32[]{:S(2)}) %collective-permute-start.46) | collective-permute-done | bytes 1572896 | tf_op jit(solution)/shard_map/ppermute | solution.py:309
  691.2 9.0 shard_map.310
  735.0 9.0 shard_map.316
  746.1 16.9 %shard_map.314 = (f32[6,256,128]{2,1,0:T(8,128)S(1)}, f32[6,256,512]{2,1,0:T(8,128)S(1)}) custom-call(s32[8]{0:T(128)S(1)} %copy-done.72, bf16[6,256,640]{2,1,0:T(8,128)(2,1)S(1)} %bitcast.124, f32[6,256,8]{2,1,0:T(8,128)S(1)} %copy-done.5, f32[6,8,256]{2,1,0:T(8,128)S(1)} %copy-done.55, bf16[6,256,512]{2,1,0:T(8,128)(2,1)S(1)} %get-tuple-element.146.gnum_ref, ...), custom_call_target="tpu_custom_call" | custom-call | flops 138412032 | bytes 293632 | tf_op jit(solution)/shard_map/pallas_call | solution.py:241
  764.8 74.0 %collective-permute-done.60 = bf16[3,160,128]{2,1,0:T(8,128)(2,1)S(1)} collective-permute-done((bf16[3,160,128]{2,1,0:T(8,128)(2,1)S(1)}, bf16[3,160,128]{2,1,0:T(8,128)(2,1)S(1)}, u32[]{:S(2)}, u32[]{:S(2)}) %collective-permute-start.60) | collective-permute-done | bytes 122912 | tf_op jit(solution)/shard_map/ppermute | solution.py:309
  876.5 8.0 shard_map.315
  910.9 24.3 %collective-permute-start.72 = (bf16[256,1408]{1,0:T(8,128)(2,1)}, bf16[256,1408]{1,0:T(8,128)(2,1)S(1)}, u32[]{:S(2)}, u32[]{:S(2)}) collective-permute-start(bf16[256,1408]{1,0:T(8,128)(2,1)} %get-tuple-element.222), channel_id=1, source_target_pairs={{0,8},{4,12},{8,0},{12,4},{16,24},{20,28},{24,16},{28,20},{1,9},{5... | collective-permute-start | bytes 2162696 | tf_op jit(solution)/shard_map/ppermute | solution.py:309
  935.2 9.7 shard_map.319
  945.6 30.8 %collective-permute-done.74 = bf16[256,512]{1,0:T(8,128)(2,1)S(1)} collective-permute-done((bf16[256,512]{1,0:T(8,128)(2,1)S(1)}, bf16[256,512]{1,0:T(8,128)(2,1)S(1)}, u32[]{:S(2)}, u32[]{:S(2)}) %collective-permute-start.74) | collective-permute-done | bytes 262176 | tf_op jit(solution)/shard_map/ppermute | solution.py:309
  998.6 25.7 %collective-permute-done.83 = bf16[256,640]{1,0:T(8,128)(2,1)} collective-permute-done((bf16[256,640]{1,0:T(8,128)(2,1)}, bf16[256,640]{1,0:T(8,128)(2,1)}, u32[]{:S(2)}, u32[]{:S(2)}) %collective-permute-start.83) | collective-permute-done | bytes 327712 | tf_op jit(solution)/shard_map/ppermute | solution.py:309
  (506 shorter events, 392.9 us)
Async XLA Ops:
  7.2 118.0 %all-gather.3.cloned.1.call-start = ((), (), s32[]{:S(2)}) async-start(), calls=%async_computation.1 | async-start | bytes 6488064 | tf_op jit(solution)/shard_map/all_gather | solution.py:760
  10.9 466.4 %all-gather.5.cloned.1.call-start = ((), (), s32[]{:S(2)}) async-start(), calls=%async_computation.2 | async-start | bytes 6488064 | tf_op jit(solution)/shard_map/all_gather | solution.py:761
  11.4 116.0 %collective-permute-start.5 = (bf16[256,640]{1,0:T(8,128)(2,1)S(1)}, bf16[256,640]{1,0:T(8,128)(2,1)S(1)}, u32[]{:S(2)}, u32[]{:S(2)}) collective-permute-start(bf16[256,640]{1,0:T(8,128)(2,1)S(1)} %fusion.4.refs_0_), channel_id=1, source_target_pairs={{0,24},{4,28},{8,16},{12,20},{16,8},{20,12},{24,0},{28,4},{1,25},{... | collective-permute-start | bytes 983048 | tf_op jit(solution)/shard_map/ppermute | solution.py:309
  16.5 111.5 %collective-permute-start.3 = (bf16[256,640]{1,0:T(8,128)(2,1)S(1)}, bf16[256,640]{1,0:T(8,128)(2,1)S(1)}, u32[]{:S(2)}, u32[]{:S(2)}) collective-permute-start(bf16[256,640]{1,0:T(8,128)(2,1)S(1)} %fusion.4.refs_0_), channel_id=1, source_target_pairs={{0,16},{4,20},{8,24},{12,28},{16,0},{20,4},{24,8},{28,12},{1,17},{... | collective-permute-start | bytes 983048 | tf_op jit(solution)/shard_map/ppermute | solution.py:309
  16.5 113.0 %collective-permute-start.1 = (bf16[256,640]{1,0:T(8,128)(2,1)S(1)}, bf16[256,640]{1,0:T(8,128)(2,1)S(1)}, u32[]{:S(2)}, u32[]{:S(2)}) collective-permute-start(bf16[256,640]{1,0:T(8,128)(2,1)S(1)} %fusion.4.refs_0_), channel_id=1, source_target_pairs={{0,8},{4,12},{8,0},{12,4},{16,24},{20,28},{24,16},{28,20},{1,9},{5... | collective-permute-start | bytes 983048 | tf_op jit(solution)/shard_map/ppermute | solution.py:309
  17.2 145.5 %collective-permute-start = (bf16[256,640]{1,0:T(8,128)(2,1)S(1)}, bf16[256,640]{1,0:T(8,128)(2,1)S(1)}, u32[]{:S(2)}, u32[]{:S(2)}) collective-permute-start(bf16[256,640]{1,0:T(8,128)(2,1)S(1)} %fusion.4.refs_0_), channel_id=1, source_target_pairs={{0,4},{4,0},{8,12},{12,8},{16,20},{20,16},{24,28},{28,24},{1,5},{5... | collective-permute-start | bytes 983048 | tf_op jit(solution)/shard_map/ppermute | solution.py:309
  125.3 901.7 %reduce-scatter.2.cloned.1.call-start = ((), (), s32[]{:S(2)}) async-start(), calls=%async_computation.3 | async-start | bytes 12976128 | tf_op jit(solution)/shard_map/reduce_scatter | solution.py:840
  166.7 62.9 %collective-permute-start.24 = (bf16[256,512]{1,0:T(8,128)(2,1)}, bf16[256,512]{1,0:T(8,128)(2,1)S(1)}, u32[]{:S(2)}, u32[]{:S(2)}) collective-permute-start(bf16[256,512]{1,0:T(8,128)(2,1)} %bitcast.160), channel_id=1, source_target_pairs={{0,16},{4,20},{8,24},{12,28},{16,0},{20,4},{24,8},{28,12},{1,17},{... | collective-permute-start | bytes 786440 | tf_op jit(solution)/shard_map/ppermute | solution.py:309
  166.9 62.7 %collective-permute-start.22 = (bf16[256,512]{1,0:T(8,128)(2,1)}, bf16[256,512]{1,0:T(8,128)(2,1)S(1)}, u32[]{:S(2)}, u32[]{:S(2)}) collective-permute-start(bf16[256,512]{1,0:T(8,128)(2,1)} %bitcast.161), channel_id=1, source_target_pairs={{0,8},{4,12},{8,0},{12,4},{16,24},{20,28},{24,16},{28,20},{1,9},{5... | collective-permute-start | bytes 786440 | tf_op jit(solution)/shard_map/ppermute | solution.py:309
  170.0 110.9 %collective-permute-start.21 = (bf16[256,512]{1,0:T(8,128)(2,1)}, bf16[256,512]{1,0:T(8,128)(2,1)S(1)}, u32[]{:S(2)}, u32[]{:S(2)}) collective-permute-start(bf16[256,512]{1,0:T(8,128)(2,1)} %bitcast.162), channel_id=1, source_target_pairs={{0,4},{4,0},{8,12},{12,8},{16,20},{20,16},{24,28},{28,24},{1,5},{5... | collective-permute-start | bytes 786440 | tf_op jit(solution)/shard_map/ppermute | solution.py:309
  229.6 51.4 %collective-permute-start.10 = (bf16[480,128]{1,0:T(8,128)(2,1)S(1)}, bf16[480,128]{1,0:T(8,128)(2,1)S(1)}, u32[]{:S(2)}, u32[]{:S(2)}) collective-permute-start(bf16[480,128]{1,0:T(8,128)(2,1)S(1)} %get-tuple-element.245), channel_id=1, source_target_pairs={{0,16},{4,20},{8,24},{12,28},{16,0},{20,4},{24,8},{28,12},{1,17},{... | collective-permute-start | bytes 368648 | tf_op jit(solution)/shard_map/ppermute | solution.py:309
  234.9 85.9 %collective-permute-start.36 = (bf16[256,1408]{1,0:T(8,128)(2,1)S(1)}, bf16[256,1408]{1,0:T(8,128)(2,1)S(1)}, u32[]{:S(2)}, u32[]{:S(2)}) collective-permute-start(bf16[256,1408]{1,0:T(8,128)(2,1)S(1)} %bitcast.155), channel_id=1, source_target_pairs={{0,24},{4,28},{8,16},{12,20},{16,8},{20,12},{24,0},{28,4},{1,25},{... | collective-permute-start | bytes 2162696 | tf_op jit(solution)/shard_map/ppermute | solution.py:309
  319.5 101.8 %collective-permute-start.31 = (bf16[256,1408]{1,0:T(8,128)(2,1)S(1)}, bf16[256,1408]{1,0:T(8,128)(2,1)S(1)}, u32[]{:S(2)}, u32[]{:S(2)}) collective-permute-start(bf16[256,1408]{1,0:T(8,128)(2,1)S(1)} %bitcast.158), channel_id=1, source_target_pairs={{0,4},{4,0},{8,12},{12,8},{16,20},{20,16},{24,28},{28,24},{1,5},{5... | collective-permute-start | bytes 2162696 | tf_op jit(solution)/shard_map/ppermute | solution.py:309
  320.7 106.0 %collective-permute-start.37 = (bf16[256,1408]{1,0:T(8,128)(2,1)S(1)}, bf16[256,1408]{1,0:T(8,128)(2,1)S(1)}, u32[]{:S(2)}, u32[]{:S(2)}) collective-permute-start(bf16[256,1408]{1,0:T(8,128)(2,1)S(1)} %collective-permute-done.36), channel_id=1, source_target_pairs={{0,4},{4,0},{8,12},{12,8},{16,20},{20,16},{24,28},{28,24},{1,5},{5... | collective-permute-start | bytes 2162696 | tf_op jit(solution)/shard_map/ppermute | solution.py:309
  321.5 103.4 %collective-permute-start.35 = (bf16[256,1408]{1,0:T(8,128)(2,1)S(1)}, bf16[256,1408]{1,0:T(8,128)(2,1)S(1)}, u32[]{:S(2)}, u32[]{:S(2)}) collective-permute-start(bf16[256,1408]{1,0:T(8,128)(2,1)S(1)} %collective-permute-done.34), channel_id=1, source_target_pairs={{0,4},{4,0},{8,12},{12,8},{16,20},{20,16},{24,28},{28,24},{1,5},{5... | collective-permute-start | bytes 2162696 | tf_op jit(solution)/shard_map/ppermute | solution.py:309
  322.8 100.3 %collective-permute-start.33 = (bf16[256,1408]{1,0:T(8,128)(2,1)S(1)}, bf16[256,1408]{1,0:T(8,128)(2,1)S(1)}, u32[]{:S(2)}, u32[]{:S(2)}) collective-permute-start(bf16[256,1408]{1,0:T(8,128)(2,1)S(1)} %collective-permute-done.32), channel_id=1, source_target_pairs={{0,4},{4,0},{8,12},{12,8},{16,20},{20,16},{24,28},{28,24},{1,5},{5... | collective-permute-start | bytes 2162696 | tf_op jit(solution)/shard_map/ppermute | solution.py:309
  728.2 144.4 %collective-permute-start.67 = (bf16[1024,1408]{1,0:T(8,128)(2,1)}, bf16[1024,1408]{1,0:T(8,128)(2,1)}, u32[]{:S(2)}, u32[]{:S(2)}) collective-permute-start(bf16[1024,1408]{1,0:T(8,128)(2,1)} %slice.119), channel_id=1, source_target_pairs={{0,4},{4,0},{8,12},{12,8},{16,20},{20,16},{24,28},{28,24},{1,5},{5... | collective-permute-start | bytes 8650760 | tf_op jit(solution)/shard_map/ppermute | solution.py:309
  734.0 112.6 %collective-permute-start.57 = (bf16[384,2048]{1,0:T(8,128)(2,1)S(1)}, bf16[384,2048]{1,0:T(8,128)(2,1)}, u32[]{:S(2)}, u32[]{:S(2)}) collective-permute-start(bf16[384,2048]{1,0:T(8,128)(2,1)S(1)} %add_convert_fusion.1.refs_0_), channel_id=1, source_target_pairs={{0,2},{1,3},{2,0},{3,1},{4,6},{5,7},{6,4},{7,5},{8,10},{9,11},{10,... | collective-permute-start | bytes 4718600 | tf_op jit(solution)/shard_map/ppermute | solution.py:309
  745.5 124.7 %collective-permute-start.68 = (bf16[1024,512]{1,0:T(8,128)(2,1)S(1)}, bf16[1024,512]{1,0:T(8,128)(2,1)S(1)}, u32[]{:S(2)}, u32[]{:S(2)}) collective-permute-start(bf16[1024,512]{1,0:T(8,128)(2,1)S(1)} %slice.159), channel_id=1, source_target_pairs={{0,4},{4,0},{8,12},{12,8},{16,20},{20,16},{24,28},{28,24},{1,5},{5... | collective-permute-start | bytes 3145736 | tf_op jit(solution)/shard_map/ppermute | solution.py:309
  763.1 75.7 %collective-permute-start.60 = (bf16[3,160,128]{2,1,0:T(8,128)(2,1)S(1)}, bf16[3,160,128]{2,1,0:T(8,128)(2,1)S(1)}, u32[]{:S(2)}, u32[]{:S(2)}) collective-permute-start(bf16[3,160,128]{2,1,0:T(8,128)(2,1)S(1)} %copy-done.77), channel_id=1, source_target_pairs={{0,4},{4,0},{8,12},{12,8},{16,20},{20,16},{24,28},{28,24},{1,5},{5... | collective-permute-start | bytes 368648 | tf_op jit(solution)/shard_map/ppermute | solution.py:309
  764.6 75.8 %collective-permute-start.61 = (bf16[3,160,128]{2,1,0:T(8,128)(2,1)S(1)}, bf16[3,160,128]{2,1,0:T(8,128)(2,1)S(1)}, u32[]{:S(2)}, u32[]{:S(2)}) collective-permute-start(bf16[3,160,128]{2,1,0:T(8,128)(2,1)S(1)} %copy-done.75), channel_id=1, source_target_pairs={{0,8},{4,12},{8,0},{12,4},{16,24},{20,28},{24,16},{28,20},{1,9},{5... | collective-permute-start | bytes 368648 | tf_op jit(solution)/shard_map/ppermute | solution.py:309
  899.7 76.8 %collective-permute-start.69 = (bf16[384,2048]{1,0:T(8,128)(2,1)S(1)}, bf16[384,2048]{1,0:T(8,128)(2,1)S(1)}, u32[]{:S(2)}, u32[]{:S(2)}) collective-permute-start(bf16[384,2048]{1,0:T(8,128)(2,1)S(1)} %get-tuple-element.153), channel_id=1, source_target_pairs={{0,1},{1,0},{2,3},{3,2},{4,5},{5,4},{6,7},{7,6},{8,9},{9,8},{10,11... | collective-permute-start | bytes 4718600 | tf_op jit(solution)/shard_map/ppermute | solution.py:309
  901.1 75.4 %collective-permute-start.73 = (bf16[256,1408]{1,0:T(8,128)(2,1)}, bf16[256,1408]{1,0:T(8,128)(2,1)S(1)}, u32[]{:S(2)}, u32[]{:S(2)}) collective-permute-start(bf16[256,1408]{1,0:T(8,128)(2,1)} %get-tuple-element.221), channel_id=1, source_target_pairs={{0,16},{4,20},{8,24},{12,28},{16,0},{20,4},{24,8},{28,12},{1,17},{... | collective-permute-start | bytes 2162696 | tf_op jit(solution)/shard_map/ppermute | solution.py:309
  910.9 65.5 %collective-permute-start.72 = (bf16[256,1408]{1,0:T(8,128)(2,1)}, bf16[256,1408]{1,0:T(8,128)(2,1)S(1)}, u32[]{:S(2)}, u32[]{:S(2)}) collective-permute-start(bf16[256,1408]{1,0:T(8,128)(2,1)} %get-tuple-element.222), channel_id=1, source_target_pairs={{0,8},{4,12},{8,0},{12,4},{16,24},{20,28},{24,16},{28,20},{1,9},{5... | collective-permute-start | bytes 2162696 | tf_op jit(solution)/shard_map/ppermute | solution.py:309
  (178 other events, 3828.6 us)
Sparse Core Ops, SparseCore 0:
  11.0 114.2 all-gather.2
  127.4 159.8 all-gather.4
  595.1 214.9 reduce-scatter.1

commit v4 on v3

--- a/solution.py
+++ b/solution.py
@@ -17,6 +17,7 @@
 NORM_ROW = len(PAIRS)
 FLAG_ROW = NORM_ROW + 2
 BLOCKS = 8
+COST = 2
 bf16, f32 = jnp.bfloat16, jnp.float32
 
 
@@ -62,7 +63,7 @@
 
 
 def cost(flops, nbytes):
-    return pl.CostEstimate(flops=int(flops) // 32, bytes_accessed=int(nbytes) // 32, transcendentals=0)
+    return pl.CostEstimate(flops=int(flops) // COST, bytes_accessed=int(nbytes) // COST, transcendentals=0)
 
 
 def whole_spec(array):
@@ -252,19 +253,19 @@
     )(*([] if place is None else [place]), *arrays)
 
 
-def scan_kernel(backward, count, me_ref, *refs):
-    pieces, outs, (held, ahead) = refs[:count], refs[count : 2 * count], refs[2 * count :]
-    for rel in range(count):
+def scan_kernel(backward, me_ref, *refs):
+    pieces, outs, (held, ahead) = refs[:8], refs[8:16], refs[16:]
+    for rel in range(8):
         held[rel] = pieces[rel][...]
     me = me_ref[0]
     for block in range(held.shape[1]):
         run = jnp.zeros(held.shape[2:], f32)
-        for step in range(count):
-            rel = me ^ (count - 1 - step if backward else step)
+        for step in range(8):
+            rel = me ^ (7 - step if backward else step)
             ahead[rel, block] = run.astype(bf16)
             own = held[rel, block].astype(f32)
             run = own + (1.0 - own[FLAG_ROW : FLAG_ROW + 1]) * run
-    for rel in range(count):
+    for rel in range(8):
         outs[rel][...] = ahead[rel]
 
 
@@ -274,16 +275,11 @@
     if count != 8 or blocks % 8:
         return lax.all_gather(flat, "seq").astype(f32)
     per = blocks // 8
-    split = flat.reshape(8, per * TALL, VHEAD)
-    pieces = []
-    for rel in range(8):
-        part = lax.dynamic_index_in_dim(split, me ^ rel, 0, keepdims=False)
-        if rel:
-            part = send(part, "seq", rel, 8)
-        pieces.append(part.reshape(per, TALL, VHEAD))
-    pieces[0] = after(pieces[0], *earlier)
-    return pl.pallas_call(
-        functools.partial(scan_kernel, backward, 8),
+    split = flat.reshape(8, per, TALL, VHEAD)
+    parts = [lax.dynamic_index_in_dim(split, me ^ rel, 0, keepdims=False) for rel in range(8)]
+    pieces = [after(parts[0], *earlier)] + [send(parts[rel], "seq", rel, 8) for rel in range(1, 8)]
+    return pl.pallas_call(
+        functools.partial(scan_kernel, backward),
         out_shape=[jax.ShapeDtypeStruct((per, TALL, VHEAD), bf16)] * 8,
         in_specs=[pl.BlockSpec(memory_space=pltpu.SMEM)] + [pl.BlockSpec(memory_space=pltpu.VMEM)] * 8,
         out_specs=[pl.BlockSpec(memory_space=pltpu.VMEM)] * 8,
@@ -321,6 +317,11 @@
 
 def after(value, *earlier):
     return lax.optimization_barrier((value, earlier))[0]
+
+
+def swap_blocks(array, order):
+    split = array.reshape((BLOCKS, array.shape[0] // BLOCKS) + array.shape[1:])
+    return join_rows([lax.dynamic_index_in_dim(split, order[i], 0, keepdims=False) for i in range(BLOCKS)])
 
 
 def split_order(order, n_seq):
@@ -581,37 +582,38 @@
     )(quarters, *pieces, weight)
 
 
-def ffn_kernel(step, order_ref, near_ref, core_ref, gmixed_ref, gate_hbm, up_hbm, down_hbm, *refs):
-    mixed_ref, ggate_ref, gup_ref, gunit_refs, out_refs = refs[0], refs[1], refs[2], refs[3:5], refs[5:7]
-    gate_ref, up_ref, down_ref, unit_ref, sems = refs[7:]
-    width, hidden = gate_ref.shape
+def ffn_kernel(step, n_units, n_earlier, order_ref, *refs):
+    units, dy_ref, weights_hbm = refs[:n_units], refs[n_units], refs[n_units + 1]
+    earlier, refs = refs[n_units + 2 : n_units + 2 + n_earlier], refs[-8:]
+    mixed_ref, ggate_ref, gup_ref, gunit_ref, out_ref, held_ref, unit_ref, sems = refs
+    width, hidden = held_ref.shape[0], held_ref.shape[1] // 3
     rows = width // BLOCKS
     copies = []
     for i in range(BLOCKS):
         start = pl.multiple_of(order_ref[i] * rows, rows)
-        for source, held in ((gate_hbm, gate_ref), (up_hbm, up_ref)):
-            copies.append((source.at[pl.ds(start, rows)], held.at[pl.ds(i * rows, rows)]))
-    copies.append((down_hbm, down_ref))
-    copies = [pltpu.make_async_copy(*ends, sems.at[i]) for i, ends in enumerate(copies)]
+        source = weights_hbm.at[pl.ds(start, rows)]
+        copies.append(pltpu.make_async_copy(source, held_ref.at[pl.ds(i * rows, rows)], sems.at[i]))
 
     @pl.when(pl.program_id(0) == 0)
     def _():
         for copy in copies:
             copy.start()
-        unit_ref[...] = near_ref[...]
         for copy in copies:
             copy.wait()
 
-    @pl.when(pl.program_id(0) == 1)
-    def _():
-        unit_ref[...] = core_ref[...]
-
-    unit = unit_ref[...]
+    for place, unit in enumerate(units):
+
+        @pl.when(pl.program_id(0) == place)
+        def _(unit=unit):
+            unit_ref[...] = unit[...]
+
+    unit, dy = unit_ref[...], dy_ref[...]
     for start in range(0, hidden, step):
-        cols = slice(start, min(start + step, hidden))
-        gate = nn(unit, gate_ref[:, cols])
-        up = nn(unit, up_ref[:, cols])
-        gmixed = gmixed_ref[:, cols].astype(f32)
+        stop = min(start + step, hidden)
+        cols = slice(start, stop)
+        gate = nn(unit, held_ref[:, start:stop])
+        up = nn(unit, held_ref[:, hidden + start : hidden + stop])
+        gmixed = nn(dy, held_ref[:, 2 * hidden + start : 2 * hidden + stop])
         sig = jax.nn.sigmoid(gate)
         silu = gate * sig
         mixed_ref[:, cols] = (silu * up).astype(bf16)
@@ -620,38 +622,42 @@
     ggate, gup, mixed = ggate_ref[...], gup_ref[...], mixed_ref[...]
     for start in range(0, width, 512):
         cols = slice(start, start + 512)
-        gunit = (nt(ggate, gate_ref[cols]) + nt(gup, up_ref[cols])).astype(bf16)
-        out = nt(mixed, down_ref[cols]).astype(bf16)
-        for place in range(2):
-
-            @pl.when(pl.program_id(0) == place)
-            def _(place=place, cols=cols, gunit=gunit, out=out):
-                gunit_refs[place][:, cols] = gunit
-                out_refs[place][:, cols] = out
-
-
-def feed_forward(units, gmixed, half, pair, down, order):
+        gunit = nt(ggate, held_ref[cols, :hidden]) + nt(gup, held_ref[cols, hidden : 2 * hidden])
+        out = nt(mixed, held_ref[cols, 2 * hidden :])
+        if earlier:
+            gunit = gunit + earlier[0][0, :, cols].astype(f32)
+            out = out + earlier[1][0, :, cols].astype(f32)
+        gunit_ref[0, :, cols] = gunit.astype(bf16)
+        out_ref[0, :, cols] = out.astype(bf16)
+
+
+def feed_forward(units, dy, start, weights, hidden, order, held=(), earlier=()):
     rows, width = units[0].shape
-    hidden = down.shape[1]
+    line = lambda cols: pl.BlockSpec((rows, cols), lambda i, order: (i + start, 0))
+    stacked = pl.BlockSpec((1, rows, width), lambda i, order: (i + start, 0, 0))
+    shapes = [jax.ShapeDtypeStruct((4 * rows, hidden), bf16)] * 3 + [jax.ShapeDtypeStruct((4, rows, width), bf16)] * 2
+    once = pl.BlockSpec((rows, width), lambda i, order: (0, 0), pipeline_mode=pl.Buffered(1))
     anywhere = pl.BlockSpec(memory_space=pl.ANY)
-    fixed = pl.BlockSpec((rows, width), lambda i, order: (0, 0))
-    line = lambda first=0: pl.BlockSpec((rows, hidden), lambda i, order: (i + first, 0))
-    shapes = [jax.ShapeDtypeStruct((2 * rows, hidden), bf16)] * 3 + [jax.ShapeDtypeStruct((rows, width), bf16)] * 4
-    once = pl.BlockSpec((rows, width), lambda i, order: (0, 0), pipeline_mode=pl.Buffered(1))
-    return pl.pallas_call(
-        functools.partial(ffn_kernel, 256),
+    steps = len(units)
+    first = 3 + steps + len(earlier)
+    return pl.pallas_call(
+        functools.partial(ffn_kernel, 256, steps, len(earlier)),
         out_shape=shapes,
         grid_spec=pltpu.PrefetchScalarGridSpec(
             num_scalar_prefetch=1,
-            grid=(2,),
-            in_specs=[once, once, line(2 * half), anywhere, anywhere, anywhere],
-            out_specs=[line()] * 3 + [fixed] * 4,
-            scratch_shapes=[pltpu.VMEM((width, hidden), bf16)] * 3
-            + [pltpu.VMEM((rows, width), bf16), pltpu.SemaphoreType.DMA((2 * BLOCKS + 1,))],
+            grid=(steps,),
+            in_specs=[once] * steps + [line(width), anywhere] + [stacked] * len(earlier) + [anywhere] * len(held),
+            out_specs=[line(hidden)] * 3 + [stacked] * 2,
+            scratch_shapes=[
+                pltpu.VMEM((width, 3 * hidden), bf16),
+                pltpu.VMEM((rows, width), bf16),
+                pltpu.SemaphoreType.DMA((BLOCKS,)),
+            ],
         ),
+        input_output_aliases={first + i: i for i in range(len(held))},
         compiler_params=params(60),
-        cost_estimate=cost(20 * rows * width * hidden, 2 * (8 * rows * width + 3 * width * hidden)),
-    )(order, *units, gmixed, *pair, down)
+        cost_estimate=cost(12 * steps * rows * width * hidden, 2 * (4 * steps * rows + 3 * hidden) * width),
+    )(order, *units, dy, weights, *earlier, *held)
 
 
 def weight_kernel(layout, order_ref, quarters_ref, *refs):
@@ -697,32 +703,34 @@
     )(order, quarters, *arrays)
 
 
-def pair_kernel(order_ref, *refs):
-    units, (ggate0, gup0, ggate1, gup1), out = refs[:4], refs[4:8], refs[8]
-    cols = ggate0.shape[1]
-    near = jnp.concatenate([units[0][...], units[1][...]], axis=0).T
-    far = jnp.concatenate([units[2][...], units[3][...]], axis=0).T
-    out[:, :cols] = (nn(near, ggate0[...]) + nn(far, ggate1[...])).astype(bf16)
-    out[:, cols:] = (nn(near, gup0[...]) + nn(far, gup1[...])).astype(bf16)
-
-
-def pair_grads(units, grads, order):
+def ffn_weight_kernel(order_ref, *refs):
+    units, (dy_ref, mixed_ref, ggate_ref, gup_ref, out) = refs[:4], refs[4:]
+    cols = ggate_ref.shape[1]
+    unit = jnp.concatenate([item[...] for item in units], axis=0).T
+    out[:, :cols] = nn(unit, ggate_ref[...]).astype(bf16)
+    out[:, cols : 2 * cols] = nn(unit, gup_ref[...]).astype(bf16)
+    out[:, 2 * cols :] = nn(dy_ref[...].T, mixed_ref[...]).astype(bf16)
+
+
+def ffn_weight_grads(units, dy, grads, order):
     quarter, width = units[0].shape
     rows = width // BLOCKS
     cols = grads[0].shape[1]
-    held = pl.BlockSpec((2 * quarter, cols), lambda i, order: (0, 0), pipeline_mode=pl.Buffered(1))
-    return pl.pallas_call(
-        pair_kernel,
-        out_shape=jax.ShapeDtypeStruct((width, 2 * cols), bf16),
+    held = pl.BlockSpec((4 * quarter, cols), lambda i, order: (0, 0), pipeline_mode=pl.Buffered(1))
+    return pl.pallas_call(
+        ffn_weight_kernel,
+        out_shape=jax.ShapeDtypeStruct((width, 3 * cols), bf16),
         grid_spec=pltpu.PrefetchScalarGridSpec(
             num_scalar_prefetch=1,
             grid=(BLOCKS,),
-            in_specs=[pl.BlockSpec((quarter, rows), lambda i, order: (0, i))] * 4 + [held] * 4,
-            out_specs=pl.BlockSpec((rows, 2 * cols), lambda i, order: (order[i], 0)),
+            in_specs=[pl.BlockSpec((quarter, rows), lambda i, order: (0, i))] * 4
+            + [pl.BlockSpec((4 * quarter, rows), lambda i, order: (0, i))]
+            + [held] * 3,
+            out_specs=pl.BlockSpec((rows, 3 * cols), lambda i, order: (order[i], 0)),
         ),
         compiler_params=params(48),
-        cost_estimate=cost(16 * quarter * width * cols, 2 * (4 * quarter + width) * (width + 2 * cols)),
-    )(order, *units, *grads)
+        cost_estimate=cost(24 * quarter * width * cols, 2 * (8 * quarter + width) * (width + 3 * cols)),
+    )(order, *units, dy, *grads)
 
 
 def per_device(
@@ -757,18 +765,24 @@
     gain_two = gain_ffn.astype(f32)[:, None]
     scaled = lambda weight, gain: (weight.astype(f32) * gain).astype(bf16)
     qkv_own = jnp.concatenate([query_weight, key_weight, value_weight], axis=1)
-    gate_w = lax.all_gather(scaled(gate_weight, gain_two), "seq", axis=0, tiled=True)
-    up_w = lax.all_gather(after(scaled(up_weight, gain_two), gate_w), "seq", axis=0, tiled=True)
-    pair_w = (gate_w, up_w)
+    gate_own, up_own, down_own = scaled(gate_weight, gain_two), scaled(up_weight, gain_two), down_weight.T
+    hidden_units = gate_weight.shape[1]
+    cut = (hidden_units + VHEAD) // (2 * VHEAD) * VHEAD
+    groups = (slice(0, cut), slice(cut, hidden_units))
+    values = heads * VHEAD
     qkv_pieces = gather_rows(scaled(qkv_own, gain_one), n_seq)
-    tie = lambda value, found: after(value, *found) if n_seq == 8 else value
-    out_pieces = gather_rows(tie(out_weight.T, qkv_pieces), n_seq)
-    down_pieces = gather_rows(tie(down_weight.T, out_pieces[2::2]), n_seq)
+    everywhere = lambda value: lax.all_gather(value, "seq", axis=0, tiled=True)
+    out_w = everywhere(out_weight.T)
+    ffn_w = []
+    for group in groups:
+        parts = [gate_own[:, group], up_own[:, group], down_own[:, group]]
+        ffn_w.append(everywhere(jnp.concatenate(parts, axis=1)))
+    out_w = swap_blocks(out_w, order)
 
     flat = tokens.reshape(count, width)
-    unit_one = unit_rows(flat, order, quarter // 2)
     x_own = move_blocks(flat, quarters[:1], order, quarter)
     dy = move_blocks(grad_out.reshape(count, width), quarters, order, quarter)
+    unit_one = after(unit_rows(flat, order, quarter // 2), x_own, dy)
 
     docs = jnp.cumsum(doc_reset, axis=1)
     final = docs[:, -1:]
@@ -778,7 +792,6 @@
     tables, feat_rows, to_key, to_query = feature_tables(heads)
 
     lanes = 2 * heads * FEAT
-    values = heads * VHEAD
     unit_flops = 2 * rows * heads * length * WIDE * VHEAD
     qkv, qkv_w = first_product(unit_one, qkv_pieces, quarter)
     qkv = qkv.reshape(rows, length, lanes + values)
@@ -796,49 +809,47 @@
         [((length, values), f32), ((length, heads), f32)],
         flops=3 * unit_flops,
     )
-    state_in, place = scan_end(scan_begin(states, False, me, n_seq, (gate_w,)), False, me, n_seq)
+    found = scan_begin(states, False, me, n_seq, (numerator,))
+    state_in, place = scan_end(found, False, me, n_seq)
     query_tables = [(tables["qa"], False), (tables["qb"], False), (feat_rows, False)]
     key_tables = [(tables["ka"], False), (tables["kb"], False), (feat_rows, False)]
     attended, rden = by_row(
         functools.partial(attend_kernel, heads),
         rows,
-        [(qkv, True), (edges, True), (numerator, True), (denominator, True), (state_in, False)] + query_tables,
+        [(qkv, True), (edges, True), (numerator, True), (after(denominator, out_w), True), (state_in, False)]
+        + query_tables,
         [((length, values), bf16), ((length, heads), f32)],
         place=place,
         flops=3 * unit_flops,
     )
     attended_flat = attended.reshape(count, values)
-    out_w = join_rows(out_pieces)
     far = quarter_products(attended_flat, out_w, quarters, 3)
     near = quarter_products(attended_flat, out_w, quarters, 1)
     branch = [near[1], near[0], far[1], far[0]]
 
-    def grad_mixed(sent):
-        down = join_rows(down_pieces)
-        return down, nn(after(dy, sent), down).astype(bf16)
-
-    branch, (down_w, gmixed) = scatter_head(branch, beside=grad_mixed)
+    branch, _ = scatter_head(branch)
     hidden, unit_two = on_quarter(add_norm_kernel, [x_own, *branch], quarter, [f32, bf16])
-    first_half = []
+    held = []
 
     def near_rows(units):
-        first_half.extend(feed_forward(units, gmixed, 0, pair_w, down_w, order))
-        return first_half
+        held.extend(feed_forward(units, dy, 0, ffn_w[0], cut, order))
+        return held
 
     units = gather_head(unit_two, near_rows)
-    second_half = feed_forward(units[2:], gmixed, 1, pair_w, down_w, order)
-    halves = first_half, second_half
-    gunit, ffn_out = [[item[i] for item in halves for i in place] for place in ((3, 4), (5, 6))]
-
-    def ffn_weights(sent):
-        first = pair_grads([after(units[0], sent), *units[1:]], [item[i] for item in halves for i in (1, 2)], order)
-        left = after(dy, first)
-        parts = [([(left, i)], [(item[0],)]) for i, item in enumerate(halves)]
-        return first, weight_grads(parts, split_order(order, n_seq), quarters)
-
-    terms, (grad_pair, grad_down) = scatter_head(gunit, beside=ffn_weights)
-    grad_pair = lax.psum_scatter(grad_pair, "seq", scatter_dimension=0, tiled=True).astype(f32)
+    first = feed_forward(units[2:], dy, 2, ffn_w[0], cut, order, held)
+    seq_sum = lambda value: lax.psum_scatter(value, "seq", scatter_dimension=0, tiled=True).astype(f32)
+    first_grads = ffn_weight_grads(units, dy, first[:3], order)
+    ffn_grads = [seq_sum(first_grads)]
+    left = [after(units[0], first_grads), *units[1:]]
+    second = feed_forward(left, dy, 0, ffn_w[1], hidden_units - cut, order, earlier=first[3:])
+    gunit, ffn_out = [[item[i] for i in range(4)] for item in second[3:]]
+
+    def second_grads(sent):
+        return ffn_weight_grads([after(units[0], sent), *units[1:]], dy, second[:3], order)
+
+    terms, found = scatter_head(gunit, beside=second_grads)
     grad_hidden, grad_branch = on_quarter(norm_back_kernel, [hidden, dy, *terms], quarter, [f32, bf16])
+    ffn_grads.append(seq_sum(after(found, grad_hidden)))
     grad_branch = gather_head(grad_branch)
 
     grad_att = back_product(grad_branch, out_w, quarters).reshape(rows, length, values)
@@ -861,17 +872,14 @@
     )
     sides = [[(grad_branch[i],), (grad_branch[i + 1],)] for i in (0, 2)]
     parts = [(side, [(attended_flat, "q", i), (attended_flat, "q", i + 1)]) for side, i in zip(sides, (0, 2))]
-    grad_out_w = weight_grads(parts, split_order(order, n_seq), quarters)
-    found = scan_begin(carry, True, me, n_seq)
+    grad_out_w = weight_grads(parts, order, quarters)
+    found = scan_begin(carry, True, me, n_seq, (gboth, grad_out_w))
     ffn_out[3] = after(ffn_out[3], grad_att)
     terms, _ = scatter_head(ffn_out, beside=lambda _: found)
     block_own = (hidden + (terms[0].astype(f32) + terms[1].astype(f32) + terms[2].astype(f32))).astype(bf16)
-    down_pairs = scatter_begin(after(grad_down, *grad_branch), n_seq)
     carry_in, place_back = scan_end(found, True, me, n_seq)
-    carry_in = after(carry_in, block_own, *down_pairs)
-    out_pairs = scatter_begin(grad_out_w, n_seq)
-    block_all = gather_head(block_own)
-    down_terms = scatter_sends(down_pairs)
+    carry_in = after(carry_in, block_own)
+    block_all = gather_head(block_own, lambda near: (carry_in,))
     (gqkv,) = by_row(
         functools.partial(finish_back_kernel, heads),
         rows,
@@ -880,51 +888,52 @@
         place=place_back,
         flops=6 * unit_flops,
     )
-    gqkv = after(gqkv.reshape(count, lanes + values), *block_all, *out_pairs)
+    gqkv = after(gqkv.reshape(count, lanes + values), *block_all)
+    back = lambda value, kind: place_quarters(value, quarters, order, kind).reshape(rows, length, width)
+
+    def sum_head(value):
+        value = jnp.broadcast_to(value, (8, width // n_seq))
+        pairs = [send(value, "head", mask, 4) for mask in (1, 2, 3)]
+        return ((value + pairs[0]) + (pairs[1] + pairs[2]))[0]
+
+    def ffn_outputs(sums):
+        parts = [jnp.split(item, 3, axis=1) for item in sums]
+        grad_gate, grad_up, grad_down = [jnp.concatenate(items, axis=1) for items in zip(*parts)]
+        gain = jnp.sum(gate_weight.astype(f32) * grad_gate + up_weight.astype(f32) * grad_up, axis=1)
+        return (grad_gate * gain_two, grad_up * gain_two, grad_down.T), sum_head(gain)
+
+    grad_out_w = seq_sum(grad_out_w)
     far = quarter_products(gqkv, qkv_w, quarters, 3)
     near = quarter_products(gqkv, qkv_w, quarters, 1)
-    out_terms = scatter_sends(out_pairs)
     terms, grad_qkv = scatter_head(
         [near[1], near[0], far[1], far[0]],
         beside=lambda sent: weight_grads(
             [([(after(unit_one, sent),)], [(gqkv,)])], split_order(order, n_seq), quarters
         ),
     )
-    terms = after(terms, *down_terms[:2], *out_terms)
     (grad_x,) = on_quarter(norm_back_kernel, [x_own, grad_hidden, *terms], quarter, [bf16])
-    grad_x_all = gather_head(grad_x)
-    grad_x_all[0] = after(grad_x_all[0], *down_terms[2:])
-    grad_down = scatter_end(down_pairs, down_terms)
-    grad_out_w = scatter_end(out_pairs, out_terms)
-    grad_qkv = scatter_begin(grad_qkv, n_seq)
-    grad_qkv = (grad_qkv[0],) + tuple(after(pair, grad_x) for pair in grad_qkv[1:])
-    grad_qkv = scatter_end(grad_qkv, scatter_sends(grad_qkv))
-
-    back = lambda value, kind: place_quarters(value, quarters, order, kind).reshape(rows, length, width)
-    hidden_units = gate_weight.shape[1]
-    grad_gate, grad_up = grad_pair[:, :hidden_units], grad_pair[:, hidden_units:]
-    gain_sums = jnp.stack(
-        [
-            jnp.sum(qkv_own.astype(f32) * grad_qkv, axis=1),
-            jnp.sum(gate_weight.astype(f32) * grad_gate + up_weight.astype(f32) * grad_up, axis=1),
-        ]
-    )
-    gain_sums = gain_sums + send(gain_sums, "head", CORE, 4)
-    gain_sums = gain_sums + send(gain_sums, "head", ACROSS, 4)
+    qkv_pairs = scatter_begin(grad_qkv, n_seq)
+    ffn_grads, ffn_gain = ffn_outputs(after(ffn_grads, grad_x))
+    block_all = back(block_all, bf16)
+    grad_x_all = gather_head(grad_x, lambda near: (block_all, ffn_gain, *ffn_grads, *qkv_pairs))
+    qkv_terms = scatter_sends(qkv_pairs)
+    grad_x_all[0] = after(grad_x_all[0], *qkv_terms)
+    grad_x_all = back(grad_x_all, f32)
+    grad_out_w = after(grad_out_w, grad_x_all)
+    grad_qkv = scatter_end(qkv_pairs, qkv_terms)
+    qkv_gain = sum_head(jnp.sum(qkv_own.astype(f32) * grad_qkv, axis=1))
     grad_qkv = grad_qkv * gain_one
     narrow = heads * FEAT
     return (
-        back(block_all, bf16),
-        back(grad_x_all, f32),
-        gain_sums[0],
-        gain_sums[1],
+        block_all,
+        grad_x_all,
+        qkv_gain,
+        ffn_gain,
         grad_qkv[:, :narrow],
         grad_qkv[:, narrow:lanes],
         grad_qkv[:, lanes:],
         grad_out_w.T,
-        grad_gate * gain_two,
-        grad_up * gain_two,
-        grad_down.T,
+        *ffn_grads,
     )
 
 

time: 1080 us -> 844 us (0.78)
  waiting for transfers between devices: 539 us -> 302 us
  starting transfers between devices: 136 us -> 94.5 us
  local copies, waits for them, and re-layouts: 72.5 us -> 97.4 us
  between operations: 15.4 us -> 31.8 us
  Pallas kernels: 256 us -> 272 us
  matrix products: 11.7 us -> 0 us
    ppermute x87 -> x69, waiting for transfers between devices: 435 us -> 245 us  [send(): return lax.ppermute(value, axis, [(i, i ^ mask) for i in range(count)])]
    all_gather x2 -> x3, waiting for transfers between devices: 104 us -> 21.4 us  [per_device(): everywhere = lambda value: lax.all_gather(value, 'seq', axis=0, tiled=True)]
    ppermute x87 -> x69, starting transfers between devices: 136 us -> 94.3 us  [send(): return lax.ppermute(value, axis, [(i, i ^ mask) for i in range(count)])]
    reduce_scatter x1 -> x3, waiting for transfers between devices: 0.02 us -> 34.4 us  [per_device(): lax.psum_scatter(value, 'seq', scatter_dimension=0, tiled=True).astype(f32)]
    pallas_call x5 -> x7, Pallas kernels: 108 us -> 139 us  [the longest x3 92.4 us: feed_forward(): pl.pallas_call(functools.partial(ffn_kernel, 256, steps, len(earlier)), o...]
    pallas_call x3 -> x2, Pallas kernels: 33.4 us -> 18.4 us  [weight_grads(): pl.pallas_call(functools.partial(weight_kernel, tuple(((len(lefts), len(r...]
    unnamed x261 -> x269, local copies, waits for them, and re-layouts: 57.2 us -> 70.8 us
    dot_general x1 -> x0, matrix products: 11.7 us -> none  [nn(): lax.dot_general(left, right, (((1,), (0,)), ((), ())), preferred_element_...]
  transfers between devices with their start and end apart: 90 -> 75, of which waited for: 38 -> 29; matrix products, arithmetic and copies ran while one was open for 7% -> 9% of each run, Pallas kernels for 18% -> 32%
where the time goes in v4:
time: 844 us; the launch traced here: 832 us
  waiting for transfers between devices  302 us (36%)
  Pallas kernels  272 us (32%)
  local copies, waits for them, and re-layouts  97.4 us (12%)
  starting transfers between devices  94.5 us (11%)
  other arithmetic  33.9 us (4%)
  between operations  31.8 us (4%)
    ppermute x69, waiting for transfers between devices, send(): return lax.ppermute(value, axis, [(i, i ^ mask) for i in range(count)])  245 us
    ppermute x69, starting transfers between devices, send(): return lax.ppermute(value, axis, [(i, i ^ mask) for i in range(count)])  94.3 us
    pallas_call x3, Pallas kernels, feed_forward(): pl.pallas_call(functools.partial(ffn_kernel, 256, steps, len(earlier)), o...  92.4 us
    unnamed x269, local copies, waits for them, and re-layouts  70.8 us
    pallas_call x6, Pallas kernels, by_row(): pl.pallas_call(kernel, out_shape=shapes, grid_spec=pltpu.PrefetchScalarGr...  52.9 us
    pallas_call x2, Pallas kernels, ffn_weight_grads(): pl.pallas_call(ffn_weight_kernel, out_shape=jax.ShapeDtypeStruct((width,...  43.7 us
    reduce_scatter x3, waiting for transfers between devices, per_device(): lax.psum_scatter(value, 'seq', scatter_dimension=0, tiled=True).astype(f32)  34.4 us
    all_gather x3, waiting for transfers between devices, per_device(): everywhere = lambda value: lax.all_gather(value, 'seq', axis=0, tiled=True)  21.4 us
  transfers between devices with their start and end apart: 75, of which 29 were waited for; matrix products, arithmetic and copies ran while one was open for 9% of the time, Pallas kernels for 32%

profile of v4, /device:TPU:0, one launch (start us, length us, event | category | flops | bytes accessed | tf_op | source)
XLA Modules:
  0.0 831.8 jit_solution(5151732615215557541)
XLA Ops:
  24.9 10.2 %collective-permute-done.1.refs_2_ = bf16[256,640]{1,0:T(8,128)(2,1)S(1)} collective-permute-done((bf16[256,640]{1,0:T(8,128)(2,1)S(1)}, bf16[256,640]{1,0:T(8,128)(2,1)S(1)}, u32[]{:S(2)}, u32[]{:S(2)}) %collective-permute-start.1) | collective-permute-done | bytes 327712 | tf_op jit(solution)/shard_map/ppermute | solution.py:305
  35.4 14.8 %collective-permute-done.3.refs_4_ = bf16[256,640]{1,0:T(8,128)(2,1)S(1)} collective-permute-done((bf16[256,640]{1,0:T(8,128)(2,1)S(1)}, bf16[256,640]{1,0:T(8,128)(2,1)S(1)}, u32[]{:S(2)}, u32[]{:S(2)}) %collective-permute-start.3) | collective-permute-done | bytes 327712 | tf_op jit(solution)/shard_map/ppermute | solution.py:305
  116.8 9.1 %collective-permute-done.8.refs_2_ = bf16[3,160,128]{2,1,0:T(8,128)(2,1)S(1)} collective-permute-done((bf16[3,160,128]{2,1,0:T(8,128)(2,1)S(1)}, bf16[3,160,128]{2,1,0:T(8,128)(2,1)S(1)}, u32[]{:S(2)}, u32[]{:S(2)}) %collective-permute-start.8) | collective-permute-done | bytes 122912 | tf_op jit(solution)/shard_map/ppermute | solution.py:305
  172.0 12.6 %collective-permute-done.17 = bf16[3,160,128]{2,1,0:T(8,128)(2,1)S(1)} collective-permute-done((bf16[3,160,128]{2,1,0:T(8,128)(2,1)S(1)}, bf16[3,160,128]{2,1,0:T(8,128)(2,1)S(1)}, u32[]{:S(2)}, u32[]{:S(2)}) %collective-permute-start.17) | collective-permute-done | bytes 122912 | tf_op jit(solution)/shard_map/ppermute | solution.py:305
  184.6 11.2 %collective-permute-done.18 = bf16[3,160,128]{2,1,0:T(8,128)(2,1)S(1)} collective-permute-done((bf16[3,160,128]{2,1,0:T(8,128)(2,1)S(1)}, bf16[3,160,128]{2,1,0:T(8,128)(2,1)S(1)}, u32[]{:S(2)}, u32[]{:S(2)}) %collective-permute-start.18) | collective-permute-done | bytes 122912 | tf_op jit(solution)/shard_map/ppermute | solution.py:305
  231.4 35.1 %collective-permute-done.23.c_ref = bf16[384,2048]{1,0:T(8,128)(2,1)S(1)} collective-permute-done((bf16[384,2048]{1,0:T(8,128)(2,1)S(1)}, bf16[384,2048]{1,0:T(8,128)(2,1)S(1)}, u32[]{:S(2)}, u32[]{:S(2)}) %collective-permute-start.23) | collective-permute-done | bytes 1572896 | tf_op jit(solution)/shard_map/ppermute | solution.py:305
  274.7 24.5 %shard_map.286 = (bf16[1536,768]{1,0:T(8,128)(2,1)}, bf16[1536,768]{1,0:T(8,128)(2,1)}, bf16[1536,768]{1,0:T(8,128)(2,1)}, bf16[4,384,2048]{2,1,0:T(8,128)(2,1)}, bf16[4,384,2048]{2,1,0:T(8,128)(2,1)}) custom-call(s32[8]{0:T(128)} %copy-done.72, bf16[384,2048]{1,0:T(8,128)(2,1)} %get-tuple-element.121.refs_0_, ...), custom_call_target="tpu_custom_call" | custom-call | flops 7247757312 | bytes 11010048 | tf_op jit(solution)/shard_map/pallas_call | solution.py:643
  311.8 24.8 %shard_map.287 = (bf16[1536,768]{1,0:T(8,128)(2,1)}, bf16[1536,768]{1,0:T(8,128)(2,1)}, bf16[1536,768]{1,0:T(8,128)(2,1)}, bf16[4,384,2048]{2,1,0:T(8,128)(2,1)}, bf16[4,384,2048]{2,1,0:T(8,128)(2,1)}) custom-call(s32[8]{0:T(128)} %copy-done.72, ...), custom_call_target="tpu_custom_call", output_to_operand_aliasing={{0}: (5, {}), {1}: (6, {}), {2}: (7, {}), {3}: (8, {}), {4}... | custom-call | flops 7247757312 | bytes 11010048 | tf_op jit(solution)/shard_map/pallas_call | solution.py:643
  336.7 22.1 %shard_map.288 = bf16[2048,2304]{1,0:T(8,128)(2,1)} custom-call(s32[8]{0:T(128)S(1)} %copy-done.73, bf16[384,2048]{1,0:T(8,128)(2,1)} %get-tuple-element.121.refs_0_, bf16[384,2048]{1,0:T(8,128)(2,1)} %collective-permute-done.24.refs_1_, bf16[384,2048]{1,0:T(8,128)(2,1)} %collective-permute-done.25.refs_0_.refs_2_, ...), custom_call_target="tpu_custom_call" | custom-call | flops 7247757312 | bytes 22282240 | tf_op jit(solution)/shard_map/pallas_call | solution.py:720
  358.8 21.4 %all-gather.8.cloned.1.call-done.refs_5_ = bf16[2048,1920]{1,0:T(8,128)(2,1)} async-done(((bf16[256,1920]{1,0:T(8,128)(2,1)}), bf16[2048,1920]{1,0:T(8,128)(2,1)}) %all-gather.8.cloned.1.call-update) | async-done | bytes 7864336 | tf_op jit(solution)/shard_map/all_gather | solution.py:774
  380.2 43.1 %shard_map.289 = (bf16[1536,640]{1,0:T(8,128)(2,1)}, bf16[1536,640]{1,0:T(8,128)(2,1)}, bf16[1536,640]{1,0:T(8,128)(2,1)}, bf16[4,384,2048]{2,1,0:T(8,128)(2,1)}, bf16[4,384,2048]{2,1,0:T(8,128)(2,1)}) custom-call(s32[8]{0:T(128)} %copy-done.72, bf16[384,2048]{1,0:T(8,128)(2,1)} %get-tuple-element.121.refs_0_, ...), custom_call_target="tpu_custom_call" | custom-call | flops 12079595520 | bytes 16515072 | tf_op jit(solution)/shard_map/pallas_call | solution.py:643
  436.1 21.7 %shard_map.290 = bf16[2048,1920]{1,0:T(8,128)(2,1)} custom-call(s32[8]{0:T(128)S(1)} %copy-done.74, bf16[384,2048]{1,0:T(8,128)(2,1)} %get-tuple-element.121.refs_0_, bf16[384,2048]{1,0:T(8,128)(2,1)} %collective-permute-done.24.refs_1_, bf16[384,2048]{1,0:T(8,128)(2,1)} %collective-permute-done.25.refs_0_.refs_2_, ...), custom_call_target="tpu_custom_call" | custom-call | flops 6039797760 | bytes 20316160 | tf_op jit(solution)/shard_map/pallas_call | solution.py:720
  457.8 13.7 %collective-permute-done.30.c_ref = bf16[384,2048]{1,0:T(8,128)(2,1)} collective-permute-done((bf16[384,2048]{1,0:T(8,128)(2,1)}, bf16[384,2048]{1,0:T(8,128)(2,1)}, u32[]{:S(2)}, u32[]{:S(2)}) %collective-permute-start.30) | collective-permute-done | bytes 1572896 | tf_op jit(solution)/shard_map/ppermute | solution.py:305
  486.1 34.6 %collective-permute-done.32.refs_2_.refs_4_ = bf16[384,2048]{1,0:T(8,128)(2,1)S(1)} collective-permute-done((bf16[384,2048]{1,0:T(8,128)(2,1)}, bf16[384,2048]{1,0:T(8,128)(2,1)S(1)}, u32[]{:S(2)}, u32[]{:S(2)}) %collective-permute-start.32) | collective-permute-done | bytes 1572896 | tf_op jit(solution)/shard_map/ppermute | solution.py:305
  537.9 9.0 %shard_map.293 = (bf16[6,4,160,128]{3,2,1,0:T(8,128)(2,1)S(1)}, bf16[6,256,512]{2,1,0:T(8,128)(2,1)S(1)}, f32[6,256,4]{2,1,0:T(8,128)S(1)}) custom-call(bf16[6,256,640]{2,1,0:T(8,128)(2,1)S(1)} %bitcast.146, f32[6,256,8]{2,1,0:T(8,128)S(1)} %copy-done.8, bf16[6,256,512]{2,1,0:T(8,128)(2,1)S(1)} %bitcast.156, ...), custom_call_target="tpu_custom_call" | custom-call | flops 603979776 | bytes 4161536 | tf_op jit(solution)/shard_map/pallas_call | solution.py:242
  555.6 16.8 %shard_map.294 = (f32[6,256,128]{2,1,0:T(8,128)S(1)}, f32[6,256,512]{2,1,0:T(8,128)S(1)}) custom-call(s32[8]{0:T(128)S(1)} %copy-done.74, bf16[6,256,640]{2,1,0:T(8,128)(2,1)S(1)} %bitcast.147, f32[6,256,8]{2,1,0:T(8,128)S(1)} %copy-done.8, f32[6,8,256]{2,1,0:T(8,128)S(1)} %copy-done.76, bf16[6,256,512]{2,1,0:T(8,128)(2,1)S(1)} %get-tuple-element.130.gnum_ref, ...), custom_call_target="tpu_custom_call" | custom-call | flops 2214592512 | bytes 4698112 | tf_op jit(solution)/shard_map/pallas_call | solution.py:242
  583.0 9.0 %shard_map.295 = bf16[2048,512]{1,0:T(8,128)(2,1)} custom-call(s32[8]{0:T(128)S(1)} %copy-done.74, s32[4]{0:T(128)S(1)} %iota_xor_fusion.1.rows_ref.order_ref.quarters_ref, bf16[384,2048]{1,0:T(8,128)(2,1)S(1)} %copy-done.26, bf16[384,2048]{1,0:T(8,128)(2,1)S(1)} %collective-permute-done.31.refs_1_, bf16[1536,512]{1,0:T(8,128)(2,1)S(1)} %bitcast.139, ...), custom_call_target="tpu_custom_call" | custom-call | flops 1610612736 | bytes 9175040 | tf_op jit(solution)/shard_map/pallas_call | solution.py:692
  604.2 16.3 %collective-permute-start.45 = (bf16[3,160,128]{2,1,0:T(8,128)(2,1)S(1)}, bf16[3,160,128]{2,1,0:T(8,128)(2,1)S(1)}, u32[]{:S(2)}, u32[]{:S(2)}) collective-permute-start(bf16[3,160,128]{2,1,0:T(8,128)(2,1)S(1)} %get-tuple-element.136), channel_id=1, source_target_pairs={{0,8},{4,12},{8,0},{12,4},{16,24},{20,28},{24,16},{28,20},{1,9},{5... | collective-permute-start | bytes 368648 | tf_op jit(solution)/shard_map/ppermute | solution.py:305
  645.4 9.2 %collective-permute-done.48 = bf16[3,160,128]{2,1,0:T(8,128)(2,1)S(1)} collective-permute-done((bf16[3,160,128]{2,1,0:T(8,128)(2,1)S(1)}, bf16[3,160,128]{2,1,0:T(8,128)(2,1)S(1)}, u32[]{:S(2)}, u32[]{:S(2)}) %collective-permute-start.48) | collective-permute-done | bytes 122912 | tf_op jit(solution)/shard_map/ppermute | solution.py:305
  655.5 9.5 %collective-permute-done.43.refs_0_ = bf16[384,2048]{1,0:T(8,128)(2,1)S(1)} collective-permute-done((bf16[384,2048]{1,0:T(8,128)(2,1)S(1)}, bf16[384,2048]{1,0:T(8,128)(2,1)S(1)}, u32[]{:S(2)}, u32[]{:S(2)}) %collective-permute-start.43) | collective-permute-done | bytes 1572896 | tf_op jit(solution)/shard_map/ppermute | solution.py:305
  691.3 9.4 %shard_map.302 = bf16[2048,640]{1,0:T(8,128)(2,1)S(1)} custom-call(s32[8]{0:T(128)S(1)} %copy-done.91, s32[4]{0:T(128)S(1)} %iota_xor_fusion.1.rows_ref.order_ref.quarters_ref, bf16[1536,2048]{1,0:T(8,128)(2,1)} %copy-done.2, bf16[1536,640]{1,0:T(8,128)(2,1)S(1)} %bitcast.151), custom_call_target="tpu_custom_call" | custom-call | flops 2013265920 | bytes 9633792 | tf_op jit(solution)/shard_map/pallas_call | solution.py:692
  708.4 13.7 %collective-permute-done.55.c_ref = bf16[384,2048]{1,0:T(8,128)(2,1)S(1)} collective-permute-done((bf16[384,2048]{1,0:T(8,128)(2,1)S(1)}, bf16[384,2048]{1,0:T(8,128)(2,1)S(1)}, u32[]{:S(2)}, u32[]{:S(2)}) %collective-permute-start.55) | collective-permute-done | bytes 1572896 | tf_op jit(solution)/shard_map/ppermute | solution.py:305
  748.0 12.2 %collective-permute-done.59 = f32[8,256]{1,0:T(8,128)S(1)} collective-permute-done((f32[8,256]{1,0:T(8,128)S(1)}, f32[8,256]{1,0:T(8,128)S(1)}, u32[]{:S(2)}, u32[]{:S(2)}) %collective-permute-start.59) | collective-permute-done | bytes 8224 | tf_op jit(solution)/shard_map/ppermute | solution.py:305
  766.9 34.4 %reduce-scatter.8.cloned.1.call-done = bf16[256,512]{1,0:T(8,128)(2,1)} async-done(((bf16[2048,512]{1,0:T(8,128)(2,1)}), bf16[256,512]{1,0:T(8,128)(2,1)}) %reduce-scatter.8.cloned.1.call-update) | async-done | bytes 262160 | tf_op jit(solution)/shard_map/reduce_scatter | solution.py:840
  (496 shorter events, 361.7 us)
Async XLA Ops:
  7.2 189.5 %all-gather.4.cloned.1.call-start = ((), (), s32[]{:S(2)}) async-start(), calls=%async_computation.3 | async-start | bytes 2359296 | tf_op jit(solution)/shard_map/all_gather | solution.py:774
  7.9 266.8 %all-gather.6.cloned.1.call-start = ((), (), s32[]{:S(2)}) async-start(), calls=%async_computation.4 | async-start | bytes 10616832 | tf_op jit(solution)/shard_map/all_gather | solution.py:774
  12.0 368.2 %all-gather.8.cloned.1.call-start = ((), (), s32[]{:S(2)}) async-start(), calls=%async_computation.5 | async-start | bytes 8847360 | tf_op jit(solution)/shard_map/all_gather | solution.py:774
  12.6 66.1 %collective-permute-start = (bf16[256,640]{1,0:T(8,128)(2,1)S(1)}, bf16[256,640]{1,0:T(8,128)(2,1)S(1)}, u32[]{:S(2)}, u32[]{:S(2)}) collective-permute-start(bf16[256,640]{1,0:T(8,128)(2,1)S(1)} %fusion.11.refs_0_), channel_id=1, source_target_pairs={{0,4},{4,0},{8,12},{12,8},{16,20},{20,16},{24,28},{28,24},{1,5},{5... | collective-permute-start | bytes 983048 | tf_op jit(solution)/shard_map/ppermute | solution.py:305
  22.3 712.9 %reduce-scatter.4.cloned.1.call-start = ((), (), s32[]{:S(2)}) async-start(), calls=%async_computation.6 | async-start | bytes 10616832 | tf_op jit(solution)/shard_map/reduce_scatter | solution.py:840
  35.0 44.4 %collective-permute-start.2 = (bf16[256,640]{1,0:T(8,128)(2,1)S(1)}, bf16[256,640]{1,0:T(8,128)(2,1)}, u32[]{:S(2)}, u32[]{:S(2)}) collective-permute-start(bf16[256,640]{1,0:T(8,128)(2,1)S(1)} %collective-permute-done.1.refs_2_), channel_id=1, source_target_pairs={{0,4},{4,0},{8,12},{12,8},{16,20},{20,16},{24,28},{28,24},{1,5},{5... | collective-permute-start | bytes 983048 | tf_op jit(solution)/shard_map/ppermute | solution.py:305
  109.8 41.1 %collective-permute-start.9 = (bf16[3,160,128]{2,1,0:T(8,128)(2,1)}, bf16[3,160,128]{2,1,0:T(8,128)(2,1)}, u32[]{:S(2)}, u32[]{:S(2)}) collective-permute-start(bf16[3,160,128]{2,1,0:T(8,128)(2,1)} %get-tuple-element.247), channel_id=1, source_target_pairs={{0,12},{4,8},{8,4},{12,0},{16,28},{20,24},{24,20},{28,16},{1,13},{... | collective-permute-start | bytes 368648 | tf_op jit(solution)/shard_map/ppermute | solution.py:305
  109.8 41.1 %collective-permute-start.10 = (bf16[3,160,128]{2,1,0:T(8,128)(2,1)}, bf16[3,160,128]{2,1,0:T(8,128)(2,1)}, u32[]{:S(2)}, u32[]{:S(2)}) collective-permute-start(bf16[3,160,128]{2,1,0:T(8,128)(2,1)} %get-tuple-element.246), channel_id=1, source_target_pairs={{0,16},{4,20},{8,24},{12,28},{16,0},{20,4},{24,8},{28,12},{1,17},{... | collective-permute-start | bytes 368648 | tf_op jit(solution)/shard_map/ppermute | solution.py:305
  112.9 38.1 %collective-permute-start.11 = (bf16[3,160,128]{2,1,0:T(8,128)(2,1)}, bf16[3,160,128]{2,1,0:T(8,128)(2,1)}, u32[]{:S(2)}, u32[]{:S(2)}) collective-permute-start(bf16[3,160,128]{2,1,0:T(8,128)(2,1)} %get-tuple-element.245), channel_id=1, source_target_pairs={{0,20},{4,16},{8,28},{12,24},{16,4},{20,0},{24,12},{28,8},{1,21},{... | collective-permute-start | bytes 368648 | tf_op jit(solution)/shard_map/ppermute | solution.py:305
  229.7 36.8 %collective-permute-start.23 = (bf16[384,2048]{1,0:T(8,128)(2,1)S(1)}, bf16[384,2048]{1,0:T(8,128)(2,1)S(1)}, u32[]{:S(2)}, u32[]{:S(2)}) collective-permute-start(bf16[384,2048]{1,0:T(8,128)(2,1)S(1)} %add_convert_fusion.1), channel_id=1, source_target_pairs={{0,2},{1,3},{2,0},{3,1},{4,6},{5,7},{6,4},{7,5},{8,10},{9,11},{10,... | collective-permute-start | bytes 4718600 | tf_op jit(solution)/shard_map/ppermute | solution.py:305
  271.0 37.1 %collective-permute-start.25 = (bf16[384,2048]{1,0:T(8,128)(2,1)}, bf16[384,2048]{1,0:T(8,128)(2,1)}, u32[]{:S(2)}, u32[]{:S(2)}) collective-permute-start(bf16[384,2048]{1,0:T(8,128)(2,1)} %get-tuple-element.121.refs_0_), channel_id=1, source_target_pairs={{0,2},{1,3},{2,0},{3,1},{4,6},{5,7},{6,4},{7,5},{8,10},{9,11},{10,... | collective-permute-start | bytes 4718600 | tf_op jit(solution)/shard_map/ppermute | solution.py:305
  358.8 379.4 %reduce-scatter.6.cloned.1.call-start = ((), (), s32[]{:S(2)}) async-start(), calls=%async_computation.7 | async-start | bytes 8847360 | tf_op jit(solution)/shard_map/reduce_scatter | solution.py:840
  434.6 36.9 %collective-permute-start.30 = (bf16[384,2048]{1,0:T(8,128)(2,1)}, bf16[384,2048]{1,0:T(8,128)(2,1)}, u32[]{:S(2)}, u32[]{:S(2)}) collective-permute-start(bf16[384,2048]{1,0:T(8,128)(2,1)} %fusion), channel_id=1, source_target_pairs={{0,2},{1,3},{2,0},{3,1},{4,6},{5,7},{6,4},{7,5},{8,10},{9,11},{10,... | collective-permute-start | bytes 4718600 | tf_op jit(solution)/shard_map/ppermute | solution.py:305
  484.5 316.7 %reduce-scatter.8.cloned.1.call-start = ((), (), s32[]{:S(2)}) async-start(), calls=%async_computation.8 | async-start | bytes 2359296 | tf_op jit(solution)/shard_map/reduce_scatter | solution.py:840
  486.1 38.7 %collective-permute-start.31 = (bf16[384,2048]{1,0:T(8,128)(2,1)}, bf16[384,2048]{1,0:T(8,128)(2,1)S(1)}, u32[]{:S(2)}, u32[]{:S(2)}) collective-permute-start(bf16[384,2048]{1,0:T(8,128)(2,1)} %copy-done.25), channel_id=1, source_target_pairs={{0,1},{1,0},{2,3},{3,2},{4,5},{5,4},{6,7},{7,6},{8,9},{9,8},{10,11... | collective-permute-start | bytes 4718600 | tf_op jit(solution)/shard_map/ppermute | solution.py:305
  536.3 85.6 %collective-permute-start.35 = (bf16[384,2048]{1,0:T(8,128)(2,1)}, bf16[384,2048]{1,0:T(8,128)(2,1)}, u32[]{:S(2)}, u32[]{:S(2)}) collective-permute-start(bf16[384,2048]{1,0:T(8,128)(2,1)} %fusion.1), channel_id=1, source_target_pairs={{0,2},{1,3},{2,0},{3,1},{4,6},{5,7},{6,4},{7,5},{8,10},{9,11},{10,... | collective-permute-start | bytes 4718600 | tf_op jit(solution)/shard_map/ppermute | solution.py:305
  537.8 85.1 %collective-permute-start.27 = (bf16[384,2048]{1,0:T(8,128)(2,1)}, bf16[384,2048]{1,0:T(8,128)(2,1)}, u32[]{:S(2)}, u32[]{:S(2)}) collective-permute-start(bf16[384,2048]{1,0:T(8,128)(2,1)} %get-tuple-element.216), channel_id=1, source_target_pairs={{0,1},{1,0},{2,3},{3,2},{4,5},{5,4},{6,7},{7,6},{8,9},{9,8},{10,11... | collective-permute-start | bytes 4718600 | tf_op jit(solution)/shard_map/ppermute | solution.py:305
  685.4 36.7 %collective-permute-start.55 = (bf16[384,2048]{1,0:T(8,128)(2,1)S(1)}, bf16[384,2048]{1,0:T(8,128)(2,1)S(1)}, u32[]{:S(2)}, u32[]{:S(2)}) collective-permute-start(bf16[384,2048]{1,0:T(8,128)(2,1)S(1)} %add_convert_fusion), channel_id=1, source_target_pairs={{0,2},{1,3},{2,0},{3,1},{4,6},{5,7},{6,4},{7,5},{8,10},{9,11},{10,... | collective-permute-start | bytes 4718600 | tf_op jit(solution)/shard_map/ppermute | solution.py:305
  725.3 37.1 %collective-permute-start.56 = (bf16[384,2048]{1,0:T(8,128)(2,1)}, bf16[384,2048]{1,0:T(8,128)(2,1)}, u32[]{:S(2)}, u32[]{:S(2)}) collective-permute-start(bf16[384,2048]{1,0:T(8,128)(2,1)} %shard_map.303.refs_0_), channel_id=1, source_target_pairs={{0,2},{1,3},{2,0},{3,1},{4,6},{5,7},{6,4},{7,5},{8,10},{9,11},{10,... | collective-permute-start | bytes 4718600 | tf_op jit(solution)/shard_map/ppermute | solution.py:305
  735.3 75.9 %collective-permute-start.65 = (bf16[384,2048]{1,0:T(8,128)(2,1)}, bf16[384,2048]{1,0:T(8,128)(2,1)}, u32[]{:S(2)}, u32[]{:S(2)}) collective-permute-start(bf16[384,2048]{1,0:T(8,128)(2,1)} %shard_map.303.refs_0_), channel_id=1, source_target_pairs={{0,1},{1,0},{2,3},{3,2},{4,5},{5,4},{6,7},{7,6},{8,9},{9,8},{10,11... | collective-permute-start | bytes 4718600 | tf_op jit(solution)/shard_map/ppermute | solution.py:305
  762.4 55.7 %collective-permute-start.61 = (bf16[384,2048]{1,0:T(8,128)(2,1)}, bf16[384,2048]{1,0:T(8,128)(2,1)}, u32[]{:S(2)}, u32[]{:S(2)}) collective-permute-start(bf16[384,2048]{1,0:T(8,128)(2,1)} %collective-permute-done.56.refs_0_), channel_id=1, source_target_pairs={{0,1},{1,0},{2,3},{3,2},{4,5},{5,4},{6,7},{7,6},{8,9},{9,8},{10,11... | collective-permute-start | bytes 4718600 | tf_op jit(solution)/shard_map/ppermute | solution.py:305
  762.5 40.6 %collective-permute-start.62 = (bf16[256,640]{1,0:T(8,128)(2,1)}, bf16[256,640]{1,0:T(8,128)(2,1)S(1)}, u32[]{:S(2)}, u32[]{:S(2)}) collective-permute-start(bf16[256,640]{1,0:T(8,128)(2,1)} %get-tuple-element.225), channel_id=1, source_target_pairs={{0,8},{4,12},{8,0},{12,4},{16,24},{20,28},{24,16},{28,20},{1,9},{5... | collective-permute-start | bytes 983048 | tf_op jit(solution)/shard_map/ppermute | solution.py:305
  764.0 39.1 %collective-permute-start.63 = (bf16[256,640]{1,0:T(8,128)(2,1)}, bf16[256,640]{1,0:T(8,128)(2,1)S(1)}, u32[]{:S(2)}, u32[]{:S(2)}) collective-permute-start(bf16[256,640]{1,0:T(8,128)(2,1)} %get-tuple-element.224), channel_id=1, source_target_pairs={{0,16},{4,20},{8,24},{12,28},{16,0},{20,4},{24,8},{28,12},{1,17},{... | collective-permute-start | bytes 983048 | tf_op jit(solution)/shard_map/ppermute | solution.py:305
  764.6 39.9 %collective-permute-start.64 = (bf16[256,640]{1,0:T(8,128)(2,1)}, bf16[256,640]{1,0:T(8,128)(2,1)}, u32[]{:S(2)}, u32[]{:S(2)}) collective-permute-start(bf16[256,640]{1,0:T(8,128)(2,1)} %get-tuple-element.223), channel_id=1, source_target_pairs={{0,24},{4,28},{8,16},{12,20},{16,8},{20,12},{24,0},{28,4},{1,25},{... | collective-permute-start | bytes 983048 | tf_op jit(solution)/shard_map/ppermute | solution.py:305
  (171 other events, 2324.1 us)
Sparse Core Ops, SparseCore 0:
  10.1 73.7 all-gather.3
  86.7 173.1 all-gather.5
  262.7 117.4 all-gather.7
  384.2 161.5 reduce-scatter.3
  549.3 177.3 reduce-scatter.5
  730.1 71.0 reduce-scatter.7

commit v5 on v4

--- a/solution.py
+++ b/solution.py
@@ -357,9 +357,12 @@
 CORE, ACROSS = 1, 2
 
 
-def scatter_head(quarters, beside=None):
-    core = send(quarters[3], "head", CORE, 4)
-    summed = (quarters[2].astype(f32) + core.astype(f32)).astype(bf16)
+def scatter_core(quarters):
+    return (quarters[2].astype(f32) + send(quarters[3], "head", CORE, 4).astype(f32)).astype(bf16)
+
+
+def scatter_head(quarters, beside=None, summed=None):
+    summed = scatter_core(quarters) if summed is None else summed
     across = send(summed, "head", ACROSS, 4)
     near = send(quarters[1], "head", CORE, 4)
     found = () if beside is None else beside(summed)
@@ -703,34 +706,43 @@
     )(order, quarters, *arrays)
 
 
-def ffn_weight_kernel(order_ref, *refs):
-    units, (dy_ref, mixed_ref, ggate_ref, gup_ref, out) = refs[:4], refs[4:]
+def ffn_weight_kernel(order_ref, down_order_ref, *refs):
+    units, (dy_ref, mixed_ref, ggate_ref, gup_ref), outs = refs[:4], refs[4:8], refs[8:]
     cols = ggate_ref.shape[1]
     unit = jnp.concatenate([item[...] for item in units], axis=0).T
-    out[:, :cols] = nn(unit, ggate_ref[...]).astype(bf16)
-    out[:, cols : 2 * cols] = nn(unit, gup_ref[...]).astype(bf16)
-    out[:, 2 * cols :] = nn(dy_ref[...].T, mixed_ref[...]).astype(bf16)
-
-
-def ffn_weight_grads(units, dy, grads, order):
+    outs[0][:, :cols] = nn(unit, ggate_ref[...]).astype(bf16)
+    outs[0][:, cols : 2 * cols] = nn(unit, gup_ref[...]).astype(bf16)
+    down = nn(dy_ref[...].T, mixed_ref[...]).astype(bf16)
+    if len(outs) == 2:
+        outs[1][...] = down
+    else:
+        outs[0][:, 2 * cols :] = down
+
+
+def ffn_weight_grads(units, dy, grads, order, down_order=None):
     quarter, width = units[0].shape
     rows = width // BLOCKS
     cols = grads[0].shape[1]
-    held = pl.BlockSpec((4 * quarter, cols), lambda i, order: (0, 0), pipeline_mode=pl.Buffered(1))
-    return pl.pallas_call(
+    held = pl.BlockSpec((4 * quarter, cols), lambda i, *orders: (0, 0), pipeline_mode=pl.Buffered(1))
+    sizes = [3 * cols] if down_order is None else [2 * cols, cols]
+    results = pl.pallas_call(
         ffn_weight_kernel,
-        out_shape=jax.ShapeDtypeStruct((width, 3 * cols), bf16),
+        out_shape=[jax.ShapeDtypeStruct((width, n), bf16) for n in sizes],
         grid_spec=pltpu.PrefetchScalarGridSpec(
-            num_scalar_prefetch=1,
+            num_scalar_prefetch=2,
             grid=(BLOCKS,),
-            in_specs=[pl.BlockSpec((quarter, rows), lambda i, order: (0, i))] * 4
-            + [pl.BlockSpec((4 * quarter, rows), lambda i, order: (0, i))]
+            in_specs=[pl.BlockSpec((quarter, rows), lambda i, *orders: (0, i))] * 4
+            + [pl.BlockSpec((4 * quarter, rows), lambda i, *orders: (0, i))]
             + [held] * 3,
-            out_specs=pl.BlockSpec((rows, 3 * cols), lambda i, order: (order[i], 0)),
+            out_specs=[
+                pl.BlockSpec((rows, n), lambda i, *orders, place=place: (orders[place][i], 0))
+                for place, n in enumerate(sizes)
+            ],
         ),
         compiler_params=params(48),
         cost_estimate=cost(24 * quarter * width * cols, 2 * (8 * quarter + width) * (width + 3 * cols)),
-    )(order, *units, dy, *grads)
+    )(order, order if down_order is None else down_order, *units, dy, *grads)
+    return results[0] if down_order is None else results
 
 
 def per_device(
@@ -809,7 +821,7 @@
         [((length, values), f32), ((length, heads), f32)],
         flops=3 * unit_flops,
     )
-    found = scan_begin(states, False, me, n_seq, (numerator,))
+    found = scan_begin(states, False, me, n_seq, (numerator, out_w))
     state_in, place = scan_end(found, False, me, n_seq)
     query_tables = [(tables["qa"], False), (tables["qb"], False), (feat_rows, False)]
     key_tables = [(tables["ka"], False), (tables["kb"], False), (feat_rows, False)]
@@ -838,19 +850,31 @@
     units = gather_head(unit_two, near_rows)
     first = feed_forward(units[2:], dy, 2, ffn_w[0], cut, order, held)
     seq_sum = lambda value: lax.psum_scatter(value, "seq", scatter_dimension=0, tiled=True).astype(f32)
-    first_grads = ffn_weight_grads(units, dy, first[:3], order)
-    ffn_grads = [seq_sum(first_grads)]
+    first_grads = ffn_weight_grads(units, dy, first[:3], order, split_order(order, n_seq))
+    ffn_grads = [seq_sum(first_grads[0])]
     left = [after(units[0], first_grads), *units[1:]]
     second = feed_forward(left, dy, 0, ffn_w[1], hidden_units - cut, order, earlier=first[3:])
     gunit, ffn_out = [[item[i] for i in range(4)] for item in second[3:]]
 
+    down_pairs = scatter_begin(first_grads[1], n_seq)
+    gunit[3] = after(gunit[3], *down_pairs)
+
     def second_grads(sent):
-        return ffn_weight_grads([after(units[0], sent), *units[1:]], dy, second[:3], order)
+        left = [after(units[0], sent), *units[1:]]
+        return ffn_weight_grads(left, dy, second[:3], order)
 
     terms, found = scatter_head(gunit, beside=second_grads)
+    down_terms = scatter_sends(down_pairs)
+    terms = after(terms, *down_terms)
     grad_hidden, grad_branch = on_quarter(norm_back_kernel, [hidden, dy, *terms], quarter, [f32, bf16])
     ffn_grads.append(seq_sum(after(found, grad_hidden)))
-    grad_branch = gather_head(grad_branch)
+    block_sum = []
+
+    def block_core(near):
+        block_sum.append(scatter_core(ffn_out))
+        return block_sum
+
+    grad_branch = gather_head(grad_branch, block_core)
 
     grad_att = back_product(grad_branch, out_w, quarters).reshape(rows, length, values)
     carry, gnum, gden = by_row(
@@ -872,10 +896,9 @@
     )
     sides = [[(grad_branch[i],), (grad_branch[i + 1],)] for i in (0, 2)]
     parts = [(side, [(attended_flat, "q", i), (attended_flat, "q", i + 1)]) for side, i in zip(sides, (0, 2))]
-    grad_out_w = weight_grads(parts, order, quarters)
+    grad_out_w = weight_grads(parts, split_order(order, n_seq), quarters)
     found = scan_begin(carry, True, me, n_seq, (gboth, grad_out_w))
-    ffn_out[3] = after(ffn_out[3], grad_att)
-    terms, _ = scatter_head(ffn_out, beside=lambda _: found)
+    terms, _ = scatter_head(ffn_out, beside=lambda _: gboth, summed=block_sum[0])
     block_own = (hidden + (terms[0].astype(f32) + terms[1].astype(f32) + terms[2].astype(f32))).astype(bf16)
     carry_in, place_back = scan_end(found, True, me, n_seq)
     carry_in = after(carry_in, block_own)
@@ -888,21 +911,22 @@
         place=place_back,
         flops=6 * unit_flops,
     )
-    gqkv = after(gqkv.reshape(count, lanes + values), *block_all)
+    gqkv = after(gqkv.reshape(count, lanes + values), block_all[2])
     back = lambda value, kind: place_quarters(value, quarters, order, kind).reshape(rows, length, width)
 
-    def sum_head(value):
-        value = jnp.broadcast_to(value, (8, width // n_seq))
-        pairs = [send(value, "head", mask, 4) for mask in (1, 2, 3)]
-        return ((value + pairs[0]) + (pairs[1] + pairs[2]))[0]
+    rest = hidden_units - cut
+
+    def sum_head(value, earlier):
+        pairs = after([send(value, "head", mask, 4) for mask in (1, 2, 3)], earlier)
+        return (value + pairs[0]) + (pairs[1] + pairs[2])
 
     def ffn_outputs(sums):
-        parts = [jnp.split(item, 3, axis=1) for item in sums]
-        grad_gate, grad_up, grad_down = [jnp.concatenate(items, axis=1) for items in zip(*parts)]
+        sums = jnp.concatenate(sums, axis=1)
+        parts = jnp.split(sums, np.cumsum([cut, cut, cut, rest, rest]), axis=1)
+        grad_gate, grad_up, grad_down = [jnp.concatenate([parts[i], parts[i + 3]], axis=1) for i in range(3)]
         gain = jnp.sum(gate_weight.astype(f32) * grad_gate + up_weight.astype(f32) * grad_up, axis=1)
-        return (grad_gate * gain_two, grad_up * gain_two, grad_down.T), sum_head(gain)
-
-    grad_out_w = seq_sum(grad_out_w)
+        return (grad_gate * gain_two, grad_up * gain_two, grad_down.T), gain
+
     far = quarter_products(gqkv, qkv_w, quarters, 3)
     near = quarter_products(gqkv, qkv_w, quarters, 1)
     terms, grad_qkv = scatter_head(
@@ -911,24 +935,27 @@
             [([(after(unit_one, sent),)], [(gqkv,)])], split_order(order, n_seq), quarters
         ),
     )
-    (grad_x,) = on_quarter(norm_back_kernel, [x_own, grad_hidden, *terms], quarter, [bf16])
+    (grad_x,) = on_quarter(norm_back_kernel, [x_own, grad_hidden, *after(terms, ffn_grads[0])], quarter, [bf16])
     qkv_pairs = scatter_begin(grad_qkv, n_seq)
-    ffn_grads, ffn_gain = ffn_outputs(after(ffn_grads, grad_x))
-    block_all = back(block_all, bf16)
-    grad_x_all = gather_head(grad_x, lambda near: (block_all, ffn_gain, *ffn_grads, *qkv_pairs))
     qkv_terms = scatter_sends(qkv_pairs)
-    grad_x_all[0] = after(grad_x_all[0], *qkv_terms)
+    out_pairs = scatter_begin(after(grad_out_w, grad_x), n_seq)
+    ffn_grads, ffn_gain = ffn_outputs([ffn_grads[0], scatter_end(down_pairs, down_terms), after(ffn_grads[1], grad_x)])
+    block_all = back(after(block_all, grad_x), bf16)
+    grad_x_all = gather_head(grad_x, lambda near: (*qkv_terms, *out_pairs, ffn_gain, *ffn_grads, block_all))
+    out_terms = scatter_sends(out_pairs)
+    grad_qkv = scatter_end(qkv_pairs, qkv_terms)
+    qkv_gain = jnp.sum(qkv_own.astype(f32) * grad_qkv, axis=1)
+    grad_x_all[2] = after(grad_x_all[2], *out_terms)
     grad_x_all = back(grad_x_all, f32)
-    grad_out_w = after(grad_out_w, grad_x_all)
-    grad_qkv = scatter_end(qkv_pairs, qkv_terms)
-    qkv_gain = sum_head(jnp.sum(qkv_own.astype(f32) * grad_qkv, axis=1))
+    gains = sum_head(jnp.stack([qkv_gain, ffn_gain]), grad_x_all)
+    grad_out_w = scatter_end(out_pairs, out_terms)
     grad_qkv = grad_qkv * gain_one
     narrow = heads * FEAT
     return (
         block_all,
         grad_x_all,
-        qkv_gain,
-        ffn_gain,
+        gains[0],
+        gains[1],
         grad_qkv[:, :narrow],
         grad_qkv[:, narrow:lanes],
         grad_qkv[:, lanes:],

time: 844 us -> 802 us (0.950)
  waiting for transfers between devices: 302 us -> 239 us
  starting transfers between devices: 94.5 us -> 119 us
    reduce_scatter x3 -> x2, waiting for transfers between devices: 34.4 us -> 0.01 us  [per_device(): lax.psum_scatter(value, 'seq', scatter_dimension=0, tiled=True).astype(f32)]
    ppermute x69 -> x74, waiting for transfers between devices: 245 us -> 216 us  [send(): return lax.ppermute(value, axis, [(i, i ^ mask) for i in range(count)])]
    ppermute x69 -> x74, starting transfers between devices: 94.3 us -> 119 us  [send(): return lax.ppermute(value, axis, [(i, i ^ mask) for i in range(count)])]
    unnamed x269 -> x237, local copies, waits for them, and re-layouts: 70.8 us -> 58.9 us
  transfers between devices with their start and end apart: 75 -> 79, of which waited for: 29 -> 31; matrix products, arithmetic and copies ran while one was open for 9% -> 10% of each run, Pallas kernels for 32% -> 35%
where the time goes in v5:
time: 802 us; the launch traced here: 788 us
  Pallas kernels  276 us (34%)
  waiting for transfers between devices  239 us (30%)
  starting transfers between devices  119 us (15%)
  local copies, waits for them, and re-layouts  89.2 us (11%)
  other arithmetic  34.7 us (4%)
  between operations  30.7 us (4%)
    ppermute x74, waiting for transfers between devices, send(): return lax.ppermute(value, axis, [(i, i ^ mask) for i in range(count)])  216 us
    ppermute x74, starting transfers between devices, send(): return lax.ppermute(value, axis, [(i, i ^ mask) for i in range(count)])  119 us
    pallas_call x3, Pallas kernels, feed_forward(): pl.pallas_call(functools.partial(ffn_kernel, 256, steps, len(earlier)), o...  93.1 us
    unnamed x237, local copies, waits for them, and re-layouts  58.9 us
    pallas_call x6, Pallas kernels, by_row(): pl.pallas_call(kernel, out_shape=shapes, grid_spec=pltpu.PrefetchScalarGr...  52.9 us
    pallas_call x2, Pallas kernels, ffn_weight_grads(): pl.pallas_call(ffn_weight_kernel, out_shape=[jax.ShapeDtypeStruct((width,...  43.7 us
    all_gather x3, waiting for transfers between devices, per_device(): everywhere = lambda value: lax.all_gather(value, 'seq', axis=0, tiled=True)  21.6 us
    pallas_call x4, Pallas kernels, place_quarters(): pl.pallas_call(place_kernel, out_shape=shape, grid_spec=pltpu.PrefetchSca...  19.7 us
  transfers between devices with their start and end apart: 79, of which 31 were waited for; matrix products, arithmetic and copies ran while one was open for 10% of the time, Pallas kernels for 35%

profile of v5, /device:TPU:0, one launch (start us, length us, event | category | flops | bytes accessed | tf_op | source)
XLA Modules:
  0.0 788.1 jit_solution(1262980546395219602)
XLA Ops:
  25.6 9.5 %collective-permute-done.1.refs_2_ = bf16[256,640]{1,0:T(8,128)(2,1)S(1)} collective-permute-done((bf16[256,640]{1,0:T(8,128)(2,1)S(1)}, bf16[256,640]{1,0:T(8,128)(2,1)S(1)}, u32[]{:S(2)}, u32[]{:S(2)}) %collective-permute-start.1) | collective-permute-done | bytes 327712 | tf_op jit(solution)/shard_map/ppermute | solution.py:305
  35.4 14.8 %collective-permute-done.3.refs_4_ = bf16[256,640]{1,0:T(8,128)(2,1)S(1)} collective-permute-done((bf16[256,640]{1,0:T(8,128)(2,1)S(1)}, bf16[256,640]{1,0:T(8,128)(2,1)S(1)}, u32[]{:S(2)}, u32[]{:S(2)}) %collective-permute-start.3) | collective-permute-done | bytes 327712 | tf_op jit(solution)/shard_map/ppermute | solution.py:305
  109.5 8.0 %shard_map.298 = bf16[6,4,160,128]{3,2,1,0:T(8,128)(2,1)S(1)} custom-call(bf16[6,256,640]{2,1,0:T(8,128)(2,1)S(1)} %bitcast.146, f32[6,256,8]{2,1,0:T(8,128)S(1)} %convert_element_type.256.edge_ref, bf16[128,1024]{1,0:T(8,128)(2,1)S(1)} %copy-done.44, bf16[128,1024]{1,0:T(8,128)(2,1)S(1)} %copy-done.46, f32[8,1024]{1,0:T(8,128)S(1)} %copy-done.54), custom_call_target="tpu_custom_call" | custom-call | flops 603979776 | bytes 1777664 | tf_op jit(solution)/shard_map/pallas_call | solution.py:242
  157.8 13.0 %collective-permute-start.15 = (bf16[3,160,128]{2,1,0:T(8,128)(2,1)S(1)}, bf16[3,160,128]{2,1,0:T(8,128)(2,1)S(1)}, u32[]{:S(2)}, u32[]{:S(2)}) collective-permute-start(bf16[3,160,128]{2,1,0:T(8,128)(2,1)S(1)} %get-tuple-element.109), channel_id=1, source_target_pairs={{0,8},{4,12},{8,0},{12,4},{16,24},{20,28},{24,16},{28,20},{1,9},{5... | collective-permute-start | bytes 368648 | tf_op jit(solution)/shard_map/ppermute | solution.py:305
  191.2 13.1 %collective-permute-done.18 = bf16[3,160,128]{2,1,0:T(8,128)(2,1)S(1)} collective-permute-done((bf16[3,160,128]{2,1,0:T(8,128)(2,1)S(1)}, bf16[3,160,128]{2,1,0:T(8,128)(2,1)S(1)}, u32[]{:S(2)}, u32[]{:S(2)}) %collective-permute-start.18) | collective-permute-done | bytes 122912 | tf_op jit(solution)/shard_map/ppermute | solution.py:305
  222.3 35.1 %collective-permute-done.23.c_ref = bf16[384,2048]{1,0:T(8,128)(2,1)S(1)} collective-permute-done((bf16[384,2048]{1,0:T(8,128)(2,1)S(1)}, bf16[384,2048]{1,0:T(8,128)(2,1)S(1)}, u32[]{:S(2)}, u32[]{:S(2)}) %collective-permute-start.23) | collective-permute-done | bytes 1572896 | tf_op jit(solution)/shard_map/ppermute | solution.py:305
  265.6 24.7 %shard_map.304 = (bf16[1536,768]{1,0:T(8,128)(2,1)}, bf16[1536,768]{1,0:T(8,128)(2,1)}, bf16[1536,768]{1,0:T(8,128)(2,1)}, bf16[4,384,2048]{2,1,0:T(8,128)(2,1)}, bf16[4,384,2048]{2,1,0:T(8,128)(2,1)}) custom-call(s32[8]{0:T(128)} %copy-done.64, bf16[384,2048]{1,0:T(8,128)(2,1)} %get-tuple-element.139.refs_0_, ...), custom_call_target="tpu_custom_call" | custom-call | flops 7247757312 | bytes 11010048 | tf_op jit(solution)/shard_map/pallas_call | solution.py:646
  290.3 8.7 %collective-permute-done.25.refs_0_.refs_2_ = bf16[384,2048]{1,0:T(8,128)(2,1)} collective-permute-done((bf16[384,2048]{1,0:T(8,128)(2,1)}, bf16[384,2048]{1,0:T(8,128)(2,1)}, u32[]{:S(2)}, u32[]{:S(2)}) %collective-permute-start.25) | collective-permute-done | bytes 1572896 | tf_op jit(solution)/shard_map/ppermute | solution.py:305
  302.7 25.4 %shard_map.305 = (bf16[1536,768]{1,0:T(8,128)(2,1)}, bf16[1536,768]{1,0:T(8,128)(2,1)}, bf16[1536,768]{1,0:T(8,128)(2,1)}, bf16[4,384,2048]{2,1,0:T(8,128)(2,1)}, bf16[4,384,2048]{2,1,0:T(8,128)(2,1)}) custom-call(s32[8]{0:T(128)} %copy-done.64, ...), custom_call_target="tpu_custom_call", output_to_operand_aliasing={{0}: (5, {}), {1}: (6, {}), {2}: (7, {}), {3}: (8, {}), {4}... | custom-call | flops 7247757312 | bytes 11010048 | tf_op jit(solution)/shard_map/pallas_call | solution.py:646
  328.1 22.0 %shard_map.306 = (bf16[2048,1536]{1,0:T(8,128)(2,1)}, bf16[2048,768]{1,0:T(8,128)(2,1)}) custom-call(s32[8]{0:T(128)S(1)} %copy-done.65, s32[8]{0:T(128)S(1)} %copy-done.71, bf16[384,2048]{1,0:T(8,128)(2,1)} %get-tuple-element.139.refs_0_, bf16[384,2048]{1,0:T(8,128)(2,1)} %collective-permute-done.24.refs_1_, ...), custom_call_target="tpu_custom_call" | custom-call | flops 7247757312 | bytes 22282240 | tf_op jit(solution)/shard_map/pallas_call | solution.py:728
  354.0 21.6 %all-gather.8.cloned.1.call-done.refs_5_ = bf16[2048,1920]{1,0:T(8,128)(2,1)} async-done(((bf16[256,1920]{1,0:T(8,128)(2,1)}), bf16[2048,1920]{1,0:T(8,128)(2,1)}) %all-gather.8.cloned.1.call-update) | async-done | bytes 7864336 | tf_op jit(solution)/shard_map/all_gather | solution.py:786
  375.6 43.0 %shard_map.307 = (bf16[1536,640]{1,0:T(8,128)(2,1)}, bf16[1536,640]{1,0:T(8,128)(2,1)}, bf16[1536,640]{1,0:T(8,128)(2,1)}, bf16[4,384,2048]{2,1,0:T(8,128)(2,1)}, bf16[4,384,2048]{2,1,0:T(8,128)(2,1)}) custom-call(s32[8]{0:T(128)} %copy-done.64, bf16[384,2048]{1,0:T(8,128)(2,1)} %get-tuple-element.139.refs_0_, ...), custom_call_target="tpu_custom_call" | custom-call | flops 12079595520 | bytes 16515072 | tf_op jit(solution)/shard_map/pallas_call | solution.py:646
  438.7 21.7 %shard_map.308 = bf16[2048,1920]{1,0:T(8,128)(2,1)} custom-call(s32[8]{0:T(128)S(1)} %copy-done.66, s32[8]{0:T(128)S(1)} %copy-done.66, bf16[384,2048]{1,0:T(8,128)(2,1)} %get-tuple-element.139.refs_0_, bf16[384,2048]{1,0:T(8,128)(2,1)} %collective-permute-done.24.refs_1_, bf16[384,2048]{1,0:T(8,128)(2,1)} %collective-permute-done.25.refs_0_.refs_2_, ...), custom_call_target="tpu_custom_call" | custom-call | flops 6039797760 | bytes 20316160 | tf_op jit(solution)/shard_map/pallas_call | solution.py:728
  460.4 9.3 %collective-permute-done.33.c_ref = bf16[384,2048]{1,0:T(8,128)(2,1)} collective-permute-done((bf16[384,2048]{1,0:T(8,128)(2,1)}, bf16[384,2048]{1,0:T(8,128)(2,1)}, u32[]{:S(2)}, u32[]{:S(2)}) %collective-permute-start.33) | collective-permute-done | bytes 1572896 | tf_op jit(solution)/shard_map/ppermute | solution.py:305
  493.2 30.1 %collective-permute-done.38.refs_2_.refs_4_ = bf16[384,2048]{1,0:T(8,128)(2,1)S(1)} collective-permute-done((bf16[384,2048]{1,0:T(8,128)(2,1)S(1)}, bf16[384,2048]{1,0:T(8,128)(2,1)S(1)}, u32[]{:S(2)}, u32[]{:S(2)}) %collective-permute-start.38) | collective-permute-done | bytes 1572896 | tf_op jit(solution)/shard_map/ppermute | solution.py:305
  531.4 9.0 %shard_map.311 = (bf16[6,4,160,128]{3,2,1,0:T(8,128)(2,1)S(1)}, bf16[6,256,512]{2,1,0:T(8,128)(2,1)S(1)}, f32[6,256,4]{2,1,0:T(8,128)S(1)}) custom-call(bf16[6,256,640]{2,1,0:T(8,128)(2,1)S(1)} %bitcast.149, f32[6,256,8]{2,1,0:T(8,128)S(1)} %copy-done.6, bf16[6,256,512]{2,1,0:T(8,128)(2,1)S(1)} %bitcast.159, ...), custom_call_target="tpu_custom_call" | custom-call | flops 603979776 | bytes 4161536 | tf_op jit(solution)/shard_map/pallas_call | solution.py:242
  540.5 16.7 %shard_map.312 = (f32[6,256,128]{2,1,0:T(8,128)S(1)}, f32[6,256,512]{2,1,0:T(8,128)S(1)}) custom-call(s32[8]{0:T(128)S(1)} %copy-done.66, bf16[6,256,640]{2,1,0:T(8,128)(2,1)S(1)} %bitcast.150, f32[6,256,8]{2,1,0:T(8,128)S(1)} %copy-done.6, f32[6,8,256]{2,1,0:T(8,128)S(1)} %copy-done.68, bf16[6,256,512]{2,1,0:T(8,128)(2,1)S(1)} %get-tuple-element.150.gnum_ref, ...), custom_call_target="tpu_custom_call" | custom-call | flops 2214592512 | bytes 4698112 | tf_op jit(solution)/shard_map/pallas_call | solution.py:242
  586.3 9.3 %shard_map.313 = bf16[2048,512]{1,0:T(8,128)(2,1)} custom-call(s32[8]{0:T(128)S(1)} %copy-done.71, s32[4]{0:T(128)S(1)} %iota_xor_fusion.1.rows_ref.order_ref.quarters_ref, bf16[384,2048]{1,0:T(8,128)(2,1)S(1)} %copy-done.23, bf16[384,2048]{1,0:T(8,128)(2,1)S(1)} %collective-permute-done.37.refs_1_, bf16[1536,512]{1,0:T(8,128)(2,1)S(1)} %bitcast.142, ...), custom_call_target="tpu_custom_call" | custom-call | flops 1610612736 | bytes 9175040 | tf_op jit(solution)/shard_map/pallas_call | solution.py:695
  603.5 8.2 %collective-permute-start.50 = (bf16[3,160,128]{2,1,0:T(8,128)(2,1)S(1)}, bf16[3,160,128]{2,1,0:T(8,128)(2,1)S(1)}, u32[]{:S(2)}, u32[]{:S(2)}) collective-permute-start(bf16[3,160,128]{2,1,0:T(8,128)(2,1)S(1)} %get-tuple-element.158), channel_id=1, source_target_pairs={{0,8},{4,12},{8,0},{12,4},{16,24},{20,28},{24,16},{28,20},{1,9},{5... | collective-permute-start | bytes 368648 | tf_op jit(solution)/shard_map/ppermute | solution.py:305
  632.3 8.0 %shard_map.315 = bf16[6,256,640]{2,1,0:T(8,128)(2,1)S(1)} custom-call(s32[8]{0:T(128)S(1)} %copy-done.66, bf16[6,256,640]{2,1,0:T(8,128)(2,1)S(1)} %bitcast.151, f32[6,256,8]{2,1,0:T(8,128)S(1)} %copy-done.6, bf16[8,3,160,128]{3,2,1,0:T(8,128)(2,1)S(1)} %bitcast_dynamic-update-slice_fusion.8.carry_ref, f32[6,256,128]{2,1,0:T(8,128)S(1)} %copy-done.51, ...), custom_call_target="tpu_custom_call" | custom-call | flops 1207959552 | bytes 4726784 | tf_op jit(solution)/shard_map/pallas_call | solution.py:242
  657.3 9.5 %shard_map.318 = bf16[2048,640]{1,0:T(8,128)(2,1)S(1)} custom-call(s32[8]{0:T(128)S(1)} %copy-done.71, s32[4]{0:T(128)S(1)} %iota_xor_fusion.1.rows_ref.order_ref.quarters_ref, bf16[1536,2048]{1,0:T(8,128)(2,1)} %copy-done.2, bf16[1536,640]{1,0:T(8,128)(2,1)S(1)} %bitcast.154), custom_call_target="tpu_custom_call" | custom-call | flops 2013265920 | bytes 9633792 | tf_op jit(solution)/shard_map/pallas_call | solution.py:695
  671.5 14.6 %collective-permute-done.59.c_ref = bf16[384,2048]{1,0:T(8,128)(2,1)S(1)} collective-permute-done((bf16[384,2048]{1,0:T(8,128)(2,1)S(1)}, bf16[384,2048]{1,0:T(8,128)(2,1)S(1)}, u32[]{:S(2)}, u32[]{:S(2)}) %collective-permute-start.59) | collective-permute-done | bytes 1572896 | tf_op jit(solution)/shard_map/ppermute | solution.py:305
  747.8 8.0 %collective-permute-done.66 = bf16[256,512]{1,0:T(8,128)(2,1)S(1)} collective-permute-done((bf16[256,512]{1,0:T(8,128)(2,1)}, bf16[256,512]{1,0:T(8,128)(2,1)S(1)}, u32[]{:S(2)}, u32[]{:S(2)}) %collective-permute-start.66) | collective-permute-done | bytes 262176 | tf_op jit(solution)/shard_map/ppermute | solution.py:305
  755.8 9.6 %collective-permute-done.67 = bf16[256,512]{1,0:T(8,128)(2,1)S(1)} collective-permute-done((bf16[256,512]{1,0:T(8,128)(2,1)}, bf16[256,512]{1,0:T(8,128)(2,1)S(1)}, u32[]{:S(2)}, u32[]{:S(2)}) %collective-permute-start.67) | collective-permute-done | bytes 262176 | tf_op jit(solution)/shard_map/ppermute | solution.py:305
  (473 shorter events, 364.6 us)
Async XLA Ops:
  7.2 127.7 %all-gather.4.cloned.1.call-start = ((), (), s32[]{:S(2)}) async-start(), calls=%async_computation.2 | async-start | bytes 2359296 | tf_op jit(solution)/shard_map/all_gather | solution.py:786
  7.9 257.6 %all-gather.6.cloned.1.call-start = ((), (), s32[]{:S(2)}) async-start(), calls=%async_computation.3 | async-start | bytes 10616832 | tf_op jit(solution)/shard_map/all_gather | solution.py:786
  12.0 363.6 %all-gather.8.cloned.1.call-start = ((), (), s32[]{:S(2)}) async-start(), calls=%async_computation.4 | async-start | bytes 8847360 | tf_op jit(solution)/shard_map/all_gather | solution.py:786
  12.6 81.0 %collective-permute-start = (bf16[256,640]{1,0:T(8,128)(2,1)S(1)}, bf16[256,640]{1,0:T(8,128)(2,1)S(1)}, u32[]{:S(2)}, u32[]{:S(2)}) collective-permute-start(bf16[256,640]{1,0:T(8,128)(2,1)S(1)} %fusion.11.refs_0_), channel_id=1, source_target_pairs={{0,4},{4,0},{8,12},{12,8},{16,20},{20,16},{24,28},{28,24},{1,5},{5... | collective-permute-start | bytes 983048 | tf_op jit(solution)/shard_map/ppermute | solution.py:305
  22.3 664.9 %reduce-scatter.3.cloned.1.call-start = ((), (), s32[]{:S(2)}) async-start(), calls=%async_computation.5 | async-start | bytes 7077888 | tf_op jit(solution)/shard_map/reduce_scatter | solution.py:852
  35.0 59.3 %collective-permute-start.2 = (bf16[256,640]{1,0:T(8,128)(2,1)S(1)}, bf16[256,640]{1,0:T(8,128)(2,1)}, u32[]{:S(2)}, u32[]{:S(2)}) collective-permute-start(bf16[256,640]{1,0:T(8,128)(2,1)S(1)} %collective-permute-done.1.refs_2_), channel_id=1, source_target_pairs={{0,4},{4,0},{8,12},{12,8},{16,20},{20,16},{24,28},{28,24},{1,5},{5... | collective-permute-start | bytes 983048 | tf_op jit(solution)/shard_map/ppermute | solution.py:305
  50.2 44.1 %collective-permute-start.4 = (bf16[256,640]{1,0:T(8,128)(2,1)S(1)}, bf16[256,640]{1,0:T(8,128)(2,1)}, u32[]{:S(2)}, u32[]{:S(2)}) collective-permute-start(bf16[256,640]{1,0:T(8,128)(2,1)S(1)} %collective-permute-done.3.refs_4_), channel_id=1, source_target_pairs={{0,4},{4,0},{8,12},{12,8},{16,20},{20,16},{24,28},{28,24},{1,5},{5... | collective-permute-start | bytes 983048 | tf_op jit(solution)/shard_map/ppermute | solution.py:305
  50.2 44.1 %collective-permute-start.6 = (bf16[256,640]{1,0:T(8,128)(2,1)}, bf16[256,640]{1,0:T(8,128)(2,1)}, u32[]{:S(2)}, u32[]{:S(2)}) collective-permute-start(bf16[256,640]{1,0:T(8,128)(2,1)} %collective-permute-done.5.refs_6_), channel_id=1, source_target_pairs={{0,4},{4,0},{8,12},{12,8},{16,20},{20,16},{24,28},{28,24},{1,5},{5... | collective-permute-start | bytes 983048 | tf_op jit(solution)/shard_map/ppermute | solution.py:305
  220.5 36.8 %collective-permute-start.23 = (bf16[384,2048]{1,0:T(8,128)(2,1)S(1)}, bf16[384,2048]{1,0:T(8,128)(2,1)S(1)}, u32[]{:S(2)}, u32[]{:S(2)}) collective-permute-start(bf16[384,2048]{1,0:T(8,128)(2,1)S(1)} %add_convert_fusion.1), channel_id=1, source_target_pairs={{0,2},{1,3},{2,0},{3,1},{4,6},{5,7},{6,4},{7,5},{8,10},{9,11},{10,... | collective-permute-start | bytes 4718600 | tf_op jit(solution)/shard_map/ppermute | solution.py:305
  261.8 37.1 %collective-permute-start.25 = (bf16[384,2048]{1,0:T(8,128)(2,1)}, bf16[384,2048]{1,0:T(8,128)(2,1)}, u32[]{:S(2)}, u32[]{:S(2)}) collective-permute-start(bf16[384,2048]{1,0:T(8,128)(2,1)} %get-tuple-element.139.refs_0_), channel_id=1, source_target_pairs={{0,2},{1,3},{2,0},{3,1},{4,6},{5,7},{6,4},{7,5},{8,10},{9,11},{10,... | collective-permute-start | bytes 4718600 | tf_op jit(solution)/shard_map/ppermute | solution.py:305
  350.1 375.1 %reduce-scatter.5.cloned.1.call-start = ((), (), s32[]{:S(2)}) async-start(), calls=%async_computation.6 | async-start | bytes 8847360 | tf_op jit(solution)/shard_map/reduce_scatter | solution.py:852
  352.8 70.8 %collective-permute-start.31 = (bf16[1024,768]{1,0:T(8,128)(2,1)}, bf16[1024,768]{1,0:T(8,128)(2,1)}, u32[]{:S(2)}, u32[]{:S(2)}) collective-permute-start(bf16[1024,768]{1,0:T(8,128)(2,1)} %slice.201), channel_id=1, source_target_pairs={{0,4},{4,0},{8,12},{12,8},{16,20},{20,16},{24,28},{28,24},{1,5},{5... | collective-permute-start | bytes 4718600 | tf_op jit(solution)/shard_map/ppermute | solution.py:305
  433.0 36.7 %collective-permute-start.33 = (bf16[384,2048]{1,0:T(8,128)(2,1)}, bf16[384,2048]{1,0:T(8,128)(2,1)}, u32[]{:S(2)}, u32[]{:S(2)}) collective-permute-start(bf16[384,2048]{1,0:T(8,128)(2,1)} %fusion), channel_id=1, source_target_pairs={{0,2},{1,3},{2,0},{3,1},{4,6},{5,7},{6,4},{7,5},{8,10},{9,11},{10,... | collective-permute-start | bytes 4718600 | tf_op jit(solution)/shard_map/ppermute | solution.py:305
  434.3 35.4 %collective-permute-start.30 = (bf16[384,2048]{1,0:T(8,128)(2,1)}, bf16[384,2048]{1,0:T(8,128)(2,1)}, u32[]{:S(2)}, u32[]{:S(2)}) collective-permute-start(bf16[384,2048]{1,0:T(8,128)(2,1)} %get-tuple-element.249), channel_id=1, source_target_pairs={{0,1},{1,0},{2,3},{3,2},{4,5},{5,4},{6,7},{7,6},{8,9},{9,8},{10,11... | collective-permute-start | bytes 4718600 | tf_op jit(solution)/shard_map/ppermute | solution.py:305
  486.4 36.8 %collective-permute-start.38 = (bf16[384,2048]{1,0:T(8,128)(2,1)S(1)}, bf16[384,2048]{1,0:T(8,128)(2,1)S(1)}, u32[]{:S(2)}, u32[]{:S(2)}) collective-permute-start(bf16[384,2048]{1,0:T(8,128)(2,1)S(1)} %copy-done.23), channel_id=1, source_target_pairs={{0,2},{1,3},{2,0},{3,1},{4,6},{5,7},{6,4},{7,5},{8,10},{9,11},{10,... | collective-permute-start | bytes 4718600 | tf_op jit(solution)/shard_map/ppermute | solution.py:305
  523.3 37.1 %collective-permute-start.29 = (bf16[384,2048]{1,0:T(8,128)(2,1)}, bf16[384,2048]{1,0:T(8,128)(2,1)}, u32[]{:S(2)}, u32[]{:S(2)}) collective-permute-start(bf16[384,2048]{1,0:T(8,128)(2,1)} %fusion.1), channel_id=1, source_target_pairs={{0,2},{1,3},{2,0},{3,1},{4,6},{5,7},{6,4},{7,5},{8,10},{9,11},{10,... | collective-permute-start | bytes 4718600 | tf_op jit(solution)/shard_map/ppermute | solution.py:305
  524.7 45.5 %collective-permute-start.27 = (bf16[384,2048]{1,0:T(8,128)(2,1)}, bf16[384,2048]{1,0:T(8,128)(2,1)}, u32[]{:S(2)}, u32[]{:S(2)}) collective-permute-start(bf16[384,2048]{1,0:T(8,128)(2,1)} %get-tuple-element.246), channel_id=1, source_target_pairs={{0,1},{1,0},{2,3},{3,2},{4,5},{5,4},{6,7},{7,6},{8,9},{9,8},{10,11... | collective-permute-start | bytes 4718600 | tf_op jit(solution)/shard_map/ppermute | solution.py:305
  595.6 44.7 %collective-permute-start.41 = (bf16[384,2048]{1,0:T(8,128)(2,1)}, bf16[384,2048]{1,0:T(8,128)(2,1)}, u32[]{:S(2)}, u32[]{:S(2)}) collective-permute-start(bf16[384,2048]{1,0:T(8,128)(2,1)} %fusion.4.refs_0_), channel_id=1, source_target_pairs={{0,2},{1,3},{2,0},{3,1},{4,6},{5,7},{6,4},{7,5},{8,10},{9,11},{10,... | collective-permute-start | bytes 4718600 | tf_op jit(solution)/shard_map/ppermute | solution.py:305
  649.6 36.5 %collective-permute-start.59 = (bf16[384,2048]{1,0:T(8,128)(2,1)S(1)}, bf16[384,2048]{1,0:T(8,128)(2,1)S(1)}, u32[]{:S(2)}, u32[]{:S(2)}) collective-permute-start(bf16[384,2048]{1,0:T(8,128)(2,1)S(1)} %add_convert_fusion), channel_id=1, source_target_pairs={{0,2},{1,3},{2,0},{3,1},{4,6},{5,7},{6,4},{7,5},{8,10},{9,11},{10,... | collective-permute-start | bytes 4718600 | tf_op jit(solution)/shard_map/ppermute | solution.py:305
  671.0 38.7 %collective-permute-start.40 = (bf16[384,2048]{1,0:T(8,128)(2,1)}, bf16[384,2048]{1,0:T(8,128)(2,1)}, u32[]{:S(2)}, u32[]{:S(2)}) collective-permute-start(bf16[384,2048]{1,0:T(8,128)(2,1)} %fusion.4.refs_0_), channel_id=1, source_target_pairs={{0,1},{1,0},{2,3},{3,2},{4,5},{5,4},{6,7},{7,6},{8,9},{9,8},{10,11... | collective-permute-start | bytes 4718600 | tf_op jit(solution)/shard_map/ppermute | solution.py:305
  671.3 38.6 %collective-permute-start.56 = (bf16[384,2048]{1,0:T(8,128)(2,1)}, bf16[384,2048]{1,0:T(8,128)(2,1)}, u32[]{:S(2)}, u32[]{:S(2)}) collective-permute-start(bf16[384,2048]{1,0:T(8,128)(2,1)} %collective-permute-done.41.refs_0_), channel_id=1, source_target_pairs={{0,1},{1,0},{2,3},{3,2},{4,5},{5,4},{6,7},{7,6},{8,9},{9,8},{10,11... | collective-permute-start | bytes 4718600 | tf_op jit(solution)/shard_map/ppermute | solution.py:305
  697.1 38.6 %collective-permute-start.60 = (bf16[384,2048]{1,0:T(8,128)(2,1)}, bf16[384,2048]{1,0:T(8,128)(2,1)}, u32[]{:S(2)}, u32[]{:S(2)}) collective-permute-start(bf16[384,2048]{1,0:T(8,128)(2,1)} %shard_map.319.refs_0_), channel_id=1, source_target_pairs={{0,2},{1,3},{2,0},{3,1},{4,6},{5,7},{6,4},{7,5},{8,10},{9,11},{10,... | collective-permute-start | bytes 4718600 | tf_op jit(solution)/shard_map/ppermute | solution.py:305
  723.3 45.0 %collective-permute-start.70 = (bf16[384,2048]{1,0:T(8,128)(2,1)}, bf16[384,2048]{1,0:T(8,128)(2,1)}, u32[]{:S(2)}, u32[]{:S(2)}) collective-permute-start(bf16[384,2048]{1,0:T(8,128)(2,1)} %shard_map.319.refs_0_), channel_id=1, source_target_pairs={{0,1},{1,0},{2,3},{3,2},{4,5},{5,4},{6,7},{7,6},{8,9},{9,8},{10,11... | collective-permute-start | bytes 4718600 | tf_op jit(solution)/shard_map/ppermute | solution.py:305
  735.7 39.5 %collective-permute-start.69 = (bf16[384,2048]{1,0:T(8,128)(2,1)}, bf16[384,2048]{1,0:T(8,128)(2,1)}, u32[]{:S(2)}, u32[]{:S(2)}) collective-permute-start(bf16[384,2048]{1,0:T(8,128)(2,1)} %collective-permute-done.60.refs_0_), channel_id=1, source_target_pairs={{0,1},{1,0},{2,3},{3,2},{4,5},{5,4},{6,7},{7,6},{8,9},{9,8},{10,11... | collective-permute-start | bytes 4718600 | tf_op jit(solution)/shard_map/ppermute | solution.py:305
  (159 other events, 2626.6 us)
Sparse Core Ops, SparseCore 0:
  10.1 73.7 all-gather.3
  86.7 169.0 all-gather.5
  258.5 117.0 all-gather.7
  379.0 132.3 reduce-scatter.2
  515.5 165.3 reduce-scatter.4

commit v6 on v5

--- a/solution.py
+++ b/solution.py
@@ -71,11 +71,6 @@
     return pl.BlockSpec(array.shape, lambda *_: zeros)
 
 
-def row_spec(array):
-    zeros = (0,) * (array.ndim - 1)
-    return pl.BlockSpec((1,) + array.shape[1:], lambda row, *_: (row,) + zeros)
-
-
 def pack_state(state, norm_row, flag):
     place = lax.broadcasted_iota(jnp.int32, (TALL, VHEAD), 0)
     block = state[:TALL]
@@ -93,7 +88,7 @@
     return full, jnp.concatenate([low, high], axis=1)
 
 
-def state_kernel(heads, qkv_ref, edge_ref, ka_ref, kb_ref, rows_ref, out_ref):
+def state_kernel(heads, place_ref, qkv_ref, edge_ref, ka_ref, kb_ref, rows_ref, out_ref):
     keys = qkv_ref[0, :, : 2 * heads * FEAT]
     edges = edge_ref[0]
     last, flag = edges[:, 2:3], edges[0:1, 3:4]
@@ -112,7 +107,7 @@
     return later & (edges[:, 0:1] == docs)
 
 
-def inside_kernel(heads, qkv_ref, edge_ref, doc_ref, key_ref, num_ref, den_ref):
+def inside_kernel(heads, place_ref, qkv_ref, edge_ref, doc_ref, key_ref, num_ref, den_ref):
     lanes = 2 * heads * FEAT
     both = qkv_ref[0, :, :lanes]
     mask = local_mask(edge_ref[0], doc_ref[0, 0:1])
@@ -131,8 +126,8 @@
 
 def block_at(place_ref, states_ref, row, heads, head):
     per = states_ref.shape[1]
-    index = row * heads + head
-    return states_ref[place_ref[index // per], index % per]
+    index = (place_ref[0] + row) * heads + head
+    return states_ref[place_ref[1 + index // per], index % per]
 
 
 def query_features(both, qa, qb, rows, first):
@@ -157,7 +152,9 @@
     rden_ref[0] = jnp.concatenate(rdens, axis=1)
 
 
-def carry_kernel(heads, qkv_ref, edge_ref, ga_ref, att_ref, rden_ref, qa_ref, qb_ref, rows_ref, carry_ref, gnum_ref, gden_ref):
+def carry_kernel(
+    heads, place_ref, qkv_ref, edge_ref, ga_ref, att_ref, rden_ref, qa_ref, qb_ref, rows_ref, carry_ref, gnum_ref, gden_ref
+):
     both = qkv_ref[0, :, : 2 * heads * FEAT]
     edges = edge_ref[0]
     first, flag = edges[:, 1:2], edges[0:1, 3:4]
@@ -234,23 +231,31 @@
     out_ref[0, :, :lanes] = total.astype(bf16)
 
 
-def by_row(kernel, rows, inputs, outputs, place=None, flops=0):
+def by_row(kernel, rows, inputs, outputs, place=None, flops=0, base=0, count=None):
+    count = rows if count is None else count
     arrays = [array for array, _ in inputs]
-    specs = [row_spec(array) if per_row else whole_spec(array) for array, per_row in inputs]
+
+    def spec_of(array):
+        zeros = (0,) * (array.ndim - 1)
+        return pl.BlockSpec((1,) + array.shape[1:], lambda row, scalars: (row + scalars[0],) + zeros)
+
     shapes = [jax.ShapeDtypeStruct((rows,) + shape, kind) for shape, kind in outputs]
     nbytes = sum(item.size * item.dtype.itemsize for item in arrays + shapes)
+    scalars = jnp.asarray(base, jnp.int32).reshape(1)
+    if place is not None:
+        scalars = jnp.concatenate([scalars, place])
     return pl.pallas_call(
         kernel,
         out_shape=shapes,
         grid_spec=pltpu.PrefetchScalarGridSpec(
-            num_scalar_prefetch=0 if place is None else 1,
-            grid=(rows,),
-            in_specs=specs,
-            out_specs=[row_spec(shape) for shape in shapes],
+            num_scalar_prefetch=1,
+            grid=(count,),
+            in_specs=[spec_of(array) if per_row else whole_spec(array) for array, per_row in inputs],
+            out_specs=[spec_of(shape) for shape in shapes],
         ),
         compiler_params=params(40),
-        cost_estimate=cost(flops, nbytes),
-    )(*([] if place is None else [place]), *arrays)
+        cost_estimate=cost(flops * count // rows, nbytes * count // rows),
+    )(scalars, *arrays)
 
 
 def scan_kernel(backward, me_ref, *refs):
@@ -305,12 +310,13 @@
     return lax.ppermute(value, axis, [(i, i ^ mask) for i in range(count)])
 
 
-def gather_rows(shard, count):
+def gather_rows(shard, count, earlier):
     if count != 8:
         return [lax.all_gather(shard, "seq", axis=0, tiled=True)]
     pieces = [shard, send(shard, "seq", 1, 8)]
     for mask in (2, 4, 6):
         piece = send(shard, "seq", mask, 8)
+        piece = after(piece, *earlier) if mask == 2 else piece
         pieces += [piece, send(piece, "seq", 1, 8)]
     return pieces
 
@@ -319,9 +325,11 @@
     return lax.optimization_barrier((value, earlier))[0]
 
 
-def swap_blocks(array, order):
+def swap_blocks(array, me, count):
+    if count != 8:
+        return array
     split = array.reshape((BLOCKS, array.shape[0] // BLOCKS) + array.shape[1:])
-    return join_rows([lax.dynamic_index_in_dim(split, order[i], 0, keepdims=False) for i in range(BLOCKS)])
+    return join_rows([lax.dynamic_index_in_dim(split, me ^ i, 0, keepdims=False) for i in range(BLOCKS)])
 
 
 def split_order(order, n_seq):
@@ -331,8 +339,11 @@
 def scatter_begin(whole, n_seq):
     if n_seq != 8:
         return (lax.psum_scatter(whole, "seq", scatter_dimension=0, tiled=True).astype(f32),)
+    return scatter_pairs(whole, send(whole[whole.shape[0] // 2 :], "seq", 1, 8))
+
+
+def scatter_pairs(whole, other):
     rows = whole.shape[0] // 8
-    other = send(whole[4 * rows :], "seq", 1, 8)
     pairs = [
         whole[i * rows : (i + 1) * rows].astype(f32) + other[i * rows : (i + 1) * rows].astype(f32) for i in range(4)
     ]
@@ -411,27 +422,24 @@
         pl.when(pl.program_id(0) == place)(functools.partial(move_columns, cols_ref, piece, out_ref))
 
 
-def place_quarters(pieces, row_blocks, col_blocks, out_type):
+def place_quarters(pieces, row_blocks, col_blocks, out_type, start, whole=None):
     quarter, width = pieces[0].shape
     shape = jax.ShapeDtypeStruct((4 * quarter, width), out_type)
-    whole = None
-    for start in (0, 2):
-        held = [] if whole is None else [whole]
-        whole = pl.pallas_call(
-            place_kernel,
-            out_shape=shape,
-            grid_spec=pltpu.PrefetchScalarGridSpec(
-                num_scalar_prefetch=2,
-                grid=(2,),
-                in_specs=[pl.BlockSpec((quarter, width), lambda i, rows, cols: (0, 0))] * 2
-                + [pl.BlockSpec(memory_space=pl.ANY)] * len(held),
-                out_specs=pl.BlockSpec((quarter, width), lambda i, rows, cols, start=start: (rows[start + i], 0)),
-            ),
-            input_output_aliases={4: 0} if held else {},
-            compiler_params=params(40),
-            cost_estimate=cost(0, shape.size * 4),
-        )(row_blocks, col_blocks, *pieces[start : start + 2], *held)
-    return whole
+    held = [] if whole is None else [whole]
+    return pl.pallas_call(
+        place_kernel,
+        out_shape=shape,
+        grid_spec=pltpu.PrefetchScalarGridSpec(
+            num_scalar_prefetch=2,
+            grid=(2,),
+            in_specs=[pl.BlockSpec((quarter, width), lambda i, rows, cols: (0, 0))] * 2
+            + [pl.BlockSpec(memory_space=pl.ANY)] * len(held),
+            out_specs=pl.BlockSpec((quarter, width), lambda i, rows, cols: (rows[start + i], 0)),
+        ),
+        input_output_aliases={4: 0} if held else {},
+        compiler_params=params(40),
+        cost_estimate=cost(0, shape.size * 4),
+    )(row_blocks, col_blocks, *pieces, *held)
 
 
 def unit_kernel(cols_ref, in_ref, out_ref):
@@ -594,7 +602,7 @@
     copies = []
     for i in range(BLOCKS):
         start = pl.multiple_of(order_ref[i] * rows, rows)
-        source = weights_hbm.at[pl.ds(start, rows)]
+        source = weights_hbm.at[pl.ds(start, rows), pl.ds(weights_hbm.shape[1] - 3 * hidden, 3 * hidden)]
         copies.append(pltpu.make_async_copy(source, held_ref.at[pl.ds(i * rows, rows)], sems.at[i]))
 
     @pl.when(pl.program_id(0) == 0)
@@ -779,17 +787,15 @@
     qkv_own = jnp.concatenate([query_weight, key_weight, value_weight], axis=1)
     gate_own, up_own, down_own = scaled(gate_weight, gain_two), scaled(up_weight, gain_two), down_weight.T
     hidden_units = gate_weight.shape[1]
-    cut = (hidden_units + VHEAD) // (2 * VHEAD) * VHEAD
+    cut = hidden_units // (2 * VHEAD) * VHEAD
     groups = (slice(0, cut), slice(cut, hidden_units))
     values = heads * VHEAD
-    qkv_pieces = gather_rows(scaled(qkv_own, gain_one), n_seq)
     everywhere = lambda value: lax.all_gather(value, "seq", axis=0, tiled=True)
-    out_w = everywhere(out_weight.T)
     ffn_w = []
     for group in groups:
         parts = [gate_own[:, group], up_own[:, group], down_own[:, group]]
-        ffn_w.append(everywhere(jnp.concatenate(parts, axis=1)))
-    out_w = swap_blocks(out_w, order)
+        ffn_w.append(everywhere(jnp.concatenate(parts if ffn_w else [out_weight.T] + parts, axis=1)))
+    out_w = swap_blocks(ffn_w[0][:, :values], me, n_seq)
 
     flat = tokens.reshape(count, width)
     x_own = move_blocks(flat, quarters[:1], order, quarter)
@@ -802,6 +808,7 @@
     edges = jnp.stack([docs, docs == 0, docs == final, flag] + [jnp.zeros_like(docs)] * 4, axis=2).astype(f32)
     doc_rows = jnp.broadcast_to(docs[:, None, :], (rows, 8, length)).astype(f32)
     tables, feat_rows, to_key, to_query = feature_tables(heads)
+    qkv_pieces = gather_rows(scaled(qkv_own, gain_one), n_seq, (unit_one, edges, doc_rows))
 
     lanes = 2 * heads * FEAT
     unit_flops = 2 * rows * heads * length * WIDE * VHEAD
@@ -821,7 +828,7 @@
         [((length, values), f32), ((length, heads), f32)],
         flops=3 * unit_flops,
     )
-    found = scan_begin(states, False, me, n_seq, (numerator, out_w))
+    found = scan_begin(states, False, me, n_seq, (numerator,))
     state_in, place = scan_end(found, False, me, n_seq)
     query_tables = [(tables["qa"], False), (tables["qb"], False), (feat_rows, False)]
     key_tables = [(tables["ka"], False), (tables["kb"], False), (feat_rows, False)]
@@ -856,14 +863,19 @@
     second = feed_forward(left, dy, 0, ffn_w[1], hidden_units - cut, order, earlier=first[3:])
     gunit, ffn_out = [[item[i] for i in range(4)] for item in second[3:]]
 
-    down_pairs = scatter_begin(first_grads[1], n_seq)
-    gunit[3] = after(gunit[3], *down_pairs)
+    down_pairs = ()
+    if n_seq == 8:
+        down_other = send(first_grads[1][width // 2 :], "seq", 1, 8)
+        gunit[3] = after(gunit[3], down_other)
+    else:
+        down_pairs = scatter_begin(first_grads[1], n_seq)
 
     def second_grads(sent):
-        left = [after(units[0], sent), *units[1:]]
-        return ffn_weight_grads(left, dy, second[:3], order)
-
-    terms, found = scatter_head(gunit, beside=second_grads)
+        pairs = down_pairs or scatter_pairs(after(first_grads[1], sent), down_other)
+        left = [after(units[0], sent, *pairs), *units[1:]]
+        return ffn_weight_grads(left, dy, second[:3], order), pairs
+
+    terms, (found, down_pairs) = scatter_head(gunit, beside=second_grads)
     down_terms = scatter_sends(down_pairs)
     terms = after(terms, *down_terms)
     grad_hidden, grad_branch = on_quarter(norm_back_kernel, [hidden, dy, *terms], quarter, [f32, bf16])
@@ -903,16 +915,29 @@
     carry_in, place_back = scan_end(found, True, me, n_seq)
     carry_in = after(carry_in, block_own)
     block_all = gather_head(block_own, lambda near: (carry_in,))
-    (gqkv,) = by_row(
-        functools.partial(finish_back_kernel, heads),
-        rows,
-        [(qkv, True), (edges, True), (carry_in, False), (gboth, True), (gval, True)] + key_tables,
-        [((length, lanes + values), bf16)],
-        place=place_back,
-        flops=6 * unit_flops,
-    )
-    gqkv = after(gqkv.reshape(count, lanes + values), block_all[2])
-    back = lambda value, kind: place_quarters(value, quarters, order, kind).reshape(rows, length, width)
+    far_rows, near_rows = [(head_me // 2 ^ i) * (rows // 2) for i in (1, 0)]
+
+    def finish_back(gval, base):
+        (grads,) = by_row(
+            functools.partial(finish_back_kernel, heads),
+            rows,
+            [(qkv, True), (edges, True), (carry_in, False), (gboth, True), (gval, True)] + key_tables,
+            [((length, lanes + values), bf16)],
+            place=place_back,
+            flops=6 * unit_flops,
+            base=base,
+            count=rows // 2,
+        )
+        return grads.reshape(count, lanes + values)
+
+    gqkv_far = after(finish_back(gval, far_rows), block_all[2])
+    far = quarter_products(gqkv_far, qkv_w, quarters, 3)
+    gqkv_near = finish_back(after(gval, far), near_rows)
+    near = quarter_products(gqkv_near, qkv_w, quarters, 1)
+
+    def back(value, kind):
+        whole = place_quarters(value[:2], quarters, order, kind, 0)
+        return place_quarters(value[2:], quarters, order, kind, 2, whole).reshape(rows, length, width)
 
     rest = hidden_units - cut
 
@@ -927,12 +952,15 @@
         gain = jnp.sum(gate_weight.astype(f32) * grad_gate + up_weight.astype(f32) * grad_up, axis=1)
         return (grad_gate * gain_two, grad_up * gain_two, grad_down.T), gain
 
-    far = quarter_products(gqkv, qkv_w, quarters, 3)
-    near = quarter_products(gqkv, qkv_w, quarters, 1)
     terms, grad_qkv = scatter_head(
         [near[1], near[0], far[1], far[0]],
         beside=lambda sent: weight_grads(
-            [([(after(unit_one, sent),)], [(gqkv,)])], split_order(order, n_seq), quarters
+            [
+                ([(after(unit_one, sent), "q", i), (unit_one, "q", i + 1)], [(grads, "q", i), (grads, "q", i + 1)])
+                for grads, i in ((gqkv_near, 0), (gqkv_far, 2))
+            ],
+            split_order(order, n_seq),
+            quarters,
         ),
     )
     (grad_x,) = on_quarter(norm_back_kernel, [x_own, grad_hidden, *after(terms, ffn_grads[0])], quarter, [bf16])
@@ -945,8 +973,10 @@
     out_terms = scatter_sends(out_pairs)
     grad_qkv = scatter_end(qkv_pairs, qkv_terms)
     qkv_gain = jnp.sum(qkv_own.astype(f32) * grad_qkv, axis=1)
+    near_placed = place_quarters(grad_x_all[:2], quarters, order, f32, 0)
+    out_terms = after(out_terms, near_placed)
     grad_x_all[2] = after(grad_x_all[2], *out_terms)
-    grad_x_all = back(grad_x_all, f32)
+    grad_x_all = place_quarters(grad_x_all[2:], quarters, order, f32, 2, near_placed).reshape(rows, length, width)
     gains = sum_head(jnp.stack([qkv_gain, ffn_gain]), grad_x_all)
     grad_out_w = scatter_end(out_pairs, out_terms)
     grad_qkv = grad_qkv * gain_one

time: 802 us -> 790 us (0.985)
  waiting for transfers between devices: 239 us -> 211 us
  starting transfers between devices: 119 us -> 146 us
  between operations: 30.7 us -> 15.7 us
    ppermute x74, starting transfers between devices: 119 us -> 145 us  [send(): return lax.ppermute(value, axis, [(i, i ^ mask) for i in range(count)])]
    ppermute x74, waiting for transfers between devices: 216 us -> 194 us  [send(): return lax.ppermute(value, axis, [(i, i ^ mask) for i in range(count)])]
    unnamed x237 -> x246, local copies, waits for them, and re-layouts: 58.9 us -> 64.2 us
    all_gather x3 -> x2, waiting for transfers between devices: 21.6 us -> 16.6 us  [per_device(): everywhere = lambda value: lax.all_gather(value, 'seq', axis=0, tiled=True)]
    pallas_call x6 -> x7, Pallas kernels: 52.9 us -> 53.4 us  [by_row(): pl.pallas_call(kernel, out_shape=shapes, grid_spec=pltpu.PrefetchScalarGr...]
  transfers between devices with their start and end apart: 79 -> 78, of which waited for: 31 -> 31; matrix products, arithmetic and copies ran while one was open for 10% -> 8% of each run, Pallas kernels for 35% -> 35%
where the time goes in v6:
time: 790 us; the launch traced here: 776 us
  Pallas kernels  274 us (35%)
  waiting for transfers between devices  211 us (27%)
  starting transfers between devices  146 us (18%)
  local copies, waits for them, and re-layouts  91.1 us (12%)
  other arithmetic  37.6 us (5%)
  between operations  15.7 us (2%)
    ppermute x74, waiting for transfers between devices, send(): return lax.ppermute(value, axis, [(i, i ^ mask) for i in range(count)])  194 us
    ppermute x74, starting transfers between devices, send(): return lax.ppermute(value, axis, [(i, i ^ mask) for i in range(count)])  145 us
    pallas_call x3, Pallas kernels, feed_forward(): pl.pallas_call(functools.partial(ffn_kernel, 256, steps, len(earlier)), o...  92.3 us
    unnamed x246, local copies, waits for them, and re-layouts  64.2 us
    pallas_call x7, Pallas kernels, by_row(): pl.pallas_call(kernel, out_shape=shapes, grid_spec=pltpu.PrefetchScalarGr...  53.4 us
    pallas_call x2, Pallas kernels, ffn_weight_grads(): pl.pallas_call(ffn_weight_kernel, out_shape=[jax.ShapeDtypeStruct((width,...  43.6 us
    pallas_call x2, Pallas kernels, weight_grads(): pl.pallas_call(functools.partial(weight_kernel, tuple(((len(lefts), len(r...  19.8 us
    pallas_call x4, Pallas kernels, quarter_products(): pl.pallas_call(quarter_kernel, out_shape=[jax.ShapeDtypeStruct((rows, wid...  19.2 us
  transfers between devices with their start and end apart: 78, of which 31 were waited for; matrix products, arithmetic and copies ran while one was open for 8% of the time, Pallas kernels for 35%

profile of v6, /device:TPU:0, one launch (start us, length us, event | category | flops | bytes accessed | tf_op | source)
XLA Modules:
  0.0 775.6 jit_solution(13200577982335325650)
XLA Ops:
  85.7 7.4 shard_map.296
  94.7 8.0 %shard_map.298 = bf16[6,4,160,128]{3,2,1,0:T(8,128)(2,1)S(1)} custom-call(s32[1]{0:T(128)} %constant.104.clone.1.place_ref, bf16[6,256,640]{2,1,0:T(8,128)(2,1)S(1)} %bitcast.141, f32[6,256,8]{2,1,0:T(8,128)S(1)} %convert_element_type.256.edge_ref, bf16[128,1024]{1,0:T(8,128)(2,1)S(1)} %copy-done.31, bf16[128,1024]{1,0:T(8,128)(2,1)S(1)} %copy-done.33, ...), custom_call_target="tpu_custom_call" | custom-call | flops 603979776 | bytes 1777664 | tf_op jit(solution)/shard_map/pallas_call | solution.py:247
  103.9 8.4 %collective-permute-start.8 = (bf16[3,160,128]{2,1,0:T(8,128)(2,1)}, bf16[3,160,128]{2,1,0:T(8,128)(2,1)S(1)}, u32[]{:S(2)}, u32[]{:S(2)}) collective-permute-start(bf16[3,160,128]{2,1,0:T(8,128)(2,1)} %get-tuple-element.293), channel_id=1, source_target_pairs={{0,8},{4,12},{8,0},{12,4},{16,24},{20,28},{24,16},{28,20},{1,9},{5... | collective-permute-start | bytes 368648 | tf_op jit(solution)/shard_map/ppermute | solution.py:310
  124.1 8.0 %collective-permute-start.13 = (bf16[3,160,128]{2,1,0:T(8,128)(2,1)}, bf16[3,160,128]{2,1,0:T(8,128)(2,1)S(1)}, u32[]{:S(2)}, u32[]{:S(2)}) collective-permute-start(bf16[3,160,128]{2,1,0:T(8,128)(2,1)} %get-tuple-element.288), channel_id=1, source_target_pairs={{0,28},{4,24},{8,20},{12,16},{16,12},{20,8},{24,4},{28,0},{1,29},{... | collective-permute-start | bytes 368648 | tf_op jit(solution)/shard_map/ppermute | solution.py:310
  138.4 9.0 %collective-permute-done.11.refs_5_ = bf16[3,160,128]{2,1,0:T(8,128)(2,1)S(1)} collective-permute-done((bf16[3,160,128]{2,1,0:T(8,128)(2,1)}, bf16[3,160,128]{2,1,0:T(8,128)(2,1)S(1)}, u32[]{:S(2)}, u32[]{:S(2)}) %collective-permute-start.11) | collective-permute-done | bytes 122912 | tf_op jit(solution)/shard_map/ppermute | solution.py:310
  149.8 17.9 %collective-permute-start.15 = (bf16[3,160,128]{2,1,0:T(8,128)(2,1)S(1)}, bf16[3,160,128]{2,1,0:T(8,128)(2,1)S(1)}, u32[]{:S(2)}, u32[]{:S(2)}) collective-permute-start(bf16[3,160,128]{2,1,0:T(8,128)(2,1)S(1)} %get-tuple-element.116), channel_id=1, source_target_pairs={{0,8},{4,12},{8,0},{12,4},{16,24},{20,28},{24,16},{28,20},{1,9},{5... | collective-permute-start | bytes 368648 | tf_op jit(solution)/shard_map/ppermute | solution.py:310
  188.9 15.0 %collective-permute-done.18 = bf16[3,160,128]{2,1,0:T(8,128)(2,1)S(1)} collective-permute-done((bf16[3,160,128]{2,1,0:T(8,128)(2,1)S(1)}, bf16[3,160,128]{2,1,0:T(8,128)(2,1)S(1)}, u32[]{:S(2)}, u32[]{:S(2)}) %collective-permute-start.18) | collective-permute-done | bytes 122912 | tf_op jit(solution)/shard_map/ppermute | solution.py:310
  205.0 16.6 %all-gather.3.cloned.1.call-done.refs_3_ = bf16[2048,2432]{1,0:T(8,128)(2,1)} async-done(((bf16[256,2432]{1,0:T(8,128)(2,1)}), bf16[2048,2432]{1,0:T(8,128)(2,1)}) %all-gather.3.cloned.1.call-update) | async-done | bytes 9961488 | tf_op jit(solution)/shard_map/all_gather | solution.py:793
  226.4 7.1 shard_map.300
  244.1 35.1 %collective-permute-done.23.c_ref = bf16[384,2048]{1,0:T(8,128)(2,1)S(1)} collective-permute-done((bf16[384,2048]{1,0:T(8,128)(2,1)S(1)}, bf16[384,2048]{1,0:T(8,128)(2,1)S(1)}, u32[]{:S(2)}, u32[]{:S(2)}) %collective-permute-start.23) | collective-permute-done | bytes 1572896 | tf_op jit(solution)/shard_map/ppermute | solution.py:310
  287.4 24.0 %shard_map.304 = (bf16[1536,640]{1,0:T(8,128)(2,1)}, bf16[1536,640]{1,0:T(8,128)(2,1)}, bf16[1536,640]{1,0:T(8,128)(2,1)}, bf16[4,384,2048]{2,1,0:T(8,128)(2,1)}, bf16[4,384,2048]{2,1,0:T(8,128)(2,1)}) custom-call(s32[8]{0:T(128)} %copy-done.73, bf16[384,2048]{1,0:T(8,128)(2,1)} %get-tuple-element.147.refs_0_, ...), custom_call_target="tpu_custom_call" | custom-call | flops 6039797760 | bytes 10223616 | tf_op jit(solution)/shard_map/pallas_call | solution.py:654
  311.4 9.3 %collective-permute-done.25.refs_0_.refs_2_ = bf16[384,2048]{1,0:T(8,128)(2,1)} collective-permute-done((bf16[384,2048]{1,0:T(8,128)(2,1)}, bf16[384,2048]{1,0:T(8,128)(2,1)}, u32[]{:S(2)}, u32[]{:S(2)}) %collective-permute-start.25) | collective-permute-done | bytes 1572896 | tf_op jit(solution)/shard_map/ppermute | solution.py:310
  324.5 24.4 %shard_map.305 = (bf16[1536,640]{1,0:T(8,128)(2,1)}, bf16[1536,640]{1,0:T(8,128)(2,1)}, bf16[1536,640]{1,0:T(8,128)(2,1)}, bf16[4,384,2048]{2,1,0:T(8,128)(2,1)}, bf16[4,384,2048]{2,1,0:T(8,128)(2,1)}) custom-call(s32[8]{0:T(128)} %copy-done.73, ...), custom_call_target="tpu_custom_call", output_to_operand_aliasing={{0}: (5, {}), {1}: (6, {}), {2}: (7, {}), {3}: (8, {}), {4}... | custom-call | flops 6039797760 | bytes 10223616 | tf_op jit(solution)/shard_map/pallas_call | solution.py:654
  348.9 21.4 %shard_map.306 = (bf16[2048,1280]{1,0:T(8,128)(2,1)}, bf16[2048,640]{1,0:T(8,128)(2,1)}) custom-call(s32[8]{0:T(128)S(1)} %copy-done.74, s32[8]{0:T(128)S(1)} %copy-done.76, bf16[384,2048]{1,0:T(8,128)(2,1)} %get-tuple-element.147.refs_0_, bf16[384,2048]{1,0:T(8,128)(2,1)} %collective-permute-done.24.refs_1_, ...), custom_call_target="tpu_custom_call" | custom-call | flops 6039797760 | bytes 20316160 | tf_op jit(solution)/shard_map/pallas_call | solution.py:736
  374.4 43.8 %shard_map.307 = (bf16[1536,768]{1,0:T(8,128)(2,1)}, bf16[1536,768]{1,0:T(8,128)(2,1)}, bf16[1536,768]{1,0:T(8,128)(2,1)}, bf16[4,384,2048]{2,1,0:T(8,128)(2,1)}, bf16[4,384,2048]{2,1,0:T(8,128)(2,1)}) custom-call(s32[8]{0:T(128)} %copy-done.73, bf16[384,2048]{1,0:T(8,128)(2,1)} %get-tuple-element.147.refs_0_, ...), custom_call_target="tpu_custom_call" | custom-call | flops 14495514624 | bytes 17301504 | tf_op jit(solution)/shard_map/pallas_call | solution.py:654
  438.3 22.1 %shard_map.308 = bf16[2048,2304]{1,0:T(8,128)(2,1)} custom-call(s32[8]{0:T(128)S(1)} %copy-done.75, s32[8]{0:T(128)S(1)} %copy-done.75, bf16[384,2048]{1,0:T(8,128)(2,1)} %get-tuple-element.147.refs_0_, bf16[384,2048]{1,0:T(8,128)(2,1)} %collective-permute-done.24.refs_1_, bf16[384,2048]{1,0:T(8,128)(2,1)} %collective-permute-done.25.refs_0_.refs_2_, ...), custom_call_target="tpu_custom_call" | custom-call | flops 7247757312 | bytes 22282240 | tf_op jit(solution)/shard_map/pallas_call | solution.py:736
  490.0 30.1 %collective-permute-done.38.refs_2_.refs_4_ = bf16[384,2048]{1,0:T(8,128)(2,1)S(1)} collective-permute-done((bf16[384,2048]{1,0:T(8,128)(2,1)S(1)}, bf16[384,2048]{1,0:T(8,128)(2,1)S(1)}, u32[]{:S(2)}, u32[]{:S(2)}) %collective-permute-start.38) | collective-permute-done | bytes 1572896 | tf_op jit(solution)/shard_map/ppermute | solution.py:310
  528.2 9.0 %shard_map.311 = (bf16[6,4,160,128]{3,2,1,0:T(8,128)(2,1)S(1)}, bf16[6,256,512]{2,1,0:T(8,128)(2,1)S(1)}, f32[6,256,4]{2,1,0:T(8,128)S(1)}) custom-call(s32[1]{0:T(128)} %constant.104.clone.1.place_ref, bf16[6,256,640]{2,1,0:T(8,128)(2,1)S(1)} %bitcast.144, f32[6,256,8]{2,1,0:T(8,128)S(1)} %copy-done.6, bf16[6,256,512]{2,1,0:T(8,128)(2,1)S(1)} %bitcast.158, ...), custom_call_target="tpu_custom_call" | custom-call | flops 603979776 | bytes 4161536 | tf_op jit(solution)/shard_map/pallas_call | solution.py:247
  537.3 16.7 %shard_map.312 = (f32[6,256,128]{2,1,0:T(8,128)S(1)}, f32[6,256,512]{2,1,0:T(8,128)S(1)}) custom-call(s32[9]{0:T(128)S(1)} %copy-done.79, bf16[6,256,640]{2,1,0:T(8,128)(2,1)S(1)} %bitcast.145, f32[6,256,8]{2,1,0:T(8,128)S(1)} %copy-done.6, f32[6,8,256]{2,1,0:T(8,128)S(1)} %copy-done.70, bf16[6,256,512]{2,1,0:T(8,128)(2,1)S(1)} %get-tuple-element.158.gnum_ref, ...), custom_call_target="tpu_custom_call" | custom-call | flops 2214592512 | bytes 4698112 | tf_op jit(solution)/shard_map/pallas_call | solution.py:247
  557.9 18.6 %collective-permute-start.43 = (bf16[3,160,128]{2,1,0:T(8,128)(2,1)S(1)}, bf16[3,160,128]{2,1,0:T(8,128)(2,1)S(1)}, u32[]{:S(2)}, u32[]{:S(2)}) collective-permute-start(bf16[3,160,128]{2,1,0:T(8,128)(2,1)S(1)} %get-tuple-element.285), channel_id=1, source_target_pairs={{0,8},{4,12},{8,0},{12,4},{16,24},{20,28},{24,16},{28,20},{1,9},{5... | collective-permute-start | bytes 368648 | tf_op jit(solution)/shard_map/ppermute | solution.py:310
  590.9 9.0 %shard_map.313 = bf16[2048,512]{1,0:T(8,128)(2,1)} custom-call(s32[8]{0:T(128)S(1)} %copy-done.76, s32[4]{0:T(128)S(1)} %iota_xor_fusion.1.rows_ref.order_ref.quarters_ref, bf16[384,2048]{1,0:T(8,128)(2,1)S(1)} %copy-done.22, bf16[384,2048]{1,0:T(8,128)(2,1)S(1)} %copy-done.25, bf16[1536,512]{1,0:T(8,128)(2,1)S(1)} %bitcast.137, ...), custom_call_target="tpu_custom_call" | custom-call | flops 1610612736 | bytes 9175040 | tf_op jit(solution)/shard_map/pallas_call | solution.py:703
  654.9 10.8 %shard_map.319 = bf16[2048,640]{1,0:T(8,128)(2,1)} custom-call(s32[8]{0:T(128)S(1)} %copy-done.76, s32[4]{0:T(128)S(1)} %iota_xor_fusion.1.rows_ref.order_ref.quarters_ref, bf16[1536,2048]{1,0:T(8,128)(2,1)} %copy-done, bf16[1536,2048]{1,0:T(8,128)(2,1)} %copy-done, bf16[1536,640]{1,0:T(8,128)(2,1)S(1)} %bitcast.152, bf16[1536,640]{1,0:T(8,128)(2,1)S(1)} %bitcast.153, ...), custom_call_target="tpu_custom_call" | custom-call | flops 2013265920 | bytes 9633792 | tf_op jit(solution)/shard_map/pallas_call | solution.py:703
  669.4 13.4 %collective-permute-done.59.c_ref = bf16[384,2048]{1,0:T(8,128)(2,1)S(1)} collective-permute-done((bf16[384,2048]{1,0:T(8,128)(2,1)S(1)}, bf16[384,2048]{1,0:T(8,128)(2,1)S(1)}, u32[]{:S(2)}, u32[]{:S(2)}) %collective-permute-start.59) | collective-permute-done | bytes 1572896 | tf_op jit(solution)/shard_map/ppermute | solution.py:310
  746.1 9.9 %collective-permute-done.67 = bf16[256,512]{1,0:T(8,128)(2,1)} collective-permute-done((bf16[256,512]{1,0:T(8,128)(2,1)}, bf16[256,512]{1,0:T(8,128)(2,1)}, u32[]{:S(2)}, u32[]{:S(2)}) %collective-permute-start.67) | collective-permute-done | bytes 262176 | tf_op jit(solution)/shard_map/ppermute | solution.py:310
  (480 shorter events, 364.6 us)
Async XLA Ops:
  7.2 214.4 %all-gather.3.cloned.1.call-start = ((), (), s32[]{:S(2)}) async-start(), calls=%async_computation.2 | async-start | bytes 11206656 | tf_op jit(solution)/shard_map/all_gather | solution.py:793
  12.7 361.7 %all-gather.5.cloned.1.call-start = ((), (), s32[]{:S(2)}) async-start(), calls=%async_computation.3 | async-start | bytes 10616832 | tf_op jit(solution)/shard_map/all_gather | solution.py:793
  14.1 669.9 %reduce-scatter.3.cloned.1.call-start = ((), (), s32[]{:S(2)}) async-start(), calls=%async_computation.4 | async-start | bytes 5898240 | tf_op jit(solution)/shard_map/reduce_scatter | solution.py:859
  15.5 44.2 %collective-permute-start = (bf16[256,640]{1,0:T(8,128)(2,1)S(1)}, bf16[256,640]{1,0:T(8,128)(2,1)S(1)}, u32[]{:S(2)}, u32[]{:S(2)}) collective-permute-start(bf16[256,640]{1,0:T(8,128)(2,1)S(1)} %fusion.11.refs_0_), channel_id=1, source_target_pairs={{0,4},{4,0},{8,12},{12,8},{16,20},{20,16},{24,28},{28,24},{1,5},{5... | collective-permute-start | bytes 983048 | tf_op jit(solution)/shard_map/ppermute | solution.py:310
  18.5 33.3 %collective-permute-start.1 = (bf16[256,640]{1,0:T(8,128)(2,1)S(1)}, bf16[256,640]{1,0:T(8,128)(2,1)S(1)}, u32[]{:S(2)}, u32[]{:S(2)}) collective-permute-start(bf16[256,640]{1,0:T(8,128)(2,1)S(1)} %fusion.11.refs_0_), channel_id=1, source_target_pairs={{0,8},{4,12},{8,0},{12,4},{16,24},{20,28},{24,16},{28,20},{1,9},{5... | collective-permute-start | bytes 983048 | tf_op jit(solution)/shard_map/ppermute | solution.py:310
  20.1 33.5 %collective-permute-start.3 = (bf16[256,640]{1,0:T(8,128)(2,1)S(1)}, bf16[256,640]{1,0:T(8,128)(2,1)S(1)}, u32[]{:S(2)}, u32[]{:S(2)}) collective-permute-start(bf16[256,640]{1,0:T(8,128)(2,1)S(1)} %fusion.11.refs_0_), channel_id=1, source_target_pairs={{0,16},{4,20},{8,24},{12,28},{16,0},{20,4},{24,8},{28,12},{1,17},{... | collective-permute-start | bytes 983048 | tf_op jit(solution)/shard_map/ppermute | solution.py:310
  22.7 37.0 %collective-permute-start.5 = (bf16[256,640]{1,0:T(8,128)(2,1)S(1)}, bf16[256,640]{1,0:T(8,128)(2,1)}, u32[]{:S(2)}, u32[]{:S(2)}) collective-permute-start(bf16[256,640]{1,0:T(8,128)(2,1)S(1)} %fusion.11.refs_0_), channel_id=1, source_target_pairs={{0,24},{4,28},{8,16},{12,20},{16,8},{20,12},{24,0},{28,4},{1,25},{... | collective-permute-start | bytes 983048 | tf_op jit(solution)/shard_map/ppermute | solution.py:310
  242.3 36.9 %collective-permute-start.23 = (bf16[384,2048]{1,0:T(8,128)(2,1)S(1)}, bf16[384,2048]{1,0:T(8,128)(2,1)S(1)}, u32[]{:S(2)}, u32[]{:S(2)}) collective-permute-start(bf16[384,2048]{1,0:T(8,128)(2,1)S(1)} %add_convert_fusion.1), channel_id=1, source_target_pairs={{0,2},{1,3},{2,0},{3,1},{4,6},{5,7},{6,4},{7,5},{8,10},{9,11},{10,... | collective-permute-start | bytes 4718600 | tf_op jit(solution)/shard_map/ppermute | solution.py:310
  243.9 35.3 %collective-permute-start.21 = (bf16[384,2048]{1,0:T(8,128)(2,1)S(1)}, bf16[384,2048]{1,0:T(8,128)(2,1)S(1)}, u32[]{:S(2)}, u32[]{:S(2)}) collective-permute-start(bf16[384,2048]{1,0:T(8,128)(2,1)S(1)} %get-tuple-element.124), channel_id=1, source_target_pairs={{0,1},{1,0},{2,3},{3,2},{4,5},{5,4},{6,7},{7,6},{8,9},{9,8},{10,11... | collective-permute-start | bytes 4718600 | tf_op jit(solution)/shard_map/ppermute | solution.py:310
  283.6 37.1 %collective-permute-start.25 = (bf16[384,2048]{1,0:T(8,128)(2,1)}, bf16[384,2048]{1,0:T(8,128)(2,1)}, u32[]{:S(2)}, u32[]{:S(2)}) collective-permute-start(bf16[384,2048]{1,0:T(8,128)(2,1)} %get-tuple-element.147.refs_0_), channel_id=1, source_target_pairs={{0,2},{1,3},{2,0},{3,1},{4,6},{5,7},{6,4},{7,5},{8,10},{9,11},{10,... | collective-permute-start | bytes 4718600 | tf_op jit(solution)/shard_map/ppermute | solution.py:310
  370.4 353.6 %reduce-scatter.5.cloned.1.call-start = ((), (), s32[]{:S(2)}) async-start(), calls=%async_computation.5 | async-start | bytes 10616832 | tf_op jit(solution)/shard_map/reduce_scatter | solution.py:859
  372.9 50.3 %collective-permute-start.31 = (bf16[1024,640]{1,0:T(8,128)(2,1)}, bf16[1024,640]{1,0:T(8,128)(2,1)}, u32[]{:S(2)}, u32[]{:S(2)}) collective-permute-start(bf16[1024,640]{1,0:T(8,128)(2,1)} %slice.172), channel_id=1, source_target_pairs={{0,4},{4,0},{8,12},{12,8},{16,20},{20,16},{24,28},{28,24},{1,5},{5... | collective-permute-start | bytes 3932168 | tf_op jit(solution)/shard_map/ppermute | solution.py:310
  429.9 36.7 %collective-permute-start.33 = (bf16[384,2048]{1,0:T(8,128)(2,1)}, bf16[384,2048]{1,0:T(8,128)(2,1)}, u32[]{:S(2)}, u32[]{:S(2)}) collective-permute-start(bf16[384,2048]{1,0:T(8,128)(2,1)} %fusion), channel_id=1, source_target_pairs={{0,2},{1,3},{2,0},{3,1},{4,6},{5,7},{6,4},{7,5},{8,10},{9,11},{10,... | collective-permute-start | bytes 4718600 | tf_op jit(solution)/shard_map/ppermute | solution.py:310
  431.4 35.2 %collective-permute-start.30 = (bf16[384,2048]{1,0:T(8,128)(2,1)}, bf16[384,2048]{1,0:T(8,128)(2,1)}, u32[]{:S(2)}, u32[]{:S(2)}) collective-permute-start(bf16[384,2048]{1,0:T(8,128)(2,1)} %get-tuple-element.261), channel_id=1, source_target_pairs={{0,1},{1,0},{2,3},{3,2},{4,5},{5,4},{6,7},{7,6},{8,9},{9,8},{10,11... | collective-permute-start | bytes 4718600 | tf_op jit(solution)/shard_map/ppermute | solution.py:310
  433.9 32.7 %collective-permute-start.34 = (bf16[256,640]{1,0:T(8,128)(2,1)}, bf16[256,640]{1,0:T(8,128)(2,1)}, u32[]{:S(2)}, u32[]{:S(2)}) collective-permute-start(bf16[256,640]{1,0:T(8,128)(2,1)} %get-tuple-element.270), channel_id=1, source_target_pairs={{0,8},{4,12},{8,0},{12,4},{16,24},{20,28},{24,16},{28,20},{1,9},{5... | collective-permute-start | bytes 983048 | tf_op jit(solution)/shard_map/ppermute | solution.py:310
  433.9 32.7 %collective-permute-start.35 = (bf16[256,640]{1,0:T(8,128)(2,1)}, bf16[256,640]{1,0:T(8,128)(2,1)}, u32[]{:S(2)}, u32[]{:S(2)}) collective-permute-start(bf16[256,640]{1,0:T(8,128)(2,1)} %get-tuple-element.269), channel_id=1, source_target_pairs={{0,16},{4,20},{8,24},{12,28},{16,0},{20,4},{24,8},{28,12},{1,17},{... | collective-permute-start | bytes 983048 | tf_op jit(solution)/shard_map/ppermute | solution.py:310
  483.3 36.8 %collective-permute-start.38 = (bf16[384,2048]{1,0:T(8,128)(2,1)S(1)}, bf16[384,2048]{1,0:T(8,128)(2,1)S(1)}, u32[]{:S(2)}, u32[]{:S(2)}) collective-permute-start(bf16[384,2048]{1,0:T(8,128)(2,1)S(1)} %copy-done.21), channel_id=1, source_target_pairs={{0,2},{1,3},{2,0},{3,1},{4,6},{5,7},{6,4},{7,5},{8,10},{9,11},{10,... | collective-permute-start | bytes 4718600 | tf_op jit(solution)/shard_map/ppermute | solution.py:310
  520.1 37.0 %collective-permute-start.29 = (bf16[384,2048]{1,0:T(8,128)(2,1)}, bf16[384,2048]{1,0:T(8,128)(2,1)S(1)}, u32[]{:S(2)}, u32[]{:S(2)}) collective-permute-start(bf16[384,2048]{1,0:T(8,128)(2,1)} %fusion.1), channel_id=1, source_target_pairs={{0,2},{1,3},{2,0},{3,1},{4,6},{5,7},{6,4},{7,5},{8,10},{9,11},{10,... | collective-permute-start | bytes 4718600 | tf_op jit(solution)/shard_map/ppermute | solution.py:310
  521.7 56.6 %collective-permute-start.27 = (bf16[384,2048]{1,0:T(8,128)(2,1)}, bf16[384,2048]{1,0:T(8,128)(2,1)}, u32[]{:S(2)}, u32[]{:S(2)}) collective-permute-start(bf16[384,2048]{1,0:T(8,128)(2,1)} %get-tuple-element.258), channel_id=1, source_target_pairs={{0,1},{1,0},{2,3},{3,2},{4,5},{5,4},{6,7},{7,6},{8,9},{9,8},{10,11... | collective-permute-start | bytes 4718600 | tf_op jit(solution)/shard_map/ppermute | solution.py:310
  600.0 35.9 %collective-permute-start.41 = (bf16[384,2048]{1,0:T(8,128)(2,1)}, bf16[384,2048]{1,0:T(8,128)(2,1)}, u32[]{:S(2)}, u32[]{:S(2)}) collective-permute-start(bf16[384,2048]{1,0:T(8,128)(2,1)} %fusion.4.refs_0_), channel_id=1, source_target_pairs={{0,2},{1,3},{2,0},{3,1},{4,6},{5,7},{6,4},{7,5},{8,10},{9,11},{10,... | collective-permute-start | bytes 4718600 | tf_op jit(solution)/shard_map/ppermute | solution.py:310
  646.0 36.9 %collective-permute-start.59 = (bf16[384,2048]{1,0:T(8,128)(2,1)S(1)}, bf16[384,2048]{1,0:T(8,128)(2,1)S(1)}, u32[]{:S(2)}, u32[]{:S(2)}) collective-permute-start(bf16[384,2048]{1,0:T(8,128)(2,1)S(1)} %add_convert_fusion), channel_id=1, source_target_pairs={{0,2},{1,3},{2,0},{3,1},{4,6},{5,7},{6,4},{7,5},{8,10},{9,11},{10,... | collective-permute-start | bytes 4718600 | tf_op jit(solution)/shard_map/ppermute | solution.py:310
  668.9 34.2 %collective-permute-start.40 = (bf16[384,2048]{1,0:T(8,128)(2,1)}, bf16[384,2048]{1,0:T(8,128)(2,1)}, u32[]{:S(2)}, u32[]{:S(2)}) collective-permute-start(bf16[384,2048]{1,0:T(8,128)(2,1)} %fusion.4.refs_0_), channel_id=1, source_target_pairs={{0,1},{1,0},{2,3},{3,2},{4,5},{5,4},{6,7},{7,6},{8,9},{9,8},{10,11... | collective-permute-start | bytes 4718600 | tf_op jit(solution)/shard_map/ppermute | solution.py:310
  668.9 35.9 %collective-permute-start.56 = (bf16[384,2048]{1,0:T(8,128)(2,1)}, bf16[384,2048]{1,0:T(8,128)(2,1)}, u32[]{:S(2)}, u32[]{:S(2)}) collective-permute-start(bf16[384,2048]{1,0:T(8,128)(2,1)} %collective-permute-done.41.refs_0_), channel_id=1, source_target_pairs={{0,1},{1,0},{2,3},{3,2},{4,5},{5,4},{6,7},{7,6},{8,9},{9,8},{10,11... | collective-permute-start | bytes 4718600 | tf_op jit(solution)/shard_map/ppermute | solution.py:310
  694.4 35.8 %collective-permute-start.60 = (bf16[384,2048]{1,0:T(8,128)(2,1)S(1)}, bf16[384,2048]{1,0:T(8,128)(2,1)S(1)}, u32[]{:S(2)}, u32[]{:S(2)}) collective-permute-start(bf16[384,2048]{1,0:T(8,128)(2,1)S(1)} %shard_map.320.refs_0_), channel_id=1, source_target_pairs={{0,2},{1,3},{2,0},{3,1},{4,6},{5,7},{6,4},{7,5},{8,10},{9,11},{10,... | collective-permute-start | bytes 4718600 | tf_op jit(solution)/shard_map/ppermute | solution.py:310
  (162 other events, 2105.7 us)
Sparse Core Ops, SparseCore 0:
  12.8 208.6 all-gather.2
  224.3 137.1 all-gather.4
  370.5 117.9 reduce-scatter.2
  492.5 182.1 reduce-scatter.4

commit v7 on v6

--- a/solution.py
+++ b/solution.py
@@ -861,7 +861,8 @@
     ffn_grads = [seq_sum(first_grads[0])]
     left = [after(units[0], first_grads), *units[1:]]
     second = feed_forward(left, dy, 0, ffn_w[1], hidden_units - cut, order, earlier=first[3:])
-    gunit, ffn_out = [[item[i] for i in range(4)] for item in second[3:]]
+    gunit = [None, None, second[3][2], second[3][3]]
+    ffn_out = [second[4][i] for i in range(4)]
 
     down_pairs = ()
     if n_seq == 8:
@@ -875,7 +876,10 @@
         left = [after(units[0], sent, *pairs), *units[1:]]
         return ffn_weight_grads(left, dy, second[:3], order), pairs
 
-    terms, (found, down_pairs) = scatter_head(gunit, beside=second_grads)
+    summed = scatter_core(gunit)
+    near_sums = after(second[3], summed)
+    gunit = [near_sums[0], near_sums[1], *gunit[2:]]
+    terms, (found, down_pairs) = scatter_head(gunit, beside=second_grads, summed=summed)
     down_terms = scatter_sends(down_pairs)
     terms = after(terms, *down_terms)
     grad_hidden, grad_branch = on_quarter(norm_back_kernel, [hidden, dy, *terms], quarter, [f32, bf16])

time: 790 us -> 788 us (level)
    unnamed x246 -> x248, local copies, waits for them, and re-layouts: 64.2 us -> 64.2 us
  transfers between devices with their start and end apart: 78 -> 78, of which waited for: 31 -> 32; matrix products, arithmetic and copies ran while one was open for 8% -> 8% of each run, Pallas kernels for 35% -> 35%
where the time goes in v7:
time: 788 us; the launch traced here: 774 us
  Pallas kernels  274 us (35%)
  waiting for transfers between devices  210 us (27%)
  starting transfers between devices  147 us (19%)
  local copies, waits for them, and re-layouts  90 us (11%)
  other arithmetic  37.5 us (5%)
  between operations  15.7 us (2%)
    ppermute x74, waiting for transfers between devices, send(): return lax.ppermute(value, axis, [(i, i ^ mask) for i in range(count)])  193 us
    ppermute x74, starting transfers between devices, send(): return lax.ppermute(value, axis, [(i, i ^ mask) for i in range(count)])  147 us
    pallas_call x3, Pallas kernels, feed_forward(): pl.pallas_call(functools.partial(ffn_kernel, 256, steps, len(earlier)), o...  92.3 us
    unnamed x248, local copies, waits for them, and re-layouts  64.2 us
    pallas_call x7, Pallas kernels, by_row(): pl.pallas_call(kernel, out_shape=shapes, grid_spec=pltpu.PrefetchScalarGr...  53.4 us
    pallas_call x2, Pallas kernels, ffn_weight_grads(): pl.pallas_call(ffn_weight_kernel, out_shape=[jax.ShapeDtypeStruct((width,...  43.5 us
    pallas_call x2, Pallas kernels, weight_grads(): pl.pallas_call(functools.partial(weight_kernel, tuple(((len(lefts), len(r...  19.8 us
    pallas_call x4, Pallas kernels, quarter_products(): pl.pallas_call(quarter_kernel, out_shape=[jax.ShapeDtypeStruct((rows, wid...  19.2 us
  transfers between devices with their start and end apart: 78, of which 32 were waited for; matrix products, arithmetic and copies ran while one was open for 8% of the time, Pallas kernels for 35%

profile of v7, /device:TPU:0, one launch (start us, length us, event | category | flops | bytes accessed | tf_op | source)
XLA Modules:
  0.0 774.0 jit_solution(11937750876729226811)
XLA Ops:
  85.8 7.4 shard_map.296
  94.7 8.0 %shard_map.298 = bf16[6,4,160,128]{3,2,1,0:T(8,128)(2,1)S(1)} custom-call(s32[1]{0:T(128)} %constant.104.clone.1.place_ref, bf16[6,256,640]{2,1,0:T(8,128)(2,1)S(1)} %bitcast.141, f32[6,256,8]{2,1,0:T(8,128)S(1)} %convert_element_type.256.edge_ref, bf16[128,1024]{1,0:T(8,128)(2,1)S(1)} %copy-done.31, bf16[128,1024]{1,0:T(8,128)(2,1)S(1)} %copy-done.33, ...), custom_call_target="tpu_custom_call" | custom-call | flops 603979776 | bytes 1777664 | tf_op jit(solution)/shard_map/pallas_call | solution.py:247
  104.0 8.3 %collective-permute-start.8 = (bf16[3,160,128]{2,1,0:T(8,128)(2,1)}, bf16[3,160,128]{2,1,0:T(8,128)(2,1)S(1)}, u32[]{:S(2)}, u32[]{:S(2)}) collective-permute-start(bf16[3,160,128]{2,1,0:T(8,128)(2,1)} %get-tuple-element.294), channel_id=1, source_target_pairs={{0,8},{4,12},{8,0},{12,4},{16,24},{20,28},{24,16},{28,20},{1,9},{5... | collective-permute-start | bytes 368648 | tf_op jit(solution)/shard_map/ppermute | solution.py:310
  124.1 8.0 %collective-permute-start.13 = (bf16[3,160,128]{2,1,0:T(8,128)(2,1)}, bf16[3,160,128]{2,1,0:T(8,128)(2,1)S(1)}, u32[]{:S(2)}, u32[]{:S(2)}) collective-permute-start(bf16[3,160,128]{2,1,0:T(8,128)(2,1)} %get-tuple-element.289), channel_id=1, source_target_pairs={{0,28},{4,24},{8,20},{12,16},{16,12},{20,8},{24,4},{28,0},{1,29},{... | collective-permute-start | bytes 368648 | tf_op jit(solution)/shard_map/ppermute | solution.py:310
  138.4 8.9 %collective-permute-done.11.refs_5_ = bf16[3,160,128]{2,1,0:T(8,128)(2,1)S(1)} collective-permute-done((bf16[3,160,128]{2,1,0:T(8,128)(2,1)}, bf16[3,160,128]{2,1,0:T(8,128)(2,1)S(1)}, u32[]{:S(2)}, u32[]{:S(2)}) %collective-permute-start.11) | collective-permute-done | bytes 122912 | tf_op jit(solution)/shard_map/ppermute | solution.py:310
  149.8 17.9 %collective-permute-start.15 = (bf16[3,160,128]{2,1,0:T(8,128)(2,1)S(1)}, bf16[3,160,128]{2,1,0:T(8,128)(2,1)S(1)}, u32[]{:S(2)}, u32[]{:S(2)}) collective-permute-start(bf16[3,160,128]{2,1,0:T(8,128)(2,1)S(1)} %get-tuple-element.117), channel_id=1, source_target_pairs={{0,8},{4,12},{8,0},{12,4},{16,24},{20,28},{24,16},{28,20},{1,9},{5... | collective-permute-start | bytes 368648 | tf_op jit(solution)/shard_map/ppermute | solution.py:310
  188.9 15.0 %collective-permute-done.18 = bf16[3,160,128]{2,1,0:T(8,128)(2,1)S(1)} collective-permute-done((bf16[3,160,128]{2,1,0:T(8,128)(2,1)S(1)}, bf16[3,160,128]{2,1,0:T(8,128)(2,1)S(1)}, u32[]{:S(2)}, u32[]{:S(2)}) %collective-permute-start.18) | collective-permute-done | bytes 122912 | tf_op jit(solution)/shard_map/ppermute | solution.py:310
  205.0 16.6 %all-gather.3.cloned.1.call-done.refs_3_ = bf16[2048,2432]{1,0:T(8,128)(2,1)} async-done(((bf16[256,2432]{1,0:T(8,128)(2,1)}), bf16[2048,2432]{1,0:T(8,128)(2,1)}) %all-gather.3.cloned.1.call-update) | async-done | bytes 9961488 | tf_op jit(solution)/shard_map/all_gather | solution.py:793
  226.4 7.1 shard_map.300
  244.1 35.1 %collective-permute-done.23.c_ref = bf16[384,2048]{1,0:T(8,128)(2,1)S(1)} collective-permute-done((bf16[384,2048]{1,0:T(8,128)(2,1)S(1)}, bf16[384,2048]{1,0:T(8,128)(2,1)S(1)}, u32[]{:S(2)}, u32[]{:S(2)}) %collective-permute-start.23) | collective-permute-done | bytes 1572896 | tf_op jit(solution)/shard_map/ppermute | solution.py:310
  287.4 24.0 %shard_map.304 = (bf16[1536,640]{1,0:T(8,128)(2,1)}, bf16[1536,640]{1,0:T(8,128)(2,1)}, bf16[1536,640]{1,0:T(8,128)(2,1)}, bf16[4,384,2048]{2,1,0:T(8,128)(2,1)}, bf16[4,384,2048]{2,1,0:T(8,128)(2,1)}) custom-call(s32[8]{0:T(128)} %copy-done.73, bf16[384,2048]{1,0:T(8,128)(2,1)} %get-tuple-element.149.refs_0_, ...), custom_call_target="tpu_custom_call" | custom-call | flops 6039797760 | bytes 10223616 | tf_op jit(solution)/shard_map/pallas_call | solution.py:654
  311.4 9.3 %collective-permute-done.25.refs_0_.refs_2_ = bf16[384,2048]{1,0:T(8,128)(2,1)} collective-permute-done((bf16[384,2048]{1,0:T(8,128)(2,1)}, bf16[384,2048]{1,0:T(8,128)(2,1)}, u32[]{:S(2)}, u32[]{:S(2)}) %collective-permute-start.25) | collective-permute-done | bytes 1572896 | tf_op jit(solution)/shard_map/ppermute | solution.py:310
  324.5 24.4 %shard_map.305 = (bf16[1536,640]{1,0:T(8,128)(2,1)}, bf16[1536,640]{1,0:T(8,128)(2,1)}, bf16[1536,640]{1,0:T(8,128)(2,1)}, bf16[4,384,2048]{2,1,0:T(8,128)(2,1)}, bf16[4,384,2048]{2,1,0:T(8,128)(2,1)}) custom-call(s32[8]{0:T(128)} %copy-done.73, ...), custom_call_target="tpu_custom_call", output_to_operand_aliasing={{0}: (5, {}), {1}: (6, {}), {2}: (7, {}), {3}: (8, {}), {4}... | custom-call | flops 6039797760 | bytes 10223616 | tf_op jit(solution)/shard_map/pallas_call | solution.py:654
  348.9 21.5 %shard_map.306 = (bf16[2048,1280]{1,0:T(8,128)(2,1)}, bf16[2048,640]{1,0:T(8,128)(2,1)}) custom-call(s32[8]{0:T(128)S(1)} %copy-done.74, s32[8]{0:T(128)S(1)} %copy-done.76, bf16[384,2048]{1,0:T(8,128)(2,1)} %get-tuple-element.149.refs_0_, bf16[384,2048]{1,0:T(8,128)(2,1)} %collective-permute-done.24.refs_1_, ...), custom_call_target="tpu_custom_call" | custom-call | flops 6039797760 | bytes 20316160 | tf_op jit(solution)/shard_map/pallas_call | solution.py:736
  374.5 43.8 %shard_map.307 = (bf16[1536,768]{1,0:T(8,128)(2,1)}, bf16[1536,768]{1,0:T(8,128)(2,1)}, bf16[1536,768]{1,0:T(8,128)(2,1)}, bf16[4,384,2048]{2,1,0:T(8,128)(2,1)}, bf16[4,384,2048]{2,1,0:T(8,128)(2,1)}) custom-call(s32[8]{0:T(128)} %copy-done.73, bf16[384,2048]{1,0:T(8,128)(2,1)} %get-tuple-element.149.refs_0_, ...), custom_call_target="tpu_custom_call" | custom-call | flops 14495514624 | bytes 17301504 | tf_op jit(solution)/shard_map/pallas_call | solution.py:654
  437.1 22.1 %shard_map.308 = bf16[2048,2304]{1,0:T(8,128)(2,1)} custom-call(s32[8]{0:T(128)S(1)} %copy-done.75, s32[8]{0:T(128)S(1)} %copy-done.75, bf16[384,2048]{1,0:T(8,128)(2,1)} %get-tuple-element.149.refs_0_, bf16[384,2048]{1,0:T(8,128)(2,1)} %collective-permute-done.24.refs_1_, bf16[384,2048]{1,0:T(8,128)(2,1)} %collective-permute-done.25.refs_0_.refs_2_, ...), custom_call_target="tpu_custom_call" | custom-call | flops 7247757312 | bytes 22282240 | tf_op jit(solution)/shard_map/pallas_call | solution.py:736
  486.9 30.1 %collective-permute-done.38.refs_2_.refs_4_ = bf16[384,2048]{1,0:T(8,128)(2,1)S(1)} collective-permute-done((bf16[384,2048]{1,0:T(8,128)(2,1)S(1)}, bf16[384,2048]{1,0:T(8,128)(2,1)S(1)}, u32[]{:S(2)}, u32[]{:S(2)}) %collective-permute-start.38) | collective-permute-done | bytes 1572896 | tf_op jit(solution)/shard_map/ppermute | solution.py:310
  525.1 9.0 %shard_map.311 = (bf16[6,4,160,128]{3,2,1,0:T(8,128)(2,1)S(1)}, bf16[6,256,512]{2,1,0:T(8,128)(2,1)S(1)}, f32[6,256,4]{2,1,0:T(8,128)S(1)}) custom-call(s32[1]{0:T(128)} %constant.104.clone.1.place_ref, bf16[6,256,640]{2,1,0:T(8,128)(2,1)S(1)} %bitcast.144, f32[6,256,8]{2,1,0:T(8,128)S(1)} %copy-done.6, bf16[6,256,512]{2,1,0:T(8,128)(2,1)S(1)} %bitcast.158, ...), custom_call_target="tpu_custom_call" | custom-call | flops 603979776 | bytes 4161536 | tf_op jit(solution)/shard_map/pallas_call | solution.py:247
  534.2 16.7 %shard_map.312 = (f32[6,256,128]{2,1,0:T(8,128)S(1)}, f32[6,256,512]{2,1,0:T(8,128)S(1)}) custom-call(s32[9]{0:T(128)S(1)} %copy-done.79, bf16[6,256,640]{2,1,0:T(8,128)(2,1)S(1)} %bitcast.145, f32[6,256,8]{2,1,0:T(8,128)S(1)} %copy-done.6, f32[6,8,256]{2,1,0:T(8,128)S(1)} %copy-done.70, bf16[6,256,512]{2,1,0:T(8,128)(2,1)S(1)} %get-tuple-element.160.gnum_ref, ...), custom_call_target="tpu_custom_call" | custom-call | flops 2214592512 | bytes 4698112 | tf_op jit(solution)/shard_map/pallas_call | solution.py:247
  554.7 20.4 %collective-permute-start.43 = (bf16[3,160,128]{2,1,0:T(8,128)(2,1)S(1)}, bf16[3,160,128]{2,1,0:T(8,128)(2,1)S(1)}, u32[]{:S(2)}, u32[]{:S(2)}) collective-permute-start(bf16[3,160,128]{2,1,0:T(8,128)(2,1)S(1)} %get-tuple-element.286), channel_id=1, source_target_pairs={{0,8},{4,12},{8,0},{12,4},{16,24},{20,28},{24,16},{28,20},{1,9},{5... | collective-permute-start | bytes 368648 | tf_op jit(solution)/shard_map/ppermute | solution.py:310
  589.3 9.0 %shard_map.313 = bf16[2048,512]{1,0:T(8,128)(2,1)} custom-call(s32[8]{0:T(128)S(1)} %copy-done.76, s32[4]{0:T(128)S(1)} %iota_xor_fusion.1.rows_ref.order_ref.quarters_ref, bf16[384,2048]{1,0:T(8,128)(2,1)S(1)} %copy-done.22, bf16[384,2048]{1,0:T(8,128)(2,1)S(1)} %copy-done.25, bf16[1536,512]{1,0:T(8,128)(2,1)S(1)} %bitcast.137, ...), custom_call_target="tpu_custom_call" | custom-call | flops 1610612736 | bytes 9175040 | tf_op jit(solution)/shard_map/pallas_call | solution.py:703
  653.4 10.8 %shard_map.319 = bf16[2048,640]{1,0:T(8,128)(2,1)} custom-call(s32[8]{0:T(128)S(1)} %copy-done.76, s32[4]{0:T(128)S(1)} %iota_xor_fusion.1.rows_ref.order_ref.quarters_ref, bf16[1536,2048]{1,0:T(8,128)(2,1)} %copy-done, bf16[1536,2048]{1,0:T(8,128)(2,1)} %copy-done, bf16[1536,640]{1,0:T(8,128)(2,1)S(1)} %bitcast.152, bf16[1536,640]{1,0:T(8,128)(2,1)S(1)} %bitcast.153, ...), custom_call_target="tpu_custom_call" | custom-call | flops 2013265920 | bytes 9633792 | tf_op jit(solution)/shard_map/pallas_call | solution.py:703
  667.9 13.5 %collective-permute-done.59.c_ref = bf16[384,2048]{1,0:T(8,128)(2,1)S(1)} collective-permute-done((bf16[384,2048]{1,0:T(8,128)(2,1)S(1)}, bf16[384,2048]{1,0:T(8,128)(2,1)S(1)}, u32[]{:S(2)}, u32[]{:S(2)}) %collective-permute-start.59) | collective-permute-done | bytes 1572896 | tf_op jit(solution)/shard_map/ppermute | solution.py:310
  744.5 9.9 %collective-permute-done.67 = bf16[256,512]{1,0:T(8,128)(2,1)} collective-permute-done((bf16[256,512]{1,0:T(8,128)(2,1)}, bf16[256,512]{1,0:T(8,128)(2,1)}, u32[]{:S(2)}, u32[]{:S(2)}) %collective-permute-start.67) | collective-permute-done | bytes 262176 | tf_op jit(solution)/shard_map/ppermute | solution.py:310
  (483 shorter events, 361.3 us)
Async XLA Ops:
  7.2 214.4 %all-gather.3.cloned.1.call-start = ((), (), s32[]{:S(2)}) async-start(), calls=%async_computation.2 | async-start | bytes 11206656 | tf_op jit(solution)/shard_map/all_gather | solution.py:793
  12.7 361.7 %all-gather.5.cloned.1.call-start = ((), (), s32[]{:S(2)}) async-start(), calls=%async_computation.3 | async-start | bytes 10616832 | tf_op jit(solution)/shard_map/all_gather | solution.py:793
  14.1 668.6 %reduce-scatter.3.cloned.1.call-start = ((), (), s32[]{:S(2)}) async-start(), calls=%async_computation.4 | async-start | bytes 5898240 | tf_op jit(solution)/shard_map/reduce_scatter | solution.py:859
  15.6 44.2 %collective-permute-start = (bf16[256,640]{1,0:T(8,128)(2,1)S(1)}, bf16[256,640]{1,0:T(8,128)(2,1)S(1)}, u32[]{:S(2)}, u32[]{:S(2)}) collective-permute-start(bf16[256,640]{1,0:T(8,128)(2,1)S(1)} %fusion.11.refs_0_), channel_id=1, source_target_pairs={{0,4},{4,0},{8,12},{12,8},{16,20},{20,16},{24,28},{28,24},{1,5},{5... | collective-permute-start | bytes 983048 | tf_op jit(solution)/shard_map/ppermute | solution.py:310
  18.5 33.4 %collective-permute-start.1 = (bf16[256,640]{1,0:T(8,128)(2,1)S(1)}, bf16[256,640]{1,0:T(8,128)(2,1)S(1)}, u32[]{:S(2)}, u32[]{:S(2)}) collective-permute-start(bf16[256,640]{1,0:T(8,128)(2,1)S(1)} %fusion.11.refs_0_), channel_id=1, source_target_pairs={{0,8},{4,12},{8,0},{12,4},{16,24},{20,28},{24,16},{28,20},{1,9},{5... | collective-permute-start | bytes 983048 | tf_op jit(solution)/shard_map/ppermute | solution.py:310
  20.1 33.5 %collective-permute-start.3 = (bf16[256,640]{1,0:T(8,128)(2,1)S(1)}, bf16[256,640]{1,0:T(8,128)(2,1)S(1)}, u32[]{:S(2)}, u32[]{:S(2)}) collective-permute-start(bf16[256,640]{1,0:T(8,128)(2,1)S(1)} %fusion.11.refs_0_), channel_id=1, source_target_pairs={{0,16},{4,20},{8,24},{12,28},{16,0},{20,4},{24,8},{28,12},{1,17},{... | collective-permute-start | bytes 983048 | tf_op jit(solution)/shard_map/ppermute | solution.py:310
  22.7 37.0 %collective-permute-start.5 = (bf16[256,640]{1,0:T(8,128)(2,1)S(1)}, bf16[256,640]{1,0:T(8,128)(2,1)}, u32[]{:S(2)}, u32[]{:S(2)}) collective-permute-start(bf16[256,640]{1,0:T(8,128)(2,1)S(1)} %fusion.11.refs_0_), channel_id=1, source_target_pairs={{0,24},{4,28},{8,16},{12,20},{16,8},{20,12},{24,0},{28,4},{1,25},{... | collective-permute-start | bytes 983048 | tf_op jit(solution)/shard_map/ppermute | solution.py:310
  242.4 36.9 %collective-permute-start.23 = (bf16[384,2048]{1,0:T(8,128)(2,1)S(1)}, bf16[384,2048]{1,0:T(8,128)(2,1)S(1)}, u32[]{:S(2)}, u32[]{:S(2)}) collective-permute-start(bf16[384,2048]{1,0:T(8,128)(2,1)S(1)} %add_convert_fusion.1), channel_id=1, source_target_pairs={{0,2},{1,3},{2,0},{3,1},{4,6},{5,7},{6,4},{7,5},{8,10},{9,11},{10,... | collective-permute-start | bytes 4718600 | tf_op jit(solution)/shard_map/ppermute | solution.py:310
  243.9 35.3 %collective-permute-start.21 = (bf16[384,2048]{1,0:T(8,128)(2,1)S(1)}, bf16[384,2048]{1,0:T(8,128)(2,1)S(1)}, u32[]{:S(2)}, u32[]{:S(2)}) collective-permute-start(bf16[384,2048]{1,0:T(8,128)(2,1)S(1)} %get-tuple-element.125), channel_id=1, source_target_pairs={{0,1},{1,0},{2,3},{3,2},{4,5},{5,4},{6,7},{7,6},{8,9},{9,8},{10,11... | collective-permute-start | bytes 4718600 | tf_op jit(solution)/shard_map/ppermute | solution.py:310
  283.6 37.1 %collective-permute-start.25 = (bf16[384,2048]{1,0:T(8,128)(2,1)}, bf16[384,2048]{1,0:T(8,128)(2,1)}, u32[]{:S(2)}, u32[]{:S(2)}) collective-permute-start(bf16[384,2048]{1,0:T(8,128)(2,1)} %get-tuple-element.149.refs_0_), channel_id=1, source_target_pairs={{0,2},{1,3},{2,0},{3,1},{4,6},{5,7},{6,4},{7,5},{8,10},{9,11},{10,... | collective-permute-start | bytes 4718600 | tf_op jit(solution)/shard_map/ppermute | solution.py:310
  370.4 352.0 %reduce-scatter.5.cloned.1.call-start = ((), (), s32[]{:S(2)}) async-start(), calls=%async_computation.5 | async-start | bytes 10616832 | tf_op jit(solution)/shard_map/reduce_scatter | solution.py:859
  373.0 47.1 %collective-permute-start.30 = (bf16[1024,640]{1,0:T(8,128)(2,1)}, bf16[1024,640]{1,0:T(8,128)(2,1)}, u32[]{:S(2)}, u32[]{:S(2)}) collective-permute-start(bf16[1024,640]{1,0:T(8,128)(2,1)} %slice.170), channel_id=1, source_target_pairs={{0,4},{4,0},{8,12},{12,8},{16,20},{20,16},{24,28},{28,24},{1,5},{5... | collective-permute-start | bytes 3932168 | tf_op jit(solution)/shard_map/ppermute | solution.py:310
  426.7 36.8 %collective-permute-start.33 = (bf16[384,2048]{1,0:T(8,128)(2,1)}, bf16[384,2048]{1,0:T(8,128)(2,1)}, u32[]{:S(2)}, u32[]{:S(2)}) collective-permute-start(bf16[384,2048]{1,0:T(8,128)(2,1)} %fusion), channel_id=1, source_target_pairs={{0,2},{1,3},{2,0},{3,1},{4,6},{5,7},{6,4},{7,5},{8,10},{9,11},{10,... | collective-permute-start | bytes 4718600 | tf_op jit(solution)/shard_map/ppermute | solution.py:310
  430.2 33.4 %collective-permute-start.32 = (bf16[384,2048]{1,0:T(8,128)(2,1)}, bf16[384,2048]{1,0:T(8,128)(2,1)}, u32[]{:S(2)}, u32[]{:S(2)}) collective-permute-start(bf16[384,2048]{1,0:T(8,128)(2,1)} %get-tuple-element.262), channel_id=1, source_target_pairs={{0,1},{1,0},{2,3},{3,2},{4,5},{5,4},{6,7},{7,6},{8,9},{9,8},{10,11... | collective-permute-start | bytes 4718600 | tf_op jit(solution)/shard_map/ppermute | solution.py:310
  480.2 36.8 %collective-permute-start.38 = (bf16[384,2048]{1,0:T(8,128)(2,1)S(1)}, bf16[384,2048]{1,0:T(8,128)(2,1)S(1)}, u32[]{:S(2)}, u32[]{:S(2)}) collective-permute-start(bf16[384,2048]{1,0:T(8,128)(2,1)S(1)} %copy-done.21), channel_id=1, source_target_pairs={{0,2},{1,3},{2,0},{3,1},{4,6},{5,7},{6,4},{7,5},{8,10},{9,11},{10,... | collective-permute-start | bytes 4718600 | tf_op jit(solution)/shard_map/ppermute | solution.py:310
  486.8 32.0 %collective-permute-start.37 = (bf16[384,2048]{1,0:T(8,128)(2,1)S(1)}, bf16[384,2048]{1,0:T(8,128)(2,1)S(1)}, u32[]{:S(2)}, u32[]{:S(2)}) collective-permute-start(bf16[384,2048]{1,0:T(8,128)(2,1)S(1)} %copy-done.21), channel_id=1, source_target_pairs={{0,1},{1,0},{2,3},{3,2},{4,5},{5,4},{6,7},{7,6},{8,9},{9,8},{10,11... | collective-permute-start | bytes 4718600 | tf_op jit(solution)/shard_map/ppermute | solution.py:310
  517.0 37.0 %collective-permute-start.29 = (bf16[384,2048]{1,0:T(8,128)(2,1)}, bf16[384,2048]{1,0:T(8,128)(2,1)S(1)}, u32[]{:S(2)}, u32[]{:S(2)}) collective-permute-start(bf16[384,2048]{1,0:T(8,128)(2,1)} %fusion.1), channel_id=1, source_target_pairs={{0,2},{1,3},{2,0},{3,1},{4,6},{5,7},{6,4},{7,5},{8,10},{9,11},{10,... | collective-permute-start | bytes 4718600 | tf_op jit(solution)/shard_map/ppermute | solution.py:310
  518.5 58.6 %collective-permute-start.27 = (bf16[384,2048]{1,0:T(8,128)(2,1)}, bf16[384,2048]{1,0:T(8,128)(2,1)}, u32[]{:S(2)}, u32[]{:S(2)}) collective-permute-start(bf16[384,2048]{1,0:T(8,128)(2,1)} %get-tuple-element.260), channel_id=1, source_target_pairs={{0,1},{1,0},{2,3},{3,2},{4,5},{5,4},{6,7},{7,6},{8,9},{9,8},{10,11... | collective-permute-start | bytes 4718600 | tf_op jit(solution)/shard_map/ppermute | solution.py:310
  598.4 36.1 %collective-permute-start.41 = (bf16[384,2048]{1,0:T(8,128)(2,1)}, bf16[384,2048]{1,0:T(8,128)(2,1)}, u32[]{:S(2)}, u32[]{:S(2)}) collective-permute-start(bf16[384,2048]{1,0:T(8,128)(2,1)} %fusion.4.refs_0_), channel_id=1, source_target_pairs={{0,2},{1,3},{2,0},{3,1},{4,6},{5,7},{6,4},{7,5},{8,10},{9,11},{10,... | collective-permute-start | bytes 4718600 | tf_op jit(solution)/shard_map/ppermute | solution.py:310
  644.6 36.9 %collective-permute-start.59 = (bf16[384,2048]{1,0:T(8,128)(2,1)S(1)}, bf16[384,2048]{1,0:T(8,128)(2,1)S(1)}, u32[]{:S(2)}, u32[]{:S(2)}) collective-permute-start(bf16[384,2048]{1,0:T(8,128)(2,1)S(1)} %add_convert_fusion), channel_id=1, source_target_pairs={{0,2},{1,3},{2,0},{3,1},{4,6},{5,7},{6,4},{7,5},{8,10},{9,11},{10,... | collective-permute-start | bytes 4718600 | tf_op jit(solution)/shard_map/ppermute | solution.py:310
  667.4 34.1 %collective-permute-start.40 = (bf16[384,2048]{1,0:T(8,128)(2,1)}, bf16[384,2048]{1,0:T(8,128)(2,1)}, u32[]{:S(2)}, u32[]{:S(2)}) collective-permute-start(bf16[384,2048]{1,0:T(8,128)(2,1)} %fusion.4.refs_0_), channel_id=1, source_target_pairs={{0,1},{1,0},{2,3},{3,2},{4,5},{5,4},{6,7},{7,6},{8,9},{9,8},{10,11... | collective-permute-start | bytes 4718600 | tf_op jit(solution)/shard_map/ppermute | solution.py:310
  667.4 36.0 %collective-permute-start.56 = (bf16[384,2048]{1,0:T(8,128)(2,1)}, bf16[384,2048]{1,0:T(8,128)(2,1)}, u32[]{:S(2)}, u32[]{:S(2)}) collective-permute-start(bf16[384,2048]{1,0:T(8,128)(2,1)} %collective-permute-done.41.refs_0_), channel_id=1, source_target_pairs={{0,1},{1,0},{2,3},{3,2},{4,5},{5,4},{6,7},{7,6},{8,9},{9,8},{10,11... | collective-permute-start | bytes 4718600 | tf_op jit(solution)/shard_map/ppermute | solution.py:310
  693.0 35.8 %collective-permute-start.60 = (bf16[384,2048]{1,0:T(8,128)(2,1)S(1)}, bf16[384,2048]{1,0:T(8,128)(2,1)S(1)}, u32[]{:S(2)}, u32[]{:S(2)}) collective-permute-start(bf16[384,2048]{1,0:T(8,128)(2,1)S(1)} %shard_map.320.refs_0_), channel_id=1, source_target_pairs={{0,2},{1,3},{2,0},{3,1},{4,6},{5,7},{6,4},{7,5},{8,10},{9,11},{10,... | collective-permute-start | bytes 4718600 | tf_op jit(solution)/shard_map/ppermute | solution.py:310
  728.8 32.0 %collective-permute-start.70 = (bf16[384,2048]{1,0:T(8,128)(2,1)S(1)}, bf16[384,2048]{1,0:T(8,128)(2,1)}, u32[]{:S(2)}, u32[]{:S(2)}) collective-permute-start(bf16[384,2048]{1,0:T(8,128)(2,1)S(1)} %collective-permute-done.60.refs_0_), channel_id=1, source_target_pairs={{0,1},{1,0},{2,3},{3,2},{4,5},{5,4},{6,7},{7,6},{8,9},{9,8},{10,11... | collective-permute-start | bytes 4718600 | tf_op jit(solution)/shard_map/ppermute | solution.py:310
  (163 other events, 2121.3 us)
Sparse Core Ops, SparseCore 0:
  12.8 208.7 all-gather.2
  224.4 137.1 all-gather.4
  370.6 116.7 reduce-scatter.2
  491.4 181.7 reduce-scatter.4
